TPU v7x, 32 devices: a whole 2x2x4 slice. The times are simulated.
32 devices in a mesh: dp: 4 (over y, x), pipe: 8 (over z, core).
Axes of the slice: x: 2, y: 2, z: 4, core: 2. Of those that a mesh axis runs over, the one named last changes fastest.
Arguments:
- activations: bfloat16 [8, 2048, 8192], P('pipe', 'dp'), may hold values from -6 to 6
- cotangent: bfloat16 [2048, 8192], P('dp'), may hold values from -6 to 6
- adapter_down: bfloat16 [8, 8192, 512], P('pipe'), may hold values from -0.0625 to 0.0625
- adapter_expand: bfloat16 [8, 512, 8192], P('pipe'), may hold values from -0.25 to 0.25
- value_rows: bfloat16 [8, 32, 8192], P('pipe', 'dp'), may hold values from -0.0625 to 0.0625
- input_rows: bfloat16 [8, 32, 8192], P('pipe', 'dp'), may hold values from -0.0625 to 0.0625
- hidden_cols: bfloat16 [8, 32, 512], P('pipe'), may hold values from -0.25 to 0.25
- inner_cols: bfloat16 [8, 32, 512], P('pipe'), may hold values from -0.25 to 0.25
- lengths: int32 [16], P('dp'), may hold values from 1 to 128, as said below
- query_example: int32 [32], replicated, may hold values from 0 to 15
Outputs:
- scores: float32 [16, 32], P('dp')
Inputs may be any that keep to these rules, and one draw needn't show every extreme that they name: `lengths`: live tokens of each example; the rest of its 128 positions is padding.
All inputs are finite; a program needn't handle non-finite values.
Results may differ from a plain program's by a relative error of at most 0.022.
Values may be sent and summed in bfloat16 or wider, within the bound.
No kernel may reach another device: no remote copies, remote signals or barrier semaphores. Data moves between devices by JAX's collectives and lax.ppermute only.
A program may use at most 128 MiB of HBM per device.

v0:
```python
import jax
import jax.numpy as jnp
from jax import lax
from jax.sharding import PartitionSpec as P

SLOT = 128


adapter_scale = 0.25


def from_behind(value, axis, steps):
    count = lax.axis_size(axis)
    first, last = (max(0, -steps), min(count, count - steps))
    return lax.ppermute(value, axis, [(source, source + steps) for source in range(first, last)])


def local(
    activations,
    cotangent,
    adapter_down,
    adapter_expand,
    value_rows,
    input_rows,
    hidden_cols,
    inner_cols,
    lengths,
    query_example,
):
    section_total = lax.axis_size("pipe")
    section_index = lax.axis_index("pipe")
    tok_dev = activations.shape[1]
    ex_dev = tok_dev // SLOT
    query_total = hidden_cols.shape[1]
    value_all, input_all = (
        lax.all_gather(value_rows[0], "dp", axis=0, tiled=True),
        lax.all_gather(input_rows[0], "dp", axis=0, tiled=True),
    )
    down_map = adapter_down[0]
    up_map = adapter_expand[0]
    hid_factor = hidden_cols[0]
    inn_factor = inner_cols[0]
    act_local = activations[0]
    block_rows = SLOT
    block_count = tok_dev // block_rows
    step_count = block_count + section_total - 1
    is_last = section_index == section_total - 1

    def advance(step_index, carry):
        incoming, per_token = carry
        block_index = step_index - (section_total - 1 - section_index)
        is_valid = (block_index >= 0) & (block_index < block_count)
        row_start = jnp.clip(block_index, 0, block_count - 1) * block_rows
        seed_rows = lax.dynamic_slice_in_dim(cotangent, row_start, block_rows, 0)
        gradient_leaving = jnp.where(is_last, seed_rows, incoming)

        def compute(unused):
            act_rows = lax.dynamic_slice_in_dim(act_local, row_start, block_rows, 0)
            hidden = jnp.dot(act_rows, down_map, preferred_element_type=jnp.float32).astype(
                jnp.bfloat16
            )
            inner_gradient = (
                adapter_scale
                * jnp.einsum(
                    "td,rd->tr", gradient_leaving, up_map, preferred_element_type=jnp.float32
                )
            ).astype(jnp.bfloat16)
            gradient_entering = (
                gradient_leaving.astype(jnp.float32)
                + jnp.einsum(
                    "tr,dr->td", inner_gradient, down_map, preferred_element_type=jnp.float32
                )
            ).astype(jnp.bfloat16)
            hidden_projection = jnp.einsum(
                "tr,qr->tq", hidden, hid_factor, preferred_element_type=jnp.float32
            )
            value_projection = jnp.einsum(
                "td,qd->tq", gradient_leaving, value_all, preferred_element_type=jnp.float32
            )
            input_projection = jnp.einsum(
                "td,qd->tq", act_rows, input_all, preferred_element_type=jnp.float32
            )
            inner_projection = jnp.einsum(
                "tr,qr->tq", inner_gradient, inn_factor, preferred_element_type=jnp.float32
            )
            return (
                gradient_entering,
                adapter_scale * hidden_projection * value_projection
                + input_projection * inner_projection,
            )

        def skipped(unused):
            return (
                jnp.zeros_like(gradient_leaving),
                jnp.zeros((block_rows, query_total), jnp.float32),
            )

        gradient_entering, summand_rows = lax.cond(is_valid, compute, skipped, 0)
        previous = lax.dynamic_slice_in_dim(per_token, row_start, block_rows, 0)
        per_token = lax.dynamic_update_slice_in_dim(
            per_token, previous + summand_rows, row_start, 0
        )
        incoming = from_behind(gradient_entering, "pipe", -1)
        return (incoming, per_token)

    start_grad = jnp.zeros((block_rows, act_local.shape[1]), jnp.bfloat16)
    start_terms = jnp.zeros((tok_dev, query_total), jnp.float32)
    final_grad, per_token = lax.fori_loop(0, step_count, advance, (start_grad, start_terms))
    offsets = lax.broadcasted_iota(jnp.int32, (tok_dev,), 0) % SLOT
    live_mask = (offsets < jnp.repeat(lengths, SLOT, total_repeat_length=tok_dev)).astype(
        jnp.float32
    )
    masked = per_token * live_mask[:, None]
    local_sums = jnp.sum(masked.reshape(ex_dev, SLOT, query_total), axis=1)
    totals = lax.psum(local_sums, "pipe") * SLOT ** (-0.5)
    example_ids = lax.axis_index("dp") * ex_dev + lax.broadcasted_iota(jnp.int32, (ex_dev,), 0)
    keep_mask = (example_ids[:, None] != query_example[None, :]).astype(jnp.float32)
    return totals * keep_mask


def solution(mesh):
    in_specs = (
        P("pipe", "dp", None),
        P("dp", None),
        P("pipe", None, None),
        P("pipe", None, None),
        P("pipe", "dp", None),
        P("pipe", "dp", None),
        P("pipe", None, None),
        P("pipe", None, None),
        P("dp"),
        P(),
    )
    out_specs = P("dp", None)
    return jax.shard_map(local, mesh=mesh, in_specs=in_specs, out_specs=out_specs, check_vma=False)
```

profile of v0, /device:TPU:0, one launch (start us, length us, event | category | flops | bytes accessed | tf_op | source)
XLA Modules:
  0.0 512.1 jit_solution(4357237131172630051)
XLA Ops:
  0.0 12.0 %all-gather = bf16[1,32,8192]{2,1,0:T(8,128)(2,1)S(1)} all-gather(bf16[1,8,8192]{2,1,0:T(8,128)(2,1)} %param.20), channel_id=2, replica_groups=mesh['dp'=4,'pipe'=8] {'dp'}, dimensions={1}, use_global_device_ids=true | all-gather | bytes 655360 | tf_op jit(solution)/shard_map/all_gather | solution.py:36
  12.0 10.4 %all-gather.1 = bf16[1,32,8192]{2,1,0:T(8,128)(2,1)S(1)} all-gather(bf16[1,8,8192]{2,1,0:T(8,128)(2,1)} %param.21), channel_id=3, replica_groups=mesh['dp'=4,'pipe'=8] {'dp'}, dimensions={1}, use_global_device_ids=true | all-gather | bytes 655360 | tf_op jit(solution)/shard_map/all_gather | solution.py:37
  22.6 437.8 %while.18 = (s32[]{:T(128)}, bf16[128,8192]{1,0:T(8,128)(2,1)S(1)}, f32[512,32]{0,1:T(8,128)S(1)}, s32[]{:T(128)}, pred[]{:T(512)}, /*index=5*/bf16[512,8192]{1,...) while((s32[]{:T(128)}, bf16[128,8192]{1,0:T(8,128)(2,1)S(1)}, ...), condition=%wide.region_3.4_spmd, body=%wide.region_0.3_spmd.sunk | while | flops 3368243200 | bytes 79266320 | solution.py:108
  33.3 25.7 %collective-permute-done = bf16[128,8192]{1,0:T(8,128)(2,1)S(1)} collective-permute-done((bf16[128,8192]{1,0:T(8,128)(2,1)}, bf16[128,8192]{1,0:T(8,128)(2,1)S(1)}, u32[]{:S(2)}, u32[]{:S(2)}) %collective-permute-start) | collective-permute-done | bytes 2097184 | tf_op jit(solution)/shard_map/while/body/eval_jaxpr/ppermute | solution.py:15
  61.9 26.2 %collective-permute-done = bf16[128,8192]{1,0:T(8,128)(2,1)S(1)} collective-permute-done((bf16[128,8192]{1,0:T(8,128)(2,1)}, bf16[128,8192]{1,0:T(8,128)(2,1)S(1)}, u32[]{:S(2)}, u32[]{:S(2)}) %collective-permute-start) | collective-permute-done | bytes 2097184 | tf_op jit(solution)/shard_map/while/body/eval_jaxpr/ppermute | solution.py:15
  91.0 26.2 %collective-permute-done = bf16[128,8192]{1,0:T(8,128)(2,1)S(1)} collective-permute-done((bf16[128,8192]{1,0:T(8,128)(2,1)}, bf16[128,8192]{1,0:T(8,128)(2,1)S(1)}, u32[]{:S(2)}, u32[]{:S(2)}) %collective-permute-start) | collective-permute-done | bytes 2097184 | tf_op jit(solution)/shard_map/while/body/eval_jaxpr/ppermute | solution.py:15
  120.1 26.2 %collective-permute-done = bf16[128,8192]{1,0:T(8,128)(2,1)S(1)} collective-permute-done((bf16[128,8192]{1,0:T(8,128)(2,1)}, bf16[128,8192]{1,0:T(8,128)(2,1)S(1)}, u32[]{:S(2)}, u32[]{:S(2)}) %collective-permute-start) | collective-permute-done | bytes 2097184 | tf_op jit(solution)/shard_map/while/body/eval_jaxpr/ppermute | solution.py:15
  149.2 26.2 %collective-permute-done = bf16[128,8192]{1,0:T(8,128)(2,1)S(1)} collective-permute-done((bf16[128,8192]{1,0:T(8,128)(2,1)}, bf16[128,8192]{1,0:T(8,128)(2,1)S(1)}, u32[]{:S(2)}, u32[]{:S(2)}) %collective-permute-start) | collective-permute-done | bytes 2097184 | tf_op jit(solution)/shard_map/while/body/eval_jaxpr/ppermute | solution.py:15
  178.3 104.1 %collective-permute-done = bf16[128,8192]{1,0:T(8,128)(2,1)S(1)} collective-permute-done((bf16[128,8192]{1,0:T(8,128)(2,1)}, bf16[128,8192]{1,0:T(8,128)(2,1)S(1)}, u32[]{:S(2)}, u32[]{:S(2)}) %collective-permute-start) | collective-permute-done | bytes 2097184 | tf_op jit(solution)/shard_map/while/body/eval_jaxpr/ppermute | solution.py:15
  282.4 22.1 %conditional.2 = (bf16[128,8192]{1,0:T(8,128)(2,1)}, f32[128,32]{0,1:T(8,128)S(1)}) conditional(s32[]{:T(128)} %convert_element_type.46, () %tuple.54, (pred[]{:T(512)}, bf16[512,8192]{1,0:T(8,128)(2,1)}, s32[]{:T(128)}, bf16[128,8192]{1,0:T(8,128)(2,1)S(1)}, bf16[512,8192]{1,0:T(8,128)(2,1)}, /*index=5*/bf16[8192,512]{1,0:T(8,128)(2,1)}, s32[]{:T(128)}, ...), branch_computations={%region_1.1_spmd, %region_2.2_spmd} | conditional | flops 3368239104 | bytes 70828144 | solution.py:98
  285.0 6.5 %fusion.5 = bf16[128,512]{1,0:T(8,128)(2,1)S(1)} fusion(bf16[128,8192]{1,0:T(8,128)(2,1)S(1)} %dynamic-slice_select_fusion, bf16[512,8192]{1,0:T(8,128)(2,1)} %get-tuple-element.354), kind=kOutput, calls=%fused_computation.8 | convolution fusion | flops 1073872896 | bytes 10616832 | tf_op jit(solution)/shard_map/while/body/eval_jaxpr/cond/branch_1_fun/td,rd->tr/dot_general | solution.py:64
  296.5 5.5 %fusion.15 = f32[128,32]{0,1:T(8,128)S(1)} fusion(f32[128,32]{0,1:T(8,128)S(1)} %fusion.30, bf16[32,512]{1,0:T(8,128)(2,1)S(1)} %get-tuple-element.358, bf16[8192,512]{1,0:T(8,128)(2,1)} %get-tuple-element.355, bf16[512,8192]{1,0:T(8,128)(2,1)} %get-tuple-element.356, s32[]{:T(128)S(6)} %select_n.71), kind=kOutput, calls=%fused_computation.12 | convolution fusion | flops 1078009856 | bytes 10551300 | tf_op jit(solution)/shard_map/while/body/eval_jaxpr/cond/branch_1_fun/tr,qr->tq/dot_general | solution.py:74
  305.8 26.2 %collective-permute-done = bf16[128,8192]{1,0:T(8,128)(2,1)S(1)} collective-permute-done((bf16[128,8192]{1,0:T(8,128)(2,1)}, bf16[128,8192]{1,0:T(8,128)(2,1)S(1)}, u32[]{:S(2)}, u32[]{:S(2)}) %collective-permute-start) | collective-permute-done | bytes 2097184 | tf_op jit(solution)/shard_map/while/body/eval_jaxpr/ppermute | solution.py:15
  332.1 22.1 %conditional.2 = (bf16[128,8192]{1,0:T(8,128)(2,1)}, f32[128,32]{0,1:T(8,128)S(1)}) conditional(s32[]{:T(128)} %convert_element_type.46, () %tuple.54, (pred[]{:T(512)}, bf16[512,8192]{1,0:T(8,128)(2,1)}, s32[]{:T(128)}, bf16[128,8192]{1,0:T(8,128)(2,1)S(1)}, bf16[512,8192]{1,0:T(8,128)(2,1)}, /*index=5*/bf16[8192,512]{1,0:T(8,128)(2,1)}, s32[]{:T(128)}, ...), branch_computations={%region_1.1_spmd, %region_2.2_spmd} | conditional | flops 3368239104 | bytes 70828144 | solution.py:98
  334.6 6.5 %fusion.5 = bf16[128,512]{1,0:T(8,128)(2,1)S(1)} fusion(bf16[128,8192]{1,0:T(8,128)(2,1)S(1)} %dynamic-slice_select_fusion, bf16[512,8192]{1,0:T(8,128)(2,1)} %get-tuple-element.354), kind=kOutput, calls=%fused_computation.8 | convolution fusion | flops 1073872896 | bytes 10616832 | tf_op jit(solution)/shard_map/while/body/eval_jaxpr/cond/branch_1_fun/td,rd->tr/dot_general | solution.py:64
  355.5 26.2 %collective-permute-done = bf16[128,8192]{1,0:T(8,128)(2,1)S(1)} collective-permute-done((bf16[128,8192]{1,0:T(8,128)(2,1)}, bf16[128,8192]{1,0:T(8,128)(2,1)S(1)}, u32[]{:S(2)}, u32[]{:S(2)}) %collective-permute-start) | collective-permute-done | bytes 2097184 | tf_op jit(solution)/shard_map/while/body/eval_jaxpr/ppermute | solution.py:15
  381.7 22.1 %conditional.2 = (bf16[128,8192]{1,0:T(8,128)(2,1)}, f32[128,32]{0,1:T(8,128)S(1)}) conditional(s32[]{:T(128)} %convert_element_type.46, () %tuple.54, (pred[]{:T(512)}, bf16[512,8192]{1,0:T(8,128)(2,1)}, s32[]{:T(128)}, bf16[128,8192]{1,0:T(8,128)(2,1)S(1)}, bf16[512,8192]{1,0:T(8,128)(2,1)}, /*index=5*/bf16[8192,512]{1,0:T(8,128)(2,1)}, s32[]{:T(128)}, ...), branch_computations={%region_1.1_spmd, %region_2.2_spmd} | conditional | flops 3368239104 | bytes 70828144 | solution.py:98
  384.3 6.5 %fusion.5 = bf16[128,512]{1,0:T(8,128)(2,1)S(1)} fusion(bf16[128,8192]{1,0:T(8,128)(2,1)S(1)} %dynamic-slice_select_fusion, bf16[512,8192]{1,0:T(8,128)(2,1)} %get-tuple-element.354), kind=kOutput, calls=%fused_computation.8 | convolution fusion | flops 1073872896 | bytes 10616832 | tf_op jit(solution)/shard_map/while/body/eval_jaxpr/cond/branch_1_fun/td,rd->tr/dot_general | solution.py:64
  395.8 5.5 %fusion.15 = f32[128,32]{0,1:T(8,128)S(1)} fusion(f32[128,32]{0,1:T(8,128)S(1)} %fusion.30, bf16[32,512]{1,0:T(8,128)(2,1)S(1)} %get-tuple-element.358, bf16[8192,512]{1,0:T(8,128)(2,1)} %get-tuple-element.355, bf16[512,8192]{1,0:T(8,128)(2,1)} %get-tuple-element.356, s32[]{:T(128)S(6)} %select_n.71), kind=kOutput, calls=%fused_computation.12 | convolution fusion | flops 1078009856 | bytes 10551300 | tf_op jit(solution)/shard_map/while/body/eval_jaxpr/cond/branch_1_fun/tr,qr->tq/dot_general | solution.py:74
  405.1 26.1 %collective-permute-done = bf16[128,8192]{1,0:T(8,128)(2,1)S(1)} collective-permute-done((bf16[128,8192]{1,0:T(8,128)(2,1)}, bf16[128,8192]{1,0:T(8,128)(2,1)S(1)}, u32[]{:S(2)}, u32[]{:S(2)}) %collective-permute-start) | collective-permute-done | bytes 2097184 | tf_op jit(solution)/shard_map/while/body/eval_jaxpr/ppermute | solution.py:15
  431.3 22.0 %conditional.2 = (bf16[128,8192]{1,0:T(8,128)(2,1)}, f32[128,32]{0,1:T(8,128)S(1)}) conditional(s32[]{:T(128)} %convert_element_type.46, () %tuple.54, (pred[]{:T(512)}, bf16[512,8192]{1,0:T(8,128)(2,1)}, s32[]{:T(128)}, bf16[128,8192]{1,0:T(8,128)(2,1)S(1)}, bf16[512,8192]{1,0:T(8,128)(2,1)}, /*index=5*/bf16[8192,512]{1,0:T(8,128)(2,1)}, s32[]{:T(128)}, ...), branch_computations={%region_1.1_spmd, %region_2.2_spmd} | conditional | flops 3368239104 | bytes 70828144 | solution.py:98
  433.8 6.5 %fusion.5 = bf16[128,512]{1,0:T(8,128)(2,1)S(1)} fusion(bf16[128,8192]{1,0:T(8,128)(2,1)S(1)} %dynamic-slice_select_fusion, bf16[512,8192]{1,0:T(8,128)(2,1)} %get-tuple-element.354), kind=kOutput, calls=%fused_computation.8 | convolution fusion | flops 1073872896 | bytes 10616832 | tf_op jit(solution)/shard_map/while/body/eval_jaxpr/cond/branch_1_fun/td,rd->tr/dot_general | solution.py:64
  454.6 5.8 %collective-permute-done = bf16[128,8192]{1,0:T(8,128)(2,1)S(1)} collective-permute-done((bf16[128,8192]{1,0:T(8,128)(2,1)}, bf16[128,8192]{1,0:T(8,128)(2,1)S(1)}, u32[]{:S(2)}, u32[]{:S(2)}) %collective-permute-start) | collective-permute-done | bytes 2097184 | tf_op jit(solution)/shard_map/while/body/eval_jaxpr/ppermute | solution.py:15
  463.8 47.6 %psum.7 = f32[4,32]{0,1:T(8,128)S(1)} all-reduce(f32[4,32]{0,1:T(8,128)S(1)} %reduce_sum.9), channel_id=1, replica_groups=mesh['dp'=4,'pipe'=8] {'pipe'}, use_global_device_ids=true, to_apply=%region_5.6 | all-reduce | flops 128 | bytes 1024 | tf_op jit(solution)/shard_map/psum | solution.py:115
  (107 shorter events, 96.6 us)
Async XLA Ops:
  0.0 22.6 %copy-start = (bf16[1,32,512]{2,1,0:T(8,128)(2,1)S(1)}, bf16[1,32,512]{2,1,0:T(8,128)(2,1)}, u32[]{:S(2)}) copy-start(bf16[1,32,512]{2,1,0:T(8,128)(2,1)} %param.22) | copy-start | bytes 98308
  0.0 22.6 %copy-start.1 = (bf16[1,32,512]{2,1,0:T(8,128)(2,1)S(1)}, bf16[1,32,512]{2,1,0:T(8,128)(2,1)}, u32[]{:S(2)}) copy-start(bf16[1,32,512]{2,1,0:T(8,128)(2,1)} %param.23) | copy-start | bytes 98308
  22.6 437.8 %copy-start.2 = (s32[4]{0:T(128)S(1)}, s32[4]{0:T(128)}, u32[]{:S(2)}) copy-start(s32[4]{0:T(128)} %param.24) | copy-start | bytes 52
  22.6 488.8 %copy-start.3 = (s32[32]{0:T(128)S(1)}, s32[32]{0:T(128)}, u32[]{:S(2)}) copy-start(s32[32]{0:T(128)} %param.25) | copy-start | bytes 388
  24.2 6.3 %collective-permute-start = (bf16[128,8192]{1,0:T(8,128)(2,1)}, bf16[128,8192]{1,0:T(8,128)(2,1)S(1)}, u32[]{:S(2)}, u32[]{:S(2)}) collective-permute-start(bf16[128,8192]{1,0:T(8,128)(2,1)} %get-tuple-element.491), channel_id=1, source_target_pairs={{1,0},{2,1},{3,2},{4,3},{5,4},{6,5},{7,6},{9,8},{10,9},{11,10},{12... | collective-permute-start | bytes 6291464 | tf_op jit(solution)/shard_map/while/body/eval_jaxpr/ppermute | solution.py:15
  32.0 27.0 %collective-permute-start = (bf16[128,8192]{1,0:T(8,128)(2,1)}, bf16[128,8192]{1,0:T(8,128)(2,1)S(1)}, u32[]{:S(2)}, u32[]{:S(2)}) collective-permute-start(bf16[128,8192]{1,0:T(8,128)(2,1)} %get-tuple-element.491), channel_id=1, source_target_pairs={{1,0},{2,1},{3,2},{4,3},{5,4},{6,5},{7,6},{9,8},{10,9},{11,10},{12... | collective-permute-start | bytes 6291464 | tf_op jit(solution)/shard_map/while/body/eval_jaxpr/ppermute | solution.py:15
  60.6 27.6 %collective-permute-start = (bf16[128,8192]{1,0:T(8,128)(2,1)}, bf16[128,8192]{1,0:T(8,128)(2,1)S(1)}, u32[]{:S(2)}, u32[]{:S(2)}) collective-permute-start(bf16[128,8192]{1,0:T(8,128)(2,1)} %get-tuple-element.491), channel_id=1, source_target_pairs={{1,0},{2,1},{3,2},{4,3},{5,4},{6,5},{7,6},{9,8},{10,9},{11,10},{12... | collective-permute-start | bytes 6291464 | tf_op jit(solution)/shard_map/while/body/eval_jaxpr/ppermute | solution.py:15
  89.7 27.6 %collective-permute-start = (bf16[128,8192]{1,0:T(8,128)(2,1)}, bf16[128,8192]{1,0:T(8,128)(2,1)S(1)}, u32[]{:S(2)}, u32[]{:S(2)}) collective-permute-start(bf16[128,8192]{1,0:T(8,128)(2,1)} %get-tuple-element.491), channel_id=1, source_target_pairs={{1,0},{2,1},{3,2},{4,3},{5,4},{6,5},{7,6},{9,8},{10,9},{11,10},{12... | collective-permute-start | bytes 6291464 | tf_op jit(solution)/shard_map/while/body/eval_jaxpr/ppermute | solution.py:15
  118.8 27.6 %collective-permute-start = (bf16[128,8192]{1,0:T(8,128)(2,1)}, bf16[128,8192]{1,0:T(8,128)(2,1)S(1)}, u32[]{:S(2)}, u32[]{:S(2)}) collective-permute-start(bf16[128,8192]{1,0:T(8,128)(2,1)} %get-tuple-element.491), channel_id=1, source_target_pairs={{1,0},{2,1},{3,2},{4,3},{5,4},{6,5},{7,6},{9,8},{10,9},{11,10},{12... | collective-permute-start | bytes 6291464 | tf_op jit(solution)/shard_map/while/body/eval_jaxpr/ppermute | solution.py:15
  147.9 27.6 %collective-permute-start = (bf16[128,8192]{1,0:T(8,128)(2,1)}, bf16[128,8192]{1,0:T(8,128)(2,1)S(1)}, u32[]{:S(2)}, u32[]{:S(2)}) collective-permute-start(bf16[128,8192]{1,0:T(8,128)(2,1)} %get-tuple-element.491), channel_id=1, source_target_pairs={{1,0},{2,1},{3,2},{4,3},{5,4},{6,5},{7,6},{9,8},{10,9},{11,10},{12... | collective-permute-start | bytes 6291464 | tf_op jit(solution)/shard_map/while/body/eval_jaxpr/ppermute | solution.py:15
  177.0 105.4 %collective-permute-start = (bf16[128,8192]{1,0:T(8,128)(2,1)}, bf16[128,8192]{1,0:T(8,128)(2,1)S(1)}, u32[]{:S(2)}, u32[]{:S(2)}) collective-permute-start(bf16[128,8192]{1,0:T(8,128)(2,1)} %get-tuple-element.491), channel_id=1, source_target_pairs={{1,0},{2,1},{3,2},{4,3},{5,4},{6,5},{7,6},{9,8},{10,9},{11,10},{12... | collective-permute-start | bytes 6291464 | tf_op jit(solution)/shard_map/while/body/eval_jaxpr/ppermute | solution.py:15
  282.4 9.0 %slice-start = ((s8[8388608]{0:T(1024)(128)(4,1)}), s8[4194304]{0:T(1024)(128)(4,1)S(1)}, s32[]{:S(2)}) async-start(s8[8388608]{0:T(1024)(128)(4,1)} %bitcast.40), calls=%async_computation | async-start | bytes 8388608 | tf_op jit(solution)/shard_map/while/body/eval_jaxpr/cond
  285.0 6.5 %slice-start.1 = ((s8[8388608]{0:T(1024)(128)(4,1)}), s8[4194304]{0:T(1024)(128)(4,1)S(1)}, s32[]{:S(2)}) async-start(s8[8388608]{0:T(1024)(128)(4,1)} %bitcast.40), calls=%async_computation.1 | async-start | bytes 8388608 | tf_op jit(solution)/shard_map/while/body/eval_jaxpr/cond
  304.5 27.6 %collective-permute-start = (bf16[128,8192]{1,0:T(8,128)(2,1)}, bf16[128,8192]{1,0:T(8,128)(2,1)S(1)}, u32[]{:S(2)}, u32[]{:S(2)}) collective-permute-start(bf16[128,8192]{1,0:T(8,128)(2,1)} %get-tuple-element.491), channel_id=1, source_target_pairs={{1,0},{2,1},{3,2},{4,3},{5,4},{6,5},{7,6},{9,8},{10,9},{11,10},{12... | collective-permute-start | bytes 6291464 | tf_op jit(solution)/shard_map/while/body/eval_jaxpr/ppermute | solution.py:15
  332.1 9.0 %slice-start = ((s8[8388608]{0:T(1024)(128)(4,1)}), s8[4194304]{0:T(1024)(128)(4,1)S(1)}, s32[]{:S(2)}) async-start(s8[8388608]{0:T(1024)(128)(4,1)} %bitcast.40), calls=%async_computation | async-start | bytes 8388608 | tf_op jit(solution)/shard_map/while/body/eval_jaxpr/cond
  334.6 6.5 %slice-start.1 = ((s8[8388608]{0:T(1024)(128)(4,1)}), s8[4194304]{0:T(1024)(128)(4,1)S(1)}, s32[]{:S(2)}) async-start(s8[8388608]{0:T(1024)(128)(4,1)} %bitcast.40), calls=%async_computation.1 | async-start | bytes 8388608 | tf_op jit(solution)/shard_map/while/body/eval_jaxpr/cond
  354.2 27.6 %collective-permute-start = (bf16[128,8192]{1,0:T(8,128)(2,1)}, bf16[128,8192]{1,0:T(8,128)(2,1)S(1)}, u32[]{:S(2)}, u32[]{:S(2)}) collective-permute-start(bf16[128,8192]{1,0:T(8,128)(2,1)} %get-tuple-element.491), channel_id=1, source_target_pairs={{1,0},{2,1},{3,2},{4,3},{5,4},{6,5},{7,6},{9,8},{10,9},{11,10},{12... | collective-permute-start | bytes 6291464 | tf_op jit(solution)/shard_map/while/body/eval_jaxpr/ppermute | solution.py:15
  381.7 9.0 %slice-start = ((s8[8388608]{0:T(1024)(128)(4,1)}), s8[4194304]{0:T(1024)(128)(4,1)S(1)}, s32[]{:S(2)}) async-start(s8[8388608]{0:T(1024)(128)(4,1)} %bitcast.40), calls=%async_computation | async-start | bytes 8388608 | tf_op jit(solution)/shard_map/while/body/eval_jaxpr/cond
  384.3 6.5 %slice-start.1 = ((s8[8388608]{0:T(1024)(128)(4,1)}), s8[4194304]{0:T(1024)(128)(4,1)S(1)}, s32[]{:S(2)}) async-start(s8[8388608]{0:T(1024)(128)(4,1)} %bitcast.40), calls=%async_computation.1 | async-start | bytes 8388608 | tf_op jit(solution)/shard_map/while/body/eval_jaxpr/cond
  403.8 27.5 %collective-permute-start = (bf16[128,8192]{1,0:T(8,128)(2,1)}, bf16[128,8192]{1,0:T(8,128)(2,1)S(1)}, u32[]{:S(2)}, u32[]{:S(2)}) collective-permute-start(bf16[128,8192]{1,0:T(8,128)(2,1)} %get-tuple-element.491), channel_id=1, source_target_pairs={{1,0},{2,1},{3,2},{4,3},{5,4},{6,5},{7,6},{9,8},{10,9},{11,10},{12... | collective-permute-start | bytes 6291464 | tf_op jit(solution)/shard_map/while/body/eval_jaxpr/ppermute | solution.py:15
  431.3 9.0 %slice-start = ((s8[8388608]{0:T(1024)(128)(4,1)}), s8[4194304]{0:T(1024)(128)(4,1)S(1)}, s32[]{:S(2)}) async-start(s8[8388608]{0:T(1024)(128)(4,1)} %bitcast.40), calls=%async_computation | async-start | bytes 8388608 | tf_op jit(solution)/shard_map/while/body/eval_jaxpr/cond
  433.8 6.5 %slice-start.1 = ((s8[8388608]{0:T(1024)(128)(4,1)}), s8[4194304]{0:T(1024)(128)(4,1)S(1)}, s32[]{:S(2)}) async-start(s8[8388608]{0:T(1024)(128)(4,1)} %bitcast.40), calls=%async_computation.1 | async-start | bytes 8388608 | tf_op jit(solution)/shard_map/while/body/eval_jaxpr/cond
  453.2 7.1 %collective-permute-start = (bf16[128,8192]{1,0:T(8,128)(2,1)}, bf16[128,8192]{1,0:T(8,128)(2,1)S(1)}, u32[]{:S(2)}, u32[]{:S(2)}) collective-permute-start(bf16[128,8192]{1,0:T(8,128)(2,1)} %get-tuple-element.491), channel_id=1, source_target_pairs={{1,0},{2,1},{3,2},{4,3},{5,4},{6,5},{7,6},{9,8},{10,9},{11,10},{12... | collective-permute-start | bytes 6291464 | tf_op jit(solution)/shard_map/while/body/eval_jaxpr/ppermute | solution.py:15
where the time goes:
time: 513 us; the launch traced here: 512 us
  waiting for transfers between devices  324 us (63%)
  matrix products  77.8 us (15%)
  blocking collectives  69.9 us (14%)
  starting transfers between devices  14.2 us (3%)
  other arithmetic  13 us (3%)
  local copies, waits for them, and re-layouts  12.5 us (2%)
    ppermute x11, waiting for transfers between devices, from_behind(): lax.ppermute(value, axis, [(source, source + steps) for source in range(f...  324 us
    psum x1, blocking collectives, local(): totals = lax.psum(local_sums, 'pipe') * SLOT ** (-0.5)  47.6 us
    dot_general x4, matrix products, compute(): jnp.einsum('td,rd->tr', gradient_leaving, up_map, preferred_element_type=...  25.8 us
    dot_general x4, matrix products, compute(): jnp.einsum('tr,qr->tq', hidden, hid_factor, preferred_element_type=jnp.fl...  21.8 us
    dot_general x4, matrix products, compute(): jnp.einsum('tr,dr->td', inner_gradient, down_map, preferred_element_type=...  16.8 us
    ppermute x11, starting transfers between devices, from_behind(): lax.ppermute(value, axis, [(source, source + steps) for source in range(f...  14.2 us
    all_gather x1, blocking collectives, local(): lax.all_gather(value_rows[0], 'dp', axis=0, tiled=True)  12 us
    another operation x15, local copies, waits for them, and re-layouts  11.1 us
  transfers between devices with their start and end apart: 11, of which 11 were waited for; matrix products, arithmetic and copies ran while one was open for 0% of the time, Pallas kernels for 0%

commit v1 on v0

v1 whole, which is shorter than its diff:
```python
import jax
import jax.numpy as jnp
from jax import lax
from jax.sharding import PartitionSpec as P

SLOT = 128


adapter_scale = 0.25


def dot_nn(a, b):
    return lax.dot_general(a, b, (((1,), (0,)), ((), ())), preferred_element_type=jnp.float32)


def dot_nt(a, b):
    return lax.dot_general(a, b, (((1,), (1,)), ((), ())), preferred_element_type=jnp.float32)


def swap(value, axis, distance):
    count = lax.axis_size(axis)
    return lax.ppermute(value, axis, [(source, source ^ distance) for source in range(count)])


def upward(value, axis):
    count = lax.axis_size(axis)
    return lax.ppermute(value, axis, [(source, source + 1) for source in range(count - 1)])


def local(
    activations,
    cotangent,
    adapter_down,
    adapter_expand,
    value_rows,
    input_rows,
    hidden_cols,
    inner_cols,
    lengths,
    query_example,
):
    columns = lax.axis_size("dp")
    layers = lax.axis_size("pipe")
    column = lax.axis_index("dp")
    layer = lax.axis_index("pipe")
    tok_dev = activations.shape[1]
    ex_dev = tok_dev // SLOT
    q_dev = value_rows.shape[1]
    act = activations[0]
    down = adapter_down[0]
    expand = adapter_expand[0]
    values = value_rows[0]
    inputs = input_rows[0]
    bf16 = jnp.bfloat16

    def relative(rows):
        return [
            lax.dynamic_slice_in_dim(rows, (column ^ d) * q_dev, q_dev, 0) for d in range(columns)
        ]

    hid_blocks = relative(hidden_cols[0])
    inn_blocks = relative(inner_cols[0])
    own = jnp.concatenate([values, inputs])
    blocks = [own] + [swap(own, "dp", d) for d in range(1, columns)]
    value_all = jnp.concatenate([b[:q_dev] for b in blocks])
    input_all = jnp.concatenate([b[q_dev:] for b in blocks])
    hid_all = jnp.concatenate(hid_blocks)
    inn_all = jnp.concatenate(inn_blocks)

    raised = (adapter_scale * dot_nn(inn_blocks[0], expand)).astype(bf16)
    moving = jnp.concatenate([values, raised])
    seen = []
    for step in range(layers - 1):
        arrived = upward(moving, "pipe")
        ranks = dot_nn(arrived, down).astype(bf16)
        seen.append(ranks)
        if step < layers - 2:
            moving = (
                arrived.astype(jnp.float32) + adapter_scale * dot_nn(ranks, expand)
            ).astype(bf16)

    hidden = dot_nn(act, down).astype(bf16)
    offsets = lax.broadcasted_iota(jnp.int32, (ex_dev, SLOT, 1), 1)
    live = (offsets < lengths[:, None, None]).astype(jnp.float32).reshape(tok_dev, 1)
    weight = live * SLOT ** (-0.5)
    left = jnp.concatenate(
        [adapter_scale * dot_nt(hidden, hid_all), dot_nt(act, input_all)], axis=1
    ) * weight
    lifted = (adapter_scale * dot_nt(cotangent, expand)).astype(bf16)
    right = jnp.concatenate([dot_nt(cotangent, value_all), dot_nt(lifted, inn_all)], axis=1)
    terms = left * right

    stack = left.astype(bf16)[None]
    order = 1
    while order < layers:
        stack = jnp.concatenate([stack, swap(stack, "pipe", order)])
        order *= 2

    for step, ranks in enumerate(seen):
        every = [ranks] + [swap(ranks, "dp", d) for d in range(1, columns)]
        every = jnp.concatenate([b[:q_dev] for b in every] + [b[q_dev:] for b in every])
        source = jnp.maximum(layer - 1 - step, 0)
        weights = lax.dynamic_index_in_dim(stack, source ^ layer, 0, keepdims=False)
        terms = terms + weights.astype(jnp.float32) * dot_nt(lifted, every)

    sums = jnp.sum(terms.reshape(ex_dev, SLOT, -1), axis=1)
    q_all = columns * q_dev
    sums = sums[:, :q_all] + sums[:, q_all:]
    order = 1
    while order < layers:
        sums = sums + swap(sums, "pipe", order)
        order *= 2

    sums = sums.reshape(ex_dev, columns, q_dev)
    totals = jnp.concatenate(
        [lax.dynamic_index_in_dim(sums, column ^ c, 1, keepdims=False) for c in range(columns)],
        axis=1,
    )
    example_ids = column * ex_dev + lax.broadcasted_iota(jnp.int32, (ex_dev,), 0)
    keep_mask = (example_ids[:, None] != query_example[None, :]).astype(jnp.float32)
    return totals * keep_mask


def solution(mesh):
    in_specs = (
        P("pipe", "dp", None),
        P("dp", None),
        P("pipe", None, None),
        P("pipe", None, None),
        P("pipe", "dp", None),
        P("pipe", "dp", None),
        P("pipe", None, None),
        P("pipe", None, None),
        P("dp"),
        P(),
    )
    out_specs = P("dp", None)
    return jax.shard_map(local, mesh=mesh, in_specs=in_specs, out_specs=out_specs, check_vma=False)
```

time: 513 us -> 157 us (0.31)
  waiting for transfers between devices: 324 us -> 17.6 us
  blocking collectives: 69.9 us -> 0 us
  starting transfers between devices: 14.2 us -> 74.3 us
  matrix products: 77.8 us -> 53.8 us
  other arithmetic: 13 us -> 2.6 us
  local copies, waits for them, and re-layouts: 12.5 us -> 7.06 us
    ppermute x11 -> x37, waiting for transfers between devices: 324 us -> 17.6 us  [the longest x30 15.5 us: swap(): lax.ppermute(value, axis, [(source, source ^ distance) for source in rang...]
    ppermute x11 -> x37, starting transfers between devices: 14.2 us -> 74.3 us  [the longest x30 46.6 us: swap(): lax.ppermute(value, axis, [(source, source ^ distance) for source in rang...]
    psum x1 -> x0, blocking collectives: 47.6 us -> none  [local(): totals = lax.psum(local_sums, 'pipe') * SLOT ** (-0.5)]
    dot_general x24 -> x26, matrix products: 77.8 us -> 53.8 us  [the longest x12 28.5 us: dot_nt(): lax.dot_general(a, b, (((1,), (1,)), ((), ())), preferred_element_type=jn...]
    all_gather x2 -> x0, blocking collectives: 22.3 us -> none  [the longest x1 12 us: local(): lax.all_gather(value_rows[0], 'dp', axis=0, tiled=True)]
    another operation x15 -> x0, local copies, waits for them, and re-layouts: 11.1 us -> none
    select_n x4 -> x0, other arithmetic: 10.1 us -> none  [advance(): gradient_leaving = jnp.where(is_last, seed_rows, incoming)]
  transfers between devices with their start and end apart: 11 -> 37, of which waited for: 11 -> 12; matrix products, arithmetic and copies ran while one was open for 0% -> 32% of each run, Pallas kernels for 0% -> 0%
where the time goes in v1:
time: 157 us; the launch traced here: 156 us
  starting transfers between devices  74.3 us (47%)
  matrix products  53.8 us (34%)
  waiting for transfers between devices  17.6 us (11%)
  local copies, waits for them, and re-layouts  7.06 us (4%)
  other arithmetic  2.6 us (2%)
    ppermute x30, starting transfers between devices, swap(): lax.ppermute(value, axis, [(source, source ^ distance) for source in rang...  46.6 us
    dot_general x12, matrix products, dot_nt(): lax.dot_general(a, b, (((1,), (1,)), ((), ())), preferred_element_type=jn...  28.5 us
    ppermute x7, starting transfers between devices, upward(): lax.ppermute(value, axis, [(source, source + 1) for source in range(count...  27.7 us
    dot_general x14, matrix products, dot_nn(): lax.dot_general(a, b, (((1,), (0,)), ((), ())), preferred_element_type=jn...  25.3 us
    ppermute x30, waiting for transfers between devices, swap(): lax.ppermute(value, axis, [(source, source ^ distance) for source in rang...  15.5 us
    slice x3, local copies, waits for them, and re-layouts, local(): value_all = jnp.concatenate([b[:q_dev] for b in blocks])  4.12 us
  transfers between devices with their start and end apart: 37, of which 12 were waited for; matrix products, arithmetic and copies ran while one was open for 32% of the time, Pallas kernels for 0%

profile of v1, /device:TPU:0, one launch (start us, length us, event | category | flops | bytes accessed | tf_op | source)
XLA Modules:
  0.0 156.1 jit_solution(16195946290525503682)
XLA Ops:
  0.9 5.1 %fusion = bf16[8,8192]{1,0:T(8,128)(2,1)S(1)} fusion(bf16[8,512]{1,0:T(8,128)(2,1)S(1)} %get-tuple-element.13, bf16[1,512,8192]{2,1,0:T(8,128)(2,1)} %param.13), kind=kOutput, calls=%fused_computation.7 | convolution fusion | flops 67239936 | bytes 8527872 | tf_op jit(solution)/shard_map/dot_general | solution.py:13
  6.8 3.9 %collective-permute-start.2 = (bf16[16,8192]{1,0:T(8,128)(2,1)}, bf16[16,8192]{1,0:T(8,128)(2,1)S(1)}, u32[]{:S(2)}, u32[]{:S(2)}) collective-permute-start(bf16[16,8192]{1,0:T(8,128)(2,1)} %get-tuple-element.12), channel_id=1, source_target_pairs={{0,24},{8,16},{16,8},{24,0},{1,25},{9,17},{17,9},{25,1},{2,26},{10... | collective-permute-start | bytes 786440 | tf_op jit(solution)/shard_map/ppermute | solution.py:22
  12.6 7.1 %fusion.32 = bf16[512,512]{1,0:T(8,128)(2,1)S(1)} fusion(bf16[512,8192]{1,0:T(8,128)(2,1)} %param.11, bf16[1,512,8192]{2,1,0:T(8,128)(2,1)S(1)} %copy-done), kind=kOutput, calls=%fused_computation.37 | convolution fusion | flops 4295491584 | bytes 17301504 | tf_op jit(solution)/shard_map/dot_general | solution.py:17
  19.7 11.1 %fusion.45 = f32[512,32]{0,1:T(8,128)} fusion(bf16[1,8192,512]{2,1,0:T(8,128)(2,1)} %param.12, bf16[1,512,8192]{2,1,0:T(8,128)(2,1)} %param.10, bf16[8,512]{1,0:T(8,128)(2,1)S(1)} %get-tuple-element.26, bf16[8,512]{1,0:T(8,128)(2,1)S(1)} %get-tuple-element.25, bf16[8,512]{1,0:T(8,128)(2,1)S(1)} %get-tuple-element.27, bf16[8,512]{1,0:T(8,128)(2,1)S(1)} %get-tuple-element.28), kind=kOutput, calls=%fused_computation.40 | convolution fusion | flops 4312154112 | bytes 16875520 | tf_op jit(solution)/shard_map/dot_general | solution.py:17
  31.7 5.0 %fusion.50 = bf16[16,512]{1,0:T(8,128)(2,1)S(1)} fusion(bf16[16,8192]{1,0:T(8,128)(2,1)S(1)} %collective-permute-done.6, bf16[1,8192,512]{2,1,0:T(8,128)(2,1)} %param.12), kind=kOutput, calls=%fused_computation.42 | convolution fusion | flops 134225920 | bytes 8667136 | tf_op jit(solution)/shard_map/dot_general | solution.py:13
  36.8 2.9 %collective-permute-start.9 = (bf16[16,512]{1,0:T(8,128)(2,1)S(1)}, bf16[16,512]{1,0:T(8,128)(2,1)S(1)}, u32[]{:S(2)}, u32[]{:S(2)}) collective-permute-start(bf16[16,512]{1,0:T(8,128)(2,1)S(1)} %fusion.50), channel_id=1, source_target_pairs={{0,24},{8,16},{16,8},{24,0},{1,25},{9,17},{17,9},{25,1},{2,26},{10... | collective-permute-start | bytes 49160 | tf_op jit(solution)/shard_map/ppermute | solution.py:22
  43.0 4.0 %collective-permute-start.10 = (bf16[16,8192]{1,0:T(8,128)(2,1)}, bf16[16,8192]{1,0:T(8,128)(2,1)S(1)}, u32[]{:S(2)}, u32[]{:S(2)}) collective-permute-start(bf16[16,8192]{1,0:T(8,128)(2,1)} %add_convert_fusion.5), channel_id=1, source_target_pairs={{0,1},{1,2},{2,3},{3,4},{4,5},{5,6},{6,7},{8,9},{9,10},{10,11},{11... | collective-permute-start | bytes 786440 | tf_op jit(solution)/shard_map/ppermute | solution.py:27
  50.4 3.8 %fusion.26 = f32[32,512]{1,0:T(8,128)S(1)} fusion(bf16[1,512,8192]{2,1,0:T(8,128)(2,1)S(1)} %bitcast.172, bf16[8,8192]{1,0:T(8,128)(2,1)} %get-tuple-element.10, bf16[8,8192]{1,0:T(8,128)(2,1)} %get-tuple-element.8, bf16[8,8192]{1,0:T(8,128)(2,1)} %get-tuple-element.6, bf16[8,8192]{1,0:T(8,128)(2,1)S(1)} %bitcast.178), kind=kOutput, calls=%fused_computation.33 | convolution fusion | flops 270532608 | bytes 8978432 | tf_op jit(solution)/shard_map/dot_general | solution.py:17
  55.9 3.8 %convolution_bitcast_fusion = f32[512,32]{0,1:T(8,128)S(1)} fusion(bf16[512,8192]{1,0:T(8,128)(2,1)S(1)} %bitcast.174, bf16[8,8192]{1,0:T(8,128)(2,1)} %get-tuple-element.9, bf16[8,8192]{1,0:T(8,128)(2,1)} %get-tuple-element.7, bf16[8,8192]{1,0:T(8,128)(2,1)} %get-tuple-element.5, bf16[8,8192]{1,0:T(8,128)(2,1)S(1)} %bitcast.180), kind=kOutput, calls=%fused_computation.41 | convolution fusion | flops 270532608 | bytes 8978432 | tf_op jit(solution)/shard_map/dot_general | solution.py:17
  63.1 3.6 %collective-permute-done.4 = bf16[2,512,64]{1,2,0:T(8,128)(2,1)S(1)} collective-permute-done((bf16[2,512,64]{1,2,0:T(8,128)(2,1)S(1)}, bf16[2,512,64]{1,2,0:T(8,128)(2,1)S(1)}, u32[]{:S(2)}, u32[]{:S(2)}) %collective-permute-start.4) | collective-permute-done | bytes 131104 | tf_op jit(solution)/shard_map/ppermute | solution.py:22
  66.8 2.7 %collective-permute-start.5 = (bf16[4,512,64]{1,2,0:T(8,128)(2,1)S(1)}, bf16[4,512,64]{1,2,0:T(8,128)(2,1)S(1)}, u32[]{:S(2)}, u32[]{:S(2)}) collective-permute-start(bf16[4,512,64]{1,2,0:T(8,128)(2,1)S(1)} %pad_maximum_fusion.3), channel_id=1, source_target_pairs={{0,4},{1,5},{2,6},{3,7},{4,0},{5,1},{6,2},{7,3},{8,12},{9,13},{10,... | collective-permute-start | bytes 786440 | tf_op jit(solution)/shard_map/ppermute | solution.py:22
  70.6 2.5 %collective-permute-start.13 = (bf16[16,512]{1,0:T(8,128)(2,1)S(1)}, bf16[16,512]{1,0:T(8,128)(2,1)S(1)}, u32[]{:S(2)}, u32[]{:S(2)}) collective-permute-start(bf16[16,512]{1,0:T(8,128)(2,1)S(1)} %fusion.53), channel_id=1, source_target_pairs={{0,24},{8,16},{16,8},{24,0},{1,25},{9,17},{17,9},{25,1},{2,26},{10... | collective-permute-start | bytes 49160 | tf_op jit(solution)/shard_map/ppermute | solution.py:22
  77.7 3.1 %collective-permute-done.5 = bf16[4,512,64]{1,2,0:T(8,128)(2,1)S(1)} collective-permute-done((bf16[4,512,64]{1,2,0:T(8,128)(2,1)S(1)}, bf16[4,512,64]{1,2,0:T(8,128)(2,1)S(1)}, u32[]{:S(2)}, u32[]{:S(2)}) %collective-permute-start.5) | collective-permute-done | bytes 262176 | tf_op jit(solution)/shard_map/ppermute | solution.py:22
  82.0 2.5 %collective-permute-start.17 = (bf16[16,512]{1,0:T(8,128)(2,1)S(1)}, bf16[16,512]{1,0:T(8,128)(2,1)S(1)}, u32[]{:S(2)}, u32[]{:S(2)}) collective-permute-start(bf16[16,512]{1,0:T(8,128)(2,1)S(1)} %fusion.56), channel_id=1, source_target_pairs={{0,24},{8,16},{16,8},{24,0},{1,25},{9,17},{17,9},{25,1},{2,26},{10... | collective-permute-start | bytes 49160 | tf_op jit(solution)/shard_map/ppermute | solution.py:22
  90.4 2.5 %collective-permute-start.21 = (bf16[16,512]{1,0:T(8,128)(2,1)S(1)}, bf16[16,512]{1,0:T(8,128)(2,1)S(1)}, u32[]{:S(2)}, u32[]{:S(2)}) collective-permute-start(bf16[16,512]{1,0:T(8,128)(2,1)S(1)} %fusion.59), channel_id=1, source_target_pairs={{0,24},{8,16},{16,8},{24,0},{1,25},{9,17},{17,9},{25,1},{2,26},{10... | collective-permute-start | bytes 49160 | tf_op jit(solution)/shard_map/ppermute | solution.py:22
  95.1 6.7 %collective-permute-start.22 = (bf16[16,8192]{1,0:T(8,128)(2,1)S(1)}, bf16[16,8192]{1,0:T(8,128)(2,1)S(1)}, u32[]{:S(2)}, u32[]{:S(2)}) collective-permute-start(bf16[16,8192]{1,0:T(8,128)(2,1)S(1)} %add_convert_fusion.2), channel_id=1, source_target_pairs={{0,1},{1,2},{2,3},{3,4},{4,5},{5,6},{6,7},{8,9},{9,10},{10,11},{11... | collective-permute-start | bytes 786440 | tf_op jit(solution)/shard_map/ppermute | solution.py:27
  103.9 2.5 %collective-permute-start.25 = (bf16[16,512]{1,0:T(8,128)(2,1)S(1)}, bf16[16,512]{1,0:T(8,128)(2,1)S(1)}, u32[]{:S(2)}, u32[]{:S(2)}) collective-permute-start(bf16[16,512]{1,0:T(8,128)(2,1)S(1)} %fusion.62), channel_id=1, source_target_pairs={{0,24},{8,16},{16,8},{24,0},{1,25},{9,17},{17,9},{25,1},{2,26},{10... | collective-permute-start | bytes 49160 | tf_op jit(solution)/shard_map/ppermute | solution.py:22
  108.7 6.6 %collective-permute-start.26 = (bf16[16,8192]{1,0:T(8,128)(2,1)S(1)}, bf16[16,8192]{1,0:T(8,128)(2,1)S(1)}, u32[]{:S(2)}, u32[]{:S(2)}) collective-permute-start(bf16[16,8192]{1,0:T(8,128)(2,1)S(1)} %add_convert_fusion.1), channel_id=1, source_target_pairs={{0,1},{1,2},{2,3},{3,4},{4,5},{5,6},{6,7},{8,9},{9,10},{10,11},{11... | collective-permute-start | bytes 786440 | tf_op jit(solution)/shard_map/ppermute | solution.py:27
  117.5 2.5 %collective-permute-start.29 = (bf16[16,512]{1,0:T(8,128)(2,1)S(1)}, bf16[16,512]{1,0:T(8,128)(2,1)S(1)}, u32[]{:S(2)}, u32[]{:S(2)}) collective-permute-start(bf16[16,512]{1,0:T(8,128)(2,1)S(1)} %fusion.65), channel_id=1, source_target_pairs={{0,24},{8,16},{16,8},{24,0},{1,25},{9,17},{17,9},{25,1},{2,26},{10... | collective-permute-start | bytes 49160 | tf_op jit(solution)/shard_map/ppermute | solution.py:22
  122.3 6.6 %collective-permute-start.30 = (bf16[16,8192]{1,0:T(8,128)(2,1)S(1)}, bf16[16,8192]{1,0:T(8,128)(2,1)S(1)}, u32[]{:S(2)}, u32[]{:S(2)}) collective-permute-start(bf16[16,8192]{1,0:T(8,128)(2,1)S(1)} %add_convert_fusion), channel_id=1, source_target_pairs={{0,1},{1,2},{2,3},{3,4},{4,5},{5,6},{6,7},{8,9},{9,10},{10,11},{11... | collective-permute-start | bytes 786440 | tf_op jit(solution)/shard_map/ppermute | solution.py:27
  134.7 3.2 %collective-permute-done.31 = bf16[16,512]{1,0:T(8,128)(2,1)S(1)} collective-permute-done((bf16[16,512]{1,0:T(8,128)(2,1)S(1)}, bf16[16,512]{1,0:T(8,128)(2,1)S(1)}, u32[]{:S(2)}, u32[]{:S(2)}) %collective-permute-start.31) | collective-permute-done | bytes 16416 | tf_op jit(solution)/shard_map/ppermute | solution.py:22
  138.5 3.8 %collective-permute-start.34 = (f32[4,32]{0,1:T(8,128)S(1)}, f32[4,32]{0,1:T(8,128)S(1)}, u32[]{:S(2)}, u32[]{:S(2)}) collective-permute-start(f32[4,32]{0,1:T(8,128)S(1)} %slice_add_fusion), channel_id=1, source_target_pairs={{0,1},{1,0},{2,3},{3,2},{4,5},{5,4},{6,7},{7,6},{8,9},{9,8},{10,11... | collective-permute-start | bytes 1544 | tf_op jit(solution)/shard_map/ppermute | solution.py:22
  143.2 4.4 %collective-permute-start.35 = (f32[4,32]{0,1:T(8,128)S(1)}, f32[4,32]{0,1:T(8,128)S(1)}, u32[]{:S(2)}, u32[]{:S(2)}) collective-permute-start(f32[4,32]{0,1:T(8,128)S(1)} %fusion.165), channel_id=1, source_target_pairs={{0,2},{1,3},{2,0},{3,1},{4,6},{5,7},{6,4},{7,5},{8,10},{9,11},{10,... | collective-permute-start | bytes 1544 | tf_op jit(solution)/shard_map/ppermute | solution.py:22
  149.3 4.1 %collective-permute-start.36 = (f32[4,32]{0,1:T(8,128)S(1)}, f32[4,32]{0,1:T(8,128)S(1)}, u32[]{:S(2)}, u32[]{:S(2)}) collective-permute-start(f32[4,32]{0,1:T(8,128)S(1)} %add.159), channel_id=1, source_target_pairs={{0,4},{1,5},{2,6},{3,7},{4,0},{5,1},{6,2},{7,3},{8,12},{9,13},{10,... | collective-permute-start | bytes 1544 | tf_op jit(solution)/shard_map/ppermute | solution.py:22
  (189 shorter events, 51.7 us)
Async XLA Ops:
  6.8 33.4 %collective-permute-start.2 = (bf16[16,8192]{1,0:T(8,128)(2,1)}, bf16[16,8192]{1,0:T(8,128)(2,1)S(1)}, u32[]{:S(2)}, u32[]{:S(2)}) collective-permute-start(bf16[16,8192]{1,0:T(8,128)(2,1)} %get-tuple-element.12), channel_id=1, source_target_pairs={{0,24},{8,16},{16,8},{24,0},{1,25},{9,17},{17,9},{25,1},{2,26},{10... | collective-permute-start | bytes 786440 | tf_op jit(solution)/shard_map/ppermute | solution.py:22
  10.7 32.2 %collective-permute-start.1 = (bf16[16,8192]{1,0:T(8,128)(2,1)}, bf16[16,8192]{1,0:T(8,128)(2,1)}, u32[]{:S(2)}, u32[]{:S(2)}) collective-permute-start(bf16[16,8192]{1,0:T(8,128)(2,1)} %get-tuple-element.12), channel_id=1, source_target_pairs={{0,16},{8,24},{16,0},{24,8},{1,17},{9,25},{17,1},{25,9},{2,18},{10... | collective-permute-start | bytes 786440 | tf_op jit(solution)/shard_map/ppermute | solution.py:22
  11.2 37.4 %collective-permute-start = (bf16[16,8192]{1,0:T(8,128)(2,1)}, bf16[16,8192]{1,0:T(8,128)(2,1)}, u32[]{:S(2)}, u32[]{:S(2)}) collective-permute-start(bf16[16,8192]{1,0:T(8,128)(2,1)} %get-tuple-element.12), channel_id=1, source_target_pairs={{0,8},{8,0},{16,24},{24,16},{1,9},{9,1},{17,25},{25,17},{2,10},{10... | collective-permute-start | bytes 786440 | tf_op jit(solution)/shard_map/ppermute | solution.py:22
  11.3 20.4 %collective-permute-start.6 = (bf16[16,8192]{1,0:T(8,128)(2,1)S(1)}, bf16[16,8192]{1,0:T(8,128)(2,1)S(1)}, u32[]{:S(2)}, u32[]{:S(2)}) collective-permute-start(bf16[16,8192]{1,0:T(8,128)(2,1)S(1)} %get-tuple-element.11), channel_id=1, source_target_pairs={{0,1},{1,2},{2,3},{3,4},{4,5},{5,6},{6,7},{8,9},{9,10},{10,11},{11... | collective-permute-start | bytes 786440 | tf_op jit(solution)/shard_map/ppermute | solution.py:27
  36.8 23.7 %collective-permute-start.9 = (bf16[16,512]{1,0:T(8,128)(2,1)S(1)}, bf16[16,512]{1,0:T(8,128)(2,1)S(1)}, u32[]{:S(2)}, u32[]{:S(2)}) collective-permute-start(bf16[16,512]{1,0:T(8,128)(2,1)S(1)} %fusion.50), channel_id=1, source_target_pairs={{0,24},{8,16},{16,8},{24,0},{1,25},{9,17},{17,9},{25,1},{2,26},{10... | collective-permute-start | bytes 49160 | tf_op jit(solution)/shard_map/ppermute | solution.py:22
  39.7 20.8 %collective-permute-start.8 = (bf16[16,512]{1,0:T(8,128)(2,1)S(1)}, bf16[16,512]{1,0:T(8,128)(2,1)S(1)}, u32[]{:S(2)}, u32[]{:S(2)}) collective-permute-start(bf16[16,512]{1,0:T(8,128)(2,1)S(1)} %fusion.50), channel_id=1, source_target_pairs={{0,16},{8,24},{16,0},{24,8},{1,17},{9,25},{17,1},{25,9},{2,18},{10... | collective-permute-start | bytes 49160 | tf_op jit(solution)/shard_map/ppermute | solution.py:22
  40.2 19.5 %collective-permute-start.7 = (bf16[16,512]{1,0:T(8,128)(2,1)S(1)}, bf16[16,512]{1,0:T(8,128)(2,1)}, u32[]{:S(2)}, u32[]{:S(2)}) collective-permute-start(bf16[16,512]{1,0:T(8,128)(2,1)S(1)} %fusion.50), channel_id=1, source_target_pairs={{0,8},{8,0},{16,24},{24,16},{1,9},{9,1},{17,25},{25,17},{2,10},{10... | collective-permute-start | bytes 49160 | tf_op jit(solution)/shard_map/ppermute | solution.py:22
  43.0 26.4 %collective-permute-start.10 = (bf16[16,8192]{1,0:T(8,128)(2,1)}, bf16[16,8192]{1,0:T(8,128)(2,1)S(1)}, u32[]{:S(2)}, u32[]{:S(2)}) collective-permute-start(bf16[16,8192]{1,0:T(8,128)(2,1)} %add_convert_fusion.5), channel_id=1, source_target_pairs={{0,1},{1,2},{2,3},{3,4},{4,5},{5,6},{6,7},{8,9},{9,10},{10,11},{11... | collective-permute-start | bytes 786440 | tf_op jit(solution)/shard_map/ppermute | solution.py:27
  66.8 14.0 %collective-permute-start.5 = (bf16[4,512,64]{1,2,0:T(8,128)(2,1)S(1)}, bf16[4,512,64]{1,2,0:T(8,128)(2,1)S(1)}, u32[]{:S(2)}, u32[]{:S(2)}) collective-permute-start(bf16[4,512,64]{1,2,0:T(8,128)(2,1)S(1)} %pad_maximum_fusion.3), channel_id=1, source_target_pairs={{0,4},{1,5},{2,6},{3,7},{4,0},{5,1},{6,2},{7,3},{8,12},{9,13},{10,... | collective-permute-start | bytes 786440 | tf_op jit(solution)/shard_map/ppermute | solution.py:22
  70.6 6.7 %collective-permute-start.13 = (bf16[16,512]{1,0:T(8,128)(2,1)S(1)}, bf16[16,512]{1,0:T(8,128)(2,1)S(1)}, u32[]{:S(2)}, u32[]{:S(2)}) collective-permute-start(bf16[16,512]{1,0:T(8,128)(2,1)S(1)} %fusion.53), channel_id=1, source_target_pairs={{0,24},{8,16},{16,8},{24,0},{1,25},{9,17},{17,9},{25,1},{2,26},{10... | collective-permute-start | bytes 49160 | tf_op jit(solution)/shard_map/ppermute | solution.py:22
  82.0 6.7 %collective-permute-start.17 = (bf16[16,512]{1,0:T(8,128)(2,1)S(1)}, bf16[16,512]{1,0:T(8,128)(2,1)S(1)}, u32[]{:S(2)}, u32[]{:S(2)}) collective-permute-start(bf16[16,512]{1,0:T(8,128)(2,1)S(1)} %fusion.56), channel_id=1, source_target_pairs={{0,24},{8,16},{16,8},{24,0},{1,25},{9,17},{17,9},{25,1},{2,26},{10... | collective-permute-start | bytes 49160 | tf_op jit(solution)/shard_map/ppermute | solution.py:22
  90.4 11.5 %collective-permute-start.21 = (bf16[16,512]{1,0:T(8,128)(2,1)S(1)}, bf16[16,512]{1,0:T(8,128)(2,1)S(1)}, u32[]{:S(2)}, u32[]{:S(2)}) collective-permute-start(bf16[16,512]{1,0:T(8,128)(2,1)S(1)} %fusion.59), channel_id=1, source_target_pairs={{0,24},{8,16},{16,8},{24,0},{1,25},{9,17},{17,9},{25,1},{2,26},{10... | collective-permute-start | bytes 49160 | tf_op jit(solution)/shard_map/ppermute | solution.py:22
  92.8 9.1 %collective-permute-start.20 = (bf16[16,512]{1,0:T(8,128)(2,1)S(1)}, bf16[16,512]{1,0:T(8,128)(2,1)S(1)}, u32[]{:S(2)}, u32[]{:S(2)}) collective-permute-start(bf16[16,512]{1,0:T(8,128)(2,1)S(1)} %fusion.59), channel_id=1, source_target_pairs={{0,16},{8,24},{16,0},{24,8},{1,17},{9,25},{17,1},{25,9},{2,18},{10... | collective-permute-start | bytes 49160 | tf_op jit(solution)/shard_map/ppermute | solution.py:22
  93.3 8.5 %collective-permute-start.19 = (bf16[16,512]{1,0:T(8,128)(2,1)S(1)}, bf16[16,512]{1,0:T(8,128)(2,1)S(1)}, u32[]{:S(2)}, u32[]{:S(2)}) collective-permute-start(bf16[16,512]{1,0:T(8,128)(2,1)S(1)} %fusion.59), channel_id=1, source_target_pairs={{0,8},{8,0},{16,24},{24,16},{1,9},{9,1},{17,25},{25,17},{2,10},{10... | collective-permute-start | bytes 49160 | tf_op jit(solution)/shard_map/ppermute | solution.py:22
  95.1 7.7 %collective-permute-start.22 = (bf16[16,8192]{1,0:T(8,128)(2,1)S(1)}, bf16[16,8192]{1,0:T(8,128)(2,1)S(1)}, u32[]{:S(2)}, u32[]{:S(2)}) collective-permute-start(bf16[16,8192]{1,0:T(8,128)(2,1)S(1)} %add_convert_fusion.2), channel_id=1, source_target_pairs={{0,1},{1,2},{2,3},{3,4},{4,5},{5,6},{6,7},{8,9},{9,10},{10,11},{11... | collective-permute-start | bytes 786440 | tf_op jit(solution)/shard_map/ppermute | solution.py:27
  103.9 11.3 %collective-permute-start.25 = (bf16[16,512]{1,0:T(8,128)(2,1)S(1)}, bf16[16,512]{1,0:T(8,128)(2,1)S(1)}, u32[]{:S(2)}, u32[]{:S(2)}) collective-permute-start(bf16[16,512]{1,0:T(8,128)(2,1)S(1)} %fusion.62), channel_id=1, source_target_pairs={{0,24},{8,16},{16,8},{24,0},{1,25},{9,17},{17,9},{25,1},{2,26},{10... | collective-permute-start | bytes 49160 | tf_op jit(solution)/shard_map/ppermute | solution.py:22
  106.4 8.9 %collective-permute-start.24 = (bf16[16,512]{1,0:T(8,128)(2,1)S(1)}, bf16[16,512]{1,0:T(8,128)(2,1)S(1)}, u32[]{:S(2)}, u32[]{:S(2)}) collective-permute-start(bf16[16,512]{1,0:T(8,128)(2,1)S(1)} %fusion.62), channel_id=1, source_target_pairs={{0,16},{8,24},{16,0},{24,8},{1,17},{9,25},{17,1},{25,9},{2,18},{10... | collective-permute-start | bytes 49160 | tf_op jit(solution)/shard_map/ppermute | solution.py:22
  106.9 8.3 %collective-permute-start.23 = (bf16[16,512]{1,0:T(8,128)(2,1)S(1)}, bf16[16,512]{1,0:T(8,128)(2,1)S(1)}, u32[]{:S(2)}, u32[]{:S(2)}) collective-permute-start(bf16[16,512]{1,0:T(8,128)(2,1)S(1)} %fusion.62), channel_id=1, source_target_pairs={{0,8},{8,0},{16,24},{24,16},{1,9},{9,1},{17,25},{25,17},{2,10},{10... | collective-permute-start | bytes 49160 | tf_op jit(solution)/shard_map/ppermute | solution.py:22
  108.7 7.7 %collective-permute-start.26 = (bf16[16,8192]{1,0:T(8,128)(2,1)S(1)}, bf16[16,8192]{1,0:T(8,128)(2,1)S(1)}, u32[]{:S(2)}, u32[]{:S(2)}) collective-permute-start(bf16[16,8192]{1,0:T(8,128)(2,1)S(1)} %add_convert_fusion.1), channel_id=1, source_target_pairs={{0,1},{1,2},{2,3},{3,4},{4,5},{5,6},{6,7},{8,9},{9,10},{10,11},{11... | collective-permute-start | bytes 786440 | tf_op jit(solution)/shard_map/ppermute | solution.py:27
  117.5 11.3 %collective-permute-start.29 = (bf16[16,512]{1,0:T(8,128)(2,1)S(1)}, bf16[16,512]{1,0:T(8,128)(2,1)S(1)}, u32[]{:S(2)}, u32[]{:S(2)}) collective-permute-start(bf16[16,512]{1,0:T(8,128)(2,1)S(1)} %fusion.65), channel_id=1, source_target_pairs={{0,24},{8,16},{16,8},{24,0},{1,25},{9,17},{17,9},{25,1},{2,26},{10... | collective-permute-start | bytes 49160 | tf_op jit(solution)/shard_map/ppermute | solution.py:22
  120.0 8.9 %collective-permute-start.28 = (bf16[16,512]{1,0:T(8,128)(2,1)S(1)}, bf16[16,512]{1,0:T(8,128)(2,1)S(1)}, u32[]{:S(2)}, u32[]{:S(2)}) collective-permute-start(bf16[16,512]{1,0:T(8,128)(2,1)S(1)} %fusion.65), channel_id=1, source_target_pairs={{0,16},{8,24},{16,0},{24,8},{1,17},{9,25},{17,1},{25,9},{2,18},{10... | collective-permute-start | bytes 49160 | tf_op jit(solution)/shard_map/ppermute | solution.py:22
  120.5 8.3 %collective-permute-start.27 = (bf16[16,512]{1,0:T(8,128)(2,1)S(1)}, bf16[16,512]{1,0:T(8,128)(2,1)S(1)}, u32[]{:S(2)}, u32[]{:S(2)}) collective-permute-start(bf16[16,512]{1,0:T(8,128)(2,1)S(1)} %fusion.65), channel_id=1, source_target_pairs={{0,8},{8,0},{16,24},{24,16},{1,9},{9,1},{17,25},{25,17},{2,10},{10... | collective-permute-start | bytes 49160 | tf_op jit(solution)/shard_map/ppermute | solution.py:22
  122.3 7.7 %collective-permute-start.30 = (bf16[16,8192]{1,0:T(8,128)(2,1)S(1)}, bf16[16,8192]{1,0:T(8,128)(2,1)S(1)}, u32[]{:S(2)}, u32[]{:S(2)}) collective-permute-start(bf16[16,8192]{1,0:T(8,128)(2,1)S(1)} %add_convert_fusion), channel_id=1, source_target_pairs={{0,1},{1,2},{2,3},{3,4},{4,5},{5,6},{6,7},{8,9},{9,10},{10,11},{11... | collective-permute-start | bytes 786440 | tf_op jit(solution)/shard_map/ppermute | solution.py:27
  131.2 6.7 %collective-permute-start.33 = (bf16[16,512]{1,0:T(8,128)(2,1)S(1)}, bf16[16,512]{1,0:T(8,128)(2,1)S(1)}, u32[]{:S(2)}, u32[]{:S(2)}) collective-permute-start(bf16[16,512]{1,0:T(8,128)(2,1)S(1)} %fusion.68), channel_id=1, source_target_pairs={{0,24},{8,16},{16,8},{24,0},{1,25},{9,17},{17,9},{25,1},{2,26},{10... | collective-permute-start | bytes 49160 | tf_op jit(solution)/shard_map/ppermute | solution.py:22
  (28 other events, 260.9 us)

commit v2 on v1

v2 whole, which is shorter than its diff:
```python
import jax
import jax.numpy as jnp
from jax import lax
from jax.sharding import PartitionSpec as P

SLOT = 128


adapter_scale = 0.25


def dot_nn(a, b):
    return lax.dot_general(a, b, (((1,), (0,)), ((), ())), preferred_element_type=jnp.float32)


def dot_nt(a, b):
    return lax.dot_general(a, b, (((1,), (1,)), ((), ())), preferred_element_type=jnp.float32)


def swap(value, axis, distance):
    count = lax.axis_size(axis)
    return lax.ppermute(value, axis, [(source, source ^ distance) for source in range(count)])


def spread(value, axis):
    return [value] + [swap(value, axis, d) for d in range(1, lax.axis_size(axis))]


def upward(value, first, hop, stride):
    count = lax.axis_size("pipe")
    return lax.ppermute(
        value, "pipe", [(source, source + hop) for source in range(first, count - hop, stride)]
    )


def tie(values, token):
    *values, _ = lax.optimization_barrier((*values, token))
    return values


def local(
    activations,
    cotangent,
    adapter_down,
    adapter_expand,
    value_rows,
    input_rows,
    hidden_cols,
    inner_cols,
    lengths,
    query_example,
):
    bf16 = jnp.bfloat16
    columns = lax.axis_size("dp")
    chips = lax.axis_size("pipe") // 2
    column = lax.axis_index("dp")
    upper = lax.axis_index("pipe") % 2 == 1
    tok_dev = activations.shape[1]
    ex_dev = tok_dev // SLOT
    q_dev = value_rows.shape[1]
    rows = 2 * q_dev
    act = activations[0]
    down = adapter_down[0]
    expand = adapter_expand[0]

    def blocks_of(cols):
        return jnp.concatenate(
            [lax.dynamic_slice_in_dim(cols, (column ^ d) * q_dev, q_dev, 0) for d in range(columns)]
        )

    def weave(first, second):
        parts = []
        for d in range(columns):
            parts += [first[d], second[d]]
        return jnp.concatenate(parts)

    def cut(stacked, size):
        return [stacked[d * size : (d + 1) * size] for d in range(columns)]

    def through(arrived):
        ranks = dot_nn(arrived, down).astype(bf16)
        leaving = arrived.astype(jnp.float32) + adapter_scale * dot_nn(ranks, expand)
        return ranks, leaving.astype(bf16)

    raised = (adapter_scale * dot_nn(blocks_of(inner_cols[0]), expand)).astype(bf16)
    raised = cut(raised, q_dev)
    own = jnp.concatenate([value_rows[0], raised[0]])

    arrived = upward(own, 0, 1, 2)
    ranks, leaving = through(arrived)
    lower_ranks = ranks
    moving = jnp.concatenate([leaving, own])

    arrived = upward(moving, 1, 1, 2)
    width_rows, cot = tie([jnp.concatenate([value_rows[0], input_rows[0]]), cotangent], moving)
    width_rows = spread(width_rows, "dp")
    lifted = (adapter_scale * dot_nt(cot, expand)).astype(bf16)
    arrived, lifted = lax.optimization_barrier((arrived, lifted))

    slots = []
    left = right = None
    for slot in range(1, chips):
        ranks_even, leaving = through(arrived)
        arrived = upward(leaving, 0, 1, 2)
        ranks_odd, leaving = through(arrived)
        slots.append(jnp.where(upper, ranks_odd, ranks_even))
        if slot == chips - 1:
            break
        arrived = upward(leaving, 1, 1, 2)
        if slot == 1:
            x, hid = tie([act, blocks_of(hidden_cols[0])], leaving)
            hid = (adapter_scale * dot_nt(hid, down)).astype(bf16)
            inputs = [b[q_dev:] for b in width_rows]
            left = dot_nt(x, weave(cut(hid, q_dev), inputs))
            offsets = lax.broadcasted_iota(jnp.int32, (ex_dev, SLOT, 1), 1)
            live = (offsets < lengths[:, None, None]).astype(jnp.float32).reshape(tok_dev, 1)
            left = left * live
            left_own = left.astype(bf16)
            left_up = [left_own] + [
                upward(left_own, 0, 2 * hop, 1) for hop in range(1, chips)
            ]
            arrived, left_own = lax.optimization_barrier((arrived, left_own))
        if slot == 2 or chips == 3:
            (cot,) = tie([cotangent], leaving)
            right = dot_nt(cot, weave([b[:q_dev] for b in width_rows], raised))
            left_up = jnp.stack(left_up)
            left_other = swap(left_up, "pipe", 1)
            left_even = jnp.where(upper, left_other, left_up)
            left_odd = jnp.where(upper, left_up, left_other)
            arrived, right = lax.optimization_barrier((arrived, right))

    def weighed(weights, ranks):
        return weights.astype(jnp.float32) * dot_nt(lifted, ranks)

    early = jnp.concatenate([lower_ranks] + slots[:-1])
    early = spread(early, "dp")
    terms = left * right + weighed(left_even[0], jnp.concatenate([b[:rows] for b in early]))
    for slot in range(1, chips - 1):
        at = rows * (2 * slot - 1)
        terms += weighed(left_even[slot], jnp.concatenate([b[at : at + rows] for b in early]))
        at += rows
        terms += weighed(left_odd[slot], jnp.concatenate([b[at : at + rows] for b in early]))

    late = spread(slots[-1], "dp")
    terms += weighed(left_even[-1], jnp.concatenate([b[:rows] for b in late]))
    terms += weighed(left_odd[-1], jnp.concatenate([b[rows:] for b in late]))

    sums = jnp.sum(terms.reshape(ex_dev, SLOT, columns, 2, q_dev), axis=(1, 3))
    sums = sums.reshape(ex_dev, columns * q_dev)
    sums = sums + swap(sums, "pipe", 1)
    parts = [swap(sums, "pipe", 2 * hop) for hop in range(1, chips)]
    for part in parts:
        sums = sums + part

    sums = sums.reshape(ex_dev, columns, q_dev)
    totals = jnp.concatenate(
        [lax.dynamic_index_in_dim(sums, column ^ c, 1, keepdims=False) for c in range(columns)],
        axis=1,
    )
    example_ids = column * ex_dev + lax.broadcasted_iota(jnp.int32, (ex_dev,), 0)
    keep_mask = (example_ids[:, None] != query_example[None, :]).astype(jnp.float32)
    return totals * SLOT ** (-0.5) * keep_mask


def solution(mesh):
    in_specs = (
        P("pipe", "dp", None),
        P("dp", None),
        P("pipe", None, None),
        P("pipe", None, None),
        P("pipe", "dp", None),
        P("pipe", "dp", None),
        P("pipe", None, None),
        P("pipe", None, None),
        P("dp"),
        P(),
    )
    out_specs = P("dp", None)
    return jax.shard_map(local, mesh=mesh, in_specs=in_specs, out_specs=out_specs, check_vma=False)
```

time: 157 us -> 124 us (0.79)
  starting transfers between devices: 74.3 us -> 45 us
  local copies, waits for them, and re-layouts: 7.06 us -> 2.92 us
  matrix products: 53.8 us -> 57.2 us
    ppermute x30 -> x14, starting transfers between devices: 46.6 us -> 18.9 us  [swap(): lax.ppermute(value, axis, [(source, source ^ distance) for source in rang...]
    dot_general x14, matrix products: 25.3 us -> 36.7 us  [dot_nn(): lax.dot_general(a, b, (((1,), (0,)), ((), ())), preferred_element_type=jn...]
    dot_general x12 -> x11, matrix products: 28.5 us -> 20.5 us  [dot_nt(): lax.dot_general(a, b, (((1,), (1,)), ((), ())), preferred_element_type=jn...]
    ppermute x30 -> x14, waiting for transfers between devices: 15.5 us -> 10.9 us  [swap(): lax.ppermute(value, axis, [(source, source ^ distance) for source in rang...]
    slice x3 -> x10, local copies, waits for them, and re-layouts: 4.12 us -> 0.06 us  [the longest x3 0.03 us: local(): b[:rows]]
    ppermute x7 -> x10, waiting for transfers between devices: 2.09 us -> 5.46 us  [upward(): lax.ppermute(value, 'pipe', [(source, source + hop) for source in range(f...]
    ppermute x7 -> x10, starting transfers between devices: 27.7 us -> 26.1 us  [upward(): lax.ppermute(value, 'pipe', [(source, source + hop) for source in range(f...]
  transfers between devices with their start and end apart: 37 -> 24, of which waited for: 12 -> 11; matrix products, arithmetic and copies ran while one was open for 32% -> 30% of each run, Pallas kernels for 0% -> 0%
where the time goes in v2:
time: 124 us
  matrix products  57.2 us (46%)
  starting transfers between devices  45 us (36%)
  waiting for transfers between devices  16.3 us (13%)
  local copies, waits for them, and re-layouts  2.92 us (2%)
  other arithmetic  1.74 us (1%)
    dot_general x14, matrix products, dot_nn(): lax.dot_general(a, b, (((1,), (0,)), ((), ())), preferred_element_type=jn...  36.7 us
    ppermute x10, starting transfers between devices, upward(): lax.ppermute(value, 'pipe', [(source, source + hop) for source in range(f...  26.1 us
    dot_general x11, matrix products, dot_nt(): lax.dot_general(a, b, (((1,), (1,)), ((), ())), preferred_element_type=jn...  20.5 us
    ppermute x14, starting transfers between devices, swap(): lax.ppermute(value, axis, [(source, source ^ distance) for source in rang...  18.9 us
    ppermute x14, waiting for transfers between devices, swap(): lax.ppermute(value, axis, [(source, source ^ distance) for source in rang...  10.9 us
    ppermute x10, waiting for transfers between devices, upward(): lax.ppermute(value, 'pipe', [(source, source + hop) for source in range(f...  5.46 us
  transfers between devices with their start and end apart: 24, of which 11 were waited for; matrix products, arithmetic and copies ran while one was open for 30% of the time, Pallas kernels for 0%

profile of v2, /device:TPU:0, one launch (start us, length us, event | category | flops | bytes accessed | tf_op | source)
XLA Modules:
  0.0 123.9 jit_solution(18178389845956717005)
XLA Ops:
  0.9 5.5 %fusion = bf16[32,8192]{1,0:T(8,128)(2,1)S(1)} fusion(bf16[1,512,8192]{2,1,0:T(8,128)(2,1)} %param.13, bf16[8,512]{1,0:T(8,128)(2,1)S(1)} %get-tuple-element.70, bf16[8,512]{1,0:T(8,128)(2,1)S(1)} %get-tuple-element.71, bf16[8,512]{1,0:T(8,128)(2,1)S(1)} %get-tuple-element.69, bf16[8,512]{1,0:T(8,128)(2,1)S(1)} %get-tuple-element.68), kind=kOutput, calls=%fused_computation.7 | convolution fusion | flops 269090816 | bytes 8945664 | tf_op jit(solution)/shard_map/dot_general | solution.py:13
  7.2 2.6 %collective-permute-start = (bf16[16,8192]{1,0:T(8,128)(2,1)S(1)}, bf16[16,8192]{1,0:T(8,128)(2,1)S(1)}, u32[]{:S(2)}, u32[]{:S(2)}) collective-permute-start(bf16[16,8192]{1,0:T(8,128)(2,1)S(1)} %get-tuple-element.36), channel_id=1, source_target_pairs={{0,1},{2,3},{4,5},{6,7},{8,9},{10,11},{12,13},{14,15},{16,17},{18,... | collective-permute-start | bytes 786440 | tf_op jit(solution)/shard_map/ppermute | solution.py:31
  14.1 7.1 %fusion.29 = bf16[512,512]{1,0:T(8,128)(2,1)S(1)} fusion(bf16[512,8192]{1,0:T(8,128)(2,1)} %param.11, bf16[1,512,8192]{2,1,0:T(8,128)(2,1)S(1)} %bitcast.164), kind=kOutput, calls=%fused_computation.35 | convolution fusion | flops 4295491584 | bytes 17301504 | tf_op jit(solution)/shard_map/dot_general | solution.py:17
  22.7 1.6 %add_convert_fusion.4 = bf16[32,8192]{1,0:T(8,128)(2,1)S(1)} fusion(bf16[32,8192]{1,0:T(8,128)(2,1)S(1)} %collective-permute-done.1, bf16[32,512]{1,0:T(8,128)(2,1)S(1)} %fusion.32, bf16[1,512,8192]{2,1,0:T(8,128)(2,1)S(1)} %bitcast.164), kind=kOutput, calls=%fused_computation.49 | convolution fusion | flops 269484032 | bytes 9469952 | tf_op jit(solution)/shard_map/dot_general | solution.py:13
  24.3 5.8 %collective-permute-start.2 = (bf16[32,8192]{1,0:T(8,128)(2,1)S(1)}, bf16[32,8192]{1,0:T(8,128)(2,1)S(1)}, u32[]{:S(2)}, u32[]{:S(2)}) collective-permute-start(bf16[32,8192]{1,0:T(8,128)(2,1)S(1)} %add_convert_fusion.4), channel_id=1, source_target_pairs={{0,1},{2,3},{4,5},{6,7},{8,9},{10,11},{12,13},{14,15},{16,17},{18,... | collective-permute-start | bytes 1572872 | tf_op jit(solution)/shard_map/ppermute | solution.py:31
  33.8 4.9 %broadcast_select_fusion.3 = (bf16[32,512]{1,0:T(8,128)(2,1)S(1)}, bf16[32,512]{1,0:T(8,128)(2,1)S(1)}) fusion(bf16[32,512]{1,0:T(8,128)(2,1)S(1)} %fusion.32, pred[]{:T(512)S(6)} %eq.5, bf16[32,8192]{1,0:T(8,128)(2,1)S(1)} %collective-permute-done.2, bf16[1,8192,512]{2,1,0:T(8,128)(2,1)} %param.12), kind=kOutput, calls=%fused_computation.160 | convolution fusion | flops 268468224 | bytes 9011201 | tf_op jit(solution)/shard_map/dot_general | solution.py:13
  38.7 2.4 %add_convert_fusion.3 = bf16[32,8192]{1,0:T(8,128)(2,1)} fusion(bf16[32,8192]{1,0:T(8,128)(2,1)S(1)} %collective-permute-done.2, bf16[32,512]{1,0:T(8,128)(2,1)S(1)} %get-tuple-element.81, bf16[1,512,8192]{2,1,0:T(8,128)(2,1)S(1)} %bitcast.166), kind=kOutput, calls=%fused_computation.48 | convolution fusion | flops 269484032 | bytes 9469952 | tf_op jit(solution)/shard_map/dot_general | solution.py:13
  42.0 6.1 %fusion.1 = bf16[32,8192]{1,0:T(8,128)(2,1)S(1)} fusion(bf16[32,512]{1,0:T(8,128)(2,1)S(1)} %pad_maximum_fusion.5, bf16[1,8192,512]{2,1,0:T(8,128)(2,1)} %param.12), kind=kOutput, calls=%fused_computation.8 | convolution fusion | flops 268959744 | bytes 8945664 | tf_op jit(solution)/shard_map/dot_general | solution.py:17
  49.4 2.7 %fusion.158 = (bf16[512,64]{0,1:T(8,128)(2,1)S(1)}, f32[512,64]{0,1:T(8,128)S(1)}) fusion(f32[512]{0:T(512)S(1)} %convert_bitcast_fusion, bf16[512,8192]{1,0:T(8,128)(2,1)S(1)} %bitcast.173, bf16[64,8192]{1,0:T(8,128)(2,1)S(1)} %get-tuple-element.28), kind=kOutput, calls=%fused_computation.196 | convolution fusion | flops 536936448 | bytes 9635840 | tf_op jit(solution)/shard_map/dot_general | solution.py:17
  52.1 4.1 %collective-permute-start.9 = (bf16[512,64]{0,1:T(8,128)(2,1)S(1)}, bf16[512,64]{0,1:T(8,128)(2,1)S(1)}, u32[]{:S(2)}, u32[]{:S(2)}) collective-permute-start(bf16[512,64]{0,1:T(8,128)(2,1)S(1)} %get-tuple-element.76), channel_id=1, source_target_pairs={{0,2},{1,3},{2,4},{3,5},{4,6},{5,7},{8,10},{9,11},{10,12},{11,13},... | collective-permute-start | bytes 196616 | tf_op jit(solution)/shard_map/ppermute | solution.py:31
  56.2 3.7 %collective-permute-start.10 = (bf16[512,64]{0,1:T(8,128)(2,1)S(1)}, bf16[512,64]{0,1:T(8,128)(2,1)S(1)}, u32[]{:S(2)}, u32[]{:S(2)}) collective-permute-start(bf16[512,64]{0,1:T(8,128)(2,1)S(1)} %get-tuple-element.76), channel_id=1, source_target_pairs={{0,4},{1,5},{2,6},{3,7},{8,12},{9,13},{10,14},{11,15},{16,20},{17,... | collective-permute-start | bytes 196616 | tf_op jit(solution)/shard_map/ppermute | solution.py:31
  64.1 5.2 %fusion.38 = bf16[32,512]{1,0:T(8,128)(2,1)S(1)} fusion(bf16[32,8192]{1,0:T(8,128)(2,1)S(1)} %collective-permute-done.6, bf16[1,8192,512]{2,1,0:T(8,128)(2,1)} %param.12), kind=kOutput, calls=%fused_computation.39 | convolution fusion | flops 268451840 | bytes 8945664 | tf_op jit(solution)/shard_map/dot_general | solution.py:13
  69.4 1.6 %add_convert_fusion.2 = bf16[32,8192]{1,0:T(8,128)(2,1)S(1)} fusion(bf16[32,8192]{1,0:T(8,128)(2,1)S(1)} %collective-permute-done.6, bf16[32,512]{1,0:T(8,128)(2,1)S(1)} %fusion.38, bf16[1,512,8192]{2,1,0:T(8,128)(2,1)S(1)} %bitcast.168), kind=kOutput, calls=%fused_computation.47 | convolution fusion | flops 269484032 | bytes 9469952 | tf_op jit(solution)/shard_map/dot_general | solution.py:13
  71.0 2.0 %collective-permute-start.7 = (bf16[32,8192]{1,0:T(8,128)(2,1)S(1)}, bf16[32,8192]{1,0:T(8,128)(2,1)S(1)}, u32[]{:S(2)}, u32[]{:S(2)}) collective-permute-start(bf16[32,8192]{1,0:T(8,128)(2,1)S(1)} %add_convert_fusion.2), channel_id=1, source_target_pairs={{0,1},{2,3},{4,5},{6,7},{8,9},{10,11},{12,13},{14,15},{16,17},{18,... | collective-permute-start | bytes 1572872 | tf_op jit(solution)/shard_map/ppermute | solution.py:31
  74.4 5.5 %broadcast_select_fusion.2 = (bf16[32,512]{1,0:T(8,128)(2,1)S(1)}, bf16[32,512]{1,0:T(8,128)(2,1)S(1)}) fusion(bf16[32,512]{1,0:T(8,128)(2,1)S(1)} %fusion.38, pred[]{:T(512)S(6)} %eq.5, bf16[32,8192]{1,0:T(8,128)(2,1)S(1)} %collective-permute-done.7, bf16[1,8192,512]{2,1,0:T(8,128)(2,1)} %param.12), kind=kOutput, calls=%fused_computation.159 | convolution fusion | flops 268468224 | bytes 9011201 | tf_op jit(solution)/shard_map/dot_general | solution.py:13
  80.0 1.6 %collective-permute-start.13 = (bf16[80,512]{1,0:T(8,128)(2,1)S(1)}, bf16[80,512]{1,0:T(8,128)(2,1)S(1)}, u32[]{:S(2)}, u32[]{:S(2)}) collective-permute-start(bf16[80,512]{1,0:T(8,128)(2,1)S(1)} %pad_maximum_fusion.4), channel_id=1, source_target_pairs={{0,8},{8,0},{16,24},{24,16},{1,9},{9,1},{17,25},{25,17},{2,10},{10... | collective-permute-start | bytes 245768 | tf_op jit(solution)/shard_map/ppermute | solution.py:22
  86.1 2.7 %fusion.159 = f32[512,64]{0,1:T(8,128)S(1)} fusion(bf16[512,8192]{1,0:T(8,128)(2,1)S(1)} %bitcast.170, bf16[64,8192]{1,0:T(8,128)(2,1)S(1)} %slice_dynamic-update-slice_fusion), kind=kOutput, calls=%fused_computation.197 | convolution fusion | flops 536870912 | bytes 9568256 | tf_op jit(solution)/shard_map/dot_general | solution.py:17
  90.9 1.6 %add_convert_fusion = bf16[32,8192]{1,0:T(8,128)(2,1)S(1)} fusion(bf16[32,8192]{1,0:T(8,128)(2,1)S(1)} %collective-permute-done.8, bf16[32,512]{1,0:T(8,128)(2,1)S(1)} %fusion.44, bf16[1,512,8192]{2,1,0:T(8,128)(2,1)S(1)} %bitcast.168), kind=kOutput, calls=%fused_computation.45 | convolution fusion | flops 269484032 | bytes 9469952 | tf_op jit(solution)/shard_map/dot_general | solution.py:13
  92.5 4.1 %collective-permute-start.16 = (bf16[32,8192]{1,0:T(8,128)(2,1)S(1)}, bf16[32,8192]{1,0:T(8,128)(2,1)S(1)}, u32[]{:S(2)}, u32[]{:S(2)}) collective-permute-start(bf16[32,8192]{1,0:T(8,128)(2,1)S(1)} %add_convert_fusion), channel_id=1, source_target_pairs={{0,1},{2,3},{4,5},{6,7},{8,9},{10,11},{12,13},{14,15},{16,17},{18,... | collective-permute-start | bytes 1572872 | tf_op jit(solution)/shard_map/ppermute | solution.py:31
  105.1 2.4 %collective-permute-done.19 = bf16[32,512]{1,0:T(8,128)(2,1)S(1)} collective-permute-done((bf16[32,512]{1,0:T(8,128)(2,1)S(1)}, bf16[32,512]{1,0:T(8,128)(2,1)S(1)}, u32[]{:S(2)}, u32[]{:S(2)}) %collective-permute-start.19) | collective-permute-done | bytes 32800 | tf_op jit(solution)/shard_map/ppermute | solution.py:22
  109.4 4.4 %collective-permute-start.21 = (f32[4,32]{1,0:T(4,128)S(1)}, f32[4,32]{1,0:T(4,128)S(1)}, u32[]{:S(2)}, u32[]{:S(2)}) collective-permute-start(f32[4,32]{1,0:T(4,128)S(1)} %add.114), channel_id=1, source_target_pairs={{0,2},{1,3},{2,0},{3,1},{4,6},{5,7},{6,4},{7,5},{8,10},{9,11},{10,... | collective-permute-start | bytes 1544 | tf_op jit(solution)/shard_map/ppermute | solution.py:22
  113.9 3.8 %collective-permute-start.22 = (f32[4,32]{1,0:T(4,128)S(1)}, f32[4,32]{1,0:T(4,128)S(1)}, u32[]{:S(2)}, u32[]{:S(2)}) collective-permute-start(f32[4,32]{1,0:T(4,128)S(1)} %add.114), channel_id=1, source_target_pairs={{0,4},{1,5},{2,6},{3,7},{4,0},{5,1},{6,2},{7,3},{8,12},{9,13},{10,... | collective-permute-start | bytes 1544 | tf_op jit(solution)/shard_map/ppermute | solution.py:22
  117.7 1.6 %collective-permute-done.22 = f32[4,32]{1,0:T(4,128)S(1)} collective-permute-done((f32[4,32]{1,0:T(4,128)S(1)}, f32[4,32]{1,0:T(4,128)S(1)}, u32[]{:S(2)}, u32[]{:S(2)}) %collective-permute-start.22) | collective-permute-done | bytes 544 | tf_op jit(solution)/shard_map/ppermute | solution.py:22
  119.3 3.8 %collective-permute-done.23 = f32[4,32]{1,0:T(4,128)S(1)} collective-permute-done((f32[4,32]{1,0:T(4,128)S(1)}, f32[4,32]{1,0:T(4,128)S(1)}, u32[]{:S(2)}, u32[]{:S(2)}) %collective-permute-start.23) | collective-permute-done | bytes 544 | tf_op jit(solution)/shard_map/ppermute | solution.py:22
  (136 shorter events, 36.5 us)
Async XLA Ops:
  7.2 3.8 %collective-permute-start = (bf16[16,8192]{1,0:T(8,128)(2,1)S(1)}, bf16[16,8192]{1,0:T(8,128)(2,1)S(1)}, u32[]{:S(2)}, u32[]{:S(2)}) collective-permute-start(bf16[16,8192]{1,0:T(8,128)(2,1)S(1)} %get-tuple-element.36), channel_id=1, source_target_pairs={{0,1},{2,3},{4,5},{6,7},{8,9},{10,11},{12,13},{14,15},{16,17},{18,... | collective-permute-start | bytes 786440 | tf_op jit(solution)/shard_map/ppermute | solution.py:31
  13.4 7.8 %collective-permute-start.1 = (bf16[32,8192]{1,0:T(8,128)(2,1)S(1)}, bf16[32,8192]{1,0:T(8,128)(2,1)S(1)}, u32[]{:S(2)}, u32[]{:S(2)}) collective-permute-start(bf16[32,8192]{1,0:T(8,128)(2,1)S(1)} %pad_maximum_fusion), channel_id=1, source_target_pairs={{1,2},{3,4},{5,6},{9,10},{11,12},{13,14},{17,18},{19,20},{21,22},{... | collective-permute-start | bytes 1572872 | tf_op jit(solution)/shard_map/ppermute | solution.py:31
  24.3 9.5 %collective-permute-start.2 = (bf16[32,8192]{1,0:T(8,128)(2,1)S(1)}, bf16[32,8192]{1,0:T(8,128)(2,1)S(1)}, u32[]{:S(2)}, u32[]{:S(2)}) collective-permute-start(bf16[32,8192]{1,0:T(8,128)(2,1)S(1)} %add_convert_fusion.4), channel_id=1, source_target_pairs={{0,1},{2,3},{4,5},{6,7},{8,9},{10,11},{12,13},{14,15},{16,17},{18,... | collective-permute-start | bytes 1572872 | tf_op jit(solution)/shard_map/ppermute | solution.py:31
  30.3 18.9 %collective-permute-start.3 = (bf16[16,8192]{1,0:T(8,128)(2,1)}, bf16[16,8192]{1,0:T(8,128)(2,1)S(1)}, u32[]{:S(2)}, u32[]{:S(2)}) collective-permute-start(bf16[16,8192]{1,0:T(8,128)(2,1)} %get-tuple-element.19), channel_id=1, source_target_pairs={{0,8},{8,0},{16,24},{24,16},{1,9},{9,1},{17,25},{25,17},{2,10},{10... | collective-permute-start | bytes 786440 | tf_op jit(solution)/shard_map/ppermute | solution.py:22
  31.8 17.4 %collective-permute-start.4 = (bf16[16,8192]{1,0:T(8,128)(2,1)}, bf16[16,8192]{1,0:T(8,128)(2,1)S(1)}, u32[]{:S(2)}, u32[]{:S(2)}) collective-permute-start(bf16[16,8192]{1,0:T(8,128)(2,1)} %get-tuple-element.19), channel_id=1, source_target_pairs={{0,16},{8,24},{16,0},{24,8},{1,17},{9,25},{17,1},{25,9},{2,18},{10... | collective-permute-start | bytes 786440 | tf_op jit(solution)/shard_map/ppermute | solution.py:22
  33.3 16.0 %collective-permute-start.5 = (bf16[16,8192]{1,0:T(8,128)(2,1)}, bf16[16,8192]{1,0:T(8,128)(2,1)S(1)}, u32[]{:S(2)}, u32[]{:S(2)}) collective-permute-start(bf16[16,8192]{1,0:T(8,128)(2,1)} %get-tuple-element.19), channel_id=1, source_target_pairs={{0,24},{8,16},{16,8},{24,0},{1,25},{9,17},{17,9},{25,1},{2,26},{10... | collective-permute-start | bytes 786440 | tf_op jit(solution)/shard_map/ppermute | solution.py:22
  41.1 22.5 %collective-permute-start.6 = (bf16[32,8192]{1,0:T(8,128)(2,1)}, bf16[32,8192]{1,0:T(8,128)(2,1)S(1)}, u32[]{:S(2)}, u32[]{:S(2)}) collective-permute-start(bf16[32,8192]{1,0:T(8,128)(2,1)} %add_convert_fusion.3), channel_id=1, source_target_pairs={{1,2},{3,4},{5,6},{9,10},{11,12},{13,14},{17,18},{19,20},{21,22},{... | collective-permute-start | bytes 1572872 | tf_op jit(solution)/shard_map/ppermute | solution.py:31
  52.1 9.1 %collective-permute-start.9 = (bf16[512,64]{0,1:T(8,128)(2,1)S(1)}, bf16[512,64]{0,1:T(8,128)(2,1)S(1)}, u32[]{:S(2)}, u32[]{:S(2)}) collective-permute-start(bf16[512,64]{0,1:T(8,128)(2,1)S(1)} %get-tuple-element.76), channel_id=1, source_target_pairs={{0,2},{1,3},{2,4},{3,5},{4,6},{5,7},{8,10},{9,11},{10,12},{11,13},... | collective-permute-start | bytes 196616 | tf_op jit(solution)/shard_map/ppermute | solution.py:31
  56.2 6.0 %collective-permute-start.10 = (bf16[512,64]{0,1:T(8,128)(2,1)S(1)}, bf16[512,64]{0,1:T(8,128)(2,1)S(1)}, u32[]{:S(2)}, u32[]{:S(2)}) collective-permute-start(bf16[512,64]{0,1:T(8,128)(2,1)S(1)} %get-tuple-element.76), channel_id=1, source_target_pairs={{0,4},{1,5},{2,6},{3,7},{8,12},{9,13},{10,14},{11,15},{16,20},{17,... | collective-permute-start | bytes 196616 | tf_op jit(solution)/shard_map/ppermute | solution.py:31
  59.8 3.7 %collective-permute-start.11 = (bf16[512,64]{0,1:T(8,128)(2,1)S(1)}, bf16[512,64]{0,1:T(8,128)(2,1)S(1)}, u32[]{:S(2)}, u32[]{:S(2)}) collective-permute-start(bf16[512,64]{0,1:T(8,128)(2,1)S(1)} %get-tuple-element.76), channel_id=1, source_target_pairs={{0,6},{1,7},{8,14},{9,15},{16,22},{17,23},{24,30},{25,31}} | collective-permute-start | bytes 196616 | tf_op jit(solution)/shard_map/ppermute | solution.py:31
  63.6 9.4 %collective-permute-start.12 = (bf16[4,512,64]{1,2,0:T(8,128)(2,1)S(1)}, bf16[4,512,64]{1,2,0:T(8,128)(2,1)S(1)}, u32[]{:S(2)}, u32[]{:S(2)}) collective-permute-start(bf16[4,512,64]{1,2,0:T(8,128)(2,1)S(1)} %pad_maximum_fusion.3), channel_id=1, source_target_pairs={{0,1},{1,0},{2,3},{3,2},{4,5},{5,4},{6,7},{7,6},{8,9},{9,8},{10,11... | collective-permute-start | bytes 786440 | tf_op jit(solution)/shard_map/ppermute | solution.py:22
  71.0 3.5 %collective-permute-start.7 = (bf16[32,8192]{1,0:T(8,128)(2,1)S(1)}, bf16[32,8192]{1,0:T(8,128)(2,1)S(1)}, u32[]{:S(2)}, u32[]{:S(2)}) collective-permute-start(bf16[32,8192]{1,0:T(8,128)(2,1)S(1)} %add_convert_fusion.2), channel_id=1, source_target_pairs={{0,1},{2,3},{4,5},{6,7},{8,9},{10,11},{12,13},{14,15},{16,17},{18,... | collective-permute-start | bytes 1572872 | tf_op jit(solution)/shard_map/ppermute | solution.py:31
  80.0 8.7 %collective-permute-start.13 = (bf16[80,512]{1,0:T(8,128)(2,1)S(1)}, bf16[80,512]{1,0:T(8,128)(2,1)S(1)}, u32[]{:S(2)}, u32[]{:S(2)}) collective-permute-start(bf16[80,512]{1,0:T(8,128)(2,1)S(1)} %pad_maximum_fusion.4), channel_id=1, source_target_pairs={{0,8},{8,0},{16,24},{24,16},{1,9},{9,1},{17,25},{25,17},{2,10},{10... | collective-permute-start | bytes 245768 | tf_op jit(solution)/shard_map/ppermute | solution.py:22
  81.5 7.2 %collective-permute-start.14 = (bf16[80,512]{1,0:T(8,128)(2,1)S(1)}, bf16[80,512]{1,0:T(8,128)(2,1)S(1)}, u32[]{:S(2)}, u32[]{:S(2)}) collective-permute-start(bf16[80,512]{1,0:T(8,128)(2,1)S(1)} %pad_maximum_fusion.4), channel_id=1, source_target_pairs={{0,16},{8,24},{16,0},{24,8},{1,17},{9,25},{17,1},{25,9},{2,18},{10... | collective-permute-start | bytes 245768 | tf_op jit(solution)/shard_map/ppermute | solution.py:22
  83.1 5.7 %collective-permute-start.15 = (bf16[80,512]{1,0:T(8,128)(2,1)S(1)}, bf16[80,512]{1,0:T(8,128)(2,1)S(1)}, u32[]{:S(2)}, u32[]{:S(2)}) collective-permute-start(bf16[80,512]{1,0:T(8,128)(2,1)S(1)} %pad_maximum_fusion.4), channel_id=1, source_target_pairs={{0,24},{8,16},{16,8},{24,0},{1,25},{9,17},{17,9},{25,1},{2,26},{10... | collective-permute-start | bytes 245768 | tf_op jit(solution)/shard_map/ppermute | solution.py:22
  85.1 4.3 %collective-permute-start.8 = (bf16[32,8192]{1,0:T(8,128)(2,1)S(1)}, bf16[32,8192]{1,0:T(8,128)(2,1)S(1)}, u32[]{:S(2)}, u32[]{:S(2)}) collective-permute-start(bf16[32,8192]{1,0:T(8,128)(2,1)S(1)} %add_convert_fusion.1), channel_id=1, source_target_pairs={{1,2},{3,4},{5,6},{9,10},{11,12},{13,14},{17,18},{19,20},{21,22},{... | collective-permute-start | bytes 1572872 | tf_op jit(solution)/shard_map/ppermute | solution.py:31
  92.5 5.6 %collective-permute-start.16 = (bf16[32,8192]{1,0:T(8,128)(2,1)S(1)}, bf16[32,8192]{1,0:T(8,128)(2,1)S(1)}, u32[]{:S(2)}, u32[]{:S(2)}) collective-permute-start(bf16[32,8192]{1,0:T(8,128)(2,1)S(1)} %add_convert_fusion), channel_id=1, source_target_pairs={{0,1},{2,3},{4,5},{6,7},{8,9},{10,11},{12,13},{14,15},{16,17},{18,... | collective-permute-start | bytes 1572872 | tf_op jit(solution)/shard_map/ppermute | solution.py:31
  99.6 4.0 %collective-permute-start.17 = (bf16[32,512]{1,0:T(8,128)(2,1)S(1)}, bf16[32,512]{1,0:T(8,128)(2,1)S(1)}, u32[]{:S(2)}, u32[]{:S(2)}) collective-permute-start(bf16[32,512]{1,0:T(8,128)(2,1)S(1)} %fusion.53), channel_id=1, source_target_pairs={{0,8},{8,0},{16,24},{24,16},{1,9},{9,1},{17,25},{25,17},{2,10},{10... | collective-permute-start | bytes 98312 | tf_op jit(solution)/shard_map/ppermute | solution.py:22
  101.2 3.9 %collective-permute-start.18 = (bf16[32,512]{1,0:T(8,128)(2,1)S(1)}, bf16[32,512]{1,0:T(8,128)(2,1)S(1)}, u32[]{:S(2)}, u32[]{:S(2)}) collective-permute-start(bf16[32,512]{1,0:T(8,128)(2,1)S(1)} %fusion.53), channel_id=1, source_target_pairs={{0,16},{8,24},{16,0},{24,8},{1,17},{9,25},{17,1},{25,9},{2,18},{10... | collective-permute-start | bytes 98312 | tf_op jit(solution)/shard_map/ppermute | solution.py:22
  102.7 4.8 %collective-permute-start.19 = (bf16[32,512]{1,0:T(8,128)(2,1)S(1)}, bf16[32,512]{1,0:T(8,128)(2,1)S(1)}, u32[]{:S(2)}, u32[]{:S(2)}) collective-permute-start(bf16[32,512]{1,0:T(8,128)(2,1)S(1)} %fusion.53), channel_id=1, source_target_pairs={{0,24},{8,16},{16,8},{24,0},{1,25},{9,17},{17,9},{25,1},{2,26},{10... | collective-permute-start | bytes 98312 | tf_op jit(solution)/shard_map/ppermute | solution.py:22
  108.3 1.2 collective-permute-start.20
  109.4 8.3 %collective-permute-start.21 = (f32[4,32]{1,0:T(4,128)S(1)}, f32[4,32]{1,0:T(4,128)S(1)}, u32[]{:S(2)}, u32[]{:S(2)}) collective-permute-start(f32[4,32]{1,0:T(4,128)S(1)} %add.114), channel_id=1, source_target_pairs={{0,2},{1,3},{2,0},{3,1},{4,6},{5,7},{6,4},{7,5},{8,10},{9,11},{10,... | collective-permute-start | bytes 1544 | tf_op jit(solution)/shard_map/ppermute | solution.py:22
  113.9 5.4 %collective-permute-start.22 = (f32[4,32]{1,0:T(4,128)S(1)}, f32[4,32]{1,0:T(4,128)S(1)}, u32[]{:S(2)}, u32[]{:S(2)}) collective-permute-start(f32[4,32]{1,0:T(4,128)S(1)} %add.114), channel_id=1, source_target_pairs={{0,4},{1,5},{2,6},{3,7},{4,0},{5,1},{6,2},{7,3},{8,12},{9,13},{10,... | collective-permute-start | bytes 1544 | tf_op jit(solution)/shard_map/ppermute | solution.py:22
  117.7 5.4 %collective-permute-start.23 = (f32[4,32]{1,0:T(4,128)S(1)}, f32[4,32]{1,0:T(4,128)S(1)}, u32[]{:S(2)}, u32[]{:S(2)}) collective-permute-start(f32[4,32]{1,0:T(4,128)S(1)} %add.114), channel_id=1, source_target_pairs={{0,6},{1,7},{2,4},{3,5},{4,2},{5,3},{6,0},{7,1},{8,14},{9,15},{10,... | collective-permute-start | bytes 1544 | tf_op jit(solution)/shard_map/ppermute | solution.py:22
  (21 other events, 170.4 us)

commit v3 on v2

v3 whole, which is shorter than its diff:
```python
import functools

import jax
import jax.numpy as jnp
from jax import lax
from jax.experimental import pallas as pl
from jax.experimental.pallas import tpu as pltpu
from jax.sharding import PartitionSpec as P

SLOT = 128


adapter_scale = 0.25
bf16 = jnp.bfloat16
f32 = jnp.float32
VMEM = pltpu.VMEM


def dot_nn(a, b):
    return lax.dot_general(a, b, (((1,), (0,)), ((), ())), preferred_element_type=f32)


def dot_nt(a, b):
    return lax.dot_general(a, b, (((1,), (1,)), ((), ())), preferred_element_type=f32)


def swap(value, axis, distance):
    count = lax.axis_size(axis)
    return lax.ppermute(value, axis, [(source, source ^ distance) for source in range(count)])


def spread(value, axis):
    return [value] + [swap(value, axis, d) for d in range(1, lax.axis_size(axis))]


def upward(value, first, hop, stride):
    count = lax.axis_size("pipe")
    return lax.ppermute(
        value, "pipe", [(source, source + hop) for source in range(first, count - hop, stride)]
    )


def tie(values, token):
    *values, _ = lax.optimization_barrier((*values, token))
    return values


def held(value):
    return pltpu.with_memory_space_constraint(value, VMEM)


def call(kernel, operands, places, outs, scratch, flops, moved):
    space = {"v": VMEM, "s": pltpu.SMEM, "a": pl.ANY}
    operands = [held(x) if place == "v" else x for x, place in zip(operands, places)]
    return pl.pallas_call(
        kernel,
        in_specs=[pl.BlockSpec(memory_space=space[place]) for place in places],
        out_specs=[pl.BlockSpec(memory_space=VMEM) for _ in outs],
        out_shape=[VMEM(shape, dtype) for shape, dtype in outs],
        scratch_shapes=scratch,
        cost_estimate=pl.CostEstimate(flops=flops, bytes_accessed=moved, transcendentals=0),
        compiler_params=pltpu.CompilerParams(vmem_limit_bytes=24 * 2**20),
    )(*operands)


PARTS = 8


def prime_kernel(cols, padded, expand, kept, raised, own, sems):
    width = expand.shape[1] // PARTS
    copies = []
    for part in range(PARTS):
        span = pl.ds(part * width, width)
        copy = pltpu.make_async_copy(expand.at[:, span], kept.at[:, span], sems.at[part])
        copy.start()
        copies.append(copy)
    rows = own.shape[0]
    for part in range(PARTS):
        copies[part].wait()
        span = slice(part * width, (part + 1) * width)
        found = adapter_scale * dot_nn(cols[...], kept[:, span])
        raised[:, span] = found.astype(bf16)
        own[:, span] = (found[:rows] + padded[:, span]).astype(bf16)


def keep_kernel(down, kept, sem):
    copy = pltpu.make_async_copy(down, kept, sem)
    copy.start()
    copy.wait()


def through_kernel(flag, arrived, before, down, expand, ranks, leaving):
    depth, width = down.shape
    step = 2 * width

    @pl.when(flag[0] == 0)
    def _():
        ranks[...] = before[...]

    @pl.when(flag[0] != 0)
    def _():
        total = jnp.zeros(ranks.shape, f32)
        for at in range(0, depth, step):
            total += dot_nn(arrived[:, at : at + step], down[at : at + step, :])
        found = total.astype(bf16)
        ranks[...] = found
        for at in range(0, depth, step):
            more = adapter_scale * dot_nn(found, expand[:, at : at + step])
            leaving[:, at : at + step] = (arrived[:, at : at + step].astype(f32) + more).astype(bf16)


def last_kernel(flag, arrived, before, down, ranks):
    depth, width = down.shape
    step = 2 * width

    @pl.when(flag[0] == 0)
    def _():
        ranks[...] = before[...]

    @pl.when(flag[0] != 0)
    def _():
        total = jnp.zeros(ranks.shape, f32)
        for at in range(0, depth, step):
            total += dot_nn(arrived[:, at : at + step], down[at : at + step, :])
        ranks[...] = total.astype(bf16)


def start_rows(source, buffer, sems):
    copies = []
    for part in range(source.shape[0] // SLOT):
        span = pl.ds(part * SLOT, SLOT)
        copy = pltpu.make_async_copy(source.at[span], buffer.at[span], sems.at[part])
        copy.start()
        copies.append(copy)
    return copies


def lift_kernel(cotangent, expand, lifted, buffer, sems):
    copies = start_rows(cotangent, buffer, sems)
    ranks = expand.shape[0]
    half = ranks // 2
    for pair in range(0, len(copies), 2):
        copies[pair].wait()
        copies[pair + 1].wait()
        span = slice(pair * SLOT, (pair + 2) * SLOT)
        for at in range(0, ranks, half):
            found = adapter_scale * dot_nt(buffer[span, :], expand[at : at + half, :])
            lifted[span, at : at + half] = found.astype(bf16)


def value_row(shape, q_dev):
    return (lax.broadcasted_iota(jnp.int32, shape, 0) // q_dev) % 2 == 0


def right_kernel(q_dev, cotangent, rows, raised, right, buffer, woven, sems):
    copies = start_rows(cotangent, buffer, sems)
    depth = rows.shape[1]
    step = depth // PARTS
    for at in range(0, depth, step):
        span = slice(at, at + step)
        first = value_row((rows.shape[0], step), q_dev)
        woven[:, span] = jnp.where(
            first, rows[:, span].astype(f32), raised[:, span].astype(f32)
        ).astype(bf16)
    for part, copy in enumerate(copies):
        copy.wait()
        span = slice(part * SLOT, (part + 1) * SLOT)
        right[span, :] = dot_nt(buffer[span, :], woven[...])


def left_kernel(q_dev, lengths, act, cols, down, rows, left, left_sent, buffer, woven, sems):
    copies = start_rows(act, buffer, sems)
    depth = rows.shape[1]
    step = depth // PARTS
    for at in range(0, depth, step):
        span = slice(at, at + step)
        first = value_row((rows.shape[0], step), q_dev)
        found = adapter_scale * dot_nt(cols[...], down[span, :])
        woven[:, span] = jnp.where(first, found, rows[:, span].astype(f32)).astype(bf16)
    for part, copy in enumerate(copies):
        copy.wait()
        span = slice(part * SLOT, (part + 1) * SLOT)
        found = dot_nt(buffer[span, :], woven[...])
        live = lax.broadcasted_iota(jnp.int32, found.shape, 0) < lengths[part]
        found = jnp.where(live, found, 0.0)
        left[span, :] = found
        left_sent[span, :] = found.astype(bf16)


def local(
    activations,
    cotangent,
    adapter_down,
    adapter_expand,
    value_rows,
    input_rows,
    hidden_cols,
    inner_cols,
    lengths,
    query_example,
):
    columns = lax.axis_size("dp")
    layers = lax.axis_size("pipe")
    chips = layers // 2
    top = chips - 1
    column = lax.axis_index("dp")
    layer = lax.axis_index("pipe")
    upper = (layer % 2).astype(jnp.int32)[None]
    lower = 1 - upper
    tok_dev = activations.shape[1]
    ex_dev = tok_dev // SLOT
    q_dev = value_rows.shape[1]
    rows = 2 * q_dev
    width, rank = adapter_down.shape[1:]
    act = activations[0]
    weight_bytes = 2 * width * rank
    row_sems = pltpu.SemaphoreType.DMA((ex_dev,))

    def woven(cols, place):
        empty = jnp.zeros((q_dev, rank), bf16)
        parts = []
        for d in range(columns):
            block = lax.dynamic_slice_in_dim(cols, (column ^ d) * q_dev, q_dev, 0)
            parts += [block, empty] if place == 0 else [empty, block]
        return jnp.concatenate(parts)

    def through(flag, arrived, before):
        return call(
            through_kernel,
            (flag, arrived, before, down, expand),
            "svvvv",
            [(before.shape, bf16), (arrived.shape, bf16)],
            [],
            4 * arrived.shape[0] * width * rank,
            2 * weight_bytes,
        )

    padded = jnp.concatenate([value_rows[0], jnp.zeros_like(input_rows[0])])
    expand, raised, own = call(
        prime_kernel,
        (woven(inner_cols[0], 1), padded, adapter_expand[0]),
        "vva",
        [((rank, width), bf16), ((columns * rows, width), bf16), ((rows, width), bf16)],
        [pltpu.SemaphoreType.DMA((PARTS,))],
        2 * columns * rows * width * rank,
        2 * weight_bytes,
    )

    arrived = upward(own, 0, 1, 2)
    (source,) = tie([adapter_down[0]], own)
    (down,) = call(
        keep_kernel,
        (source,),
        "a",
        [((width, rank), bf16)],
        [pltpu.SemaphoreType.DMA],
        0,
        2 * weight_bytes,
    )
    empty = jnp.zeros((rows, rank), bf16)
    lower_ranks, leaving = through(upper, arrived, empty)
    moving = jnp.concatenate([leaving, own])

    arrived = upward(moving, 1, 1, 2)
    width_rows, cot = tie([jnp.concatenate([value_rows[0], input_rows[0]]), cotangent], moving)
    width_rows = spread(width_rows, "dp")
    (lifted,) = call(
        lift_kernel,
        (cot, expand),
        "av",
        [((tok_dev, rank), bf16)],
        [VMEM((tok_dev, width), bf16), row_sems],
        2 * tok_dev * width * rank,
        2 * weight_bytes,
    )
    arrived, lifted = lax.optimization_barrier((arrived, lifted))

    slots = []
    empty = jnp.zeros((2 * rows, rank), bf16)
    for slot in range(1, chips):
        found, leaving = through(lower, arrived, empty)
        arrived = upward(leaving, 0, 1, 2)
        if slot == 1:
            width_rows = jnp.concatenate(width_rows)
            arrived, width_rows = lax.optimization_barrier((arrived, width_rows))
        if slot == top:
            break
        found, leaving = through(upper, arrived, found)
        slots.append(found)
        arrived = upward(leaving, 1, 1, 2)
        if slot == 1:
            (x,) = tie([act], leaving)
            left, left_own = call(
                functools.partial(left_kernel, q_dev),
                (lengths, x, woven(hidden_cols[0], 0), down, width_rows),
                "savvv",
                [((tok_dev, columns * rows), f32), ((tok_dev, columns * rows), bf16)],
                [
                    VMEM((tok_dev, width), bf16),
                    VMEM((columns * rows, width), bf16),
                    row_sems,
                ],
                2 * columns * rows * width * (rank + tok_dev),
                2 * weight_bytes,
            )
            left_up = [left_own] + [upward(left_own, 0, 2 * hop, 1) for hop in range(1, chips)]
            arrived, left_own = lax.optimization_barrier((arrived, left_own))
        if slot == top - 1:
            early = jnp.concatenate([lower_ranks] + slots)
            cot, early = tie([cotangent, early], leaving)
            early = spread(early, "dp")
            (right,) = call(
                functools.partial(right_kernel, q_dev),
                (cot, width_rows, raised),
                "avv",
                [((tok_dev, columns * rows), f32)],
                [
                    VMEM((tok_dev, width), bf16),
                    VMEM((columns * rows, width), bf16),
                    row_sems,
                ],
                2 * columns * rows * width * tok_dev,
                weight_bytes,
            )
            left_up = jnp.stack(left_up)
            left_other = swap(left_up, "pipe", 1)
            left_even = jnp.where(upper > 0, left_other, left_up)
            left_odd = jnp.where(upper > 0, left_up, left_other)
            arrived, right = lax.optimization_barrier((arrived, right))

    def weighed(weights, ranks):
        return weights.astype(f32) * dot_nt(lifted, ranks)

    def summed(terms):
        terms = jnp.sum(terms.reshape(ex_dev, SLOT, columns, 2, q_dev), axis=(1, 3))
        return terms.reshape(ex_dev, columns * q_dev)

    terms = left * right + weighed(left_even[0], jnp.concatenate([b[:rows] for b in early]))
    for slot in range(1, top):
        at = rows * (2 * slot - 1)
        terms += weighed(left_even[slot], jnp.concatenate([b[at : at + rows] for b in early]))
        at += rows
        terms += weighed(left_odd[slot], jnp.concatenate([b[at : at + rows] for b in early]))
    sums = summed(terms)
    arrived, sums = lax.optimization_barrier((arrived, sums))

    def between(value, steps):
        pairs = [(2 * a + core, 2 * b + core) for a, b in steps for core in range(2)]
        return lax.ppermute(value, "pipe", pairs)

    parts = [between(sums, [(chip, top)]) for chip in range(top)]
    for part in parts:
        sums = sums + part

    (late,) = call(
        last_kernel,
        (upper, arrived, found, down),
        "svvv",
        [((2 * rows, rank), bf16)],
        [],
        2 * arrived.shape[0] * width * rank,
        weight_bytes,
    )
    late = spread(late, "dp")
    terms = weighed(left_even[-1], jnp.concatenate([b[:rows] for b in late]))
    terms += weighed(left_odd[-1], jnp.concatenate([b[rows:] for b in late]))
    sums = sums + summed(terms)
    sums = sums + lax.ppermute(
        sums, "pipe", [(2 * top, 2 * top + 1), (2 * top + 1, 2 * top)]
    )
    received = [between(sums, [(top, chip)]) for chip in range(top)]
    elsewhere = received[0]
    for part in received[1:]:
        elsewhere = elsewhere + part
    sums = jnp.where(layer >= 2 * top, sums, elsewhere)

    sums = sums.reshape(ex_dev, columns, q_dev)
    totals = jnp.concatenate(
        [lax.dynamic_index_in_dim(sums, column ^ c, 1, keepdims=False) for c in range(columns)],
        axis=1,
    )
    example_ids = column * ex_dev + lax.broadcasted_iota(jnp.int32, (ex_dev,), 0)
    keep_mask = (example_ids[:, None] != query_example[None, :]).astype(f32)
    return totals * SLOT ** (-0.5) * keep_mask


def solution(mesh):
    in_specs = (
        P("pipe", "dp", None),
        P("dp", None),
        P("pipe", None, None),
        P("pipe", None, None),
        P("pipe", "dp", None),
        P("pipe", "dp", None),
        P("pipe", None, None),
        P("pipe", None, None),
        P("dp"),
        P(),
    )
    out_specs = P("dp", None)
    return jax.shard_map(local, mesh=mesh, in_specs=in_specs, out_specs=out_specs, check_vma=False)
```

time: 124 us -> 151 us (1.22)
  matrix products: 57.2 us -> 2.92 us
  local copies, waits for them, and re-layouts: 2.92 us -> 49.7 us
  Pallas kernels: 0 us -> 34.5 us
  other arithmetic: 1.74 us -> 4.31 us
  starting transfers between devices: 45 us -> 42.9 us
    dot_general x25 -> x7, matrix products: 57.2 us -> 2.92 us  [dot_nt(): lax.dot_general(a, b, (((1,), (1,)), ((), ())), preferred_element_type=f32)]
    unnamed x53 -> x66, local copies, waits for them, and re-layouts: 1.72 us -> 48.4 us
    pallas_call x0 -> x12, Pallas kernels: none -> 34.5 us  [call(): pl.pallas_call(kernel, in_specs=[pl.BlockSpec(memory_space=space[place])...]
    ppermute x14 -> x10, waiting for transfers between devices: 10.9 us -> 0.03 us  [swap(): lax.ppermute(value, axis, [(source, source ^ distance) for source in rang...]
    ppermute x0 -> x7, starting transfers between devices: none -> 10.2 us  [the longest x6 9.5 us: between(): return lax.ppermute(value, 'pipe', pairs)]
    ppermute x14 -> x10, starting transfers between devices: 18.9 us -> 11.1 us  [swap(): lax.ppermute(value, axis, [(source, source ^ distance) for source in rang...]
    ppermute x0 -> x7, waiting for transfers between devices: none -> 7.18 us  [the longest x6 7.18 us: between(): return lax.ppermute(value, 'pipe', pairs)]
    ppermute x10, starting transfers between devices: 26.1 us -> 21.7 us  [upward(): lax.ppermute(value, 'pipe', [(source, source + hop) for source in range(f...]
  transfers between devices with their start and end apart: 24 -> 27, of which waited for: 11 -> 7; matrix products, arithmetic and copies ran while one was open for 30% -> 4% of each run, Pallas kernels for 0% -> 18%
where the time goes in v3:
time: 151 us; the launch traced here: 150 us
  local copies, waits for them, and re-layouts  49.7 us (33%)
  starting transfers between devices  42.9 us (28%)
  Pallas kernels  34.5 us (23%)
  waiting for transfers between devices  15.2 us (10%)
  other arithmetic  4.31 us (3%)
  matrix products  2.92 us (2%)
    unnamed x66, local copies, waits for them, and re-layouts  48.4 us
    pallas_call x12, Pallas kernels, call(): pl.pallas_call(kernel, in_specs=[pl.BlockSpec(memory_space=space[place])...  34.5 us
    ppermute x10, starting transfers between devices, upward(): lax.ppermute(value, 'pipe', [(source, source + hop) for source in range(f...  21.7 us
    ppermute x10, starting transfers between devices, swap(): lax.ppermute(value, axis, [(source, source ^ distance) for source in rang...  11.1 us
    ppermute x6, starting transfers between devices, between(): return lax.ppermute(value, 'pipe', pairs)  9.5 us
    ppermute x10, waiting for transfers between devices, upward(): lax.ppermute(value, 'pipe', [(source, source + hop) for source in range(f...  8.01 us
    ppermute x6, waiting for transfers between devices, between(): return lax.ppermute(value, 'pipe', pairs)  7.18 us
  transfers between devices with their start and end apart: 27, of which 7 were waited for; matrix products, arithmetic and copies ran while one was open for 4% of the time, Pallas kernels for 18%

profile of v3, /device:TPU:0, one launch (start us, length us, event | category | flops | bytes accessed | tf_op | source)
XLA Modules:
  0.0 150.4 jit_solution(6183068554274386623)
XLA Ops:
  3.9 3.4 %copy-done.11 = bf16[1,512,8192]{2,1,0:T(8,128)(2,1)S(1)} copy-done((bf16[1,512,8192]{2,1,0:T(8,128)(2,1)S(1)}, bf16[1,512,8192]{2,1,0:T(8,128)(2,1)}, u32[]{:S(2)}) %copy-start.11) | copy-done | bytes 8388632
  7.3 4.5 %shard_map.100 = (bf16[512,8192]{1,0:T(8,128)(2,1)S(1)}, bf16[64,8192]{1,0:T(8,128)(2,1)S(1)}, bf16[16,8192]{1,0:T(8,128)(2,1)S(1)}) custom-call(bf16[64,512]{1,0:T(8,128)(2,1)S(1)} %constant_dynamic-update-slice_fusion.cols, bf16[16,8192]{1,0:T(8,128)(2,1)S(1)} %get-tuple-element.72.padded, bf16[512,8192]{1,0:T(8,128)(2,1)S(1)} %bitcast.81), custom_call_target="tpu_custom_call" | custom-call | flops 536870912 | bytes 16777216 | tf_op jit(solution)/shard_map/pallas_call | solution.py:55
  11.8 3.3 %copy-done.5 = bf16[512,8192]{1,0:T(8,128)(2,1)} copy-done((bf16[512,8192]{1,0:T(8,128)(2,1)}, bf16[512,8192]{1,0:T(8,128)(2,1)S(1)}, u32[]{:S(2)}) %copy-start.5) | copy-done | bytes 8388632
  17.5 3.4 %copy-done.12 = bf16[1,8192,512]{2,1,0:T(8,128)(2,1)S(1)} copy-done((bf16[1,8192,512]{2,1,0:T(8,128)(2,1)S(1)}, bf16[1,8192,512]{2,1,0:T(8,128)(2,1)}, u32[]{:S(2)}) %copy-start.12) | copy-done | bytes 8388632
  21.4 3.3 %copy-done = bf16[8192,512]{1,0:T(8,128)(2,1)} copy-done((bf16[8192,512]{1,0:T(8,128)(2,1)}, bf16[8192,512]{1,0:T(8,128)(2,1)S(1)}, u32[]{:S(2)}) %copy-start) | copy-done | bytes 8388632
  24.8 3.4 %copy-done.1 = bf16[8192,512]{1,0:T(8,128)(2,1)S(1)} copy-done((bf16[8192,512]{1,0:T(8,128)(2,1)S(1)}, bf16[8192,512]{1,0:T(8,128)(2,1)}, u32[]{:S(2)}) %copy-start.1) | copy-done | bytes 8388632
  28.1 3.4 %copy-done.6 = bf16[512,8192]{1,0:T(8,128)(2,1)S(1)} copy-done((bf16[512,8192]{1,0:T(8,128)(2,1)S(1)}, bf16[512,8192]{1,0:T(8,128)(2,1)}, u32[]{:S(2)}) %copy-start.6) | copy-done | bytes 8388632
  32.4 3.3 %collective-permute-start.5 = (bf16[16,8192]{1,0:T(8,128)(2,1)S(1)}, bf16[16,8192]{1,0:T(8,128)(2,1)S(1)}, u32[]{:S(2)}, u32[]{:S(2)}) collective-permute-start(bf16[16,8192]{1,0:T(8,128)(2,1)S(1)} %get-tuple-element.44), channel_id=1, source_target_pairs={{0,24},{8,16},{16,8},{24,0},{1,25},{9,17},{17,9},{25,1},{2,26},{10... | collective-permute-start | bytes 786440 | tf_op jit(solution)/shard_map/ppermute | solution.py:29
  36.4 3.4 %copy-done.9 = bf16[512,8192]{1,0:T(8,128)(2,1)S(1)} copy-done((bf16[512,8192]{1,0:T(8,128)(2,1)S(1)}, bf16[512,8192]{1,0:T(8,128)(2,1)}, u32[]{:S(2)}) %copy-start.9) | copy-done | bytes 8388632
  39.8 5.3 %shard_map.103 = bf16[512,512]{1,0:T(8,128)(2,1)S(1)} custom-call(bf16[512,8192]{1,0:T(8,128)(2,1)S(1)} %copy-done.9, bf16[512,8192]{1,0:T(8,128)(2,1)S(1)} %copy-done.6), custom_call_target="tpu_custom_call" | custom-call | flops 4294967296 | bytes 16777216 | tf_op jit(solution)/shard_map/pallas_call | solution.py:55
  45.2 3.1 %shard_map.104 = (bf16[32,512]{1,0:T(8,128)(2,1)S(1)}, bf16[32,8192]{1,0:T(8,128)(2,1)S(1)}) custom-call(s32[1]{0:T(128)S(6)} %sub.3.flag, bf16[32,8192]{1,0:T(8,128)(2,1)S(1)} %collective-permute-done.1.arrived, bf16[32,512]{1,0:T(8,128)(2,1)S(1)} %broadcast_in_dim.25.before, bf16[8192,512]{1,0:T(8,128)(2,1)S(1)} %bitcast.80, bf16[512,8192]{1,0:T(8,128)(2,1)S(1)} %copy-done.6), custom_call_target="tpu_custom_call" | custom-call | flops 536870912 | bytes 16777216 | tf_op jit(solution)/shard_map/pallas_call | solution.py:55
  54.8 8.6 %shard_map.106 = (f32[512,64]{1,0:T(8,128)S(1)}, bf16[512,64]{1,0:T(8,128)(2,1)S(1)}) custom-call(s32[4]{0:T(128)S(1)} %copy-done.15, bf16[512,8192]{1,0:T(8,128)(2,1)S(1)} %bitcast.85, bf16[64,512]{1,0:T(8,128)(2,1)S(1)} %constant_dynamic-update-slice_fusion.10.cols, bf16[8192,512]{1,0:T(8,128)(2,1)S(1)} %bitcast.80, bf16[64,8192]{1,0:T(8,128)(2,1)S(1)} %pad_maximum_fusion.rows), custom_call_target="tpu_custom_call" | custom-call | flops 1073741824 | bytes 16777216 | tf_op jit(solution)/shard_map/pallas_call | solution.py:55
  63.4 6.5 %collective-permute-start.12 = (bf16[512,64]{1,0:T(8,128)(2,1)S(1)}, bf16[512,64]{1,0:T(8,128)(2,1)S(1)}, u32[]{:S(2)}, u32[]{:S(2)}) collective-permute-start(bf16[512,64]{1,0:T(8,128)(2,1)S(1)} %get-tuple-element.50), channel_id=1, source_target_pairs={{0,6},{1,7},{8,14},{9,15},{16,22},{17,23},{24,30},{25,31}} | collective-permute-start | bytes 196616 | tf_op jit(solution)/shard_map/ppermute | solution.py:38
  80.4 3.9 %shard_map.107 = (bf16[32,512]{1,0:T(8,128)(2,1)S(1)}, bf16[32,8192]{1,0:T(8,128)(2,1)}) custom-call(s32[1]{0:T(128)S(6)} %sub.3.flag, bf16[32,8192]{1,0:T(8,128)(2,1)S(1)} %collective-permute-done.6.arrived, bf16[32,512]{1,0:T(8,128)(2,1)S(1)} %broadcast_in_dim.25.before, bf16[8192,512]{1,0:T(8,128)(2,1)S(1)} %bitcast.80, bf16[512,8192]{1,0:T(8,128)(2,1)S(1)} %copy-done.6), custom_call_target="tpu_custom_call" | custom-call | flops 536870912 | bytes 16777216 | tf_op jit(solution)/shard_map/pallas_call | solution.py:55
  87.3 3.4 %copy-done.2 = bf16[8192,512]{1,0:T(8,128)(2,1)S(1)} copy-done((bf16[8192,512]{1,0:T(8,128)(2,1)S(1)}, bf16[8192,512]{1,0:T(8,128)(2,1)}, u32[]{:S(2)}) %copy-start.2) | copy-done | bytes 8388632
  90.7 3.4 %copy-done.7 = bf16[512,8192]{1,0:T(8,128)(2,1)S(1)} copy-done((bf16[512,8192]{1,0:T(8,128)(2,1)S(1)}, bf16[512,8192]{1,0:T(8,128)(2,1)}, u32[]{:S(2)}) %copy-start.7) | copy-done | bytes 8388632
  98.4 3.4 %copy-done.10 = bf16[512,8192]{1,0:T(8,128)(2,1)S(1)} copy-done((bf16[512,8192]{1,0:T(8,128)(2,1)S(1)}, bf16[512,8192]{1,0:T(8,128)(2,1)}, u32[]{:S(2)}) %copy-start.10) | copy-done | bytes 8388632
  101.7 5.5 %shard_map.109 = f32[512,64]{1,0:T(8,128)S(1)} custom-call(bf16[512,8192]{1,0:T(8,128)(2,1)S(1)} %copy-done.10, bf16[64,8192]{1,0:T(8,128)(2,1)S(1)} %pad_maximum_fusion.rows, bf16[64,8192]{1,0:T(8,128)(2,1)S(1)} %get-tuple-element.59.raised), custom_call_target="tpu_custom_call" | custom-call | flops 536870912 | bytes 8388608 | tf_op jit(solution)/shard_map/pallas_call | solution.py:55
  108.2 3.4 %copy-done.3 = bf16[8192,512]{1,0:T(8,128)(2,1)S(1)} copy-done((bf16[8192,512]{1,0:T(8,128)(2,1)S(1)}, bf16[8192,512]{1,0:T(8,128)(2,1)}, u32[]{:S(2)}) %copy-start.3) | copy-done | bytes 8388632
  111.6 3.4 %copy-done.8 = bf16[512,8192]{1,0:T(8,128)(2,1)S(1)} copy-done((bf16[512,8192]{1,0:T(8,128)(2,1)S(1)}, bf16[512,8192]{1,0:T(8,128)(2,1)}, u32[]{:S(2)}) %copy-start.8) | copy-done | bytes 8388632
  118.0 3.8 %collective-permute-start.9 = (bf16[32,8192]{1,0:T(8,128)(2,1)S(1)}, bf16[32,8192]{1,0:T(8,128)(2,1)S(1)}, u32[]{:S(2)}, u32[]{:S(2)}) collective-permute-start(bf16[32,8192]{1,0:T(8,128)(2,1)S(1)} %get-tuple-element.61), channel_id=1, source_target_pairs={{0,1},{2,3},{4,5},{6,7},{8,9},{10,11},{12,13},{14,15},{16,17},{18,... | collective-permute-start | bytes 1572872 | tf_op jit(solution)/shard_map/ppermute | solution.py:38
  123.3 3.4 %copy-done.4 = bf16[8192,512]{1,0:T(8,128)(2,1)S(1)} copy-done((bf16[8192,512]{1,0:T(8,128)(2,1)S(1)}, bf16[8192,512]{1,0:T(8,128)(2,1)}, u32[]{:S(2)}) %copy-start.4) | copy-done | bytes 8388632
  131.5 5.6 %collective-permute-start.17 = (f32[4,32]{1,0:T(4,128)S(1)}, f32[4,32]{1,0:T(4,128)S(1)}, u32[]{:S(2)}, u32[]{:S(2)}) collective-permute-start(f32[4,32]{1,0:T(4,128)S(1)} %copy.45), channel_id=1, source_target_pairs={{0,6},{1,7},{8,14},{9,15},{16,22},{17,23},{24,30},{25,31}} | collective-permute-start | bytes 1544 | tf_op jit(solution)/shard_map/ppermute | solution.py:349
  142.5 7.2 %collective-permute-done.24 = f32[4,32]{1,0:T(4,128)S(1)} collective-permute-done((f32[4,32]{1,0:T(4,128)S(1)}, f32[4,32]{1,0:T(4,128)S(1)}, u32[]{:S(2)}, u32[]{:S(2)}) %collective-permute-start.24) | collective-permute-done | bytes 544 | tf_op jit(solution)/shard_map/ppermute | solution.py:349
  (150 shorter events, 48.7 us)
Async XLA Ops:
  15.1 9.7 %collective-permute-start = (bf16[16,8192]{1,0:T(8,128)(2,1)S(1)}, bf16[16,8192]{1,0:T(8,128)(2,1)S(1)}, u32[]{:S(2)}, u32[]{:S(2)}) collective-permute-start(bf16[16,8192]{1,0:T(8,128)(2,1)S(1)} %get-tuple-element.37), channel_id=1, source_target_pairs={{0,1},{2,3},{4,5},{6,7},{8,9},{10,11},{12,13},{14,15},{16,17},{18,... | collective-permute-start | bytes 786440 | tf_op jit(solution)/shard_map/ppermute | solution.py:38
  31.6 13.6 %collective-permute-start.1 = (bf16[32,8192]{1,0:T(8,128)(2,1)S(1)}, bf16[32,8192]{1,0:T(8,128)(2,1)S(1)}, u32[]{:S(2)}, u32[]{:S(2)}) collective-permute-start(bf16[32,8192]{1,0:T(8,128)(2,1)S(1)} %constant_dynamic-update-slice_fusion.8), channel_id=1, source_target_pairs={{1,2},{3,4},{5,6},{9,10},{11,12},{13,14},{17,18},{19,20},{21,22},{... | collective-permute-start | bytes 1572872 | tf_op jit(solution)/shard_map/ppermute | solution.py:38
  32.4 17.3 %collective-permute-start.5 = (bf16[16,8192]{1,0:T(8,128)(2,1)S(1)}, bf16[16,8192]{1,0:T(8,128)(2,1)S(1)}, u32[]{:S(2)}, u32[]{:S(2)}) collective-permute-start(bf16[16,8192]{1,0:T(8,128)(2,1)S(1)} %get-tuple-element.44), channel_id=1, source_target_pairs={{0,24},{8,16},{16,8},{24,0},{1,25},{9,17},{17,9},{25,1},{2,26},{10... | collective-permute-start | bytes 786440 | tf_op jit(solution)/shard_map/ppermute | solution.py:29
  35.8 14.0 %collective-permute-start.4 = (bf16[16,8192]{1,0:T(8,128)(2,1)S(1)}, bf16[16,8192]{1,0:T(8,128)(2,1)S(1)}, u32[]{:S(2)}, u32[]{:S(2)}) collective-permute-start(bf16[16,8192]{1,0:T(8,128)(2,1)S(1)} %get-tuple-element.44), channel_id=1, source_target_pairs={{0,16},{8,24},{16,0},{24,8},{1,17},{9,25},{17,1},{25,9},{2,18},{10... | collective-permute-start | bytes 786440 | tf_op jit(solution)/shard_map/ppermute | solution.py:29
  36.3 13.5 %collective-permute-start.3 = (bf16[16,8192]{1,0:T(8,128)(2,1)S(1)}, bf16[16,8192]{1,0:T(8,128)(2,1)S(1)}, u32[]{:S(2)}, u32[]{:S(2)}) collective-permute-start(bf16[16,8192]{1,0:T(8,128)(2,1)S(1)} %get-tuple-element.44), channel_id=1, source_target_pairs={{0,8},{8,0},{16,24},{24,16},{1,9},{9,1},{17,25},{25,17},{2,10},{10... | collective-permute-start | bytes 786440 | tf_op jit(solution)/shard_map/ppermute | solution.py:29
  51.3 29.1 %collective-permute-start.6 = (bf16[32,8192]{1,0:T(8,128)(2,1)S(1)}, bf16[32,8192]{1,0:T(8,128)(2,1)S(1)}, u32[]{:S(2)}, u32[]{:S(2)}) collective-permute-start(bf16[32,8192]{1,0:T(8,128)(2,1)S(1)} %get-tuple-element.47), channel_id=1, source_target_pairs={{1,2},{3,4},{5,6},{9,10},{11,12},{13,14},{17,18},{19,20},{21,22},{... | collective-permute-start | bytes 1572872 | tf_op jit(solution)/shard_map/ppermute | solution.py:38
  63.4 10.4 %collective-permute-start.12 = (bf16[512,64]{1,0:T(8,128)(2,1)S(1)}, bf16[512,64]{1,0:T(8,128)(2,1)S(1)}, u32[]{:S(2)}, u32[]{:S(2)}) collective-permute-start(bf16[512,64]{1,0:T(8,128)(2,1)S(1)} %get-tuple-element.50), channel_id=1, source_target_pairs={{0,6},{1,7},{8,14},{9,15},{16,22},{17,23},{24,30},{25,31}} | collective-permute-start | bytes 196616 | tf_op jit(solution)/shard_map/ppermute | solution.py:38
  69.8 6.8 %collective-permute-start.11 = (bf16[512,64]{1,0:T(8,128)(2,1)S(1)}, bf16[512,64]{1,0:T(8,128)(2,1)S(1)}, u32[]{:S(2)}, u32[]{:S(2)}) collective-permute-start(bf16[512,64]{1,0:T(8,128)(2,1)S(1)} %get-tuple-element.50), channel_id=1, source_target_pairs={{0,4},{1,5},{2,6},{3,7},{8,12},{9,13},{10,14},{11,15},{16,20},{17,... | collective-permute-start | bytes 196616 | tf_op jit(solution)/shard_map/ppermute | solution.py:38
  71.1 8.3 %collective-permute-start.10 = (bf16[512,64]{1,0:T(8,128)(2,1)S(1)}, bf16[512,64]{1,0:T(8,128)(2,1)S(1)}, u32[]{:S(2)}, u32[]{:S(2)}) collective-permute-start(bf16[512,64]{1,0:T(8,128)(2,1)S(1)} %get-tuple-element.50), channel_id=1, source_target_pairs={{0,2},{1,3},{2,4},{3,5},{4,6},{5,7},{8,10},{9,11},{10,12},{11,13},... | collective-permute-start | bytes 196616 | tf_op jit(solution)/shard_map/ppermute | solution.py:38
  80.3 5.3 %collective-permute-start.13 = (bf16[4,512,64]{2,1,0:T(8,128)(2,1)}, bf16[4,512,64]{2,1,0:T(8,128)(2,1)}, u32[]{:S(2)}, u32[]{:S(2)}) collective-permute-start(bf16[4,512,64]{2,1,0:T(8,128)(2,1)} %pad_maximum_fusion.1), channel_id=1, source_target_pairs={{0,1},{1,0},{2,3},{3,2},{4,5},{5,4},{6,7},{7,6},{8,9},{9,8},{10,11... | collective-permute-start | bytes 786440 | tf_op jit(solution)/shard_map/ppermute | solution.py:29
  84.3 3.0 %collective-permute-start.7 = (bf16[32,8192]{1,0:T(8,128)(2,1)}, bf16[32,8192]{1,0:T(8,128)(2,1)S(1)}, u32[]{:S(2)}, u32[]{:S(2)}) collective-permute-start(bf16[32,8192]{1,0:T(8,128)(2,1)} %get-tuple-element.52), channel_id=1, source_target_pairs={{0,1},{2,3},{4,5},{6,7},{8,9},{10,11},{12,13},{14,15},{16,17},{18,... | collective-permute-start | bytes 1572872 | tf_op jit(solution)/shard_map/ppermute | solution.py:38
  94.1 14.1 %collective-permute-start.8 = (bf16[32,8192]{1,0:T(8,128)(2,1)S(1)}, bf16[32,8192]{1,0:T(8,128)(2,1)S(1)}, u32[]{:S(2)}, u32[]{:S(2)}) collective-permute-start(bf16[32,8192]{1,0:T(8,128)(2,1)S(1)} %get-tuple-element.54), channel_id=1, source_target_pairs={{1,2},{3,4},{5,6},{9,10},{11,12},{13,14},{17,18},{19,20},{21,22},{... | collective-permute-start | bytes 1572872 | tf_op jit(solution)/shard_map/ppermute | solution.py:38
  94.8 12.4 %collective-permute-start.16 = (bf16[80,512]{1,0:T(8,128)(2,1)S(1)}, bf16[80,512]{1,0:T(8,128)(2,1)S(1)}, u32[]{:S(2)}, u32[]{:S(2)}) collective-permute-start(bf16[80,512]{1,0:T(8,128)(2,1)S(1)} %pad_maximum_fusion.3), channel_id=1, source_target_pairs={{0,24},{8,16},{16,8},{24,0},{1,25},{9,17},{17,9},{25,1},{2,26},{10... | collective-permute-start | bytes 245768 | tf_op jit(solution)/shard_map/ppermute | solution.py:29
  97.3 10.0 %collective-permute-start.15 = (bf16[80,512]{1,0:T(8,128)(2,1)S(1)}, bf16[80,512]{1,0:T(8,128)(2,1)S(1)}, u32[]{:S(2)}, u32[]{:S(2)}) collective-permute-start(bf16[80,512]{1,0:T(8,128)(2,1)S(1)} %pad_maximum_fusion.3), channel_id=1, source_target_pairs={{0,16},{8,24},{16,0},{24,8},{1,17},{9,25},{17,1},{25,9},{2,18},{10... | collective-permute-start | bytes 245768 | tf_op jit(solution)/shard_map/ppermute | solution.py:29
  97.8 9.5 %collective-permute-start.14 = (bf16[80,512]{1,0:T(8,128)(2,1)S(1)}, bf16[80,512]{1,0:T(8,128)(2,1)S(1)}, u32[]{:S(2)}, u32[]{:S(2)}) collective-permute-start(bf16[80,512]{1,0:T(8,128)(2,1)S(1)} %pad_maximum_fusion.3), channel_id=1, source_target_pairs={{0,8},{8,0},{16,24},{24,16},{1,9},{9,1},{17,25},{25,17},{2,10},{10... | collective-permute-start | bytes 245768 | tf_op jit(solution)/shard_map/ppermute | solution.py:29
  118.0 5.3 %collective-permute-start.9 = (bf16[32,8192]{1,0:T(8,128)(2,1)S(1)}, bf16[32,8192]{1,0:T(8,128)(2,1)S(1)}, u32[]{:S(2)}, u32[]{:S(2)}) collective-permute-start(bf16[32,8192]{1,0:T(8,128)(2,1)S(1)} %get-tuple-element.61), channel_id=1, source_target_pairs={{0,1},{2,3},{4,5},{6,7},{8,9},{10,11},{12,13},{14,15},{16,17},{18,... | collective-permute-start | bytes 1572872 | tf_op jit(solution)/shard_map/ppermute | solution.py:38
  126.7 4.8 %collective-permute-start.22 = (bf16[32,512]{1,0:T(8,128)(2,1)S(1)}, bf16[32,512]{1,0:T(8,128)(2,1)S(1)}, u32[]{:S(2)}, u32[]{:S(2)}) collective-permute-start(bf16[32,512]{1,0:T(8,128)(2,1)S(1)} %shard_map.111), channel_id=1, source_target_pairs={{0,24},{8,16},{16,8},{24,0},{1,25},{9,17},{17,9},{25,1},{2,26},{10... | collective-permute-start | bytes 98312 | tf_op jit(solution)/shard_map/ppermute | solution.py:29
  129.1 8.0 %collective-permute-start.21 = (bf16[32,512]{1,0:T(8,128)(2,1)S(1)}, bf16[32,512]{1,0:T(8,128)(2,1)S(1)}, u32[]{:S(2)}, u32[]{:S(2)}) collective-permute-start(bf16[32,512]{1,0:T(8,128)(2,1)S(1)} %shard_map.111), channel_id=1, source_target_pairs={{0,16},{8,24},{16,0},{24,8},{1,17},{9,25},{17,1},{25,9},{2,18},{10... | collective-permute-start | bytes 98312 | tf_op jit(solution)/shard_map/ppermute | solution.py:29
  129.6 7.5 %collective-permute-start.20 = (bf16[32,512]{1,0:T(8,128)(2,1)S(1)}, bf16[32,512]{1,0:T(8,128)(2,1)S(1)}, u32[]{:S(2)}, u32[]{:S(2)}) collective-permute-start(bf16[32,512]{1,0:T(8,128)(2,1)S(1)} %shard_map.111), channel_id=1, source_target_pairs={{0,8},{8,0},{16,24},{24,16},{1,9},{9,1},{17,25},{25,17},{2,10},{10... | collective-permute-start | bytes 98312 | tf_op jit(solution)/shard_map/ppermute | solution.py:29
  130.2 8.9 %collective-permute-start.19 = (f32[4,32]{1,0:T(4,128)S(1)}, f32[4,32]{1,0:T(4,128)S(1)}, u32[]{:S(2)}, u32[]{:S(2)}) collective-permute-start(f32[4,32]{1,0:T(4,128)S(1)} %copy.45), channel_id=1, source_target_pairs={{4,6},{5,7},{12,14},{13,15},{20,22},{21,23},{28,30},{29,31}} | collective-permute-start | bytes 1544 | tf_op jit(solution)/shard_map/ppermute | solution.py:349
  130.8 8.2 %collective-permute-start.18 = (f32[4,32]{1,0:T(4,128)S(1)}, f32[4,32]{1,0:T(4,128)S(1)}, u32[]{:S(2)}, u32[]{:S(2)}) collective-permute-start(f32[4,32]{1,0:T(4,128)S(1)} %copy.45), channel_id=1, source_target_pairs={{2,6},{3,7},{10,14},{11,15},{18,22},{19,23},{26,30},{27,31}} | collective-permute-start | bytes 1544 | tf_op jit(solution)/shard_map/ppermute | solution.py:349
  131.5 7.6 %collective-permute-start.17 = (f32[4,32]{1,0:T(4,128)S(1)}, f32[4,32]{1,0:T(4,128)S(1)}, u32[]{:S(2)}, u32[]{:S(2)}) collective-permute-start(f32[4,32]{1,0:T(4,128)S(1)} %copy.45), channel_id=1, source_target_pairs={{0,6},{1,7},{8,14},{9,15},{16,22},{17,23},{24,30},{25,31}} | collective-permute-start | bytes 1544 | tf_op jit(solution)/shard_map/ppermute | solution.py:349
  140.5 9.2 %collective-permute-start.24 = (f32[4,32]{1,0:T(4,128)S(1)}, f32[4,32]{1,0:T(4,128)S(1)}, u32[]{:S(2)}, u32[]{:S(2)}) collective-permute-start(f32[4,32]{1,0:T(4,128)S(1)} %add.101), channel_id=1, source_target_pairs={{6,0},{7,1},{14,8},{15,9},{22,16},{23,17},{30,24},{31,25}} | collective-permute-start | bytes 1544 | tf_op jit(solution)/shard_map/ppermute | solution.py:349
  141.8 7.9 %collective-permute-start.25 = (f32[4,32]{1,0:T(4,128)S(1)}, f32[4,32]{1,0:T(4,128)S(1)}, u32[]{:S(2)}, u32[]{:S(2)}) collective-permute-start(f32[4,32]{1,0:T(4,128)S(1)} %add.101), channel_id=1, source_target_pairs={{6,2},{7,3},{14,10},{15,11},{22,18},{23,19},{30,26},{31,27}} | collective-permute-start | bytes 1544 | tf_op jit(solution)/shard_map/ppermute | solution.py:349
  (29 other events, 223.5 us)

commit v4 on v2

v4 whole, which is shorter than its diff:
```python
import functools

import jax
import jax.numpy as jnp
from jax import lax
from jax.experimental import pallas as pl
from jax.experimental.pallas import tpu as pltpu
from jax.sharding import PartitionSpec as P

SLOT = 128
PARTS = 8


adapter_scale = 0.25
bf16 = jnp.bfloat16
f32 = jnp.float32
VMEM = pltpu.VMEM


def dot_nn(a, b, precision=None):
    return lax.dot_general(
        a, b, (((1,), (0,)), ((), ())), preferred_element_type=f32, precision=precision
    )


def dot_nt(a, b, precision=None):
    return lax.dot_general(
        a, b, (((1,), (1,)), ((), ())), preferred_element_type=f32, precision=precision
    )


def swap(value, axis, distance):
    count = lax.axis_size(axis)
    return lax.ppermute(value, axis, [(source, source ^ distance) for source in range(count)])


def spread(value, axis):
    return [value] + [swap(value, axis, d) for d in range(1, lax.axis_size(axis))]


def upward(value, first, hop, stride):
    count = lax.axis_size("pipe")
    return lax.ppermute(
        value, "pipe", [(source, source + hop) for source in range(first, count - hop, stride)]
    )


def between(value, source, target):
    return lax.ppermute(
        value, "pipe", [(2 * source + core, 2 * target + core) for core in range(2)]
    )


def tie(values, token):
    *values, _ = lax.optimization_barrier((*values, token))
    return values


def call(kernel, operands, places, outs, scratch=(), flops=0, moved=0):
    space = {"v": VMEM, "s": pltpu.SMEM, "h": pltpu.HBM}
    operands = [
        x if place == "s" else pltpu.with_memory_space_constraint(x, space[place])
        for x, place in zip(operands, places)
    ]
    return pl.pallas_call(
        kernel,
        in_specs=[pl.BlockSpec(memory_space=space[place]) for place in places],
        out_specs=[pl.BlockSpec(memory_space=VMEM) for _ in outs],
        out_shape=[VMEM(shape, dtype) for shape, dtype in outs],
        scratch_shapes=list(scratch),
        cost_estimate=pl.CostEstimate(flops=flops, bytes_accessed=moved, transcendentals=0),
        compiler_params=pltpu.CompilerParams(vmem_limit_bytes=16 * 2**20),
    )(*operands)


def picks(shape, q_dev, place):
    row = lax.broadcasted_iota(jnp.int32, shape, 0)
    query = lax.broadcasted_iota(jnp.int32, shape, 1)
    block = lax.axis_index("dp") ^ (row // (2 * q_dev))
    wanted = block * q_dev + row % q_dev
    found = (query == wanted) & ((row // q_dev) % 2 == place)
    return jnp.where(found, 1.0, 0.0)


def halves(shape, q_dev, place):
    row = lax.broadcasted_iota(jnp.int32, shape, 0)
    source = lax.broadcasted_iota(jnp.int32, shape, 1)
    return jnp.where(row == source + place * q_dev, 1.0, 0.0).astype(bf16)


def prime_kernel(cols, values, inputs, expand, kept, raised, own, wide, sems):
    step = expand.shape[1] // PARTS
    copies = []
    for part in range(PARTS):
        span = pl.ds(part * step, step)
        copy = pltpu.make_async_copy(expand.at[:, span], kept.at[:, span], sems.at[part])
        copy.start()
        copies.append(copy)
    rows = own.shape[0]
    q_dev = rows // 2
    laid = picks((raised.shape[0], cols.shape[0]), q_dev, 1).astype(bf16)
    laid = dot_nn(laid, cols[...]).astype(bf16)
    first = halves((rows, q_dev), q_dev, 0)
    second = halves((rows, q_dev), q_dev, 1)
    for part in range(PARTS):
        span = slice(part * step, (part + 1) * step)
        above = dot_nn(first, values[:, span])
        wide[:, span] = (above + dot_nn(second, inputs[:, span])).astype(bf16)
        copies[part].wait()
        found = adapter_scale * dot_nn(laid, kept[:, span])
        raised[:, span] = found.astype(bf16)
        own[:, span] = (found[:rows] + above).astype(bf16)


def keep_kernel(down, kept, sem):
    copy = pltpu.make_async_copy(down, kept, sem)
    copy.start()
    copy.wait()


def through_kernel(turn, arrived, before, down, expand, ranks, leaving):
    depth, width = down.shape
    step = 2 * width
    mine = lax.axis_index("pipe") % 2 == turn

    @pl.when(jnp.logical_not(mine))
    def _():
        ranks[...] = before[...]

    @pl.when(mine)
    def _():
        total = jnp.zeros(ranks.shape, f32)
        for at in range(0, depth, step):
            total += dot_nn(arrived[:, at : at + step], down[at : at + step, :])
        found = total.astype(bf16)
        ranks[...] = found
        for at in range(0, depth, step):
            more = adapter_scale * dot_nn(found, expand[:, at : at + step])
            leaving[:, at : at + step] = (arrived[:, at : at + step].astype(f32) + more).astype(bf16)


def last_kernel(arrived, before, down, ranks):
    depth, width = down.shape
    step = 2 * width
    mine = lax.axis_index("pipe") % 2 == 1

    @pl.when(jnp.logical_not(mine))
    def _():
        ranks[...] = before[...]

    @pl.when(mine)
    def _():
        total = jnp.zeros(ranks.shape, f32)
        for at in range(0, depth, step):
            total += dot_nn(arrived[:, at : at + step], down[at : at + step, :])
        ranks[...] = total.astype(bf16)


def lift_kernel(cotangent, expand, lifted, buffer, sems):
    copies = []
    for part in range(cotangent.shape[0] // SLOT):
        span = pl.ds(part * SLOT, SLOT)
        copy = pltpu.make_async_copy(cotangent.at[span], buffer.at[span], sems.at[part])
        copy.start()
        copies.append(copy)
    ranks = expand.shape[0]
    half = ranks // 2
    for pair in range(0, len(copies), 2):
        copies[pair].wait()
        copies[pair + 1].wait()
        span = slice(pair * SLOT, (pair + 2) * SLOT)
        for at in range(0, ranks, half):
            found = adapter_scale * dot_nt(buffer[span, :], expand[at : at + half, :])
            lifted[span, at : at + half] = found.astype(bf16)


def weave_kernel(q_dev, cols, down, rows, raised, left_rows, right_rows):
    count, depth = rows.shape
    step = depth // PARTS
    laid = picks((count, cols.shape[0]), q_dev, 0).astype(bf16)
    laid = dot_nn(laid, cols[...]).astype(bf16)
    place = lax.broadcasted_iota(jnp.int32, (count, step), 0) // q_dev
    first = place % 2 == 0
    for at in range(0, depth, step):
        span = slice(at, at + step)
        found = adapter_scale * dot_nt(laid, down[span, :])
        given = rows[:, span].astype(f32)
        left_rows[:, span] = jnp.where(first, found, given).astype(bf16)
        right_rows[:, span] = jnp.where(first, given, raised[:, span].astype(f32)).astype(bf16)


def summed(terms, shape):
    example = lax.broadcasted_iota(jnp.int32, (shape[0], terms.shape[1]), 0)
    position = lax.broadcasted_iota(jnp.int32, (shape[0], terms.shape[1]), 1)
    ones = jnp.where(position // SLOT == example, 1.0, 0.0)
    return dot_nt(ones, terms, lax.Precision.HIGHEST)


def weighed(weights, blocks, at, rows, lifted):
    ranks = jnp.concatenate([block[at : at + rows, :].astype(f32) for block in blocks])
    return weights.astype(f32) * dot_nt(ranks.astype(bf16), lifted[...])


def by_layer(own, other):
    upper = jnp.full(own.shape, lax.axis_index("pipe") % 2, jnp.int32) == 1
    own, other = own.astype(f32), other.astype(f32)
    return jnp.where(upper, other, own), jnp.where(upper, own, other)


def early_kernel(chips, rows, left, right, lifted, others, *refs):
    ups, blocks, sums = refs[:chips], refs[chips:-1], refs[-1]
    terms = left[...] * right[...]
    for slot in range(chips - 1):
        lower, upper = by_layer(ups[slot][...], others[slot])
        if slot == 0:
            terms += weighed(lower, blocks, 0, rows, lifted)
        else:
            at = rows * (2 * slot - 1)
            terms += weighed(lower, blocks, at, rows, lifted)
            terms += weighed(upper, blocks, at + rows, rows, lifted)
    sums[...] = summed(terms, sums.shape)


def late_kernel(chips, rows, own, others, lifted, *refs):
    parts, blocks, sums = refs[:chips], refs[chips:-1], refs[-1]
    lower, upper = by_layer(own[...], others[chips - 1])
    terms = weighed(lower, blocks, 0, rows, lifted)
    terms += weighed(upper, blocks, rows, rows, lifted)
    total = summed(terms, sums.shape)
    for part in parts:
        total += part[...]
    sums[...] = total


def final_kernel(chips, q_dev, queries, top_sums, *refs):
    received, scores = refs[:-1], refs[-1]
    total = received[0][...]
    for part in received[1:]:
        total += part[...]
    layer = jnp.full(total.shape, lax.axis_index("pipe"), jnp.int32)
    total = jnp.where(layer >= 2 * (chips - 1), top_sums[...], total)
    ex_dev, q_all = scores.shape
    shape = (total.shape[1], q_all)
    laid = picks(shape, q_dev, 0) + picks(shape, q_dev, 1)
    total = dot_nn(total, laid, lax.Precision.HIGHEST)[:ex_dev]
    example = lax.axis_index("dp") * ex_dev + lax.broadcasted_iota(jnp.int32, scores.shape, 0)
    keep = example != jnp.broadcast_to(queries[...], scores.shape)
    scores[...] = jnp.where(keep, total * SLOT ** (-0.5), 0.0)


def local(
    activations,
    cotangent,
    adapter_down,
    adapter_expand,
    value_rows,
    input_rows,
    hidden_cols,
    inner_cols,
    lengths,
    query_example,
):
    columns = lax.axis_size("dp")
    chips = lax.axis_size("pipe") // 2
    top = chips - 1
    tok_dev = activations.shape[1]
    ex_dev = tok_dev // SLOT
    q_dev = value_rows.shape[1]
    rows = 2 * q_dev
    count = columns * rows
    width, rank = adapter_down.shape[1:]
    weight_bytes = 2 * width * rank
    pass_flops = 2 * rows * width * rank

    offsets = lax.broadcasted_iota(jnp.int32, (ex_dev, SLOT), 1)
    live = (offsets < lengths[:, None]).astype(f32).reshape(1, tok_dev)

    def through(turn, arrived, before):
        return call(
            functools.partial(through_kernel, turn),
            (arrived, before, down, expand),
            "vvvv",
            [(before.shape, bf16), (arrived.shape, bf16)],
            flops=2 * pass_flops,
            moved=weight_bytes,
        )

    expand, raised, own, wide = call(
        prime_kernel,
        (inner_cols[0], value_rows[0], input_rows[0], adapter_expand[0]),
        "vvvh",
        [((rank, width), bf16), ((count, width), bf16), ((rows, width), bf16), ((rows, width), bf16)],
        [pltpu.SemaphoreType.DMA((PARTS,))],
        flops=pass_flops,
        moved=2 * weight_bytes,
    )

    arrived = upward(own, 0, 1, 2)
    (source,) = tie([adapter_down[0]], own)
    (down,) = call(
        keep_kernel,
        (source,),
        "h",
        [((width, rank), bf16)],
        [pltpu.SemaphoreType.DMA],
        moved=2 * weight_bytes,
    )
    arrived, down = lax.optimization_barrier((arrived, down))
    lower_ranks, leaving = through(1, arrived, jnp.zeros((rows, rank), bf16))
    moving = jnp.concatenate([leaving, own])

    arrived = upward(moving, 1, 1, 2)
    wide, cot = tie([wide, cotangent], moving)
    wide = spread(wide, "dp")
    (lifted,) = call(
        lift_kernel,
        (cot, expand),
        "hv",
        [((tok_dev, rank), bf16)],
        [VMEM((tok_dev, width), bf16), pltpu.SemaphoreType.DMA((ex_dev,))],
        flops=2 * tok_dev * width * rank,
        moved=2 * weight_bytes,
    )
    arrived, lifted = lax.optimization_barrier((arrived, lifted))

    slots = []
    empty = jnp.zeros((2 * rows, rank), bf16)
    for slot in range(1, chips):
        found, leaving = through(0, arrived, empty)
        arrived = upward(leaving, 0, 1, 2)
        if slot == 1:
            wide, hid = tie([jnp.concatenate(wide), hidden_cols[0]], leaving)
            left_rows, right_rows = call(
                functools.partial(weave_kernel, q_dev),
                (hid, down, wide, raised),
                "vvvv",
                [((count, width), bf16), ((count, width), bf16)],
                flops=2 * count * width * rank,
                moved=weight_bytes,
            )
            arrived, left_rows = lax.optimization_barrier((arrived, left_rows))
        if slot == 2 or top == 1:
            (cot,) = tie([cotangent], leaving)
            right = dot_nt(right_rows, cot)
            arrived, right = lax.optimization_barrier((arrived, right))
        if slot == top:
            break
        found, leaving = through(1, arrived, found)
        slots.append(found)
        arrived = upward(leaving, 1, 1, 2)
        if slot == 1:
            (act,) = tie([activations[0]], leaving)
            left = dot_nt(left_rows, act) * live
            left_own = left.astype(bf16)
            left_up = [left_own] + [upward(left_own, 0, 2 * hop, 1) for hop in range(1, chips)]
            arrived, left_own = lax.optimization_barrier((arrived, left_own))
        if slot == top - 1:
            early = jnp.concatenate([lower_ranks] + slots)
            early, *left_up = tie([early, *left_up], leaving)
            early = spread(early, "dp")
            others = swap(jnp.stack(left_up), "pipe", 1)
            (sums,) = call(
                functools.partial(early_kernel, chips, rows),
                (left, right, lifted, others, *left_up, *early),
                "v" * (4 + chips + columns),
                [((max(ex_dev, 8), count), f32)],
                flops=2 * count * rank * tok_dev * (2 * chips),
                moved=weight_bytes,
            )
            arrived, sums = lax.optimization_barrier((arrived, sums))

    parts = [sums] + [between(sums, chip, top) for chip in range(top)]
    (late,) = call(
        last_kernel,
        (arrived, found, down),
        "vvv",
        [((2 * rows, rank), bf16)],
        flops=pass_flops,
        moved=weight_bytes,
    )
    late, *parts = lax.optimization_barrier((late, *parts))
    late = spread(late, "dp")
    (sums,) = call(
        functools.partial(late_kernel, chips, rows),
        (left_up[-1], others, lifted, *parts, *late),
        "v" * (3 + chips + columns),
        [(sums.shape, f32)],
        flops=2 * count * rank * tok_dev * 2,
        moved=weight_bytes // 8,
    )
    sums = sums + lax.ppermute(
        sums, "pipe", [(2 * top, 2 * top + 1), (2 * top + 1, 2 * top)]
    )
    received = [between(sums, top, chip) for chip in range(top)]
    (scores,) = call(
        functools.partial(final_kernel, chips, q_dev),
        (query_example[None], sums, *received),
        "v" * (2 + top),
        [((ex_dev, columns * q_dev), f32)],
    )
    return scores


def solution(mesh):
    in_specs = (
        P("pipe", "dp", None),
        P("dp", None),
        P("pipe", None, None),
        P("pipe", None, None),
        P("pipe", "dp", None),
        P("pipe", "dp", None),
        P("pipe", None, None),
        P("pipe", None, None),
        P("dp"),
        P(),
    )
    out_specs = P("dp", None)
    return jax.shard_map(local, mesh=mesh, in_specs=in_specs, out_specs=out_specs, check_vma=False)
```

time: 124 us -> 108 us (0.87)
  matrix products: 57.2 us -> 8.89 us
  Pallas kernels: 0 us -> 28.6 us
  starting transfers between devices: 45 us -> 48.6 us
  other arithmetic: 1.74 us -> 0.19 us
    dot_general x25 -> x2, matrix products: 57.2 us -> 8.89 us  [dot_nt(): lax.dot_general(a, b, (((1,), (1,)), ((), ())), preferred_element_type=f3...]
    pallas_call x0 -> x14, Pallas kernels: none -> 28.6 us  [call(): pl.pallas_call(kernel, in_specs=[pl.BlockSpec(memory_space=space[place])...]
    ppermute x0 -> x7, starting transfers between devices: none -> 12.6 us  [the longest x6 11.9 us: between(): lax.ppermute(value, 'pipe', [(2 * source + core, 2 * target + core) for c...]
    ppermute x14 -> x10, starting transfers between devices: 18.9 us -> 11.3 us  [swap(): lax.ppermute(value, axis, [(source, source ^ distance) for source in rang...]
    ppermute x0 -> x7, waiting for transfers between devices: none -> 7.31 us  [the longest x6 7.31 us: between(): lax.ppermute(value, 'pipe', [(2 * source + core, 2 * target + core) for c...]
    ppermute x14 -> x10, waiting for transfers between devices: 10.9 us -> 7.54 us  [swap(): lax.ppermute(value, axis, [(source, source ^ distance) for source in rang...]
    ppermute x10, waiting for transfers between devices: 5.46 us -> 2.44 us  [upward(): lax.ppermute(value, 'pipe', [(source, source + hop) for source in range(f...]
    unnamed x53 -> x18, local copies, waits for them, and re-layouts: 1.72 us -> 3.2 us
  transfers between devices with their start and end apart: 24 -> 27, of which waited for: 11 -> 9; matrix products, arithmetic and copies ran while one was open for 30% -> 8% of each run, Pallas kernels for 0% -> 16%
where the time goes in v4:
time: 108 us; the launch traced here: 107 us
  starting transfers between devices  48.6 us (45%)
  Pallas kernels  28.6 us (26%)
  waiting for transfers between devices  17.3 us (16%)
  matrix products  8.89 us (8%)
  local copies, waits for them, and re-layouts  3.23 us (3%)
    pallas_call x14, Pallas kernels, call(): pl.pallas_call(kernel, in_specs=[pl.BlockSpec(memory_space=space[place])...  28.6 us
    ppermute x10, starting transfers between devices, upward(): lax.ppermute(value, 'pipe', [(source, source + hop) for source in range(f...  24.8 us
    ppermute x6, starting transfers between devices, between(): lax.ppermute(value, 'pipe', [(2 * source + core, 2 * target + core) for c...  11.9 us
    ppermute x10, starting transfers between devices, swap(): lax.ppermute(value, axis, [(source, source ^ distance) for source in rang...  11.3 us
    dot_general x2, matrix products, dot_nt(): lax.dot_general(a, b, (((1,), (1,)), ((), ())), preferred_element_type=f3...  8.89 us
    ppermute x10, waiting for transfers between devices, swap(): lax.ppermute(value, axis, [(source, source ^ distance) for source in rang...  7.54 us
    ppermute x6, waiting for transfers between devices, between(): lax.ppermute(value, 'pipe', [(2 * source + core, 2 * target + core) for c...  7.31 us
    unnamed x18, local copies, waits for them, and re-layouts  3.2 us
  transfers between devices with their start and end apart: 27, of which 9 were waited for; matrix products, arithmetic and copies ran while one was open for 8% of the time, Pallas kernels for 16%

profile of v4, /device:TPU:0, one launch (start us, length us, event | category | flops | bytes accessed | tf_op | source)
XLA Modules:
  0.0 107.3 jit_solution(8380173583873719502)
XLA Ops:
  2.6 3.9 %shard_map.100 = (bf16[512,8192]{1,0:T(8,128)(2,1)S(1)}, bf16[64,8192]{1,0:T(8,128)(2,1)S(1)}, bf16[16,8192]{1,0:T(8,128)(2,1)S(1)}, bf16[16,8192]{1,0:T(8,128)(2,1)S(1)}) custom-call(bf16[32,512]{1,0:T(8,128)(2,1)S(1)} %bitcast.24, bf16[8,8192]{1,0:T(8,128)(2,1)S(1)} %bitcast.22, bf16[8,8192]{1,0:T(8,128)(2,1)S(1)} %bitcast.23, bf16[512,8192]{1,0:T(8,128)(2,1)} %bitcast.29), custom_call_target="tpu_custom_call" | custom-call | flops 134217728 | bytes 16777216 | tf_op jit(solution)/shard_map/pallas_call | solution.py:65
  6.5 2.4 %collective-permute-start = (bf16[16,8192]{1,0:T(8,128)(2,1)S(1)}, bf16[16,8192]{1,0:T(8,128)(2,1)S(1)}, u32[]{:S(2)}, u32[]{:S(2)}) collective-permute-start(bf16[16,8192]{1,0:T(8,128)(2,1)S(1)} %get-tuple-element.51), channel_id=1, source_target_pairs={{0,1},{2,3},{4,5},{6,7},{8,9},{10,11},{12,13},{14,15},{16,17},{18,... | collective-permute-start | bytes 786440 | tf_op jit(solution)/shard_map/ppermute | solution.py:43
  8.9 3.4 %shard_map.101.down = bf16[8192,512]{1,0:T(8,128)(2,1)S(1)} custom-call(bf16[8192,512]{1,0:T(8,128)(2,1)} %bitcast.30), custom_call_target="tpu_custom_call" | custom-call | bytes 16777216 | tf_op jit(solution)/shard_map/pallas_call | solution.py:65
  13.2 2.3 %collective-permute-start.3 = (bf16[16,8192]{1,0:T(8,128)(2,1)S(1)}, bf16[16,8192]{1,0:T(8,128)(2,1)S(1)}, u32[]{:S(2)}, u32[]{:S(2)}) collective-permute-start(bf16[16,8192]{1,0:T(8,128)(2,1)S(1)} %get-tuple-element.62), channel_id=1, source_target_pairs={{0,8},{8,0},{16,24},{24,16},{1,9},{9,1},{17,25},{25,17},{2,10},{10... | collective-permute-start | bytes 786440 | tf_op jit(solution)/shard_map/ppermute | solution.py:34
  15.5 1.5 %collective-permute-start.4 = (bf16[16,8192]{1,0:T(8,128)(2,1)S(1)}, bf16[16,8192]{1,0:T(8,128)(2,1)S(1)}, u32[]{:S(2)}, u32[]{:S(2)}) collective-permute-start(bf16[16,8192]{1,0:T(8,128)(2,1)S(1)} %get-tuple-element.62), channel_id=1, source_target_pairs={{0,16},{8,24},{16,0},{24,8},{1,17},{9,25},{17,1},{25,9},{2,18},{10... | collective-permute-start | bytes 786440 | tf_op jit(solution)/shard_map/ppermute | solution.py:34
  17.0 7.0 %shard_map.103.lifted = bf16[512,512]{1,0:T(8,128)(2,1)S(1)} custom-call(bf16[512,8192]{1,0:T(8,128)(2,1)} %cotangent, bf16[512,8192]{1,0:T(8,128)(2,1)S(1)} %get-tuple-element.55.expand), custom_call_target="tpu_custom_call" | custom-call | flops 4294967296 | bytes 16777216 | tf_op jit(solution)/shard_map/pallas_call | solution.py:65
  24.0 3.1 %shard_map.104 = (bf16[32,512]{1,0:T(8,128)(2,1)S(1)}, bf16[32,8192]{1,0:T(8,128)(2,1)S(1)}) custom-call(bf16[32,8192]{1,0:T(8,128)(2,1)S(1)} %collective-permute-done.1.arrived, bf16[32,512]{1,0:T(8,128)(2,1)S(1)} %broadcast_in_dim.12.before, bf16[8192,512]{1,0:T(8,128)(2,1)S(1)} %shard_map.101.down, bf16[512,8192]{1,0:T(8,128)(2,1)S(1)} %get-tuple-element.55.expand), custom_call_target="tpu_custom_call" | custom-call | flops 268435456 | bytes 8388608 | tf_op jit(solution)/shard_map/pallas_call | solution.py:65
  27.1 1.4 %collective-permute-start.2 = (bf16[32,8192]{1,0:T(8,128)(2,1)S(1)}, bf16[32,8192]{1,0:T(8,128)(2,1)S(1)}, u32[]{:S(2)}, u32[]{:S(2)}) collective-permute-start(bf16[32,8192]{1,0:T(8,128)(2,1)S(1)} %get-tuple-element.61), channel_id=1, source_target_pairs={{0,1},{2,3},{4,5},{6,7},{8,9},{10,11},{12,13},{14,15},{16,17},{18,... | collective-permute-start | bytes 1572872 | tf_op jit(solution)/shard_map/ppermute | solution.py:43
  28.7 2.7 %shard_map.105 = (bf16[64,8192]{1,0:T(8,128)(2,1)S(1)}, bf16[64,8192]{1,0:T(8,128)(2,1)S(1)}) custom-call(bf16[32,512]{1,0:T(8,128)(2,1)S(1)} %bitcast.25, bf16[8192,512]{1,0:T(8,128)(2,1)S(1)} %shard_map.101.down, bf16[64,8192]{1,0:T(8,128)(2,1)S(1)} %pad_maximum_fusion.rows, bf16[64,8192]{1,0:T(8,128)(2,1)S(1)} %get-tuple-element.65.raised), custom_call_target="tpu_custom_call" | custom-call | flops 536870912 | bytes 8388608 | tf_op jit(solution)/shard_map/pallas_call | solution.py:65
  32.4 6.2 %fusion = (bf16[64,512]{1,0:T(8,128)(2,1)S(1)}, f32[64,512]{1,0:T(8,128)S(1)}) fusion(f32[512]{0:T(512)S(1)} %convert_bitcast_fusion, bf16[64,8192]{1,0:T(8,128)(2,1)S(1)} %get-tuple-element.71, bf16[512,8192]{1,0:T(8,128)(2,1)} %bitcast.31), kind=kOutput, calls=%fused_computation.8 | convolution fusion | flops 536936448 | bytes 9635840 | tf_op jit(solution)/shard_map/dot_general | solution.py:27
  38.6 3.1 %shard_map.107 = (bf16[32,512]{1,0:T(8,128)(2,1)S(1)}, bf16[32,8192]{1,0:T(8,128)(2,1)S(1)}) custom-call(bf16[32,8192]{1,0:T(8,128)(2,1)S(1)} %collective-permute-done.6.arrived, bf16[32,512]{1,0:T(8,128)(2,1)S(1)} %broadcast_in_dim.12.before, bf16[8192,512]{1,0:T(8,128)(2,1)S(1)} %shard_map.101.down, bf16[512,8192]{1,0:T(8,128)(2,1)S(1)} %get-tuple-element.55.expand), custom_call_target="tpu_custom_call" | custom-call | flops 268435456 | bytes 8388608 | tf_op jit(solution)/shard_map/pallas_call | solution.py:65
  41.7 4.3 %collective-permute-start.7 = (bf16[32,8192]{1,0:T(8,128)(2,1)S(1)}, bf16[32,8192]{1,0:T(8,128)(2,1)S(1)}, u32[]{:S(2)}, u32[]{:S(2)}) collective-permute-start(bf16[32,8192]{1,0:T(8,128)(2,1)S(1)} %get-tuple-element.74), channel_id=1, source_target_pairs={{0,1},{2,3},{4,5},{6,7},{8,9},{10,11},{12,13},{14,15},{16,17},{18,... | collective-permute-start | bytes 1572872 | tf_op jit(solution)/shard_map/ppermute | solution.py:43
  46.1 2.7 %fusion.1.right = f32[64,512]{1,0:T(8,128)S(1)} fusion(bf16[64,8192]{1,0:T(8,128)(2,1)S(1)} %get-tuple-element.75, bf16[512,8192]{1,0:T(8,128)(2,1)S(1)} %bitcast.28), kind=kOutput, calls=%fused_computation.9 | convolution fusion | flops 536870912 | bytes 9568256 | tf_op jit(solution)/shard_map/dot_general | solution.py:27
  49.5 9.5 %collective-permute-start.10 = (bf16[64,512]{1,0:T(8,128)(2,1)S(1)}, bf16[64,512]{1,0:T(8,128)(2,1)S(1)}, u32[]{:S(2)}, u32[]{:S(2)}) collective-permute-start(bf16[64,512]{1,0:T(8,128)(2,1)S(1)} %get-tuple-element.82.refs_0_), channel_id=1, source_target_pairs={{0,6},{1,7},{8,14},{9,15},{16,22},{17,23},{24,30},{25,31}} | collective-permute-start | bytes 196616 | tf_op jit(solution)/shard_map/ppermute | solution.py:43
  60.2 2.5 %collective-permute-start.9 = (bf16[64,512]{1,0:T(8,128)(2,1)S(1)}, bf16[64,512]{1,0:T(8,128)(2,1)S(1)}, u32[]{:S(2)}, u32[]{:S(2)}) collective-permute-start(bf16[64,512]{1,0:T(8,128)(2,1)S(1)} %get-tuple-element.82.refs_0_), channel_id=1, source_target_pairs={{0,4},{1,5},{2,6},{3,7},{8,12},{9,13},{10,14},{11,15},{16,20},{17,... | collective-permute-start | bytes 196616 | tf_op jit(solution)/shard_map/ppermute | solution.py:43
  62.9 2.3 %collective-permute-done.9.refs_2_ = bf16[64,512]{1,0:T(8,128)(2,1)S(1)} collective-permute-done((bf16[64,512]{1,0:T(8,128)(2,1)S(1)}, bf16[64,512]{1,0:T(8,128)(2,1)S(1)}, u32[]{:S(2)}, u32[]{:S(2)}) %collective-permute-start.9) | collective-permute-done | bytes 65568 | tf_op jit(solution)/shard_map/ppermute | solution.py:43
  67.7 1.4 %collective-permute-start.15 = (bf16[80,512]{1,0:T(8,128)(2,1)S(1)}, bf16[80,512]{1,0:T(8,128)(2,1)S(1)}, u32[]{:S(2)}, u32[]{:S(2)}) collective-permute-start(bf16[80,512]{1,0:T(8,128)(2,1)S(1)} %pad_maximum_fusion.2.refs_4_), channel_id=1, source_target_pairs={{0,24},{8,16},{16,8},{24,0},{1,25},{9,17},{17,9},{25,1},{2,26},{10... | collective-permute-start | bytes 245768 | tf_op jit(solution)/shard_map/ppermute | solution.py:34
  71.3 1.7 %collective-permute-done.15.refs_7_ = bf16[80,512]{1,0:T(8,128)(2,1)S(1)} collective-permute-done((bf16[80,512]{1,0:T(8,128)(2,1)S(1)}, bf16[80,512]{1,0:T(8,128)(2,1)S(1)}, u32[]{:S(2)}, u32[]{:S(2)}) %collective-permute-start.15) | collective-permute-done | bytes 81952 | tf_op jit(solution)/shard_map/ppermute | solution.py:34
  74.2 3.2 %shard_map.110 = (bf16[32,512]{1,0:T(8,128)(2,1)S(1)}, bf16[32,8192]{1,0:T(8,128)(2,1)S(1)}) custom-call(bf16[32,8192]{1,0:T(8,128)(2,1)S(1)} %collective-permute-done.12.arrived, bf16[32,512]{1,0:T(8,128)(2,1)S(1)} %broadcast_in_dim.12.before, bf16[8192,512]{1,0:T(8,128)(2,1)S(1)} %shard_map.101.down, bf16[512,8192]{1,0:T(8,128)(2,1)S(1)} %get-tuple-element.55.expand), custom_call_target="tpu_custom_call" | custom-call | flops 268435456 | bytes 8388608 | tf_op jit(solution)/shard_map/pallas_call | solution.py:65
  78.7 8.0 %collective-permute-start.17 = (f32[8,64]{1,0:T(8,128)S(1)}, f32[8,64]{1,0:T(8,128)S(1)}, u32[]{:S(2)}, u32[]{:S(2)}) collective-permute-start(f32[8,64]{1,0:T(8,128)S(1)} %shard_map.109.refs_0_), channel_id=1, source_target_pairs={{0,6},{1,7},{8,14},{9,15},{16,22},{17,23},{24,30},{25,31}} | collective-permute-start | bytes 6152 | tf_op jit(solution)/shard_map/ppermute | solution.py:49
  88.1 1.6 %collective-permute-start.20 = (bf16[32,512]{1,0:T(8,128)(2,1)S(1)}, bf16[32,512]{1,0:T(8,128)(2,1)S(1)}, u32[]{:S(2)}, u32[]{:S(2)}) collective-permute-start(bf16[32,512]{1,0:T(8,128)(2,1)S(1)} %shard_map.111.refs_4_), channel_id=1, source_target_pairs={{0,8},{8,0},{16,24},{24,16},{1,9},{9,1},{17,25},{25,17},{2,10},{10... | collective-permute-start | bytes 98312 | tf_op jit(solution)/shard_map/ppermute | solution.py:34
  92.1 1.5 %collective-permute-done.21.refs_6_ = bf16[32,512]{1,0:T(8,128)(2,1)S(1)} collective-permute-done((bf16[32,512]{1,0:T(8,128)(2,1)S(1)}, bf16[32,512]{1,0:T(8,128)(2,1)S(1)}, u32[]{:S(2)}, u32[]{:S(2)}) %collective-permute-start.21) | collective-permute-done | bytes 32800 | tf_op jit(solution)/shard_map/ppermute | solution.py:34
  93.6 1.7 %collective-permute-done.22.refs_7_ = bf16[32,512]{1,0:T(8,128)(2,1)S(1)} collective-permute-done((bf16[32,512]{1,0:T(8,128)(2,1)S(1)}, bf16[32,512]{1,0:T(8,128)(2,1)S(1)}, u32[]{:S(2)}, u32[]{:S(2)}) %collective-permute-start.22) | collective-permute-done | bytes 32800 | tf_op jit(solution)/shard_map/ppermute | solution.py:34
  99.3 7.3 %collective-permute-done.24.refs_0_ = f32[8,64]{1,0:T(8,128)S(1)} collective-permute-done((f32[8,64]{1,0:T(8,128)S(1)}, f32[8,64]{1,0:T(8,128)S(1)}, u32[]{:S(2)}, u32[]{:S(2)}) %collective-permute-start.24) | collective-permute-done | bytes 2080 | tf_op jit(solution)/shard_map/ppermute | solution.py:49
  (73 shorter events, 22.2 us)
Async XLA Ops:
  6.5 5.8 %collective-permute-start = (bf16[16,8192]{1,0:T(8,128)(2,1)S(1)}, bf16[16,8192]{1,0:T(8,128)(2,1)S(1)}, u32[]{:S(2)}, u32[]{:S(2)}) collective-permute-start(bf16[16,8192]{1,0:T(8,128)(2,1)S(1)} %get-tuple-element.51), channel_id=1, source_target_pairs={{0,1},{2,3},{4,5},{6,7},{8,9},{10,11},{12,13},{14,15},{16,17},{18,... | collective-permute-start | bytes 786440 | tf_op jit(solution)/shard_map/ppermute | solution.py:43
  12.4 11.6 %collective-permute-start.1 = (bf16[32,8192]{1,0:T(8,128)(2,1)S(1)}, bf16[32,8192]{1,0:T(8,128)(2,1)S(1)}, u32[]{:S(2)}, u32[]{:S(2)}) collective-permute-start(bf16[32,8192]{1,0:T(8,128)(2,1)S(1)} %constant_dynamic-update-slice_fusion), channel_id=1, source_target_pairs={{1,2},{3,4},{5,6},{9,10},{11,12},{13,14},{17,18},{19,20},{21,22},{... | collective-permute-start | bytes 1572872 | tf_op jit(solution)/shard_map/ppermute | solution.py:43
  13.2 15.4 %collective-permute-start.3 = (bf16[16,8192]{1,0:T(8,128)(2,1)S(1)}, bf16[16,8192]{1,0:T(8,128)(2,1)S(1)}, u32[]{:S(2)}, u32[]{:S(2)}) collective-permute-start(bf16[16,8192]{1,0:T(8,128)(2,1)S(1)} %get-tuple-element.62), channel_id=1, source_target_pairs={{0,8},{8,0},{16,24},{24,16},{1,9},{9,1},{17,25},{25,17},{2,10},{10... | collective-permute-start | bytes 786440 | tf_op jit(solution)/shard_map/ppermute | solution.py:34
  15.5 13.1 %collective-permute-start.4 = (bf16[16,8192]{1,0:T(8,128)(2,1)S(1)}, bf16[16,8192]{1,0:T(8,128)(2,1)S(1)}, u32[]{:S(2)}, u32[]{:S(2)}) collective-permute-start(bf16[16,8192]{1,0:T(8,128)(2,1)S(1)} %get-tuple-element.62), channel_id=1, source_target_pairs={{0,16},{8,24},{16,0},{24,8},{1,17},{9,25},{17,1},{25,9},{2,18},{10... | collective-permute-start | bytes 786440 | tf_op jit(solution)/shard_map/ppermute | solution.py:34
  17.0 11.6 %collective-permute-start.5 = (bf16[16,8192]{1,0:T(8,128)(2,1)S(1)}, bf16[16,8192]{1,0:T(8,128)(2,1)S(1)}, u32[]{:S(2)}, u32[]{:S(2)}) collective-permute-start(bf16[16,8192]{1,0:T(8,128)(2,1)S(1)} %get-tuple-element.62), channel_id=1, source_target_pairs={{0,24},{8,16},{16,8},{24,0},{1,25},{9,17},{17,9},{25,1},{2,26},{10... | collective-permute-start | bytes 786440 | tf_op jit(solution)/shard_map/ppermute | solution.py:34
  27.1 4.3 %collective-permute-start.2 = (bf16[32,8192]{1,0:T(8,128)(2,1)S(1)}, bf16[32,8192]{1,0:T(8,128)(2,1)S(1)}, u32[]{:S(2)}, u32[]{:S(2)}) collective-permute-start(bf16[32,8192]{1,0:T(8,128)(2,1)S(1)} %get-tuple-element.61), channel_id=1, source_target_pairs={{0,1},{2,3},{4,5},{6,7},{8,9},{10,11},{12,13},{14,15},{16,17},{18,... | collective-permute-start | bytes 1572872 | tf_op jit(solution)/shard_map/ppermute | solution.py:43
  31.6 7.0 %collective-permute-start.6 = (bf16[32,8192]{1,0:T(8,128)(2,1)S(1)}, bf16[32,8192]{1,0:T(8,128)(2,1)S(1)}, u32[]{:S(2)}, u32[]{:S(2)}) collective-permute-start(bf16[32,8192]{1,0:T(8,128)(2,1)S(1)} %get-tuple-element.70), channel_id=1, source_target_pairs={{1,2},{3,4},{5,6},{9,10},{11,12},{13,14},{17,18},{19,20},{21,22},{... | collective-permute-start | bytes 1572872 | tf_op jit(solution)/shard_map/ppermute | solution.py:43
  41.7 7.0 %collective-permute-start.7 = (bf16[32,8192]{1,0:T(8,128)(2,1)S(1)}, bf16[32,8192]{1,0:T(8,128)(2,1)S(1)}, u32[]{:S(2)}, u32[]{:S(2)}) collective-permute-start(bf16[32,8192]{1,0:T(8,128)(2,1)S(1)} %get-tuple-element.74), channel_id=1, source_target_pairs={{0,1},{2,3},{4,5},{6,7},{8,9},{10,11},{12,13},{14,15},{16,17},{18,... | collective-permute-start | bytes 1572872 | tf_op jit(solution)/shard_map/ppermute | solution.py:43
  48.8 25.4 %collective-permute-start.12 = (bf16[32,8192]{1,0:T(8,128)(2,1)S(1)}, bf16[32,8192]{1,0:T(8,128)(2,1)S(1)}, u32[]{:S(2)}, u32[]{:S(2)}) collective-permute-start(bf16[32,8192]{1,0:T(8,128)(2,1)S(1)} %get-tuple-element.80), channel_id=1, source_target_pairs={{1,2},{3,4},{5,6},{9,10},{11,12},{13,14},{17,18},{19,20},{21,22},{... | collective-permute-start | bytes 1572872 | tf_op jit(solution)/shard_map/ppermute | solution.py:43
  49.5 13.3 %collective-permute-start.10 = (bf16[64,512]{1,0:T(8,128)(2,1)S(1)}, bf16[64,512]{1,0:T(8,128)(2,1)S(1)}, u32[]{:S(2)}, u32[]{:S(2)}) collective-permute-start(bf16[64,512]{1,0:T(8,128)(2,1)S(1)} %get-tuple-element.82.refs_0_), channel_id=1, source_target_pairs={{0,6},{1,7},{8,14},{9,15},{16,22},{17,23},{24,30},{25,31}} | collective-permute-start | bytes 196616 | tf_op jit(solution)/shard_map/ppermute | solution.py:43
  58.9 3.9 %collective-permute-start.8 = (bf16[64,512]{1,0:T(8,128)(2,1)S(1)}, bf16[64,512]{1,0:T(8,128)(2,1)S(1)}, u32[]{:S(2)}, u32[]{:S(2)}) collective-permute-start(bf16[64,512]{1,0:T(8,128)(2,1)S(1)} %get-tuple-element.82.refs_0_), channel_id=1, source_target_pairs={{0,2},{1,3},{2,4},{3,5},{4,6},{5,7},{8,10},{9,11},{10,12},{11,13},... | collective-permute-start | bytes 196616 | tf_op jit(solution)/shard_map/ppermute | solution.py:43
  60.2 4.9 %collective-permute-start.9 = (bf16[64,512]{1,0:T(8,128)(2,1)S(1)}, bf16[64,512]{1,0:T(8,128)(2,1)S(1)}, u32[]{:S(2)}, u32[]{:S(2)}) collective-permute-start(bf16[64,512]{1,0:T(8,128)(2,1)S(1)} %get-tuple-element.82.refs_0_), channel_id=1, source_target_pairs={{0,4},{1,5},{2,6},{3,7},{8,12},{9,13},{10,14},{11,15},{16,20},{17,... | collective-permute-start | bytes 196616 | tf_op jit(solution)/shard_map/ppermute | solution.py:43
  65.2 7.8 %collective-permute-start.11 = (bf16[4,64,512]{2,1,0:T(8,128)(2,1)S(1)}, bf16[4,64,512]{2,1,0:T(8,128)(2,1)S(1)}, u32[]{:S(2)}, u32[]{:S(2)}) collective-permute-start(bf16[4,64,512]{2,1,0:T(8,128)(2,1)S(1)} %pad_maximum_fusion.1), channel_id=1, source_target_pairs={{0,1},{1,0},{2,3},{3,2},{4,5},{5,4},{6,7},{7,6},{8,9},{9,8},{10,11... | collective-permute-start | bytes 786440 | tf_op jit(solution)/shard_map/ppermute | solution.py:34
  65.6 4.5 %collective-permute-start.13 = (bf16[80,512]{1,0:T(8,128)(2,1)S(1)}, bf16[80,512]{1,0:T(8,128)(2,1)S(1)}, u32[]{:S(2)}, u32[]{:S(2)}) collective-permute-start(bf16[80,512]{1,0:T(8,128)(2,1)S(1)} %pad_maximum_fusion.2.refs_4_), channel_id=1, source_target_pairs={{0,8},{8,0},{16,24},{24,16},{1,9},{9,1},{17,25},{25,17},{2,10},{10... | collective-permute-start | bytes 245768 | tf_op jit(solution)/shard_map/ppermute | solution.py:34
  66.5 4.7 %collective-permute-start.14 = (bf16[80,512]{1,0:T(8,128)(2,1)S(1)}, bf16[80,512]{1,0:T(8,128)(2,1)S(1)}, u32[]{:S(2)}, u32[]{:S(2)}) collective-permute-start(bf16[80,512]{1,0:T(8,128)(2,1)S(1)} %pad_maximum_fusion.2.refs_4_), channel_id=1, source_target_pairs={{0,16},{8,24},{16,0},{24,8},{1,17},{9,25},{17,1},{25,9},{2,18},{10... | collective-permute-start | bytes 245768 | tf_op jit(solution)/shard_map/ppermute | solution.py:34
  67.7 5.3 %collective-permute-start.15 = (bf16[80,512]{1,0:T(8,128)(2,1)S(1)}, bf16[80,512]{1,0:T(8,128)(2,1)S(1)}, u32[]{:S(2)}, u32[]{:S(2)}) collective-permute-start(bf16[80,512]{1,0:T(8,128)(2,1)S(1)} %pad_maximum_fusion.2.refs_4_), channel_id=1, source_target_pairs={{0,24},{8,16},{16,8},{24,0},{1,25},{9,17},{17,9},{25,1},{2,26},{10... | collective-permute-start | bytes 245768 | tf_op jit(solution)/shard_map/ppermute | solution.py:34
  77.4 10.6 %collective-permute-start.16 = (bf16[32,8192]{1,0:T(8,128)(2,1)S(1)}, bf16[32,8192]{1,0:T(8,128)(2,1)S(1)}, u32[]{:S(2)}, u32[]{:S(2)}) collective-permute-start(bf16[32,8192]{1,0:T(8,128)(2,1)S(1)} %get-tuple-element.89), channel_id=1, source_target_pairs={{0,1},{2,3},{4,5},{6,7},{8,9},{10,11},{12,13},{14,15},{16,17},{18,... | collective-permute-start | bytes 1572872 | tf_op jit(solution)/shard_map/ppermute | solution.py:43
  78.7 9.3 %collective-permute-start.17 = (f32[8,64]{1,0:T(8,128)S(1)}, f32[8,64]{1,0:T(8,128)S(1)}, u32[]{:S(2)}, u32[]{:S(2)}) collective-permute-start(f32[8,64]{1,0:T(8,128)S(1)} %shard_map.109.refs_0_), channel_id=1, source_target_pairs={{0,6},{1,7},{8,14},{9,15},{16,22},{17,23},{24,30},{25,31}} | collective-permute-start | bytes 6152 | tf_op jit(solution)/shard_map/ppermute | solution.py:49
  88.1 4.0 %collective-permute-start.20 = (bf16[32,512]{1,0:T(8,128)(2,1)S(1)}, bf16[32,512]{1,0:T(8,128)(2,1)S(1)}, u32[]{:S(2)}, u32[]{:S(2)}) collective-permute-start(bf16[32,512]{1,0:T(8,128)(2,1)S(1)} %shard_map.111.refs_4_), channel_id=1, source_target_pairs={{0,8},{8,0},{16,24},{24,16},{1,9},{9,1},{17,25},{25,17},{2,10},{10... | collective-permute-start | bytes 98312 | tf_op jit(solution)/shard_map/ppermute | solution.py:34
  89.6 3.9 %collective-permute-start.21 = (bf16[32,512]{1,0:T(8,128)(2,1)S(1)}, bf16[32,512]{1,0:T(8,128)(2,1)S(1)}, u32[]{:S(2)}, u32[]{:S(2)}) collective-permute-start(bf16[32,512]{1,0:T(8,128)(2,1)S(1)} %shard_map.111.refs_4_), channel_id=1, source_target_pairs={{0,16},{8,24},{16,0},{24,8},{1,17},{9,25},{17,1},{25,9},{2,18},{10... | collective-permute-start | bytes 98312 | tf_op jit(solution)/shard_map/ppermute | solution.py:34
  90.5 4.8 %collective-permute-start.22 = (bf16[32,512]{1,0:T(8,128)(2,1)S(1)}, bf16[32,512]{1,0:T(8,128)(2,1)S(1)}, u32[]{:S(2)}, u32[]{:S(2)}) collective-permute-start(bf16[32,512]{1,0:T(8,128)(2,1)S(1)} %shard_map.111.refs_4_), channel_id=1, source_target_pairs={{0,24},{8,16},{16,8},{24,0},{1,25},{9,17},{17,9},{25,1},{2,26},{10... | collective-permute-start | bytes 98312 | tf_op jit(solution)/shard_map/ppermute | solution.py:34
  96.6 9.9 %collective-permute-start.24 = (f32[8,64]{1,0:T(8,128)S(1)}, f32[8,64]{1,0:T(8,128)S(1)}, u32[]{:S(2)}, u32[]{:S(2)}) collective-permute-start(f32[8,64]{1,0:T(8,128)S(1)} %add.3.top_sums), channel_id=1, source_target_pairs={{6,0},{7,1},{14,8},{15,9},{22,16},{23,17},{30,24},{31,25}} | collective-permute-start | bytes 6152 | tf_op jit(solution)/shard_map/ppermute | solution.py:49
  97.9 8.6 %collective-permute-start.25 = (f32[8,64]{1,0:T(8,128)S(1)}, f32[8,64]{1,0:T(8,128)S(1)}, u32[]{:S(2)}, u32[]{:S(2)}) collective-permute-start(f32[8,64]{1,0:T(8,128)S(1)} %add.3.top_sums), channel_id=1, source_target_pairs={{6,2},{7,3},{14,10},{15,11},{22,18},{23,19},{30,26},{31,27}} | collective-permute-start | bytes 6152 | tf_op jit(solution)/shard_map/ppermute | solution.py:49
  98.6 8.0 %collective-permute-start.26 = (f32[8,64]{1,0:T(8,128)S(1)}, f32[8,64]{1,0:T(8,128)S(1)}, u32[]{:S(2)}, u32[]{:S(2)}) collective-permute-start(f32[8,64]{1,0:T(8,128)S(1)} %add.3.top_sums), channel_id=1, source_target_pairs={{6,4},{7,5},{14,12},{15,13},{22,20},{23,21},{30,28},{31,29}} | collective-permute-start | bytes 6152 | tf_op jit(solution)/shard_map/ppermute | solution.py:49
  (11 other events, 61.2 us)

commit v5 on v4

--- a/solution.py
+++ b/solution.py
@@ -45,9 +45,10 @@
     )
 
 
-def between(value, source, target):
+def around(value, hop):
+    count = lax.axis_size("pipe")
     return lax.ppermute(
-        value, "pipe", [(2 * source + core, 2 * target + core) for core in range(2)]
+        value, "pipe", [(source, (source + 2 * hop) % count) for source in range(count)]
     )
 
 
@@ -88,20 +89,31 @@
     return jnp.where(row == source + place * q_dev, 1.0, 0.0).astype(bf16)
 
 
-def prime_kernel(cols, values, inputs, expand, kept, raised, own, wide, sems):
+def fetch(pairs, sems):
+    copies = [
+        pltpu.make_async_copy(source, target, sems.at[at])
+        for at, (source, target) in enumerate(pairs)
+    ]
+    for copy in copies:
+        copy.start()
+    return copies
+
+
+def prime_kernel(
+    cols_hbm, values_hbm, inputs_hbm, expand, kept, raised, own, wide, cols, values, inputs, few, sems
+):
     step = expand.shape[1] // PARTS
-    copies = []
-    for part in range(PARTS):
-        span = pl.ds(part * step, step)
-        copy = pltpu.make_async_copy(expand.at[:, span], kept.at[:, span], sems.at[part])
-        copy.start()
-        copies.append(copy)
+    small = fetch([(cols_hbm, cols), (values_hbm, values), (inputs_hbm, inputs)], few)
+    spans = [pl.ds(part * step, step) for part in range(PARTS)]
+    copies = fetch([(expand.at[:, span], kept.at[:, span]) for span in spans], sems)
     rows = own.shape[0]
     q_dev = rows // 2
-    laid = picks((raised.shape[0], cols.shape[0]), q_dev, 1).astype(bf16)
-    laid = dot_nn(laid, cols[...]).astype(bf16)
     first = halves((rows, q_dev), q_dev, 0)
     second = halves((rows, q_dev), q_dev, 1)
+    laid = picks((raised.shape[0], cols.shape[0]), q_dev, 1).astype(bf16)
+    for copy in small:
+        copy.wait()
+    laid = dot_nn(laid, cols[...]).astype(bf16)
     for part in range(PARTS):
         span = slice(part * step, (part + 1) * step)
         above = dot_nn(first, values[:, span])
@@ -112,10 +124,18 @@
         own[:, span] = (found[:rows] + above).astype(bf16)
 
 
-def keep_kernel(down, kept, sem):
-    copy = pltpu.make_async_copy(down, kept, sem)
-    copy.start()
-    copy.wait()
+def keep_kernel(q_dev, cols_hbm, down, kept, raised, cols, few, sems):
+    step = down.shape[0] // PARTS
+    small = fetch([(cols_hbm, cols)], few)
+    spans = [pl.ds(part * step, step) for part in range(PARTS)]
+    copies = fetch([(down.at[span], kept.at[span]) for span in spans], sems)
+    laid = picks((raised.shape[0], cols.shape[0]), q_dev, 0).astype(bf16)
+    small[0].wait()
+    laid = dot_nn(laid, cols[...]).astype(bf16)
+    for part in range(PARTS):
+        span = slice(part * step, (part + 1) * step)
+        copies[part].wait()
+        raised[:, span] = (adapter_scale * dot_nt(laid, kept[span, :])).astype(bf16)
 
 
 def through_kernel(turn, arrived, before, down, expand, ranks, leaving):
@@ -156,36 +176,34 @@
         ranks[...] = total.astype(bf16)
 
 
-def lift_kernel(cotangent, expand, lifted, buffer, sems):
-    copies = []
-    for part in range(cotangent.shape[0] // SLOT):
-        span = pl.ds(part * SLOT, SLOT)
-        copy = pltpu.make_async_copy(cotangent.at[span], buffer.at[span], sems.at[part])
-        copy.start()
-        copies.append(copy)
-    ranks = expand.shape[0]
-    half = ranks // 2
-    for pair in range(0, len(copies), 2):
-        copies[pair].wait()
-        copies[pair + 1].wait()
-        span = slice(pair * SLOT, (pair + 2) * SLOT)
-        for at in range(0, ranks, half):
-            found = adapter_scale * dot_nt(buffer[span, :], expand[at : at + half, :])
-            lifted[span, at : at + half] = found.astype(bf16)
-
-
-def weave_kernel(q_dev, cols, down, rows, raised, left_rows, right_rows):
+def lift_kernel(start, cotangent, expand, lifted, buffer, total, sems):
+    count, depth = buffer.shape
+    parts = PARTS // 2
+    step = depth // parts
+    spans = [pl.ds(part * step, step) for part in range(parts)]
+    rows = pl.ds(start, count)
+    copies = fetch([(cotangent.at[rows, span], buffer.at[:, span]) for span in spans], sems)
+    for part in range(parts):
+        span = slice(part * step, (part + 1) * step)
+        copies[part].wait()
+        found = dot_nt(buffer[:, span], expand[:, span])
+        if part == 0:
+            total[...] = found
+        elif part < parts - 1:
+            total[...] += found
+        else:
+            lifted[...] = (adapter_scale * (total[...] + found)).astype(bf16)
+
+
+def weave_kernel(q_dev, hidden, rows, raised, left_rows, right_rows):
     count, depth = rows.shape
     step = depth // PARTS
-    laid = picks((count, cols.shape[0]), q_dev, 0).astype(bf16)
-    laid = dot_nn(laid, cols[...]).astype(bf16)
     place = lax.broadcasted_iota(jnp.int32, (count, step), 0) // q_dev
     first = place % 2 == 0
     for at in range(0, depth, step):
         span = slice(at, at + step)
-        found = adapter_scale * dot_nt(laid, down[span, :])
         given = rows[:, span].astype(f32)
-        left_rows[:, span] = jnp.where(first, found, given).astype(bf16)
+        left_rows[:, span] = jnp.where(first, hidden[:, span].astype(f32), given).astype(bf16)
         right_rows[:, span] = jnp.where(first, given, raised[:, span].astype(f32)).astype(bf16)
 
 
@@ -198,7 +216,8 @@
 
 def weighed(weights, blocks, at, rows, lifted):
     ranks = jnp.concatenate([block[at : at + rows, :].astype(f32) for block in blocks])
-    return weights.astype(f32) * dot_nt(ranks.astype(bf16), lifted[...])
+    ranks = ranks.astype(bf16)
+    return weights * jnp.concatenate([dot_nt(ranks, part[...]) for part in lifted], axis=1)
 
 
 def by_layer(own, other):
@@ -207,8 +226,8 @@
     return jnp.where(upper, other, own), jnp.where(upper, own, other)
 
 
-def early_kernel(chips, rows, left, right, lifted, others, *refs):
-    ups, blocks, sums = refs[:chips], refs[chips:-1], refs[-1]
+def early_kernel(chips, rows, left, right, others, *refs):
+    lifted, ups, blocks, sums = refs[:2], refs[2 : 2 + chips], refs[2 + chips : -1], refs[-1]
     terms = left[...] * right[...]
     for slot in range(chips - 1):
         lower, upper = by_layer(ups[slot][...], others[slot])
@@ -221,24 +240,19 @@
     sums[...] = summed(terms, sums.shape)
 
 
-def late_kernel(chips, rows, own, others, lifted, *refs):
-    parts, blocks, sums = refs[:chips], refs[chips:-1], refs[-1]
+def late_kernel(chips, rows, own, others, early, *refs):
+    lifted, blocks, sums = refs[:2], refs[2:-1], refs[-1]
     lower, upper = by_layer(own[...], others[chips - 1])
     terms = weighed(lower, blocks, 0, rows, lifted)
     terms += weighed(upper, blocks, rows, rows, lifted)
-    total = summed(terms, sums.shape)
-    for part in parts:
+    sums[...] = early[...] + summed(terms, sums.shape)
+
+
+def final_kernel(q_dev, queries, *refs):
+    parts, scores = refs[:-1], refs[-1]
+    total = parts[0][...]
+    for part in parts[1:]:
         total += part[...]
-    sums[...] = total
-
-
-def final_kernel(chips, q_dev, queries, top_sums, *refs):
-    received, scores = refs[:-1], refs[-1]
-    total = received[0][...]
-    for part in received[1:]:
-        total += part[...]
-    layer = jnp.full(total.shape, lax.axis_index("pipe"), jnp.int32)
-    total = jnp.where(layer >= 2 * (chips - 1), top_sums[...], total)
     ex_dev, q_all = scores.shape
     shape = (total.shape[1], q_all)
     laid = picks(shape, q_dev, 0) + picks(shape, q_dev, 1)
@@ -288,40 +302,61 @@
     expand, raised, own, wide = call(
         prime_kernel,
         (inner_cols[0], value_rows[0], input_rows[0], adapter_expand[0]),
-        "vvvh",
+        "hhhh",
         [((rank, width), bf16), ((count, width), bf16), ((rows, width), bf16), ((rows, width), bf16)],
-        [pltpu.SemaphoreType.DMA((PARTS,))],
+        [
+            VMEM(inner_cols.shape[1:], bf16),
+            VMEM((q_dev, width), bf16),
+            VMEM((q_dev, width), bf16),
+            pltpu.SemaphoreType.DMA((3,)),
+            pltpu.SemaphoreType.DMA((PARTS,)),
+        ],
         flops=pass_flops,
         moved=2 * weight_bytes,
     )
 
     arrived = upward(own, 0, 1, 2)
-    (source,) = tie([adapter_down[0]], own)
-    (down,) = call(
-        keep_kernel,
-        (source,),
-        "h",
-        [((width, rank), bf16)],
-        [pltpu.SemaphoreType.DMA],
+    hid, source = tie([hidden_cols[0], adapter_down[0]], own)
+    down, hidden = call(
+        functools.partial(keep_kernel, q_dev),
+        (hid, source),
+        "hh",
+        [((width, rank), bf16), ((count, width), bf16)],
+        [
+            VMEM(hidden_cols.shape[1:], bf16),
+            pltpu.SemaphoreType.DMA((1,)),
+            pltpu.SemaphoreType.DMA((PARTS,)),
+        ],
+        flops=2 * count * width * rank,
         moved=2 * weight_bytes,
     )
     arrived, down = lax.optimization_barrier((arrived, down))
     lower_ranks, leaving = through(1, arrived, jnp.zeros((rows, rank), bf16))
     moving = jnp.concatenate([leaving, own])
 
+    half = tok_dev // 2
+
+    def lift(part, token):
+        (cot,) = tie([cotangent], token)
+        return call(
+            functools.partial(lift_kernel, part * half),
+            (cot, expand),
+            "hv",
+            [((half, rank), bf16)],
+            [
+                VMEM((half, width), bf16),
+                VMEM((half, rank), f32),
+                pltpu.SemaphoreType.DMA((PARTS // 2,)),
+            ],
+            flops=2 * half * width * rank,
+            moved=weight_bytes,
+        )[0]
+
     arrived = upward(moving, 1, 1, 2)
-    wide, cot = tie([wide, cotangent], moving)
+    (wide,) = tie([wide], moving)
     wide = spread(wide, "dp")
-    (lifted,) = call(
-        lift_kernel,
-        (cot, expand),
-        "hv",
-        [((tok_dev, rank), bf16)],
-        [VMEM((tok_dev, width), bf16), pltpu.SemaphoreType.DMA((ex_dev,))],
-        flops=2 * tok_dev * width * rank,
-        moved=2 * weight_bytes,
-    )
-    arrived, lifted = lax.optimization_barrier((arrived, lifted))
+    lifted = [lift(0, moving)]
+    arrived, lifted[0] = lax.optimization_barrier((arrived, lifted[0]))
 
     slots = []
     empty = jnp.zeros((2 * rows, rank), bf16)
@@ -329,28 +364,37 @@
         found, leaving = through(0, arrived, empty)
         arrived = upward(leaving, 0, 1, 2)
         if slot == 1:
-            wide, hid = tie([jnp.concatenate(wide), hidden_cols[0]], leaving)
-            left_rows, right_rows = call(
-                functools.partial(weave_kernel, q_dev),
-                (hid, down, wide, raised),
-                "vvvv",
-                [((count, width), bf16), ((count, width), bf16)],
-                flops=2 * count * width * rank,
+            lifted.append(lift(1, leaving))
+            arrived, lifted[1] = lax.optimization_barrier((arrived, lifted[1]))
+        if slot == 2:
+            (cot,) = tie([cotangent], leaving)
+            right = dot_nt(right_rows, cot)
+            arrived, right, *left_up = lax.optimization_barrier((arrived, right, *left_up))
+        if slot == top:
+            (sums,) = call(
+                functools.partial(early_kernel, chips, rows),
+                (left, right, others, *lifted, *left_up, *early),
+                "v" * (5 + chips + columns),
+                [((max(ex_dev, 8), count), f32)],
+                flops=2 * count * rank * tok_dev * (2 * chips),
                 moved=weight_bytes,
             )
-            arrived, left_rows = lax.optimization_barrier((arrived, left_rows))
-        if slot == 2 or top == 1:
-            (cot,) = tie([cotangent], leaving)
-            right = dot_nt(right_rows, cot)
-            arrived, right = lax.optimization_barrier((arrived, right))
-        if slot == top:
+            arrived, sums = lax.optimization_barrier((arrived, sums))
             break
         found, leaving = through(1, arrived, found)
         slots.append(found)
         arrived = upward(leaving, 1, 1, 2)
         if slot == 1:
-            (act,) = tie([activations[0]], leaving)
-            left = dot_nt(left_rows, act) * live
+            wide = jnp.concatenate(tie(wide, leaving))
+            left_rows, right_rows = call(
+                functools.partial(weave_kernel, q_dev),
+                (hidden, wide, raised),
+                "vvv",
+                [((count, width), bf16), ((count, width), bf16)],
+                flops=2 * count * width,
+                moved=weight_bytes // 2,
+            )
+            left = dot_nt(left_rows, activations[0]) * live
             left_own = left.astype(bf16)
             left_up = [left_own] + [upward(left_own, 0, 2 * hop, 1) for hop in range(1, chips)]
             arrived, left_own = lax.optimization_barrier((arrived, left_own))
@@ -359,17 +403,8 @@
             early, *left_up = tie([early, *left_up], leaving)
             early = spread(early, "dp")
             others = swap(jnp.stack(left_up), "pipe", 1)
-            (sums,) = call(
-                functools.partial(early_kernel, chips, rows),
-                (left, right, lifted, others, *left_up, *early),
-                "v" * (4 + chips + columns),
-                [((max(ex_dev, 8), count), f32)],
-                flops=2 * count * rank * tok_dev * (2 * chips),
-                moved=weight_bytes,
-            )
-            arrived, sums = lax.optimization_barrier((arrived, sums))
-
-    parts = [sums] + [between(sums, chip, top) for chip in range(top)]
+            arrived, others, *early = lax.optimization_barrier((arrived, others, *early))
+
     (late,) = call(
         last_kernel,
         (arrived, found, down),
@@ -378,24 +413,21 @@
         flops=pass_flops,
         moved=weight_bytes,
     )
-    late, *parts = lax.optimization_barrier((late, *parts))
     late = spread(late, "dp")
     (sums,) = call(
         functools.partial(late_kernel, chips, rows),
-        (left_up[-1], others, lifted, *parts, *late),
-        "v" * (3 + chips + columns),
+        (left_up[-1], others, sums, *lifted, *late),
+        "v" * (5 + columns),
         [(sums.shape, f32)],
         flops=2 * count * rank * tok_dev * 2,
         moved=weight_bytes // 8,
     )
-    sums = sums + lax.ppermute(
-        sums, "pipe", [(2 * top, 2 * top + 1), (2 * top + 1, 2 * top)]
-    )
-    received = [between(sums, top, chip) for chip in range(top)]
+    sums = sums + swap(sums, "pipe", 1)
+    parts = [sums] + [around(sums, hop) for hop in range(1, chips)]
     (scores,) = call(
-        functools.partial(final_kernel, chips, q_dev),
-        (query_example[None], sums, *received),
-        "v" * (2 + top),
+        functools.partial(final_kernel, q_dev),
+        (query_example[None], *parts),
+        "v" * (1 + chips),
         [((ex_dev, columns * q_dev), f32)],
     )
     return scores

time: 108 us -> 94.8 us (0.88)
  starting transfers between devices: 48.6 us -> 38.8 us
  Pallas kernels: 28.6 us -> 32.2 us
  matrix products: 8.89 us -> 5.32 us
  local copies, waits for them, and re-layouts: 3.23 us -> 0.67 us
    ppermute x7 -> x3, starting transfers between devices: 12.6 us -> 3.83 us  [around(): lax.ppermute(value, 'pipe', [(source, (source + 2 * hop) % count) for sou...]
    ppermute x10 -> x11, waiting for transfers between devices: 7.54 us -> 14.5 us  [swap(): lax.ppermute(value, axis, [(source, source ^ distance) for source in rang...]
    ppermute x7 -> x3, waiting for transfers between devices: 7.31 us -> 2.14 us  [around(): lax.ppermute(value, 'pipe', [(source, (source + 2 * hop) % count) for sou...]
    pallas_call x14 -> x15, Pallas kernels: 28.6 us -> 32.2 us  [call(): pl.pallas_call(kernel, in_specs=[pl.BlockSpec(memory_space=space[place])...]
    dot_general x2, matrix products: 8.89 us -> 5.32 us  [dot_nt(): lax.dot_general(a, b, (((1,), (1,)), ((), ())), preferred_element_type=f3...]
    ppermute x10, starting transfers between devices: 24.8 us -> 21.3 us  [upward(): lax.ppermute(value, 'pipe', [(source, source + hop) for source in range(f...]
    unnamed x18 -> x14, local copies, waits for them, and re-layouts: 3.2 us -> 0.64 us
    ppermute x10 -> x11, starting transfers between devices: 11.3 us -> 13.6 us  [swap(): lax.ppermute(value, axis, [(source, source ^ distance) for source in rang...]
  transfers between devices with their start and end apart: 27 -> 24, of which waited for: 9 -> 12; matrix products, arithmetic and copies ran while one was open for 8% -> 6% of each run, Pallas kernels for 16% -> 20%
where the time goes in v5:
time: 94.8 us; the launch traced here: 94.5 us
  starting transfers between devices  38.8 us (41%)
  Pallas kernels  32.2 us (34%)
  waiting for transfers between devices  17 us (18%)
  matrix products  5.32 us (6%)
    pallas_call x15, Pallas kernels, call(): pl.pallas_call(kernel, in_specs=[pl.BlockSpec(memory_space=space[place])...  32.2 us
    ppermute x10, starting transfers between devices, upward(): lax.ppermute(value, 'pipe', [(source, source + hop) for source in range(f...  21.3 us
    ppermute x11, waiting for transfers between devices, swap(): lax.ppermute(value, axis, [(source, source ^ distance) for source in rang...  14.5 us
    ppermute x11, starting transfers between devices, swap(): lax.ppermute(value, axis, [(source, source ^ distance) for source in rang...  13.6 us
    dot_general x2, matrix products, dot_nt(): lax.dot_general(a, b, (((1,), (1,)), ((), ())), preferred_element_type=f3...  5.32 us
    ppermute x3, starting transfers between devices, around(): lax.ppermute(value, 'pipe', [(source, (source + 2 * hop) % count) for sou...  3.83 us
    ppermute x3, waiting for transfers between devices, around(): lax.ppermute(value, 'pipe', [(source, (source + 2 * hop) % count) for sou...  2.14 us
  transfers between devices with their start and end apart: 24, of which 12 were waited for; matrix products, arithmetic and copies ran while one was open for 6% of the time, Pallas kernels for 20%

profile of v5, /device:TPU:0, one launch (start us, length us, event | category | flops | bytes accessed | tf_op | source)
XLA Modules:
  0.0 94.5 jit_solution(13335309654388459845)
XLA Ops:
  0.0 6.0 %shard_map.100 = (bf16[512,8192]{1,0:T(8,128)(2,1)S(1)}, bf16[64,8192]{1,0:T(8,128)(2,1)S(1)}, bf16[16,8192]{1,0:T(8,128)(2,1)S(1)}, bf16[16,8192]{1,0:T(8,128)(2,1)S(1)}) custom-call(bf16[32,512]{1,0:T(8,128)(2,1)} %bitcast.36, bf16[8,8192]{1,0:T(8,128)(2,1)} %bitcast.34, bf16[8,8192]{1,0:T(8,128)(2,1)} %bitcast.35, bf16[512,8192]{1,0:T(8,128)(2,1)} %bitcast.30), custom_call_target="tpu_custom_call" | custom-call | flops 134217728 | bytes 16777216 | tf_op jit(solution)/shard_map/pallas_call | solution.py:66
  6.0 2.4 %collective-permute-start = (bf16[16,8192]{1,0:T(8,128)(2,1)S(1)}, bf16[16,8192]{1,0:T(8,128)(2,1)S(1)}, u32[]{:S(2)}, u32[]{:S(2)}) collective-permute-start(bf16[16,8192]{1,0:T(8,128)(2,1)S(1)} %get-tuple-element.61), channel_id=1, source_target_pairs={{0,1},{2,3},{4,5},{6,7},{8,9},{10,11},{12,13},{14,15},{16,17},{18,... | collective-permute-start | bytes 786440 | tf_op jit(solution)/shard_map/ppermute | solution.py:43
  8.4 6.7 %shard_map.101 = (bf16[8192,512]{1,0:T(8,128)(2,1)S(1)}, bf16[64,8192]{1,0:T(8,128)(2,1)S(1)}) custom-call(bf16[32,512]{1,0:T(8,128)(2,1)} %bitcast.37, bf16[8192,512]{1,0:T(8,128)(2,1)} %bitcast.31), custom_call_target="tpu_custom_call" | custom-call | flops 536870912 | bytes 16777216 | tf_op jit(solution)/shard_map/pallas_call | solution.py:66
  15.9 3.9 %shard_map.103.refs_0_ = bf16[256,512]{1,0:T(8,128)(2,1)S(1)} custom-call(bf16[512,8192]{1,0:T(8,128)(2,1)} %cotangent.1, bf16[512,8192]{1,0:T(8,128)(2,1)S(1)} %get-tuple-element.67.expand), custom_call_target="tpu_custom_call" | custom-call | flops 2147483648 | bytes 8388608 | tf_op jit(solution)/shard_map/pallas_call | solution.py:66
  19.8 3.1 %shard_map.104 = (bf16[32,512]{1,0:T(8,128)(2,1)S(1)}, bf16[32,8192]{1,0:T(8,128)(2,1)S(1)}) custom-call(bf16[32,8192]{1,0:T(8,128)(2,1)S(1)} %collective-permute-done.1.arrived, bf16[32,512]{1,0:T(8,128)(2,1)S(1)} %broadcast_in_dim.12.before, bf16[8192,512]{1,0:T(8,128)(2,1)S(1)} %get-tuple-element.66.down, bf16[512,8192]{1,0:T(8,128)(2,1)S(1)} %get-tuple-element.67.expand), custom_call_target="tpu_custom_call" | custom-call | flops 268435456 | bytes 8388608 | tf_op jit(solution)/shard_map/pallas_call | solution.py:66
  22.9 4.8 %collective-permute-start.2 = (bf16[32,8192]{1,0:T(8,128)(2,1)S(1)}, bf16[32,8192]{1,0:T(8,128)(2,1)S(1)}, u32[]{:S(2)}, u32[]{:S(2)}) collective-permute-start(bf16[32,8192]{1,0:T(8,128)(2,1)S(1)} %get-tuple-element.72), channel_id=1, source_target_pairs={{0,1},{2,3},{4,5},{6,7},{8,9},{10,11},{12,13},{14,15},{16,17},{18,... | collective-permute-start | bytes 1572872 | tf_op jit(solution)/shard_map/ppermute | solution.py:43
  27.7 1.6 %collective-permute-start.4 = (bf16[16,8192]{1,0:T(8,128)(2,1)S(1)}, bf16[16,8192]{1,0:T(8,128)(2,1)S(1)}, u32[]{:S(2)}, u32[]{:S(2)}) collective-permute-start(bf16[16,8192]{1,0:T(8,128)(2,1)S(1)} %get-tuple-element.81), channel_id=1, source_target_pairs={{0,8},{8,0},{16,24},{24,16},{1,9},{9,1},{17,25},{25,17},{2,10},{10... | collective-permute-start | bytes 786440 | tf_op jit(solution)/shard_map/ppermute | solution.py:34
  29.3 1.5 %collective-permute-start.5 = (bf16[16,8192]{1,0:T(8,128)(2,1)S(1)}, bf16[16,8192]{1,0:T(8,128)(2,1)S(1)}, u32[]{:S(2)}, u32[]{:S(2)}) collective-permute-start(bf16[16,8192]{1,0:T(8,128)(2,1)S(1)} %get-tuple-element.81), channel_id=1, source_target_pairs={{0,16},{8,24},{16,0},{24,8},{1,17},{9,25},{17,1},{25,9},{2,18},{10... | collective-permute-start | bytes 786440 | tf_op jit(solution)/shard_map/ppermute | solution.py:34
  31.4 4.0 %shard_map.105.refs_1_ = bf16[256,512]{1,0:T(8,128)(2,1)S(1)} custom-call(bf16[512,8192]{1,0:T(8,128)(2,1)} %cotangent.1, bf16[512,8192]{1,0:T(8,128)(2,1)S(1)} %get-tuple-element.67.expand), custom_call_target="tpu_custom_call" | custom-call | flops 2147483648 | bytes 8388608 | tf_op jit(solution)/shard_map/pallas_call | solution.py:66
  37.0 5.1 %collective-permute-done.5 = bf16[16,8192]{1,0:T(8,128)(2,1)S(1)} collective-permute-done((bf16[16,8192]{1,0:T(8,128)(2,1)S(1)}, bf16[16,8192]{1,0:T(8,128)(2,1)S(1)}, u32[]{:S(2)}, u32[]{:S(2)}) %collective-permute-start.5) | collective-permute-done | bytes 262176 | tf_op jit(solution)/shard_map/ppermute | solution.py:34
  42.5 2.7 %fusion.5 = (bf16[64,512]{1,0:T(8,128)(2,1)S(1)}, f32[64,512]{1,0:T(8,128)S(1)}) fusion(f32[512]{0:T(512)S(1)} %convert_bitcast_fusion, bf16[64,8192]{1,0:T(8,128)(2,1)S(1)} %get-tuple-element.86, bf16[1,512,8192]{2,1,0:T(8,128)(2,1)S(1)} %bitcast.33), kind=kOutput, calls=%fused_computation.10 | convolution fusion | flops 536936448 | bytes 9635840 | tf_op jit(solution)/shard_map/dot_general | solution.py:27
  45.1 5.3 %collective-permute-start.10 = (bf16[64,512]{1,0:T(8,128)(2,1)S(1)}, bf16[64,512]{1,0:T(8,128)(2,1)S(1)}, u32[]{:S(2)}, u32[]{:S(2)}) collective-permute-start(bf16[64,512]{1,0:T(8,128)(2,1)S(1)} %get-tuple-element.100.refs_2_), channel_id=1, source_target_pairs={{0,6},{1,7},{8,14},{9,15},{16,22},{17,23},{24,30},{25,31}} | collective-permute-start | bytes 196616 | tf_op jit(solution)/shard_map/ppermute | solution.py:43
  51.7 2.7 %collective-permute-start.9 = (bf16[64,512]{1,0:T(8,128)(2,1)S(1)}, bf16[64,512]{1,0:T(8,128)(2,1)S(1)}, u32[]{:S(2)}, u32[]{:S(2)}) collective-permute-start(bf16[64,512]{1,0:T(8,128)(2,1)S(1)} %get-tuple-element.100.refs_2_), channel_id=1, source_target_pairs={{0,4},{1,5},{2,6},{3,7},{8,12},{9,13},{10,14},{11,15},{16,20},{17,... | collective-permute-start | bytes 196616 | tf_op jit(solution)/shard_map/ppermute | solution.py:43
  54.5 3.1 %shard_map.108 = (bf16[32,512]{1,0:T(8,128)(2,1)S(1)}, bf16[32,8192]{1,0:T(8,128)(2,1)S(1)}) custom-call(bf16[32,8192]{1,0:T(8,128)(2,1)S(1)} %collective-permute-done.3.arrived, bf16[32,512]{1,0:T(8,128)(2,1)S(1)} %broadcast_in_dim.12.before, bf16[8192,512]{1,0:T(8,128)(2,1)S(1)} %get-tuple-element.66.down, bf16[512,8192]{1,0:T(8,128)(2,1)S(1)} %get-tuple-element.67.expand), custom_call_target="tpu_custom_call" | custom-call | flops 268435456 | bytes 8388608 | tf_op jit(solution)/shard_map/pallas_call | solution.py:66
  58.9 2.7 %fusion.6.right = f32[64,512]{1,0:T(8,128)S(1)} fusion(bf16[64,8192]{1,0:T(8,128)(2,1)S(1)} %get-tuple-element.89, bf16[512,8192]{1,0:T(8,128)(2,1)S(1)} %bitcast.29), kind=kOutput, calls=%fused_computation.11 | convolution fusion | flops 536870912 | bytes 9568256 | tf_op jit(solution)/shard_map/dot_general | solution.py:27
  62.4 2.9 %collective-permute-start.12 = (bf16[4,64,512]{2,1,0:T(8,128)(2,1)S(1)}, bf16[4,64,512]{2,1,0:T(8,128)(2,1)S(1)}, u32[]{:S(2)}, u32[]{:S(2)}) collective-permute-start(bf16[4,64,512]{2,1,0:T(8,128)(2,1)S(1)} %pad_maximum_fusion.1), channel_id=1, source_target_pairs={{0,1},{1,0},{2,3},{3,2},{4,5},{5,4},{6,7},{7,6},{8,9},{9,8},{10,11... | collective-permute-start | bytes 786440 | tf_op jit(solution)/shard_map/ppermute | solution.py:34
  67.3 1.4 %collective-permute-start.15 = (bf16[80,512]{1,0:T(8,128)(2,1)S(1)}, bf16[80,512]{1,0:T(8,128)(2,1)S(1)}, u32[]{:S(2)}, u32[]{:S(2)}) collective-permute-start(bf16[80,512]{1,0:T(8,128)(2,1)S(1)} %pad_maximum_fusion.2.refs_6_), channel_id=1, source_target_pairs={{0,24},{8,16},{16,8},{24,0},{1,25},{9,17},{17,9},{25,1},{2,26},{10... | collective-permute-start | bytes 245768 | tf_op jit(solution)/shard_map/ppermute | solution.py:34
  71.1 1.6 %collective-permute-done.15.refs_9_ = bf16[80,512]{1,0:T(8,128)(2,1)S(1)} collective-permute-done((bf16[80,512]{1,0:T(8,128)(2,1)S(1)}, bf16[80,512]{1,0:T(8,128)(2,1)S(1)}, u32[]{:S(2)}, u32[]{:S(2)}) %collective-permute-start.15) | collective-permute-done | bytes 81952 | tf_op jit(solution)/shard_map/ppermute | solution.py:34
  72.7 3.1 %shard_map.110 = (bf16[32,512]{1,0:T(8,128)(2,1)S(1)}, bf16[32,8192]{1,0:T(8,128)(2,1)S(1)}) custom-call(bf16[32,8192]{1,0:T(8,128)(2,1)S(1)} %collective-permute-done.11.arrived, bf16[32,512]{1,0:T(8,128)(2,1)S(1)} %broadcast_in_dim.12.before, bf16[8192,512]{1,0:T(8,128)(2,1)S(1)} %get-tuple-element.66.down, bf16[512,8192]{1,0:T(8,128)(2,1)S(1)} %get-tuple-element.67.expand), custom_call_target="tpu_custom_call" | custom-call | flops 268435456 | bytes 8388608 | tf_op jit(solution)/shard_map/pallas_call | solution.py:66
  78.6 1.5 %collective-permute-start.17 = (bf16[32,512]{1,0:T(8,128)(2,1)S(1)}, bf16[32,512]{1,0:T(8,128)(2,1)S(1)}, u32[]{:S(2)}, u32[]{:S(2)}) collective-permute-start(bf16[32,512]{1,0:T(8,128)(2,1)S(1)} %shard_map.112.refs_2_), channel_id=1, source_target_pairs={{0,8},{8,0},{16,24},{24,16},{1,9},{9,1},{17,25},{25,17},{2,10},{10... | collective-permute-start | bytes 98312 | tf_op jit(solution)/shard_map/ppermute | solution.py:34
  82.5 1.5 %collective-permute-done.18.refs_4_ = bf16[32,512]{1,0:T(8,128)(2,1)S(1)} collective-permute-done((bf16[32,512]{1,0:T(8,128)(2,1)S(1)}, bf16[32,512]{1,0:T(8,128)(2,1)S(1)}, u32[]{:S(2)}, u32[]{:S(2)}) %collective-permute-start.18) | collective-permute-done | bytes 32800 | tf_op jit(solution)/shard_map/ppermute | solution.py:34
  84.0 2.0 %collective-permute-done.19.refs_5_ = bf16[32,512]{1,0:T(8,128)(2,1)S(1)} collective-permute-done((bf16[32,512]{1,0:T(8,128)(2,1)S(1)}, bf16[32,512]{1,0:T(8,128)(2,1)S(1)}, u32[]{:S(2)}, u32[]{:S(2)}) %collective-permute-start.19) | collective-permute-done | bytes 32800 | tf_op jit(solution)/shard_map/ppermute | solution.py:34
  88.2 3.4 %collective-permute-start.23 = (f32[8,64]{1,0:T(8,128)S(1)}, f32[8,64]{1,0:T(8,128)S(1)}, u32[]{:S(2)}, u32[]{:S(2)}) collective-permute-start(f32[8,64]{1,0:T(8,128)S(1)} %add.3.refs_0_), channel_id=1, source_target_pairs={{0,6},{1,7},{2,0},{3,1},{4,2},{5,3},{6,4},{7,5},{8,14},{9,15},{10,... | collective-permute-start | bytes 6152 | tf_op jit(solution)/shard_map/ppermute | solution.py:50
  91.6 1.6 %collective-permute-done.21.refs_1_ = f32[8,64]{1,0:T(8,128)S(1)} collective-permute-done((f32[8,64]{1,0:T(8,128)S(1)}, f32[8,64]{1,0:T(8,128)S(1)}, u32[]{:S(2)}, u32[]{:S(2)}) %collective-permute-start.21) | collective-permute-done | bytes 2080 | tf_op jit(solution)/shard_map/ppermute | solution.py:50
  (65 shorter events, 19.8 us)
Async XLA Ops:
  6.0 9.1 %collective-permute-start = (bf16[16,8192]{1,0:T(8,128)(2,1)S(1)}, bf16[16,8192]{1,0:T(8,128)(2,1)S(1)}, u32[]{:S(2)}, u32[]{:S(2)}) collective-permute-start(bf16[16,8192]{1,0:T(8,128)(2,1)S(1)} %get-tuple-element.61), channel_id=1, source_target_pairs={{0,1},{2,3},{4,5},{6,7},{8,9},{10,11},{12,13},{14,15},{16,17},{18,... | collective-permute-start | bytes 786440 | tf_op jit(solution)/shard_map/ppermute | solution.py:43
  15.2 4.6 %collective-permute-start.1 = (bf16[32,8192]{1,0:T(8,128)(2,1)S(1)}, bf16[32,8192]{1,0:T(8,128)(2,1)S(1)}, u32[]{:S(2)}, u32[]{:S(2)}) collective-permute-start(bf16[32,8192]{1,0:T(8,128)(2,1)S(1)} %constant_dynamic-update-slice_fusion), channel_id=1, source_target_pairs={{1,2},{3,4},{5,6},{9,10},{11,12},{13,14},{17,18},{19,20},{21,22},{... | collective-permute-start | bytes 1572872 | tf_op jit(solution)/shard_map/ppermute | solution.py:43
  22.9 12.5 %collective-permute-start.2 = (bf16[32,8192]{1,0:T(8,128)(2,1)S(1)}, bf16[32,8192]{1,0:T(8,128)(2,1)S(1)}, u32[]{:S(2)}, u32[]{:S(2)}) collective-permute-start(bf16[32,8192]{1,0:T(8,128)(2,1)S(1)} %get-tuple-element.72), channel_id=1, source_target_pairs={{0,1},{2,3},{4,5},{6,7},{8,9},{10,11},{12,13},{14,15},{16,17},{18,... | collective-permute-start | bytes 1572872 | tf_op jit(solution)/shard_map/ppermute | solution.py:43
  27.7 9.3 %collective-permute-start.4 = (bf16[16,8192]{1,0:T(8,128)(2,1)S(1)}, bf16[16,8192]{1,0:T(8,128)(2,1)S(1)}, u32[]{:S(2)}, u32[]{:S(2)}) collective-permute-start(bf16[16,8192]{1,0:T(8,128)(2,1)S(1)} %get-tuple-element.81), channel_id=1, source_target_pairs={{0,8},{8,0},{16,24},{24,16},{1,9},{9,1},{17,25},{25,17},{2,10},{10... | collective-permute-start | bytes 786440 | tf_op jit(solution)/shard_map/ppermute | solution.py:34
  29.3 12.9 %collective-permute-start.5 = (bf16[16,8192]{1,0:T(8,128)(2,1)S(1)}, bf16[16,8192]{1,0:T(8,128)(2,1)S(1)}, u32[]{:S(2)}, u32[]{:S(2)}) collective-permute-start(bf16[16,8192]{1,0:T(8,128)(2,1)S(1)} %get-tuple-element.81), channel_id=1, source_target_pairs={{0,16},{8,24},{16,0},{24,8},{1,17},{9,25},{17,1},{25,9},{2,18},{10... | collective-permute-start | bytes 786440 | tf_op jit(solution)/shard_map/ppermute | solution.py:34
  30.8 11.4 %collective-permute-start.6 = (bf16[16,8192]{1,0:T(8,128)(2,1)S(1)}, bf16[16,8192]{1,0:T(8,128)(2,1)S(1)}, u32[]{:S(2)}, u32[]{:S(2)}) collective-permute-start(bf16[16,8192]{1,0:T(8,128)(2,1)S(1)} %get-tuple-element.81), channel_id=1, source_target_pairs={{0,24},{8,16},{16,8},{24,0},{1,25},{9,17},{17,9},{25,1},{2,26},{10... | collective-permute-start | bytes 786440 | tf_op jit(solution)/shard_map/ppermute | solution.py:34
  35.6 18.9 %collective-permute-start.3 = (bf16[32,8192]{1,0:T(8,128)(2,1)S(1)}, bf16[32,8192]{1,0:T(8,128)(2,1)S(1)}, u32[]{:S(2)}, u32[]{:S(2)}) collective-permute-start(bf16[32,8192]{1,0:T(8,128)(2,1)S(1)} %get-tuple-element.77), channel_id=1, source_target_pairs={{1,2},{3,4},{5,6},{9,10},{11,12},{13,14},{17,18},{19,20},{21,22},{... | collective-permute-start | bytes 1572872 | tf_op jit(solution)/shard_map/ppermute | solution.py:43
  45.1 16.4 %collective-permute-start.10 = (bf16[64,512]{1,0:T(8,128)(2,1)S(1)}, bf16[64,512]{1,0:T(8,128)(2,1)S(1)}, u32[]{:S(2)}, u32[]{:S(2)}) collective-permute-start(bf16[64,512]{1,0:T(8,128)(2,1)S(1)} %get-tuple-element.100.refs_2_), channel_id=1, source_target_pairs={{0,6},{1,7},{8,14},{9,15},{16,22},{17,23},{24,30},{25,31}} | collective-permute-start | bytes 196616 | tf_op jit(solution)/shard_map/ppermute | solution.py:43
  50.4 11.2 %collective-permute-start.8 = (bf16[64,512]{1,0:T(8,128)(2,1)S(1)}, bf16[64,512]{1,0:T(8,128)(2,1)S(1)}, u32[]{:S(2)}, u32[]{:S(2)}) collective-permute-start(bf16[64,512]{1,0:T(8,128)(2,1)S(1)} %get-tuple-element.100.refs_2_), channel_id=1, source_target_pairs={{0,2},{1,3},{2,4},{3,5},{4,6},{5,7},{8,10},{9,11},{10,12},{11,13},... | collective-permute-start | bytes 196616 | tf_op jit(solution)/shard_map/ppermute | solution.py:43
  51.7 9.9 %collective-permute-start.9 = (bf16[64,512]{1,0:T(8,128)(2,1)S(1)}, bf16[64,512]{1,0:T(8,128)(2,1)S(1)}, u32[]{:S(2)}, u32[]{:S(2)}) collective-permute-start(bf16[64,512]{1,0:T(8,128)(2,1)S(1)} %get-tuple-element.100.refs_2_), channel_id=1, source_target_pairs={{0,4},{1,5},{2,6},{3,7},{8,12},{9,13},{10,14},{11,15},{16,20},{17,... | collective-permute-start | bytes 196616 | tf_op jit(solution)/shard_map/ppermute | solution.py:43
  57.6 4.0 %collective-permute-start.7 = (bf16[32,8192]{1,0:T(8,128)(2,1)S(1)}, bf16[32,8192]{1,0:T(8,128)(2,1)S(1)}, u32[]{:S(2)}, u32[]{:S(2)}) collective-permute-start(bf16[32,8192]{1,0:T(8,128)(2,1)S(1)} %get-tuple-element.88), channel_id=1, source_target_pairs={{0,1},{2,3},{4,5},{6,7},{8,9},{10,11},{12,13},{14,15},{16,17},{18,... | collective-permute-start | bytes 1572872 | tf_op jit(solution)/shard_map/ppermute | solution.py:43
  61.7 11.0 %collective-permute-start.11 = (bf16[32,8192]{1,0:T(8,128)(2,1)S(1)}, bf16[32,8192]{1,0:T(8,128)(2,1)S(1)}, u32[]{:S(2)}, u32[]{:S(2)}) collective-permute-start(bf16[32,8192]{1,0:T(8,128)(2,1)S(1)} %get-tuple-element.98), channel_id=1, source_target_pairs={{1,2},{3,4},{5,6},{9,10},{11,12},{13,14},{17,18},{19,20},{21,22},{... | collective-permute-start | bytes 1572872 | tf_op jit(solution)/shard_map/ppermute | solution.py:43
  62.4 10.3 %collective-permute-start.12 = (bf16[4,64,512]{2,1,0:T(8,128)(2,1)S(1)}, bf16[4,64,512]{2,1,0:T(8,128)(2,1)S(1)}, u32[]{:S(2)}, u32[]{:S(2)}) collective-permute-start(bf16[4,64,512]{2,1,0:T(8,128)(2,1)S(1)} %pad_maximum_fusion.1), channel_id=1, source_target_pairs={{0,1},{1,0},{2,3},{3,2},{4,5},{5,4},{6,7},{7,6},{8,9},{9,8},{10,11... | collective-permute-start | bytes 786440 | tf_op jit(solution)/shard_map/ppermute | solution.py:34
  65.3 4.4 %collective-permute-start.13 = (bf16[80,512]{1,0:T(8,128)(2,1)S(1)}, bf16[80,512]{1,0:T(8,128)(2,1)S(1)}, u32[]{:S(2)}, u32[]{:S(2)}) collective-permute-start(bf16[80,512]{1,0:T(8,128)(2,1)S(1)} %pad_maximum_fusion.2.refs_6_), channel_id=1, source_target_pairs={{0,8},{8,0},{16,24},{24,16},{1,9},{9,1},{17,25},{25,17},{2,10},{10... | collective-permute-start | bytes 245768 | tf_op jit(solution)/shard_map/ppermute | solution.py:34
  66.2 4.8 %collective-permute-start.14 = (bf16[80,512]{1,0:T(8,128)(2,1)S(1)}, bf16[80,512]{1,0:T(8,128)(2,1)S(1)}, u32[]{:S(2)}, u32[]{:S(2)}) collective-permute-start(bf16[80,512]{1,0:T(8,128)(2,1)S(1)} %pad_maximum_fusion.2.refs_6_), channel_id=1, source_target_pairs={{0,16},{8,24},{16,0},{24,8},{1,17},{9,25},{17,1},{25,9},{2,18},{10... | collective-permute-start | bytes 245768 | tf_op jit(solution)/shard_map/ppermute | solution.py:34
  67.3 5.3 %collective-permute-start.15 = (bf16[80,512]{1,0:T(8,128)(2,1)S(1)}, bf16[80,512]{1,0:T(8,128)(2,1)S(1)}, u32[]{:S(2)}, u32[]{:S(2)}) collective-permute-start(bf16[80,512]{1,0:T(8,128)(2,1)S(1)} %pad_maximum_fusion.2.refs_6_), channel_id=1, source_target_pairs={{0,24},{8,16},{16,8},{24,0},{1,25},{9,17},{17,9},{25,1},{2,26},{10... | collective-permute-start | bytes 245768 | tf_op jit(solution)/shard_map/ppermute | solution.py:34
  75.8 2.8 %collective-permute-start.16 = (bf16[32,8192]{1,0:T(8,128)(2,1)S(1)}, bf16[32,8192]{1,0:T(8,128)(2,1)S(1)}, u32[]{:S(2)}, u32[]{:S(2)}) collective-permute-start(bf16[32,8192]{1,0:T(8,128)(2,1)S(1)} %get-tuple-element.106), channel_id=1, source_target_pairs={{0,1},{2,3},{4,5},{6,7},{8,9},{10,11},{12,13},{14,15},{16,17},{18,... | collective-permute-start | bytes 1572872 | tf_op jit(solution)/shard_map/ppermute | solution.py:43
  78.6 3.9 %collective-permute-start.17 = (bf16[32,512]{1,0:T(8,128)(2,1)S(1)}, bf16[32,512]{1,0:T(8,128)(2,1)S(1)}, u32[]{:S(2)}, u32[]{:S(2)}) collective-permute-start(bf16[32,512]{1,0:T(8,128)(2,1)S(1)} %shard_map.112.refs_2_), channel_id=1, source_target_pairs={{0,8},{8,0},{16,24},{24,16},{1,9},{9,1},{17,25},{25,17},{2,10},{10... | collective-permute-start | bytes 98312 | tf_op jit(solution)/shard_map/ppermute | solution.py:34
  80.1 3.9 %collective-permute-start.18 = (bf16[32,512]{1,0:T(8,128)(2,1)S(1)}, bf16[32,512]{1,0:T(8,128)(2,1)S(1)}, u32[]{:S(2)}, u32[]{:S(2)}) collective-permute-start(bf16[32,512]{1,0:T(8,128)(2,1)S(1)} %shard_map.112.refs_2_), channel_id=1, source_target_pairs={{0,16},{8,24},{16,0},{24,8},{1,17},{9,25},{17,1},{25,9},{2,18},{10... | collective-permute-start | bytes 98312 | tf_op jit(solution)/shard_map/ppermute | solution.py:34
  81.1 4.8 %collective-permute-start.19 = (bf16[32,512]{1,0:T(8,128)(2,1)S(1)}, bf16[32,512]{1,0:T(8,128)(2,1)S(1)}, u32[]{:S(2)}, u32[]{:S(2)}) collective-permute-start(bf16[32,512]{1,0:T(8,128)(2,1)S(1)} %shard_map.112.refs_2_), channel_id=1, source_target_pairs={{0,24},{8,16},{16,8},{24,0},{1,25},{9,17},{17,9},{25,1},{2,26},{10... | collective-permute-start | bytes 98312 | tf_op jit(solution)/shard_map/ppermute | solution.py:34
  86.6 1.2 %collective-permute-start.20 = (f32[8,64]{1,0:T(8,128)S(1)}, f32[8,64]{1,0:T(8,128)S(1)}, u32[]{:S(2)}, u32[]{:S(2)}) collective-permute-start(f32[8,64]{1,0:T(8,128)S(1)} %shard_map.113), channel_id=1, source_target_pairs={{0,1},{1,0},{2,3},{3,2},{4,5},{5,4},{6,7},{7,6},{8,9},{9,8},{10,11... | collective-permute-start | bytes 6152 | tf_op jit(solution)/shard_map/ppermute | solution.py:34
  87.8 5.4 %collective-permute-start.21 = (f32[8,64]{1,0:T(8,128)S(1)}, f32[8,64]{1,0:T(8,128)S(1)}, u32[]{:S(2)}, u32[]{:S(2)}) collective-permute-start(f32[8,64]{1,0:T(8,128)S(1)} %add.3.refs_0_), channel_id=1, source_target_pairs={{0,2},{1,3},{2,4},{3,5},{4,6},{5,7},{6,0},{7,1},{8,10},{9,11},{10,... | collective-permute-start | bytes 6152 | tf_op jit(solution)/shard_map/ppermute | solution.py:50
  88.2 5.0 %collective-permute-start.22 = (f32[8,64]{1,0:T(8,128)S(1)}, f32[8,64]{1,0:T(8,128)S(1)}, u32[]{:S(2)}, u32[]{:S(2)}) collective-permute-start(f32[8,64]{1,0:T(8,128)S(1)} %add.3.refs_0_), channel_id=1, source_target_pairs={{0,4},{1,5},{2,6},{3,7},{4,0},{5,1},{6,2},{7,3},{8,12},{9,13},{10,... | collective-permute-start | bytes 6152 | tf_op jit(solution)/shard_map/ppermute | solution.py:50
  88.2 5.5 %collective-permute-start.23 = (f32[8,64]{1,0:T(8,128)S(1)}, f32[8,64]{1,0:T(8,128)S(1)}, u32[]{:S(2)}, u32[]{:S(2)}) collective-permute-start(f32[8,64]{1,0:T(8,128)S(1)} %add.3.refs_0_), channel_id=1, source_target_pairs={{0,6},{1,7},{2,0},{3,1},{4,2},{5,3},{6,4},{7,5},{8,14},{9,15},{10,... | collective-permute-start | bytes 6152 | tf_op jit(solution)/shard_map/ppermute | solution.py:50
  (6 other events, 75.2 us)

commit v6 on v5

--- a/solution.py
+++ b/solution.py
@@ -8,7 +8,8 @@
 from jax.sharding import PartitionSpec as P
 
 SLOT = 128
-PARTS = 8
+PARTS = 16
+AHEAD = 6
 
 
 adapter_scale = 0.25
@@ -57,7 +58,7 @@
     return values
 
 
-def call(kernel, operands, places, outs, scratch=(), flops=0, moved=0):
+def call(kernel, operands, places, outs, scratch=(), flops=0, moved=0, kept=VMEM):
     space = {"v": VMEM, "s": pltpu.SMEM, "h": pltpu.HBM}
     operands = [
         x if place == "s" else pltpu.with_memory_space_constraint(x, space[place])
@@ -67,7 +68,7 @@
         kernel,
         in_specs=[pl.BlockSpec(memory_space=space[place]) for place in places],
         out_specs=[pl.BlockSpec(memory_space=VMEM) for _ in outs],
-        out_shape=[VMEM(shape, dtype) for shape, dtype in outs],
+        out_shape=[kept(shape, dtype) for shape, dtype in outs],
         scratch_shapes=list(scratch),
         cost_estimate=pl.CostEstimate(flops=flops, bytes_accessed=moved, transcendentals=0),
         compiler_params=pltpu.CompilerParams(vmem_limit_bytes=16 * 2**20),
@@ -83,58 +84,61 @@
     return jnp.where(found, 1.0, 0.0)
 
 
-def halves(shape, q_dev, place):
-    row = lax.broadcasted_iota(jnp.int32, shape, 0)
-    source = lax.broadcasted_iota(jnp.int32, shape, 1)
-    return jnp.where(row == source + place * q_dev, 1.0, 0.0).astype(bf16)
-
-
 def fetch(pairs, sems):
-    copies = [
+    return [
         pltpu.make_async_copy(source, target, sems.at[at])
         for at, (source, target) in enumerate(pairs)
     ]
-    for copy in copies:
+
+
+def begin(copies):
+    for copy in copies[:AHEAD]:
         copy.start()
-    return copies
+
+
+def arrive(copies, part):
+    copies[part].wait()
+    if part + AHEAD < len(copies):
+        copies[part + AHEAD].start()
 
 
 def prime_kernel(
-    cols_hbm, values_hbm, inputs_hbm, expand, kept, raised, own, wide, cols, values, inputs, few, sems
+    cols_hbm, values_hbm, expand, kept, raised, own, cols, values, few, sems
 ):
     step = expand.shape[1] // PARTS
-    small = fetch([(cols_hbm, cols), (values_hbm, values), (inputs_hbm, inputs)], few)
+    small = fetch([(cols_hbm, cols), (values_hbm, values)], few)
+    begin(small)
     spans = [pl.ds(part * step, step) for part in range(PARTS)]
     copies = fetch([(expand.at[:, span], kept.at[:, span]) for span in spans], sems)
+    begin(copies)
     rows = own.shape[0]
     q_dev = rows // 2
-    first = halves((rows, q_dev), q_dev, 0)
-    second = halves((rows, q_dev), q_dev, 1)
     laid = picks((raised.shape[0], cols.shape[0]), q_dev, 1).astype(bf16)
     for copy in small:
         copy.wait()
     laid = dot_nn(laid, cols[...]).astype(bf16)
     for part in range(PARTS):
         span = slice(part * step, (part + 1) * step)
-        above = dot_nn(first, values[:, span])
-        wide[:, span] = (above + dot_nn(second, inputs[:, span])).astype(bf16)
-        copies[part].wait()
+        arrive(copies, part)
         found = adapter_scale * dot_nn(laid, kept[:, span])
         raised[:, span] = found.astype(bf16)
-        own[:, span] = (found[:rows] + above).astype(bf16)
+        above = jnp.concatenate([values[:, span].astype(f32), found[q_dev:rows]])
+        own[:, span] = above.astype(bf16)
 
 
 def keep_kernel(q_dev, cols_hbm, down, kept, raised, cols, few, sems):
     step = down.shape[0] // PARTS
     small = fetch([(cols_hbm, cols)], few)
+    begin(small)
     spans = [pl.ds(part * step, step) for part in range(PARTS)]
     copies = fetch([(down.at[span], kept.at[span]) for span in spans], sems)
+    begin(copies)
     laid = picks((raised.shape[0], cols.shape[0]), q_dev, 0).astype(bf16)
     small[0].wait()
     laid = dot_nn(laid, cols[...]).astype(bf16)
     for part in range(PARTS):
         span = slice(part * step, (part + 1) * step)
-        copies[part].wait()
+        arrive(copies, part)
         raised[:, span] = (adapter_scale * dot_nt(laid, kept[span, :])).astype(bf16)
 
 
@@ -183,9 +187,10 @@
     spans = [pl.ds(part * step, step) for part in range(parts)]
     rows = pl.ds(start, count)
     copies = fetch([(cotangent.at[rows, span], buffer.at[:, span]) for span in spans], sems)
+    begin(copies)
     for part in range(parts):
         span = slice(part * step, (part + 1) * step)
-        copies[part].wait()
+        arrive(copies, part)
         found = dot_nt(buffer[:, span], expand[:, span])
         if part == 0:
             total[...] = found
@@ -299,16 +304,15 @@
             moved=weight_bytes,
         )
 
-    expand, raised, own, wide = call(
+    expand, raised, own = call(
         prime_kernel,
-        (inner_cols[0], value_rows[0], input_rows[0], adapter_expand[0]),
-        "hhhh",
-        [((rank, width), bf16), ((count, width), bf16), ((rows, width), bf16), ((rows, width), bf16)],
+        (inner_cols[0], value_rows[0], adapter_expand[0]),
+        "hhh",
+        [((rank, width), bf16), ((count, width), bf16), ((rows, width), bf16)],
         [
             VMEM(inner_cols.shape[1:], bf16),
             VMEM((q_dev, width), bf16),
-            VMEM((q_dev, width), bf16),
-            pltpu.SemaphoreType.DMA((3,)),
+            pltpu.SemaphoreType.DMA((2,)),
             pltpu.SemaphoreType.DMA((PARTS,)),
         ],
         flops=pass_flops,
@@ -353,8 +357,8 @@
         )[0]
 
     arrived = upward(moving, 1, 1, 2)
-    (wide,) = tie([wide], moving)
-    wide = spread(wide, "dp")
+    wide = tie([value_rows[0], input_rows[0]], moving)
+    wide = spread(jnp.concatenate(wide), "dp")
     lifted = [lift(0, moving)]
     arrived, lifted[0] = lax.optimization_barrier((arrived, lifted[0]))
 
@@ -365,7 +369,8 @@
         arrived = upward(leaving, 0, 1, 2)
         if slot == 1:
             lifted.append(lift(1, leaving))
-            arrived, lifted[1] = lax.optimization_barrier((arrived, lifted[1]))
+            wide = jnp.concatenate(tie(wide, lifted[1]))
+            arrived, wide = lax.optimization_barrier((arrived, wide))
         if slot == 2:
             (cot,) = tie([cotangent], leaving)
             right = dot_nt(right_rows, cot)
@@ -385,7 +390,6 @@
         slots.append(found)
         arrived = upward(leaving, 1, 1, 2)
         if slot == 1:
-            wide = jnp.concatenate(tie(wide, leaving))
             left_rows, right_rows = call(
                 functools.partial(weave_kernel, q_dev),
                 (hidden, wide, raised),
@@ -399,11 +403,10 @@
             left_up = [left_own] + [upward(left_own, 0, 2 * hop, 1) for hop in range(1, chips)]
             arrived, left_own = lax.optimization_barrier((arrived, left_own))
         if slot == top - 1:
-            early = jnp.concatenate([lower_ranks] + slots)
-            early, *left_up = tie([early, *left_up], leaving)
+            (early,) = tie([jnp.concatenate([lower_ranks] + slots)], leaving)
             early = spread(early, "dp")
-            others = swap(jnp.stack(left_up), "pipe", 1)
-            arrived, others, *early = lax.optimization_barrier((arrived, others, *early))
+            arrived, *early = lax.optimization_barrier((arrived, *early))
+            others = swap(jnp.stack(tie(left_up, early[-1])), "pipe", 1)
 
     (late,) = call(
         last_kernel,
@@ -429,6 +432,7 @@
         (query_example[None], *parts),
         "v" * (1 + chips),
         [((ex_dev, columns * q_dev), f32)],
+        kept=jax.ShapeDtypeStruct,
     )
     return scores
 

time: 94.8 us -> 92.3 us (0.974)
  waiting for transfers between devices: 17 us -> 13.1 us
  local copies, waits for them, and re-layouts: 0.67 us -> 2.26 us
    ppermute x11, waiting for transfers between devices: 14.5 us -> 10.9 us  [swap(): lax.ppermute(value, axis, [(source, source ^ distance) for source in rang...]
    ppermute x3, starting transfers between devices: 3.83 us -> 6.16 us  [around(): lax.ppermute(value, 'pipe', [(source, (source + 2 * hop) % count) for sou...]
    ppermute x11, starting transfers between devices: 13.6 us -> 11.3 us  [swap(): lax.ppermute(value, axis, [(source, source ^ distance) for source in rang...]
    unnamed x14 -> x18, local copies, waits for them, and re-layouts: 0.64 us -> 2.22 us
  transfers between devices with their start and end apart: 24 -> 24, of which waited for: 12 -> 9; matrix products, arithmetic and copies ran while one was open for 6% -> 6% of each run, Pallas kernels for 20% -> 24%
where the time goes in v6:
time: 92.3 us; the launch traced here: 92 us
  starting transfers between devices  38.5 us (42%)
  Pallas kernels  32.2 us (35%)
  waiting for transfers between devices  13.1 us (14%)
  matrix products  5.32 us (6%)
  local copies, waits for them, and re-layouts  2.26 us (2%)
    pallas_call x15, Pallas kernels, call(): pl.pallas_call(kernel, in_specs=[pl.BlockSpec(memory_space=space[place])...  32.2 us
    ppermute x10, starting transfers between devices, upward(): lax.ppermute(value, 'pipe', [(source, source + hop) for source in range(f...  21 us
    ppermute x11, starting transfers between devices, swap(): lax.ppermute(value, axis, [(source, source ^ distance) for source in rang...  11.3 us
    ppermute x11, waiting for transfers between devices, swap(): lax.ppermute(value, axis, [(source, source ^ distance) for source in rang...  10.9 us
    ppermute x3, starting transfers between devices, around(): lax.ppermute(value, 'pipe', [(source, (source + 2 * hop) % count) for sou...  6.16 us
    dot_general x2, matrix products, dot_nt(): lax.dot_general(a, b, (((1,), (1,)), ((), ())), preferred_element_type=f3...  5.32 us
    unnamed x18, local copies, waits for them, and re-layouts  2.22 us
    ppermute x3, waiting for transfers between devices, around(): lax.ppermute(value, 'pipe', [(source, (source + 2 * hop) % count) for sou...  2.14 us
  transfers between devices with their start and end apart: 24, of which 9 were waited for; matrix products, arithmetic and copies ran while one was open for 6% of the time, Pallas kernels for 24%

profile of v6, /device:TPU:0, one launch (start us, length us, event | category | flops | bytes accessed | tf_op | source)
XLA Modules:
  0.0 92.0 jit_solution(14684632264810318190)
XLA Ops:
  0.0 5.4 %shard_map.100 = (bf16[512,8192]{1,0:T(8,128)(2,1)S(1)}, bf16[64,8192]{1,0:T(8,128)(2,1)S(1)}, bf16[16,8192]{1,0:T(8,128)(2,1)S(1)}) custom-call(bf16[32,512]{1,0:T(8,128)(2,1)} %bitcast.37, bf16[8,8192]{1,0:T(8,128)(2,1)} %bitcast.34, bf16[512,8192]{1,0:T(8,128)(2,1)} %bitcast.30), custom_call_target="tpu_custom_call" | custom-call | flops 134217728 | bytes 16777216 | tf_op jit(solution)/shard_map/pallas_call | solution.py:67
  5.5 2.4 %collective-permute-start = (bf16[16,8192]{1,0:T(8,128)(2,1)S(1)}, bf16[16,8192]{1,0:T(8,128)(2,1)S(1)}, u32[]{:S(2)}, u32[]{:S(2)}) collective-permute-start(bf16[16,8192]{1,0:T(8,128)(2,1)S(1)} %get-tuple-element.60), channel_id=1, source_target_pairs={{0,1},{2,3},{4,5},{6,7},{8,9},{10,11},{12,13},{14,15},{16,17},{18,... | collective-permute-start | bytes 786440 | tf_op jit(solution)/shard_map/ppermute | solution.py:44
  7.8 6.4 %shard_map.101 = (bf16[8192,512]{1,0:T(8,128)(2,1)S(1)}, bf16[64,8192]{1,0:T(8,128)(2,1)S(1)}) custom-call(bf16[32,512]{1,0:T(8,128)(2,1)} %bitcast.38, bf16[8192,512]{1,0:T(8,128)(2,1)} %bitcast.31), custom_call_target="tpu_custom_call" | custom-call | flops 536870912 | bytes 16777216 | tf_op jit(solution)/shard_map/pallas_call | solution.py:67
  15.4 2.4 %collective-permute-start.3 = (bf16[16,8192]{1,0:T(8,128)(2,1)S(1)}, bf16[16,8192]{1,0:T(8,128)(2,1)S(1)}, u32[]{:S(2)}, u32[]{:S(2)}) collective-permute-start(bf16[16,8192]{1,0:T(8,128)(2,1)S(1)} %constant_dynamic-update-slice_fusion.2), channel_id=1, source_target_pairs={{0,8},{8,0},{16,24},{24,16},{1,9},{9,1},{17,25},{25,17},{2,10},{10... | collective-permute-start | bytes 786440 | tf_op jit(solution)/shard_map/ppermute | solution.py:35
  17.7 1.5 %collective-permute-start.4 = (bf16[16,8192]{1,0:T(8,128)(2,1)S(1)}, bf16[16,8192]{1,0:T(8,128)(2,1)S(1)}, u32[]{:S(2)}, u32[]{:S(2)}) collective-permute-start(bf16[16,8192]{1,0:T(8,128)(2,1)S(1)} %constant_dynamic-update-slice_fusion.2), channel_id=1, source_target_pairs={{0,16},{8,24},{16,0},{24,8},{1,17},{9,25},{17,1},{25,9},{2,18},{10... | collective-permute-start | bytes 786440 | tf_op jit(solution)/shard_map/ppermute | solution.py:35
  19.3 4.1 %shard_map.103.refs_0_ = bf16[256,512]{1,0:T(8,128)(2,1)S(1)} custom-call(bf16[512,8192]{1,0:T(8,128)(2,1)} %cotangent.1, bf16[512,8192]{1,0:T(8,128)(2,1)S(1)} %get-tuple-element.66.expand), custom_call_target="tpu_custom_call" | custom-call | flops 2147483648 | bytes 8388608 | tf_op jit(solution)/shard_map/pallas_call | solution.py:67
  23.4 3.1 %shard_map.104 = (bf16[32,512]{1,0:T(8,128)(2,1)S(1)}, bf16[32,8192]{1,0:T(8,128)(2,1)S(1)}) custom-call(bf16[32,8192]{1,0:T(8,128)(2,1)S(1)} %collective-permute-done.1.arrived, bf16[32,512]{1,0:T(8,128)(2,1)S(1)} %broadcast_in_dim.12.before, bf16[8192,512]{1,0:T(8,128)(2,1)S(1)} %get-tuple-element.65.down, bf16[512,8192]{1,0:T(8,128)(2,1)S(1)} %get-tuple-element.66.expand), custom_call_target="tpu_custom_call" | custom-call | flops 268435456 | bytes 8388608 | tf_op jit(solution)/shard_map/pallas_call | solution.py:67
  27.9 4.1 %shard_map.105.refs_1_ = bf16[256,512]{1,0:T(8,128)(2,1)S(1)} custom-call(bf16[512,8192]{1,0:T(8,128)(2,1)} %cotangent.1, bf16[512,8192]{1,0:T(8,128)(2,1)S(1)} %get-tuple-element.66.expand), custom_call_target="tpu_custom_call" | custom-call | flops 2147483648 | bytes 8388608 | tf_op jit(solution)/shard_map/pallas_call | solution.py:67
  35.5 2.7 %fusion.5 = (bf16[64,512]{1,0:T(8,128)(2,1)S(1)}, f32[64,512]{1,0:T(8,128)S(1)}) fusion(f32[512]{0:T(512)S(1)} %convert_bitcast_fusion, bf16[64,8192]{1,0:T(8,128)(2,1)S(1)} %get-tuple-element.84, bf16[1,512,8192]{2,1,0:T(8,128)(2,1)S(1)} %bitcast.33), kind=kOutput, calls=%fused_computation.12 | convolution fusion | flops 536936448 | bytes 9635840 | tf_op jit(solution)/shard_map/dot_general | solution.py:28
  38.2 8.2 %collective-permute-start.10 = (bf16[64,512]{1,0:T(8,128)(2,1)S(1)}, bf16[64,512]{1,0:T(8,128)(2,1)S(1)}, u32[]{:S(2)}, u32[]{:S(2)}) collective-permute-start(bf16[64,512]{1,0:T(8,128)(2,1)S(1)} %get-tuple-element.101.refs_2_), channel_id=1, source_target_pairs={{0,6},{1,7},{8,14},{9,15},{16,22},{17,23},{24,30},{25,31}} | collective-permute-start | bytes 196616 | tf_op jit(solution)/shard_map/ppermute | solution.py:44
  47.7 2.7 %collective-permute-start.9 = (bf16[64,512]{1,0:T(8,128)(2,1)S(1)}, bf16[64,512]{1,0:T(8,128)(2,1)S(1)}, u32[]{:S(2)}, u32[]{:S(2)}) collective-permute-start(bf16[64,512]{1,0:T(8,128)(2,1)S(1)} %get-tuple-element.101.refs_2_), channel_id=1, source_target_pairs={{0,4},{1,5},{2,6},{3,7},{8,12},{9,13},{10,14},{11,15},{16,20},{17,... | collective-permute-start | bytes 196616 | tf_op jit(solution)/shard_map/ppermute | solution.py:44
  50.5 3.1 %shard_map.108 = (bf16[32,512]{1,0:T(8,128)(2,1)S(1)}, bf16[32,8192]{1,0:T(8,128)(2,1)S(1)}) custom-call(bf16[32,8192]{1,0:T(8,128)(2,1)S(1)} %collective-permute-done.6.arrived, bf16[32,512]{1,0:T(8,128)(2,1)S(1)} %broadcast_in_dim.12.before, bf16[8192,512]{1,0:T(8,128)(2,1)S(1)} %get-tuple-element.65.down, bf16[512,8192]{1,0:T(8,128)(2,1)S(1)} %get-tuple-element.66.expand), custom_call_target="tpu_custom_call" | custom-call | flops 268435456 | bytes 8388608 | tf_op jit(solution)/shard_map/pallas_call | solution.py:67
  54.9 2.7 %fusion.6.right = f32[64,512]{1,0:T(8,128)S(1)} fusion(bf16[64,8192]{1,0:T(8,128)(2,1)S(1)} %get-tuple-element.87, bf16[512,8192]{1,0:T(8,128)(2,1)S(1)} %bitcast.29), kind=kOutput, calls=%fused_computation.13 | convolution fusion | flops 536870912 | bytes 9568256 | tf_op jit(solution)/shard_map/dot_general | solution.py:28
  58.4 1.6 %collective-permute-start.12 = (bf16[80,512]{1,0:T(8,128)(2,1)S(1)}, bf16[80,512]{1,0:T(8,128)(2,1)S(1)}, u32[]{:S(2)}, u32[]{:S(2)}) collective-permute-start(bf16[80,512]{1,0:T(8,128)(2,1)S(1)} %pad_maximum_fusion.2.refs_6_), channel_id=1, source_target_pairs={{0,8},{8,0},{16,24},{24,16},{1,9},{9,1},{17,25},{25,17},{2,10},{10... | collective-permute-start | bytes 245768 | tf_op jit(solution)/shard_map/ppermute | solution.py:35
  59.9 1.5 %collective-permute-start.13 = (bf16[80,512]{1,0:T(8,128)(2,1)S(1)}, bf16[80,512]{1,0:T(8,128)(2,1)S(1)}, u32[]{:S(2)}, u32[]{:S(2)}) collective-permute-start(bf16[80,512]{1,0:T(8,128)(2,1)S(1)} %pad_maximum_fusion.2.refs_6_), channel_id=1, source_target_pairs={{0,16},{8,24},{16,0},{24,8},{1,17},{9,25},{17,1},{25,9},{2,18},{10... | collective-permute-start | bytes 245768 | tf_op jit(solution)/shard_map/ppermute | solution.py:35
  62.9 1.5 %collective-permute-done.13.refs_8_ = bf16[80,512]{1,0:T(8,128)(2,1)S(1)} collective-permute-done((bf16[80,512]{1,0:T(8,128)(2,1)S(1)}, bf16[80,512]{1,0:T(8,128)(2,1)S(1)}, u32[]{:S(2)}, u32[]{:S(2)}) %collective-permute-start.13) | collective-permute-done | bytes 81952 | tf_op jit(solution)/shard_map/ppermute | solution.py:35
  64.4 2.4 %collective-permute-done.14.refs_9_ = bf16[80,512]{1,0:T(8,128)(2,1)S(1)} collective-permute-done((bf16[80,512]{1,0:T(8,128)(2,1)S(1)}, bf16[80,512]{1,0:T(8,128)(2,1)S(1)}, u32[]{:S(2)}, u32[]{:S(2)}) %collective-permute-start.14) | collective-permute-done | bytes 81952 | tf_op jit(solution)/shard_map/ppermute | solution.py:35
  66.8 3.1 %shard_map.110 = (bf16[32,512]{1,0:T(8,128)(2,1)S(1)}, bf16[32,8192]{1,0:T(8,128)(2,1)S(1)}) custom-call(bf16[32,8192]{1,0:T(8,128)(2,1)S(1)} %collective-permute-done.11.arrived, bf16[32,512]{1,0:T(8,128)(2,1)S(1)} %broadcast_in_dim.12.before, bf16[8192,512]{1,0:T(8,128)(2,1)S(1)} %get-tuple-element.65.down, bf16[512,8192]{1,0:T(8,128)(2,1)S(1)} %get-tuple-element.66.expand), custom_call_target="tpu_custom_call" | custom-call | flops 268435456 | bytes 8388608 | tf_op jit(solution)/shard_map/pallas_call | solution.py:67
  71.3 1.7 %collective-permute-done.15.others = bf16[4,64,512]{2,1,0:T(8,128)(2,1)S(1)} collective-permute-done((bf16[4,64,512]{2,1,0:T(8,128)(2,1)S(1)}, bf16[4,64,512]{2,1,0:T(8,128)(2,1)S(1)}, u32[]{:S(2)}, u32[]{:S(2)}) %collective-permute-start.15) | collective-permute-done | bytes 262176 | tf_op jit(solution)/shard_map/ppermute | solution.py:35
  76.3 1.5 %collective-permute-start.19 = (bf16[32,512]{1,0:T(8,128)(2,1)S(1)}, bf16[32,512]{1,0:T(8,128)(2,1)S(1)}, u32[]{:S(2)}, u32[]{:S(2)}) collective-permute-start(bf16[32,512]{1,0:T(8,128)(2,1)S(1)} %shard_map.112.refs_2_), channel_id=1, source_target_pairs={{0,24},{8,16},{16,8},{24,0},{1,25},{9,17},{17,9},{25,1},{2,26},{10... | collective-permute-start | bytes 98312 | tf_op jit(solution)/shard_map/ppermute | solution.py:35
  79.6 1.5 %collective-permute-done.19.refs_5_ = bf16[32,512]{1,0:T(8,128)(2,1)S(1)} collective-permute-done((bf16[32,512]{1,0:T(8,128)(2,1)S(1)}, bf16[32,512]{1,0:T(8,128)(2,1)S(1)}, u32[]{:S(2)}, u32[]{:S(2)}) %collective-permute-start.19) | collective-permute-done | bytes 32800 | tf_op jit(solution)/shard_map/ppermute | solution.py:35
  83.0 3.8 %collective-permute-start.21 = (f32[8,64]{1,0:T(8,128)S(1)}, f32[8,64]{1,0:T(8,128)S(1)}, u32[]{:S(2)}, u32[]{:S(2)}) collective-permute-start(f32[8,64]{1,0:T(8,128)S(1)} %add.3.refs_0_), channel_id=1, source_target_pairs={{0,2},{1,3},{2,4},{3,5},{4,6},{5,7},{6,0},{7,1},{8,10},{9,11},{10,... | collective-permute-start | bytes 6152 | tf_op jit(solution)/shard_map/ppermute | solution.py:51
  86.8 2.4 %collective-permute-start.23 = (f32[8,64]{1,0:T(8,128)S(1)}, f32[8,64]{1,0:T(8,128)S(1)}, u32[]{:S(2)}, u32[]{:S(2)}) collective-permute-start(f32[8,64]{1,0:T(8,128)S(1)} %add.3.refs_0_), channel_id=1, source_target_pairs={{0,6},{1,7},{2,0},{3,1},{4,2},{5,3},{6,4},{7,5},{8,14},{9,15},{10,... | collective-permute-start | bytes 6152 | tf_op jit(solution)/shard_map/ppermute | solution.py:51
  89.1 2.1 %collective-permute-done.22.refs_2_ = f32[8,64]{1,0:T(8,128)S(1)} collective-permute-done((f32[8,64]{1,0:T(8,128)S(1)}, f32[8,64]{1,0:T(8,128)S(1)}, u32[]{:S(2)}, u32[]{:S(2)}) %collective-permute-start.22) | collective-permute-done | bytes 2080 | tf_op jit(solution)/shard_map/ppermute | solution.py:51
  (70 shorter events, 19.8 us)
Async XLA Ops:
  5.5 8.9 %collective-permute-start = (bf16[16,8192]{1,0:T(8,128)(2,1)S(1)}, bf16[16,8192]{1,0:T(8,128)(2,1)S(1)}, u32[]{:S(2)}, u32[]{:S(2)}) collective-permute-start(bf16[16,8192]{1,0:T(8,128)(2,1)S(1)} %get-tuple-element.60), channel_id=1, source_target_pairs={{0,1},{2,3},{4,5},{6,7},{8,9},{10,11},{12,13},{14,15},{16,17},{18,... | collective-permute-start | bytes 786440 | tf_op jit(solution)/shard_map/ppermute | solution.py:44
  14.5 8.9 %collective-permute-start.1 = (bf16[32,8192]{1,0:T(8,128)(2,1)S(1)}, bf16[32,8192]{1,0:T(8,128)(2,1)S(1)}, u32[]{:S(2)}, u32[]{:S(2)}) collective-permute-start(bf16[32,8192]{1,0:T(8,128)(2,1)S(1)} %constant_dynamic-update-slice_fusion), channel_id=1, source_target_pairs={{1,2},{3,4},{5,6},{9,10},{11,12},{13,14},{17,18},{19,20},{21,22},{... | collective-permute-start | bytes 1572872 | tf_op jit(solution)/shard_map/ppermute | solution.py:44
  15.4 16.7 %collective-permute-start.3 = (bf16[16,8192]{1,0:T(8,128)(2,1)S(1)}, bf16[16,8192]{1,0:T(8,128)(2,1)S(1)}, u32[]{:S(2)}, u32[]{:S(2)}) collective-permute-start(bf16[16,8192]{1,0:T(8,128)(2,1)S(1)} %constant_dynamic-update-slice_fusion.2), channel_id=1, source_target_pairs={{0,8},{8,0},{16,24},{24,16},{1,9},{9,1},{17,25},{25,17},{2,10},{10... | collective-permute-start | bytes 786440 | tf_op jit(solution)/shard_map/ppermute | solution.py:35
  17.7 14.3 %collective-permute-start.4 = (bf16[16,8192]{1,0:T(8,128)(2,1)S(1)}, bf16[16,8192]{1,0:T(8,128)(2,1)S(1)}, u32[]{:S(2)}, u32[]{:S(2)}) collective-permute-start(bf16[16,8192]{1,0:T(8,128)(2,1)S(1)} %constant_dynamic-update-slice_fusion.2), channel_id=1, source_target_pairs={{0,16},{8,24},{16,0},{24,8},{1,17},{9,25},{17,1},{25,9},{2,18},{10... | collective-permute-start | bytes 786440 | tf_op jit(solution)/shard_map/ppermute | solution.py:35
  19.3 12.8 %collective-permute-start.5 = (bf16[16,8192]{1,0:T(8,128)(2,1)S(1)}, bf16[16,8192]{1,0:T(8,128)(2,1)S(1)}, u32[]{:S(2)}, u32[]{:S(2)}) collective-permute-start(bf16[16,8192]{1,0:T(8,128)(2,1)S(1)} %constant_dynamic-update-slice_fusion.2), channel_id=1, source_target_pairs={{0,24},{8,16},{16,8},{24,0},{1,25},{9,17},{17,9},{25,1},{2,26},{10... | collective-permute-start | bytes 786440 | tf_op jit(solution)/shard_map/ppermute | solution.py:35
  26.5 5.7 %collective-permute-start.2 = (bf16[32,8192]{1,0:T(8,128)(2,1)S(1)}, bf16[32,8192]{1,0:T(8,128)(2,1)S(1)}, u32[]{:S(2)}, u32[]{:S(2)}) collective-permute-start(bf16[32,8192]{1,0:T(8,128)(2,1)S(1)} %get-tuple-element.70), channel_id=1, source_target_pairs={{0,1},{2,3},{4,5},{6,7},{8,9},{10,11},{12,13},{14,15},{16,17},{18,... | collective-permute-start | bytes 1572872 | tf_op jit(solution)/shard_map/ppermute | solution.py:44
  32.4 18.1 %collective-permute-start.6 = (bf16[32,8192]{1,0:T(8,128)(2,1)S(1)}, bf16[32,8192]{1,0:T(8,128)(2,1)S(1)}, u32[]{:S(2)}, u32[]{:S(2)}) collective-permute-start(bf16[32,8192]{1,0:T(8,128)(2,1)S(1)} %get-tuple-element.80), channel_id=1, source_target_pairs={{1,2},{3,4},{5,6},{9,10},{11,12},{13,14},{17,18},{19,20},{21,22},{... | collective-permute-start | bytes 1572872 | tf_op jit(solution)/shard_map/ppermute | solution.py:44
  38.2 19.4 %collective-permute-start.10 = (bf16[64,512]{1,0:T(8,128)(2,1)S(1)}, bf16[64,512]{1,0:T(8,128)(2,1)S(1)}, u32[]{:S(2)}, u32[]{:S(2)}) collective-permute-start(bf16[64,512]{1,0:T(8,128)(2,1)S(1)} %get-tuple-element.101.refs_2_), channel_id=1, source_target_pairs={{0,6},{1,7},{8,14},{9,15},{16,22},{17,23},{24,30},{25,31}} | collective-permute-start | bytes 196616 | tf_op jit(solution)/shard_map/ppermute | solution.py:44
  46.4 11.2 %collective-permute-start.8 = (bf16[64,512]{1,0:T(8,128)(2,1)S(1)}, bf16[64,512]{1,0:T(8,128)(2,1)S(1)}, u32[]{:S(2)}, u32[]{:S(2)}) collective-permute-start(bf16[64,512]{1,0:T(8,128)(2,1)S(1)} %get-tuple-element.101.refs_2_), channel_id=1, source_target_pairs={{0,2},{1,3},{2,4},{3,5},{4,6},{5,7},{8,10},{9,11},{10,12},{11,13},... | collective-permute-start | bytes 196616 | tf_op jit(solution)/shard_map/ppermute | solution.py:44
  47.7 9.9 %collective-permute-start.9 = (bf16[64,512]{1,0:T(8,128)(2,1)S(1)}, bf16[64,512]{1,0:T(8,128)(2,1)S(1)}, u32[]{:S(2)}, u32[]{:S(2)}) collective-permute-start(bf16[64,512]{1,0:T(8,128)(2,1)S(1)} %get-tuple-element.101.refs_2_), channel_id=1, source_target_pairs={{0,4},{1,5},{2,6},{3,7},{8,12},{9,13},{10,14},{11,15},{16,20},{17,... | collective-permute-start | bytes 196616 | tf_op jit(solution)/shard_map/ppermute | solution.py:44
  53.6 4.0 %collective-permute-start.7 = (bf16[32,8192]{1,0:T(8,128)(2,1)S(1)}, bf16[32,8192]{1,0:T(8,128)(2,1)S(1)}, u32[]{:S(2)}, u32[]{:S(2)}) collective-permute-start(bf16[32,8192]{1,0:T(8,128)(2,1)S(1)} %get-tuple-element.86), channel_id=1, source_target_pairs={{0,1},{2,3},{4,5},{6,7},{8,9},{10,11},{12,13},{14,15},{16,17},{18,... | collective-permute-start | bytes 1572872 | tf_op jit(solution)/shard_map/ppermute | solution.py:44
  57.6 9.1 %collective-permute-start.11 = (bf16[32,8192]{1,0:T(8,128)(2,1)S(1)}, bf16[32,8192]{1,0:T(8,128)(2,1)S(1)}, u32[]{:S(2)}, u32[]{:S(2)}) collective-permute-start(bf16[32,8192]{1,0:T(8,128)(2,1)S(1)} %get-tuple-element.95), channel_id=1, source_target_pairs={{1,2},{3,4},{5,6},{9,10},{11,12},{13,14},{17,18},{19,20},{21,22},{... | collective-permute-start | bytes 1572872 | tf_op jit(solution)/shard_map/ppermute | solution.py:44
  58.4 4.5 %collective-permute-start.12 = (bf16[80,512]{1,0:T(8,128)(2,1)S(1)}, bf16[80,512]{1,0:T(8,128)(2,1)S(1)}, u32[]{:S(2)}, u32[]{:S(2)}) collective-permute-start(bf16[80,512]{1,0:T(8,128)(2,1)S(1)} %pad_maximum_fusion.2.refs_6_), channel_id=1, source_target_pairs={{0,8},{8,0},{16,24},{24,16},{1,9},{9,1},{17,25},{25,17},{2,10},{10... | collective-permute-start | bytes 245768 | tf_op jit(solution)/shard_map/ppermute | solution.py:35
  59.9 4.4 %collective-permute-start.13 = (bf16[80,512]{1,0:T(8,128)(2,1)S(1)}, bf16[80,512]{1,0:T(8,128)(2,1)S(1)}, u32[]{:S(2)}, u32[]{:S(2)}) collective-permute-start(bf16[80,512]{1,0:T(8,128)(2,1)S(1)} %pad_maximum_fusion.2.refs_6_), channel_id=1, source_target_pairs={{0,16},{8,24},{16,0},{24,8},{1,17},{9,25},{17,1},{25,9},{2,18},{10... | collective-permute-start | bytes 245768 | tf_op jit(solution)/shard_map/ppermute | solution.py:35
  61.4 5.3 %collective-permute-start.14 = (bf16[80,512]{1,0:T(8,128)(2,1)S(1)}, bf16[80,512]{1,0:T(8,128)(2,1)S(1)}, u32[]{:S(2)}, u32[]{:S(2)}) collective-permute-start(bf16[80,512]{1,0:T(8,128)(2,1)S(1)} %pad_maximum_fusion.2.refs_6_), channel_id=1, source_target_pairs={{0,24},{8,16},{16,8},{24,0},{1,25},{9,17},{17,9},{25,1},{2,26},{10... | collective-permute-start | bytes 245768 | tf_op jit(solution)/shard_map/ppermute | solution.py:35
  69.9 4.4 %collective-permute-start.16 = (bf16[32,8192]{1,0:T(8,128)(2,1)S(1)}, bf16[32,8192]{1,0:T(8,128)(2,1)S(1)}, u32[]{:S(2)}, u32[]{:S(2)}) collective-permute-start(bf16[32,8192]{1,0:T(8,128)(2,1)S(1)} %get-tuple-element.106), channel_id=1, source_target_pairs={{0,1},{2,3},{4,5},{6,7},{8,9},{10,11},{12,13},{14,15},{16,17},{18,... | collective-permute-start | bytes 1572872 | tf_op jit(solution)/shard_map/ppermute | solution.py:44
  71.2 1.8 %collective-permute-start.15 = (bf16[4,64,512]{2,1,0:T(8,128)(2,1)S(1)}, bf16[4,64,512]{2,1,0:T(8,128)(2,1)S(1)}, u32[]{:S(2)}, u32[]{:S(2)}) collective-permute-start(bf16[4,64,512]{2,1,0:T(8,128)(2,1)S(1)} %pad_maximum_fusion.1), channel_id=1, source_target_pairs={{0,1},{1,0},{2,3},{3,2},{4,5},{5,4},{6,7},{7,6},{8,9},{9,8},{10,11... | collective-permute-start | bytes 786440 | tf_op jit(solution)/shard_map/ppermute | solution.py:35
  74.2 4.0 %collective-permute-start.17 = (bf16[32,512]{1,0:T(8,128)(2,1)S(1)}, bf16[32,512]{1,0:T(8,128)(2,1)S(1)}, u32[]{:S(2)}, u32[]{:S(2)}) collective-permute-start(bf16[32,512]{1,0:T(8,128)(2,1)S(1)} %shard_map.112.refs_2_), channel_id=1, source_target_pairs={{0,8},{8,0},{16,24},{24,16},{1,9},{9,1},{17,25},{25,17},{2,10},{10... | collective-permute-start | bytes 98312 | tf_op jit(solution)/shard_map/ppermute | solution.py:35
  75.7 3.9 %collective-permute-start.18 = (bf16[32,512]{1,0:T(8,128)(2,1)S(1)}, bf16[32,512]{1,0:T(8,128)(2,1)S(1)}, u32[]{:S(2)}, u32[]{:S(2)}) collective-permute-start(bf16[32,512]{1,0:T(8,128)(2,1)S(1)} %shard_map.112.refs_2_), channel_id=1, source_target_pairs={{0,16},{8,24},{16,0},{24,8},{1,17},{9,25},{17,1},{25,9},{2,18},{10... | collective-permute-start | bytes 98312 | tf_op jit(solution)/shard_map/ppermute | solution.py:35
  76.3 4.8 %collective-permute-start.19 = (bf16[32,512]{1,0:T(8,128)(2,1)S(1)}, bf16[32,512]{1,0:T(8,128)(2,1)S(1)}, u32[]{:S(2)}, u32[]{:S(2)}) collective-permute-start(bf16[32,512]{1,0:T(8,128)(2,1)S(1)} %shard_map.112.refs_2_), channel_id=1, source_target_pairs={{0,24},{8,16},{16,8},{24,0},{1,25},{9,17},{17,9},{25,1},{2,26},{10... | collective-permute-start | bytes 98312 | tf_op jit(solution)/shard_map/ppermute | solution.py:35
  81.8 1.2 %collective-permute-start.20 = (f32[8,64]{1,0:T(8,128)S(1)}, f32[8,64]{1,0:T(8,128)S(1)}, u32[]{:S(2)}, u32[]{:S(2)}) collective-permute-start(f32[8,64]{1,0:T(8,128)S(1)} %shard_map.113), channel_id=1, source_target_pairs={{0,1},{1,0},{2,3},{3,2},{4,5},{5,4},{6,7},{7,6},{8,9},{9,8},{10,11... | collective-permute-start | bytes 6152 | tf_op jit(solution)/shard_map/ppermute | solution.py:35
  83.0 6.2 %collective-permute-start.21 = (f32[8,64]{1,0:T(8,128)S(1)}, f32[8,64]{1,0:T(8,128)S(1)}, u32[]{:S(2)}, u32[]{:S(2)}) collective-permute-start(f32[8,64]{1,0:T(8,128)S(1)} %add.3.refs_0_), channel_id=1, source_target_pairs={{0,2},{1,3},{2,4},{3,5},{4,6},{5,7},{6,0},{7,1},{8,10},{9,11},{10,... | collective-permute-start | bytes 6152 | tf_op jit(solution)/shard_map/ppermute | solution.py:51
  86.8 4.5 %collective-permute-start.22 = (f32[8,64]{1,0:T(8,128)S(1)}, f32[8,64]{1,0:T(8,128)S(1)}, u32[]{:S(2)}, u32[]{:S(2)}) collective-permute-start(f32[8,64]{1,0:T(8,128)S(1)} %add.3.refs_0_), channel_id=1, source_target_pairs={{0,4},{1,5},{2,6},{3,7},{4,0},{5,1},{6,2},{7,3},{8,12},{9,13},{10,... | collective-permute-start | bytes 6152 | tf_op jit(solution)/shard_map/ppermute | solution.py:51
  86.8 4.5 %collective-permute-start.23 = (f32[8,64]{1,0:T(8,128)S(1)}, f32[8,64]{1,0:T(8,128)S(1)}, u32[]{:S(2)}, u32[]{:S(2)}) collective-permute-start(f32[8,64]{1,0:T(8,128)S(1)} %add.3.refs_0_), channel_id=1, source_target_pairs={{0,6},{1,7},{2,0},{3,1},{4,2},{5,3},{6,4},{7,5},{8,14},{9,15},{10,... | collective-permute-start | bytes 6152 | tf_op jit(solution)/shard_map/ppermute | solution.py:51
  (8 other events, 76.5 us)

commit v7 on v6

--- a/solution.py
+++ b/solution.py
@@ -8,8 +8,8 @@
 from jax.sharding import PartitionSpec as P
 
 SLOT = 128
-PARTS = 16
-AHEAD = 6
+PARTS = 4
+AHEAD = 2
 
 
 adapter_scale = 0.25
@@ -182,7 +182,7 @@
 
 def lift_kernel(start, cotangent, expand, lifted, buffer, total, sems):
     count, depth = buffer.shape
-    parts = PARTS // 2
+    parts = PARTS
     step = depth // parts
     spans = [pl.ds(part * step, step) for part in range(parts)]
     rows = pl.ds(start, count)
@@ -202,7 +202,7 @@
 
 def weave_kernel(q_dev, hidden, rows, raised, left_rows, right_rows):
     count, depth = rows.shape
-    step = depth // PARTS
+    step = depth // 8
     place = lax.broadcasted_iota(jnp.int32, (count, step), 0) // q_dev
     first = place % 2 == 0
     for at in range(0, depth, step):
@@ -350,7 +350,7 @@
             [
                 VMEM((half, width), bf16),
                 VMEM((half, rank), f32),
-                pltpu.SemaphoreType.DMA((PARTS // 2,)),
+                pltpu.SemaphoreType.DMA((PARTS,)),
             ],
             flops=2 * half * width * rank,
             moved=weight_bytes,
@@ -405,8 +405,8 @@
         if slot == top - 1:
             (early,) = tie([jnp.concatenate([lower_ranks] + slots)], leaving)
             early = spread(early, "dp")
-            arrived, *early = lax.optimization_barrier((arrived, *early))
-            others = swap(jnp.stack(tie(left_up, early[-1])), "pipe", 1)
+            others = swap(jnp.stack(tie(left_up, early[1])), "pipe", 1)
+            arrived, others, *early = lax.optimization_barrier((arrived, others, *early))
 
     (late,) = call(
         last_kernel,

time: 92.3 us -> 91.2 us (0.988)
  Pallas kernels: 32.2 us -> 29.5 us
  waiting for transfers between devices: 13.1 us -> 14.2 us
    pallas_call x15, Pallas kernels: 32.2 us -> 29.5 us  [call(): pl.pallas_call(kernel, in_specs=[pl.BlockSpec(memory_space=space[place])...]
    ppermute x11, starting transfers between devices: 11.3 us -> 13.9 us  [swap(): lax.ppermute(value, axis, [(source, source ^ distance) for source in rang...]
    ppermute x3, starting transfers between devices: 6.16 us -> 3.82 us  [around(): lax.ppermute(value, 'pipe', [(source, (source + 2 * hop) % count) for sou...]
  transfers between devices with their start and end apart: 24 -> 24, of which waited for: 9 -> 10; matrix products, arithmetic and copies ran while one was open for 6% -> 6% of each run, Pallas kernels for 24% -> 22%
where the time goes in v7:
time: 91.2 us; the launch traced here: 90.8 us
  starting transfers between devices  38.9 us (43%)
  Pallas kernels  29.5 us (32%)
  waiting for transfers between devices  14.2 us (16%)
  matrix products  5.32 us (6%)
  local copies, waits for them, and re-layouts  2.3 us (3%)
    pallas_call x15, Pallas kernels, call(): pl.pallas_call(kernel, in_specs=[pl.BlockSpec(memory_space=space[place])...  29.5 us
    ppermute x10, starting transfers between devices, upward(): lax.ppermute(value, 'pipe', [(source, source + hop) for source in range(f...  21.2 us
    ppermute x11, starting transfers between devices, swap(): lax.ppermute(value, axis, [(source, source ^ distance) for source in rang...  13.9 us
    ppermute x11, waiting for transfers between devices, swap(): lax.ppermute(value, axis, [(source, source ^ distance) for source in rang...  11.7 us
    dot_general x2, matrix products, dot_nt(): lax.dot_general(a, b, (((1,), (1,)), ((), ())), preferred_element_type=f3...  5.32 us
    ppermute x3, starting transfers between devices, around(): lax.ppermute(value, 'pipe', [(source, (source + 2 * hop) % count) for sou...  3.82 us
    unnamed x18, local copies, waits for them, and re-layouts  2.26 us
    ppermute x3, waiting for transfers between devices, around(): lax.ppermute(value, 'pipe', [(source, (source + 2 * hop) % count) for sou...  2.14 us
  transfers between devices with their start and end apart: 24, of which 10 were waited for; matrix products, arithmetic and copies ran while one was open for 6% of the time, Pallas kernels for 22%

profile of v7, /device:TPU:0, one launch (start us, length us, event | category | flops | bytes accessed | tf_op | source)
XLA Modules:
  0.0 90.8 jit_solution(5168791754911626354)
XLA Ops:
  0.0 4.6 %shard_map.100 = (bf16[512,8192]{1,0:T(8,128)(2,1)S(1)}, bf16[64,8192]{1,0:T(8,128)(2,1)S(1)}, bf16[16,8192]{1,0:T(8,128)(2,1)S(1)}) custom-call(bf16[32,512]{1,0:T(8,128)(2,1)} %bitcast.37, bf16[8,8192]{1,0:T(8,128)(2,1)} %bitcast.34, bf16[512,8192]{1,0:T(8,128)(2,1)} %bitcast.30), custom_call_target="tpu_custom_call" | custom-call | flops 134217728 | bytes 16777216 | tf_op jit(solution)/shard_map/pallas_call | solution.py:67
  4.6 2.4 %collective-permute-start = (bf16[16,8192]{1,0:T(8,128)(2,1)S(1)}, bf16[16,8192]{1,0:T(8,128)(2,1)S(1)}, u32[]{:S(2)}, u32[]{:S(2)}) collective-permute-start(bf16[16,8192]{1,0:T(8,128)(2,1)S(1)} %get-tuple-element.61), channel_id=1, source_target_pairs={{0,1},{2,3},{4,5},{6,7},{8,9},{10,11},{12,13},{14,15},{16,17},{18,... | collective-permute-start | bytes 786440 | tf_op jit(solution)/shard_map/ppermute | solution.py:44
  7.0 4.9 %shard_map.101 = (bf16[8192,512]{1,0:T(8,128)(2,1)S(1)}, bf16[64,8192]{1,0:T(8,128)(2,1)S(1)}) custom-call(bf16[32,512]{1,0:T(8,128)(2,1)} %bitcast.38, bf16[8192,512]{1,0:T(8,128)(2,1)} %bitcast.31), custom_call_target="tpu_custom_call" | custom-call | flops 536870912 | bytes 16777216 | tf_op jit(solution)/shard_map/pallas_call | solution.py:67
  13.0 2.4 %collective-permute-start.3 = (bf16[16,8192]{1,0:T(8,128)(2,1)S(1)}, bf16[16,8192]{1,0:T(8,128)(2,1)S(1)}, u32[]{:S(2)}, u32[]{:S(2)}) collective-permute-start(bf16[16,8192]{1,0:T(8,128)(2,1)S(1)} %constant_dynamic-update-slice_fusion.2), channel_id=1, source_target_pairs={{0,8},{8,0},{16,24},{24,16},{1,9},{9,1},{17,25},{25,17},{2,10},{10... | collective-permute-start | bytes 786440 | tf_op jit(solution)/shard_map/ppermute | solution.py:35
  15.3 1.5 %collective-permute-start.4 = (bf16[16,8192]{1,0:T(8,128)(2,1)S(1)}, bf16[16,8192]{1,0:T(8,128)(2,1)S(1)}, u32[]{:S(2)}, u32[]{:S(2)}) collective-permute-start(bf16[16,8192]{1,0:T(8,128)(2,1)S(1)} %constant_dynamic-update-slice_fusion.2), channel_id=1, source_target_pairs={{0,16},{8,24},{16,0},{24,8},{1,17},{9,25},{17,1},{25,9},{2,18},{10... | collective-permute-start | bytes 786440 | tf_op jit(solution)/shard_map/ppermute | solution.py:35
  16.9 3.9 %shard_map.103.refs_0_ = bf16[256,512]{1,0:T(8,128)(2,1)S(1)} custom-call(bf16[512,8192]{1,0:T(8,128)(2,1)} %cotangent.1, bf16[512,8192]{1,0:T(8,128)(2,1)S(1)} %get-tuple-element.67.expand), custom_call_target="tpu_custom_call" | custom-call | flops 2147483648 | bytes 8388608 | tf_op jit(solution)/shard_map/pallas_call | solution.py:67
  20.8 3.1 %shard_map.104 = (bf16[32,512]{1,0:T(8,128)(2,1)S(1)}, bf16[32,8192]{1,0:T(8,128)(2,1)S(1)}) custom-call(bf16[32,8192]{1,0:T(8,128)(2,1)S(1)} %collective-permute-done.1.arrived, bf16[32,512]{1,0:T(8,128)(2,1)S(1)} %broadcast_in_dim.12.before, bf16[8192,512]{1,0:T(8,128)(2,1)S(1)} %get-tuple-element.66.down, bf16[512,8192]{1,0:T(8,128)(2,1)S(1)} %get-tuple-element.67.expand), custom_call_target="tpu_custom_call" | custom-call | flops 268435456 | bytes 8388608 | tf_op jit(solution)/shard_map/pallas_call | solution.py:67
  25.4 3.9 %shard_map.105.refs_1_ = bf16[256,512]{1,0:T(8,128)(2,1)S(1)} custom-call(bf16[512,8192]{1,0:T(8,128)(2,1)} %cotangent.1, bf16[512,8192]{1,0:T(8,128)(2,1)S(1)} %get-tuple-element.67.expand), custom_call_target="tpu_custom_call" | custom-call | flops 2147483648 | bytes 8388608 | tf_op jit(solution)/shard_map/pallas_call | solution.py:67
  32.9 2.7 %fusion.5 = (bf16[64,512]{1,0:T(8,128)(2,1)S(1)}, f32[64,512]{1,0:T(8,128)S(1)}) fusion(f32[512]{0:T(512)S(1)} %convert_bitcast_fusion, bf16[64,8192]{1,0:T(8,128)(2,1)S(1)} %get-tuple-element.85, bf16[1,512,8192]{2,1,0:T(8,128)(2,1)S(1)} %bitcast.33), kind=kOutput, calls=%fused_computation.12 | convolution fusion | flops 536936448 | bytes 9635840 | tf_op jit(solution)/shard_map/dot_general | solution.py:28
  35.5 8.3 %collective-permute-start.10 = (bf16[64,512]{1,0:T(8,128)(2,1)S(1)}, bf16[64,512]{1,0:T(8,128)(2,1)S(1)}, u32[]{:S(2)}, u32[]{:S(2)}) collective-permute-start(bf16[64,512]{1,0:T(8,128)(2,1)S(1)} %get-tuple-element.101.refs_2_), channel_id=1, source_target_pairs={{0,6},{1,7},{8,14},{9,15},{16,22},{17,23},{24,30},{25,31}} | collective-permute-start | bytes 196616 | tf_op jit(solution)/shard_map/ppermute | solution.py:44
  45.2 2.7 %collective-permute-start.9 = (bf16[64,512]{1,0:T(8,128)(2,1)S(1)}, bf16[64,512]{1,0:T(8,128)(2,1)S(1)}, u32[]{:S(2)}, u32[]{:S(2)}) collective-permute-start(bf16[64,512]{1,0:T(8,128)(2,1)S(1)} %get-tuple-element.101.refs_2_), channel_id=1, source_target_pairs={{0,4},{1,5},{2,6},{3,7},{8,12},{9,13},{10,14},{11,15},{16,20},{17,... | collective-permute-start | bytes 196616 | tf_op jit(solution)/shard_map/ppermute | solution.py:44
  47.9 3.1 %shard_map.108 = (bf16[32,512]{1,0:T(8,128)(2,1)S(1)}, bf16[32,8192]{1,0:T(8,128)(2,1)S(1)}) custom-call(bf16[32,8192]{1,0:T(8,128)(2,1)S(1)} %collective-permute-done.6.arrived, bf16[32,512]{1,0:T(8,128)(2,1)S(1)} %broadcast_in_dim.12.before, bf16[8192,512]{1,0:T(8,128)(2,1)S(1)} %get-tuple-element.66.down, bf16[512,8192]{1,0:T(8,128)(2,1)S(1)} %get-tuple-element.67.expand), custom_call_target="tpu_custom_call" | custom-call | flops 268435456 | bytes 8388608 | tf_op jit(solution)/shard_map/pallas_call | solution.py:67
  52.4 2.7 %fusion.6.right = f32[64,512]{1,0:T(8,128)S(1)} fusion(bf16[64,8192]{1,0:T(8,128)(2,1)S(1)} %get-tuple-element.88, bf16[512,8192]{1,0:T(8,128)(2,1)S(1)} %bitcast.29), kind=kOutput, calls=%fused_computation.13 | convolution fusion | flops 536870912 | bytes 9568256 | tf_op jit(solution)/shard_map/dot_general | solution.py:28
  55.8 1.6 %collective-permute-start.12 = (bf16[80,512]{1,0:T(8,128)(2,1)S(1)}, bf16[80,512]{1,0:T(8,128)(2,1)S(1)}, u32[]{:S(2)}, u32[]{:S(2)}) collective-permute-start(bf16[80,512]{1,0:T(8,128)(2,1)S(1)} %pad_maximum_fusion.2.refs_6_), channel_id=1, source_target_pairs={{0,8},{8,0},{16,24},{24,16},{1,9},{9,1},{17,25},{25,17},{2,10},{10... | collective-permute-start | bytes 245768 | tf_op jit(solution)/shard_map/ppermute | solution.py:35
  57.4 3.0 %collective-permute-done.12.refs_7_ = bf16[80,512]{1,0:T(8,128)(2,1)S(1)} collective-permute-done((bf16[80,512]{1,0:T(8,128)(2,1)S(1)}, bf16[80,512]{1,0:T(8,128)(2,1)S(1)}, u32[]{:S(2)}, u32[]{:S(2)}) %collective-permute-start.12) | collective-permute-done | bytes 81952 | tf_op jit(solution)/shard_map/ppermute | solution.py:35
  60.4 1.7 %collective-permute-start.13 = (bf16[4,64,512]{2,1,0:T(8,128)(2,1)S(1)}, bf16[4,64,512]{2,1,0:T(8,128)(2,1)S(1)}, u32[]{:S(2)}, u32[]{:S(2)}) collective-permute-start(bf16[4,64,512]{2,1,0:T(8,128)(2,1)S(1)} %pad_maximum_fusion.1), channel_id=1, source_target_pairs={{0,1},{1,0},{2,3},{3,2},{4,5},{5,4},{6,7},{7,6},{8,9},{9,8},{10,11... | collective-permute-start | bytes 786440 | tf_op jit(solution)/shard_map/ppermute | solution.py:35
  62.1 1.5 %collective-permute-start.14 = (bf16[80,512]{1,0:T(8,128)(2,1)S(1)}, bf16[80,512]{1,0:T(8,128)(2,1)S(1)}, u32[]{:S(2)}, u32[]{:S(2)}) collective-permute-start(bf16[80,512]{1,0:T(8,128)(2,1)S(1)} %pad_maximum_fusion.2.refs_6_), channel_id=1, source_target_pairs={{0,16},{8,24},{16,0},{24,8},{1,17},{9,25},{17,1},{25,9},{2,18},{10... | collective-permute-start | bytes 245768 | tf_op jit(solution)/shard_map/ppermute | solution.py:35
  65.0 2.3 %collective-permute-done.14.refs_8_ = bf16[80,512]{1,0:T(8,128)(2,1)S(1)} collective-permute-done((bf16[80,512]{1,0:T(8,128)(2,1)S(1)}, bf16[80,512]{1,0:T(8,128)(2,1)S(1)}, u32[]{:S(2)}, u32[]{:S(2)}) %collective-permute-start.14) | collective-permute-done | bytes 81952 | tf_op jit(solution)/shard_map/ppermute | solution.py:35
  67.3 1.6 %collective-permute-done.15.refs_9_ = bf16[80,512]{1,0:T(8,128)(2,1)S(1)} collective-permute-done((bf16[80,512]{1,0:T(8,128)(2,1)S(1)}, bf16[80,512]{1,0:T(8,128)(2,1)S(1)}, u32[]{:S(2)}, u32[]{:S(2)}) %collective-permute-start.15) | collective-permute-done | bytes 81952 | tf_op jit(solution)/shard_map/ppermute | solution.py:35
  68.9 3.1 %shard_map.110 = (bf16[32,512]{1,0:T(8,128)(2,1)S(1)}, bf16[32,8192]{1,0:T(8,128)(2,1)S(1)}) custom-call(bf16[32,8192]{1,0:T(8,128)(2,1)S(1)} %collective-permute-done.11.arrived, bf16[32,512]{1,0:T(8,128)(2,1)S(1)} %broadcast_in_dim.12.before, bf16[8192,512]{1,0:T(8,128)(2,1)S(1)} %get-tuple-element.66.down, bf16[512,8192]{1,0:T(8,128)(2,1)S(1)} %get-tuple-element.67.expand), custom_call_target="tpu_custom_call" | custom-call | flops 268435456 | bytes 8388608 | tf_op jit(solution)/shard_map/pallas_call | solution.py:67
  78.8 1.5 %collective-permute-done.18.refs_4_ = bf16[32,512]{1,0:T(8,128)(2,1)S(1)} collective-permute-done((bf16[32,512]{1,0:T(8,128)(2,1)S(1)}, bf16[32,512]{1,0:T(8,128)(2,1)S(1)}, u32[]{:S(2)}, u32[]{:S(2)}) %collective-permute-start.18) | collective-permute-done | bytes 32800 | tf_op jit(solution)/shard_map/ppermute | solution.py:35
  80.2 2.0 %collective-permute-done.19.refs_5_ = bf16[32,512]{1,0:T(8,128)(2,1)S(1)} collective-permute-done((bf16[32,512]{1,0:T(8,128)(2,1)S(1)}, bf16[32,512]{1,0:T(8,128)(2,1)S(1)}, u32[]{:S(2)}, u32[]{:S(2)}) %collective-permute-start.19) | collective-permute-done | bytes 32800 | tf_op jit(solution)/shard_map/ppermute | solution.py:35
  84.1 3.8 %collective-permute-start.23 = (f32[8,64]{1,0:T(8,128)S(1)}, f32[8,64]{1,0:T(8,128)S(1)}, u32[]{:S(2)}, u32[]{:S(2)}) collective-permute-start(f32[8,64]{1,0:T(8,128)S(1)} %add.3.refs_0_), channel_id=1, source_target_pairs={{0,6},{1,7},{2,0},{3,1},{4,2},{5,3},{6,4},{7,5},{8,14},{9,15},{10,... | collective-permute-start | bytes 6152 | tf_op jit(solution)/shard_map/ppermute | solution.py:51
  87.9 1.6 %collective-permute-done.21.refs_1_ = f32[8,64]{1,0:T(8,128)S(1)} collective-permute-done((f32[8,64]{1,0:T(8,128)S(1)}, f32[8,64]{1,0:T(8,128)S(1)}, u32[]{:S(2)}, u32[]{:S(2)}) %collective-permute-start.21) | collective-permute-done | bytes 2080 | tf_op jit(solution)/shard_map/ppermute | solution.py:51
  (70 shorter events, 20.6 us)
Async XLA Ops:
  4.6 7.4 %collective-permute-start = (bf16[16,8192]{1,0:T(8,128)(2,1)S(1)}, bf16[16,8192]{1,0:T(8,128)(2,1)S(1)}, u32[]{:S(2)}, u32[]{:S(2)}) collective-permute-start(bf16[16,8192]{1,0:T(8,128)(2,1)S(1)} %get-tuple-element.61), channel_id=1, source_target_pairs={{0,1},{2,3},{4,5},{6,7},{8,9},{10,11},{12,13},{14,15},{16,17},{18,... | collective-permute-start | bytes 786440 | tf_op jit(solution)/shard_map/ppermute | solution.py:44
  12.1 8.8 %collective-permute-start.1 = (bf16[32,8192]{1,0:T(8,128)(2,1)S(1)}, bf16[32,8192]{1,0:T(8,128)(2,1)S(1)}, u32[]{:S(2)}, u32[]{:S(2)}) collective-permute-start(bf16[32,8192]{1,0:T(8,128)(2,1)S(1)} %constant_dynamic-update-slice_fusion), channel_id=1, source_target_pairs={{1,2},{3,4},{5,6},{9,10},{11,12},{13,14},{17,18},{19,20},{21,22},{... | collective-permute-start | bytes 1572872 | tf_op jit(solution)/shard_map/ppermute | solution.py:44
  13.0 16.4 %collective-permute-start.3 = (bf16[16,8192]{1,0:T(8,128)(2,1)S(1)}, bf16[16,8192]{1,0:T(8,128)(2,1)S(1)}, u32[]{:S(2)}, u32[]{:S(2)}) collective-permute-start(bf16[16,8192]{1,0:T(8,128)(2,1)S(1)} %constant_dynamic-update-slice_fusion.2), channel_id=1, source_target_pairs={{0,8},{8,0},{16,24},{24,16},{1,9},{9,1},{17,25},{25,17},{2,10},{10... | collective-permute-start | bytes 786440 | tf_op jit(solution)/shard_map/ppermute | solution.py:35
  15.3 14.0 %collective-permute-start.4 = (bf16[16,8192]{1,0:T(8,128)(2,1)S(1)}, bf16[16,8192]{1,0:T(8,128)(2,1)S(1)}, u32[]{:S(2)}, u32[]{:S(2)}) collective-permute-start(bf16[16,8192]{1,0:T(8,128)(2,1)S(1)} %constant_dynamic-update-slice_fusion.2), channel_id=1, source_target_pairs={{0,16},{8,24},{16,0},{24,8},{1,17},{9,25},{17,1},{25,9},{2,18},{10... | collective-permute-start | bytes 786440 | tf_op jit(solution)/shard_map/ppermute | solution.py:35
  16.9 12.5 %collective-permute-start.5 = (bf16[16,8192]{1,0:T(8,128)(2,1)S(1)}, bf16[16,8192]{1,0:T(8,128)(2,1)S(1)}, u32[]{:S(2)}, u32[]{:S(2)}) collective-permute-start(bf16[16,8192]{1,0:T(8,128)(2,1)S(1)} %constant_dynamic-update-slice_fusion.2), channel_id=1, source_target_pairs={{0,24},{8,16},{16,8},{24,0},{1,25},{9,17},{17,9},{25,1},{2,26},{10... | collective-permute-start | bytes 786440 | tf_op jit(solution)/shard_map/ppermute | solution.py:35
  23.9 5.5 %collective-permute-start.2 = (bf16[32,8192]{1,0:T(8,128)(2,1)S(1)}, bf16[32,8192]{1,0:T(8,128)(2,1)S(1)}, u32[]{:S(2)}, u32[]{:S(2)}) collective-permute-start(bf16[32,8192]{1,0:T(8,128)(2,1)S(1)} %get-tuple-element.71), channel_id=1, source_target_pairs={{0,1},{2,3},{4,5},{6,7},{8,9},{10,11},{12,13},{14,15},{16,17},{18,... | collective-permute-start | bytes 1572872 | tf_op jit(solution)/shard_map/ppermute | solution.py:44
  29.7 18.2 %collective-permute-start.6 = (bf16[32,8192]{1,0:T(8,128)(2,1)S(1)}, bf16[32,8192]{1,0:T(8,128)(2,1)S(1)}, u32[]{:S(2)}, u32[]{:S(2)}) collective-permute-start(bf16[32,8192]{1,0:T(8,128)(2,1)S(1)} %get-tuple-element.81), channel_id=1, source_target_pairs={{1,2},{3,4},{5,6},{9,10},{11,12},{13,14},{17,18},{19,20},{21,22},{... | collective-permute-start | bytes 1572872 | tf_op jit(solution)/shard_map/ppermute | solution.py:44
  35.5 19.5 %collective-permute-start.10 = (bf16[64,512]{1,0:T(8,128)(2,1)S(1)}, bf16[64,512]{1,0:T(8,128)(2,1)S(1)}, u32[]{:S(2)}, u32[]{:S(2)}) collective-permute-start(bf16[64,512]{1,0:T(8,128)(2,1)S(1)} %get-tuple-element.101.refs_2_), channel_id=1, source_target_pairs={{0,6},{1,7},{8,14},{9,15},{16,22},{17,23},{24,30},{25,31}} | collective-permute-start | bytes 196616 | tf_op jit(solution)/shard_map/ppermute | solution.py:44
  43.9 11.2 %collective-permute-start.8 = (bf16[64,512]{1,0:T(8,128)(2,1)S(1)}, bf16[64,512]{1,0:T(8,128)(2,1)S(1)}, u32[]{:S(2)}, u32[]{:S(2)}) collective-permute-start(bf16[64,512]{1,0:T(8,128)(2,1)S(1)} %get-tuple-element.101.refs_2_), channel_id=1, source_target_pairs={{0,2},{1,3},{2,4},{3,5},{4,6},{5,7},{8,10},{9,11},{10,12},{11,13},... | collective-permute-start | bytes 196616 | tf_op jit(solution)/shard_map/ppermute | solution.py:44
  45.2 9.9 %collective-permute-start.9 = (bf16[64,512]{1,0:T(8,128)(2,1)S(1)}, bf16[64,512]{1,0:T(8,128)(2,1)S(1)}, u32[]{:S(2)}, u32[]{:S(2)}) collective-permute-start(bf16[64,512]{1,0:T(8,128)(2,1)S(1)} %get-tuple-element.101.refs_2_), channel_id=1, source_target_pairs={{0,4},{1,5},{2,6},{3,7},{8,12},{9,13},{10,14},{11,15},{16,20},{17,... | collective-permute-start | bytes 196616 | tf_op jit(solution)/shard_map/ppermute | solution.py:44
  51.0 4.0 %collective-permute-start.7 = (bf16[32,8192]{1,0:T(8,128)(2,1)S(1)}, bf16[32,8192]{1,0:T(8,128)(2,1)S(1)}, u32[]{:S(2)}, u32[]{:S(2)}) collective-permute-start(bf16[32,8192]{1,0:T(8,128)(2,1)S(1)} %get-tuple-element.87), channel_id=1, source_target_pairs={{0,1},{2,3},{4,5},{6,7},{8,9},{10,11},{12,13},{14,15},{16,17},{18,... | collective-permute-start | bytes 1572872 | tf_op jit(solution)/shard_map/ppermute | solution.py:44
  55.1 13.8 %collective-permute-start.11 = (bf16[32,8192]{1,0:T(8,128)(2,1)S(1)}, bf16[32,8192]{1,0:T(8,128)(2,1)S(1)}, u32[]{:S(2)}, u32[]{:S(2)}) collective-permute-start(bf16[32,8192]{1,0:T(8,128)(2,1)S(1)} %get-tuple-element.93), channel_id=1, source_target_pairs={{1,2},{3,4},{5,6},{9,10},{11,12},{13,14},{17,18},{19,20},{21,22},{... | collective-permute-start | bytes 1572872 | tf_op jit(solution)/shard_map/ppermute | solution.py:44
  55.8 4.5 %collective-permute-start.12 = (bf16[80,512]{1,0:T(8,128)(2,1)S(1)}, bf16[80,512]{1,0:T(8,128)(2,1)S(1)}, u32[]{:S(2)}, u32[]{:S(2)}) collective-permute-start(bf16[80,512]{1,0:T(8,128)(2,1)S(1)} %pad_maximum_fusion.2.refs_6_), channel_id=1, source_target_pairs={{0,8},{8,0},{16,24},{24,16},{1,9},{9,1},{17,25},{25,17},{2,10},{10... | collective-permute-start | bytes 245768 | tf_op jit(solution)/shard_map/ppermute | solution.py:35
  60.4 8.6 %collective-permute-start.13 = (bf16[4,64,512]{2,1,0:T(8,128)(2,1)S(1)}, bf16[4,64,512]{2,1,0:T(8,128)(2,1)S(1)}, u32[]{:S(2)}, u32[]{:S(2)}) collective-permute-start(bf16[4,64,512]{2,1,0:T(8,128)(2,1)S(1)} %pad_maximum_fusion.1), channel_id=1, source_target_pairs={{0,1},{1,0},{2,3},{3,2},{4,5},{5,4},{6,7},{7,6},{8,9},{9,8},{10,11... | collective-permute-start | bytes 786440 | tf_op jit(solution)/shard_map/ppermute | solution.py:35
  62.1 5.3 %collective-permute-start.14 = (bf16[80,512]{1,0:T(8,128)(2,1)S(1)}, bf16[80,512]{1,0:T(8,128)(2,1)S(1)}, u32[]{:S(2)}, u32[]{:S(2)}) collective-permute-start(bf16[80,512]{1,0:T(8,128)(2,1)S(1)} %pad_maximum_fusion.2.refs_6_), channel_id=1, source_target_pairs={{0,16},{8,24},{16,0},{24,8},{1,17},{9,25},{17,1},{25,9},{2,18},{10... | collective-permute-start | bytes 245768 | tf_op jit(solution)/shard_map/ppermute | solution.py:35
  63.6 5.3 %collective-permute-start.15 = (bf16[80,512]{1,0:T(8,128)(2,1)S(1)}, bf16[80,512]{1,0:T(8,128)(2,1)S(1)}, u32[]{:S(2)}, u32[]{:S(2)}) collective-permute-start(bf16[80,512]{1,0:T(8,128)(2,1)S(1)} %pad_maximum_fusion.2.refs_6_), channel_id=1, source_target_pairs={{0,24},{8,16},{16,8},{24,0},{1,25},{9,17},{17,9},{25,1},{2,26},{10... | collective-permute-start | bytes 245768 | tf_op jit(solution)/shard_map/ppermute | solution.py:35
  72.0 2.8 %collective-permute-start.16 = (bf16[32,8192]{1,0:T(8,128)(2,1)S(1)}, bf16[32,8192]{1,0:T(8,128)(2,1)S(1)}, u32[]{:S(2)}, u32[]{:S(2)}) collective-permute-start(bf16[32,8192]{1,0:T(8,128)(2,1)S(1)} %get-tuple-element.107), channel_id=1, source_target_pairs={{0,1},{2,3},{4,5},{6,7},{8,9},{10,11},{12,13},{14,15},{16,17},{18,... | collective-permute-start | bytes 1572872 | tf_op jit(solution)/shard_map/ppermute | solution.py:44
  74.8 3.9 %collective-permute-start.17 = (bf16[32,512]{1,0:T(8,128)(2,1)S(1)}, bf16[32,512]{1,0:T(8,128)(2,1)S(1)}, u32[]{:S(2)}, u32[]{:S(2)}) collective-permute-start(bf16[32,512]{1,0:T(8,128)(2,1)S(1)} %shard_map.112.refs_2_), channel_id=1, source_target_pairs={{0,8},{8,0},{16,24},{24,16},{1,9},{9,1},{17,25},{25,17},{2,10},{10... | collective-permute-start | bytes 98312 | tf_op jit(solution)/shard_map/ppermute | solution.py:35
  76.3 3.9 %collective-permute-start.18 = (bf16[32,512]{1,0:T(8,128)(2,1)S(1)}, bf16[32,512]{1,0:T(8,128)(2,1)S(1)}, u32[]{:S(2)}, u32[]{:S(2)}) collective-permute-start(bf16[32,512]{1,0:T(8,128)(2,1)S(1)} %shard_map.112.refs_2_), channel_id=1, source_target_pairs={{0,16},{8,24},{16,0},{24,8},{1,17},{9,25},{17,1},{25,9},{2,18},{10... | collective-permute-start | bytes 98312 | tf_op jit(solution)/shard_map/ppermute | solution.py:35
  77.4 4.8 %collective-permute-start.19 = (bf16[32,512]{1,0:T(8,128)(2,1)S(1)}, bf16[32,512]{1,0:T(8,128)(2,1)S(1)}, u32[]{:S(2)}, u32[]{:S(2)}) collective-permute-start(bf16[32,512]{1,0:T(8,128)(2,1)S(1)} %shard_map.112.refs_2_), channel_id=1, source_target_pairs={{0,24},{8,16},{16,8},{24,0},{1,25},{9,17},{17,9},{25,1},{2,26},{10... | collective-permute-start | bytes 98312 | tf_op jit(solution)/shard_map/ppermute | solution.py:35
  82.9 1.2 %collective-permute-start.20 = (f32[8,64]{1,0:T(8,128)S(1)}, f32[8,64]{1,0:T(8,128)S(1)}, u32[]{:S(2)}, u32[]{:S(2)}) collective-permute-start(f32[8,64]{1,0:T(8,128)S(1)} %shard_map.113), channel_id=1, source_target_pairs={{0,1},{1,0},{2,3},{3,2},{4,5},{5,4},{6,7},{7,6},{8,9},{9,8},{10,11... | collective-permute-start | bytes 6152 | tf_op jit(solution)/shard_map/ppermute | solution.py:35
  84.1 5.4 %collective-permute-start.21 = (f32[8,64]{1,0:T(8,128)S(1)}, f32[8,64]{1,0:T(8,128)S(1)}, u32[]{:S(2)}, u32[]{:S(2)}) collective-permute-start(f32[8,64]{1,0:T(8,128)S(1)} %add.3.refs_0_), channel_id=1, source_target_pairs={{0,2},{1,3},{2,4},{3,5},{4,6},{5,7},{6,0},{7,1},{8,10},{9,11},{10,... | collective-permute-start | bytes 6152 | tf_op jit(solution)/shard_map/ppermute | solution.py:51
  84.1 5.4 %collective-permute-start.22 = (f32[8,64]{1,0:T(8,128)S(1)}, f32[8,64]{1,0:T(8,128)S(1)}, u32[]{:S(2)}, u32[]{:S(2)}) collective-permute-start(f32[8,64]{1,0:T(8,128)S(1)} %add.3.refs_0_), channel_id=1, source_target_pairs={{0,4},{1,5},{2,6},{3,7},{4,0},{5,1},{6,2},{7,3},{8,12},{9,13},{10,... | collective-permute-start | bytes 6152 | tf_op jit(solution)/shard_map/ppermute | solution.py:51
  84.1 6.0 %collective-permute-start.23 = (f32[8,64]{1,0:T(8,128)S(1)}, f32[8,64]{1,0:T(8,128)S(1)}, u32[]{:S(2)}, u32[]{:S(2)}) collective-permute-start(f32[8,64]{1,0:T(8,128)S(1)} %add.3.refs_0_), channel_id=1, source_target_pairs={{0,6},{1,7},{2,0},{3,1},{4,2},{5,3},{6,4},{7,5},{8,14},{9,15},{10,... | collective-permute-start | bytes 6152 | tf_op jit(solution)/shard_map/ppermute | solution.py:51
  (8 other events, 71.1 us)

commit v8 on v7

--- a/solution.py
+++ b/solution.py
@@ -9,7 +9,7 @@
 
 SLOT = 128
 PARTS = 4
-AHEAD = 2
+AHEAD = 3
 
 
 adapter_scale = 0.25
@@ -103,13 +103,19 @@
 
 
 def prime_kernel(
-    cols_hbm, values_hbm, expand, kept, raised, own, cols, values, few, sems
+    cols_hbm, values_hbm, expand, down, kept, kept_down, raised, own, cols, values, few, sems
 ):
     step = expand.shape[1] // PARTS
+    deep = down.shape[0] // PARTS
     small = fetch([(cols_hbm, cols), (values_hbm, values)], few)
     begin(small)
-    spans = [pl.ds(part * step, step) for part in range(PARTS)]
-    copies = fetch([(expand.at[:, span], kept.at[:, span]) for span in spans], sems)
+    wide = [pl.ds(part * step, step) for part in range(PARTS)]
+    tall = [pl.ds(part * deep, deep) for part in range(PARTS)]
+    copies = fetch(
+        [(expand.at[:, span], kept.at[:, span]) for span in wide]
+        + [(down.at[span], kept_down.at[span]) for span in tall],
+        sems,
+    )
     begin(copies)
     rows = own.shape[0]
     q_dev = rows // 2
@@ -124,22 +130,20 @@
         raised[:, span] = found.astype(bf16)
         above = jnp.concatenate([values[:, span].astype(f32), found[q_dev:rows]])
         own[:, span] = above.astype(bf16)
-
-
-def keep_kernel(q_dev, cols_hbm, down, kept, raised, cols, few, sems):
+    for part in range(PARTS, 2 * PARTS):
+        arrive(copies, part)
+
+
+def hidden_kernel(q_dev, cols_hbm, down, raised, cols, few):
     step = down.shape[0] // PARTS
     small = fetch([(cols_hbm, cols)], few)
     begin(small)
-    spans = [pl.ds(part * step, step) for part in range(PARTS)]
-    copies = fetch([(down.at[span], kept.at[span]) for span in spans], sems)
-    begin(copies)
     laid = picks((raised.shape[0], cols.shape[0]), q_dev, 0).astype(bf16)
     small[0].wait()
     laid = dot_nn(laid, cols[...]).astype(bf16)
     for part in range(PARTS):
         span = slice(part * step, (part + 1) * step)
-        arrive(copies, part)
-        raised[:, span] = (adapter_scale * dot_nt(laid, kept[span, :])).astype(bf16)
+        raised[:, span] = (adapter_scale * dot_nt(laid, down[span, :])).astype(bf16)
 
 
 def through_kernel(turn, arrived, before, down, expand, ranks, leaving):
@@ -304,62 +308,63 @@
             moved=weight_bytes,
         )
 
-    expand, raised, own = call(
+    expand, down, raised, own = call(
         prime_kernel,
-        (inner_cols[0], value_rows[0], adapter_expand[0]),
-        "hhh",
-        [((rank, width), bf16), ((count, width), bf16), ((rows, width), bf16)],
+        (inner_cols[0], value_rows[0], adapter_expand[0], adapter_down[0]),
+        "hhhh",
+        [
+            ((rank, width), bf16),
+            ((width, rank), bf16),
+            ((count, width), bf16),
+            ((rows, width), bf16),
+        ],
         [
             VMEM(inner_cols.shape[1:], bf16),
             VMEM((q_dev, width), bf16),
             pltpu.SemaphoreType.DMA((2,)),
-            pltpu.SemaphoreType.DMA((PARTS,)),
+            pltpu.SemaphoreType.DMA((2 * PARTS,)),
         ],
         flops=pass_flops,
         moved=2 * weight_bytes,
     )
 
     arrived = upward(own, 0, 1, 2)
-    hid, source = tie([hidden_cols[0], adapter_down[0]], own)
-    down, hidden = call(
-        functools.partial(keep_kernel, q_dev),
-        (hid, source),
-        "hh",
-        [((width, rank), bf16), ((count, width), bf16)],
-        [
-            VMEM(hidden_cols.shape[1:], bf16),
-            pltpu.SemaphoreType.DMA((1,)),
-            pltpu.SemaphoreType.DMA((PARTS,)),
-        ],
+    (hid,) = tie([hidden_cols[0]], own)
+    (hidden,) = call(
+        functools.partial(hidden_kernel, q_dev),
+        (hid, down),
+        "hv",
+        [((count, width), bf16)],
+        [VMEM(hidden_cols.shape[1:], bf16), pltpu.SemaphoreType.DMA((1,))],
         flops=2 * count * width * rank,
-        moved=2 * weight_bytes,
-    )
-    arrived, down = lax.optimization_barrier((arrived, down))
+        moved=weight_bytes,
+    )
+    arrived, hidden = lax.optimization_barrier((arrived, hidden))
     lower_ranks, leaving = through(1, arrived, jnp.zeros((rows, rank), bf16))
     moving = jnp.concatenate([leaving, own])
 
-    half = tok_dev // 2
-
-    def lift(part, token):
+    cut = tok_dev * 5 // 8
+
+    def lift(start, end, token):
         (cot,) = tie([cotangent], token)
         return call(
-            functools.partial(lift_kernel, part * half),
+            functools.partial(lift_kernel, start),
             (cot, expand),
             "hv",
-            [((half, rank), bf16)],
+            [((end - start, rank), bf16)],
             [
-                VMEM((half, width), bf16),
-                VMEM((half, rank), f32),
+                VMEM((end - start, width), bf16),
+                VMEM((end - start, rank), f32),
                 pltpu.SemaphoreType.DMA((PARTS,)),
             ],
-            flops=2 * half * width * rank,
+            flops=2 * (end - start) * width * rank,
             moved=weight_bytes,
         )[0]
 
     arrived = upward(moving, 1, 1, 2)
     wide = tie([value_rows[0], input_rows[0]], moving)
     wide = spread(jnp.concatenate(wide), "dp")
-    lifted = [lift(0, moving)]
+    lifted = [lift(0, cut, moving)]
     arrived, lifted[0] = lax.optimization_barrier((arrived, lifted[0]))
 
     slots = []
@@ -368,7 +373,7 @@
         found, leaving = through(0, arrived, empty)
         arrived = upward(leaving, 0, 1, 2)
         if slot == 1:
-            lifted.append(lift(1, leaving))
+            lifted.append(lift(cut, tok_dev, leaving))
             wide = jnp.concatenate(tie(wide, lifted[1]))
             arrived, wide = lax.optimization_barrier((arrived, wide))
         if slot == 2:
@@ -376,15 +381,8 @@
             right = dot_nt(right_rows, cot)
             arrived, right, *left_up = lax.optimization_barrier((arrived, right, *left_up))
         if slot == top:
-            (sums,) = call(
-                functools.partial(early_kernel, chips, rows),
-                (left, right, others, *lifted, *left_up, *early),
-                "v" * (5 + chips + columns),
-                [((max(ex_dev, 8), count), f32)],
-                flops=2 * count * rank * tok_dev * (2 * chips),
-                moved=weight_bytes,
-            )
-            arrived, sums = lax.optimization_barrier((arrived, sums))
+            others = swap(jnp.stack(tie(left_up, leaving)), "pipe", 1)
+            arrived, others = lax.optimization_barrier((arrived, others))
             break
         found, leaving = through(1, arrived, found)
         slots.append(found)
@@ -405,8 +403,7 @@
         if slot == top - 1:
             (early,) = tie([jnp.concatenate([lower_ranks] + slots)], leaving)
             early = spread(early, "dp")
-            others = swap(jnp.stack(tie(left_up, early[1])), "pipe", 1)
-            arrived, others, *early = lax.optimization_barrier((arrived, others, *early))
+            arrived, *early = lax.optimization_barrier((arrived, *early))
 
     (late,) = call(
         last_kernel,
@@ -414,6 +411,15 @@
         "vvv",
         [((2 * rows, rank), bf16)],
         flops=pass_flops,
+        moved=weight_bytes,
+    )
+    (right,) = tie([right], late)
+    (sums,) = call(
+        functools.partial(early_kernel, chips, rows),
+        (left, right, others, *lifted, *left_up, *early),
+        "v" * (5 + chips + columns),
+        [((max(ex_dev, 8), count), f32)],
+        flops=2 * count * rank * tok_dev * (2 * chips),
         moved=weight_bytes,
     )
     late = spread(late, "dp")

time: 91.2 us -> 89.5 us (0.981)
  waiting for transfers between devices: 14.2 us -> 11.7 us
  Pallas kernels: 29.5 us -> 31.1 us
    ppermute x11, starting transfers between devices: 13.9 us -> 11.3 us  [swap(): lax.ppermute(value, axis, [(source, source ^ distance) for source in rang...]
    ppermute x3, starting transfers between devices: 3.82 us -> 6.16 us  [around(): lax.ppermute(value, 'pipe', [(source, (source + 2 * hop) % count) for sou...]
    ppermute x11, waiting for transfers between devices: 11.7 us -> 9.51 us  [swap(): lax.ppermute(value, axis, [(source, source ^ distance) for source in rang...]
    pallas_call x15, Pallas kernels: 29.5 us -> 31.1 us  [call(): pl.pallas_call(kernel, in_specs=[pl.BlockSpec(memory_space=space[place])...]
  transfers between devices with their start and end apart: 24 -> 24, of which waited for: 10 -> 8; matrix products, arithmetic and copies ran while one was open for 6% -> 6% of each run, Pallas kernels for 22% -> 22%
where the time goes in v8:
time: 89.5 us; the launch traced here: 89.2 us
  starting transfers between devices  38.2 us (43%)
  Pallas kernels  31.1 us (35%)
  waiting for transfers between devices  11.7 us (13%)
  matrix products  5.32 us (6%)
  local copies, waits for them, and re-layouts  2.3 us (3%)
    pallas_call x15, Pallas kernels, call(): pl.pallas_call(kernel, in_specs=[pl.BlockSpec(memory_space=space[place])...  31.1 us
    ppermute x10, starting transfers between devices, upward(): lax.ppermute(value, 'pipe', [(source, source + hop) for source in range(f...  20.8 us
    ppermute x11, starting transfers between devices, swap(): lax.ppermute(value, axis, [(source, source ^ distance) for source in rang...  11.3 us
    ppermute x11, waiting for transfers between devices, swap(): lax.ppermute(value, axis, [(source, source ^ distance) for source in rang...  9.51 us
    ppermute x3, starting transfers between devices, around(): lax.ppermute(value, 'pipe', [(source, (source + 2 * hop) % count) for sou...  6.16 us
    dot_general x2, matrix products, dot_nt(): lax.dot_general(a, b, (((1,), (1,)), ((), ())), preferred_element_type=f3...  5.32 us
    unnamed x18, local copies, waits for them, and re-layouts  2.26 us
    ppermute x3, waiting for transfers between devices, around(): lax.ppermute(value, 'pipe', [(source, (source + 2 * hop) % count) for sou...  2.14 us
  transfers between devices with their start and end apart: 24, of which 8 were waited for; matrix products, arithmetic and copies ran while one was open for 6% of the time, Pallas kernels for 22%

profile of v8, /device:TPU:0, one launch (start us, length us, event | category | flops | bytes accessed | tf_op | source)
XLA Modules:
  0.0 89.2 jit_solution(6388650566583141579)
XLA Ops:
  0.0 6.7 %shard_map.100 = (bf16[512,8192]{1,0:T(8,128)(2,1)S(1)}, bf16[8192,512]{1,0:T(8,128)(2,1)S(1)}, bf16[64,8192]{1,0:T(8,128)(2,1)S(1)}, bf16[16,8192]{1,0:T(8,128)(2,1)S(1)}) custom-call(bf16[32,512]{1,0:T(8,128)(2,1)} %bitcast.37, bf16[8,8192]{1,0:T(8,128)(2,1)} %bitcast.34, bf16[512,8192]{1,0:T(8,128)(2,1)} %bitcast.30, bf16[8192,512]{1,0:T(8,128)(2,1)} %bitcast.31), custom_call_target="tpu_custom_call" | custom-call | flops 134217728 | bytes 16777216 | tf_op jit(solution)/shard_map/pallas_call | solution.py:67
  6.7 2.4 %collective-permute-start = (bf16[16,8192]{1,0:T(8,128)(2,1)S(1)}, bf16[16,8192]{1,0:T(8,128)(2,1)S(1)}, u32[]{:S(2)}, u32[]{:S(2)}) collective-permute-start(bf16[16,8192]{1,0:T(8,128)(2,1)S(1)} %get-tuple-element.59), channel_id=1, source_target_pairs={{0,1},{2,3},{4,5},{6,7},{8,9},{10,11},{12,13},{14,15},{16,17},{18,... | collective-permute-start | bytes 786440 | tf_op jit(solution)/shard_map/ppermute | solution.py:44
  9.1 3.5 %shard_map.101.hidden = bf16[64,8192]{1,0:T(8,128)(2,1)S(1)} custom-call(bf16[32,512]{1,0:T(8,128)(2,1)} %bitcast.38, bf16[8192,512]{1,0:T(8,128)(2,1)S(1)} %get-tuple-element.61.down), custom_call_target="tpu_custom_call" | custom-call | flops 536870912 | bytes 8388608 | tf_op jit(solution)/shard_map/pallas_call | solution.py:67
  13.6 2.4 %collective-permute-start.3 = (bf16[16,8192]{1,0:T(8,128)(2,1)S(1)}, bf16[16,8192]{1,0:T(8,128)(2,1)S(1)}, u32[]{:S(2)}, u32[]{:S(2)}) collective-permute-start(bf16[16,8192]{1,0:T(8,128)(2,1)S(1)} %constant_dynamic-update-slice_fusion.2), channel_id=1, source_target_pairs={{0,8},{8,0},{16,24},{24,16},{1,9},{9,1},{17,25},{25,17},{2,10},{10... | collective-permute-start | bytes 786440 | tf_op jit(solution)/shard_map/ppermute | solution.py:35
  16.0 1.5 %collective-permute-start.4 = (bf16[16,8192]{1,0:T(8,128)(2,1)S(1)}, bf16[16,8192]{1,0:T(8,128)(2,1)S(1)}, u32[]{:S(2)}, u32[]{:S(2)}) collective-permute-start(bf16[16,8192]{1,0:T(8,128)(2,1)S(1)} %constant_dynamic-update-slice_fusion.2), channel_id=1, source_target_pairs={{0,16},{8,24},{16,0},{24,8},{1,17},{9,25},{17,1},{25,9},{2,18},{10... | collective-permute-start | bytes 786440 | tf_op jit(solution)/shard_map/ppermute | solution.py:35
  17.6 4.5 %shard_map.103.refs_0_ = bf16[320,512]{1,0:T(8,128)(2,1)S(1)} custom-call(bf16[512,8192]{1,0:T(8,128)(2,1)} %cotangent.1, bf16[512,8192]{1,0:T(8,128)(2,1)S(1)} %get-tuple-element.63.expand), custom_call_target="tpu_custom_call" | custom-call | flops 2684354560 | bytes 8388608 | tf_op jit(solution)/shard_map/pallas_call | solution.py:67
  22.1 3.1 %shard_map.104 = (bf16[32,512]{1,0:T(8,128)(2,1)S(1)}, bf16[32,8192]{1,0:T(8,128)(2,1)S(1)}) custom-call(bf16[32,8192]{1,0:T(8,128)(2,1)S(1)} %collective-permute-done.1.arrived, bf16[32,512]{1,0:T(8,128)(2,1)S(1)} %broadcast_in_dim.12.before, bf16[8192,512]{1,0:T(8,128)(2,1)S(1)} %get-tuple-element.61.down, bf16[512,8192]{1,0:T(8,128)(2,1)S(1)} %get-tuple-element.63.expand), custom_call_target="tpu_custom_call" | custom-call | flops 268435456 | bytes 8388608 | tf_op jit(solution)/shard_map/pallas_call | solution.py:67
  26.6 4.2 %shard_map.105.refs_1_ = bf16[192,512]{1,0:T(8,128)(2,1)S(1)} custom-call(bf16[512,8192]{1,0:T(8,128)(2,1)} %cotangent.1, bf16[512,8192]{1,0:T(8,128)(2,1)S(1)} %get-tuple-element.63.expand), custom_call_target="tpu_custom_call" | custom-call | flops 1610612736 | bytes 8388608 | tf_op jit(solution)/shard_map/pallas_call | solution.py:67
  34.4 2.7 %fusion.5 = (bf16[64,512]{1,0:T(8,128)(2,1)S(1)}, f32[64,512]{1,0:T(8,128)S(1)}) fusion(f32[512]{0:T(512)S(1)} %convert_bitcast_fusion, bf16[64,8192]{1,0:T(8,128)(2,1)S(1)} %get-tuple-element.81, bf16[1,512,8192]{2,1,0:T(8,128)(2,1)S(1)} %bitcast.33), kind=kOutput, calls=%fused_computation.12 | convolution fusion | flops 536936448 | bytes 9635840 | tf_op jit(solution)/shard_map/dot_general | solution.py:28
  37.1 7.8 %collective-permute-start.10 = (bf16[64,512]{1,0:T(8,128)(2,1)S(1)}, bf16[64,512]{1,0:T(8,128)(2,1)S(1)}, u32[]{:S(2)}, u32[]{:S(2)}) collective-permute-start(bf16[64,512]{1,0:T(8,128)(2,1)S(1)} %get-tuple-element.99.refs_2_), channel_id=1, source_target_pairs={{0,6},{1,7},{8,14},{9,15},{16,22},{17,23},{24,30},{25,31}} | collective-permute-start | bytes 196616 | tf_op jit(solution)/shard_map/ppermute | solution.py:44
  46.1 2.7 %collective-permute-start.9 = (bf16[64,512]{1,0:T(8,128)(2,1)S(1)}, bf16[64,512]{1,0:T(8,128)(2,1)S(1)}, u32[]{:S(2)}, u32[]{:S(2)}) collective-permute-start(bf16[64,512]{1,0:T(8,128)(2,1)S(1)} %get-tuple-element.99.refs_2_), channel_id=1, source_target_pairs={{0,4},{1,5},{2,6},{3,7},{8,12},{9,13},{10,14},{11,15},{16,20},{17,... | collective-permute-start | bytes 196616 | tf_op jit(solution)/shard_map/ppermute | solution.py:44
  48.9 3.1 %shard_map.108 = (bf16[32,512]{1,0:T(8,128)(2,1)S(1)}, bf16[32,8192]{1,0:T(8,128)(2,1)S(1)}) custom-call(bf16[32,8192]{1,0:T(8,128)(2,1)S(1)} %collective-permute-done.6.arrived, bf16[32,512]{1,0:T(8,128)(2,1)S(1)} %broadcast_in_dim.12.before, bf16[8192,512]{1,0:T(8,128)(2,1)S(1)} %get-tuple-element.61.down, bf16[512,8192]{1,0:T(8,128)(2,1)S(1)} %get-tuple-element.63.expand), custom_call_target="tpu_custom_call" | custom-call | flops 268435456 | bytes 8388608 | tf_op jit(solution)/shard_map/pallas_call | solution.py:67
  53.3 2.7 %fusion.6.right = f32[64,512]{1,0:T(8,128)S(1)} fusion(bf16[64,8192]{1,0:T(8,128)(2,1)S(1)} %get-tuple-element.84, bf16[512,8192]{1,0:T(8,128)(2,1)S(1)} %bitcast.29), kind=kOutput, calls=%fused_computation.13 | convolution fusion | flops 536870912 | bytes 9568256 | tf_op jit(solution)/shard_map/dot_general | solution.py:28
  56.8 1.6 %collective-permute-start.12 = (bf16[80,512]{1,0:T(8,128)(2,1)S(1)}, bf16[80,512]{1,0:T(8,128)(2,1)S(1)}, u32[]{:S(2)}, u32[]{:S(2)}) collective-permute-start(bf16[80,512]{1,0:T(8,128)(2,1)S(1)} %pad_maximum_fusion.2.refs_6_), channel_id=1, source_target_pairs={{0,8},{8,0},{16,24},{24,16},{1,9},{9,1},{17,25},{25,17},{2,10},{10... | collective-permute-start | bytes 245768 | tf_op jit(solution)/shard_map/ppermute | solution.py:35
  58.3 1.5 %collective-permute-start.13 = (bf16[80,512]{1,0:T(8,128)(2,1)S(1)}, bf16[80,512]{1,0:T(8,128)(2,1)S(1)}, u32[]{:S(2)}, u32[]{:S(2)}) collective-permute-start(bf16[80,512]{1,0:T(8,128)(2,1)S(1)} %pad_maximum_fusion.2.refs_6_), channel_id=1, source_target_pairs={{0,16},{8,24},{16,0},{24,8},{1,17},{9,25},{17,1},{25,9},{2,18},{10... | collective-permute-start | bytes 245768 | tf_op jit(solution)/shard_map/ppermute | solution.py:35
  61.3 1.5 %collective-permute-done.13.refs_8_ = bf16[80,512]{1,0:T(8,128)(2,1)S(1)} collective-permute-done((bf16[80,512]{1,0:T(8,128)(2,1)S(1)}, bf16[80,512]{1,0:T(8,128)(2,1)S(1)}, u32[]{:S(2)}, u32[]{:S(2)}) %collective-permute-start.13) | collective-permute-done | bytes 81952 | tf_op jit(solution)/shard_map/ppermute | solution.py:35
  62.8 2.4 %collective-permute-done.14.refs_9_ = bf16[80,512]{1,0:T(8,128)(2,1)S(1)} collective-permute-done((bf16[80,512]{1,0:T(8,128)(2,1)S(1)}, bf16[80,512]{1,0:T(8,128)(2,1)S(1)}, u32[]{:S(2)}, u32[]{:S(2)}) %collective-permute-start.14) | collective-permute-done | bytes 81952 | tf_op jit(solution)/shard_map/ppermute | solution.py:35
  65.2 3.1 %shard_map.110 = (bf16[32,512]{1,0:T(8,128)(2,1)S(1)}, bf16[32,8192]{1,0:T(8,128)(2,1)S(1)}) custom-call(bf16[32,8192]{1,0:T(8,128)(2,1)S(1)} %collective-permute-done.11.arrived, bf16[32,512]{1,0:T(8,128)(2,1)S(1)} %broadcast_in_dim.12.before, bf16[8192,512]{1,0:T(8,128)(2,1)S(1)} %get-tuple-element.61.down, bf16[512,8192]{1,0:T(8,128)(2,1)S(1)} %get-tuple-element.63.expand), custom_call_target="tpu_custom_call" | custom-call | flops 268435456 | bytes 8388608 | tf_op jit(solution)/shard_map/pallas_call | solution.py:67
  68.3 1.5 %collective-permute-start.15 = (bf16[32,8192]{1,0:T(8,128)(2,1)S(1)}, bf16[32,8192]{1,0:T(8,128)(2,1)S(1)}, u32[]{:S(2)}, u32[]{:S(2)}) collective-permute-start(bf16[32,8192]{1,0:T(8,128)(2,1)S(1)} %get-tuple-element.95), channel_id=1, source_target_pairs={{0,1},{2,3},{4,5},{6,7},{8,9},{10,11},{12,13},{14,15},{16,17},{18,... | collective-permute-start | bytes 1572872 | tf_op jit(solution)/shard_map/ppermute | solution.py:44
  70.0 1.5 %collective-permute-done.16.others = bf16[4,64,512]{2,1,0:T(8,128)(2,1)S(1)} collective-permute-done((bf16[4,64,512]{2,1,0:T(8,128)(2,1)S(1)}, bf16[4,64,512]{2,1,0:T(8,128)(2,1)S(1)}, u32[]{:S(2)}, u32[]{:S(2)}) %collective-permute-start.16) | collective-permute-done | bytes 262176 | tf_op jit(solution)/shard_map/ppermute | solution.py:35
  76.8 1.5 %collective-permute-done.19.refs_5_ = bf16[32,512]{1,0:T(8,128)(2,1)S(1)} collective-permute-done((bf16[32,512]{1,0:T(8,128)(2,1)S(1)}, bf16[32,512]{1,0:T(8,128)(2,1)S(1)}, u32[]{:S(2)}, u32[]{:S(2)}) %collective-permute-start.19) | collective-permute-done | bytes 32800 | tf_op jit(solution)/shard_map/ppermute | solution.py:35
  80.1 3.8 %collective-permute-start.21 = (f32[8,64]{1,0:T(8,128)S(1)}, f32[8,64]{1,0:T(8,128)S(1)}, u32[]{:S(2)}, u32[]{:S(2)}) collective-permute-start(f32[8,64]{1,0:T(8,128)S(1)} %add.3.refs_0_), channel_id=1, source_target_pairs={{0,2},{1,3},{2,4},{3,5},{4,6},{5,7},{6,0},{7,1},{8,10},{9,11},{10,... | collective-permute-start | bytes 6152 | tf_op jit(solution)/shard_map/ppermute | solution.py:51
  83.9 2.4 %collective-permute-start.23 = (f32[8,64]{1,0:T(8,128)S(1)}, f32[8,64]{1,0:T(8,128)S(1)}, u32[]{:S(2)}, u32[]{:S(2)}) collective-permute-start(f32[8,64]{1,0:T(8,128)S(1)} %add.3.refs_0_), channel_id=1, source_target_pairs={{0,6},{1,7},{2,0},{3,1},{4,2},{5,3},{6,4},{7,5},{8,14},{9,15},{10,... | collective-permute-start | bytes 6152 | tf_op jit(solution)/shard_map/ppermute | solution.py:51
  86.3 2.1 %collective-permute-done.22.refs_2_ = f32[8,64]{1,0:T(8,128)S(1)} collective-permute-done((f32[8,64]{1,0:T(8,128)S(1)}, f32[8,64]{1,0:T(8,128)S(1)}, u32[]{:S(2)}, u32[]{:S(2)}) %collective-permute-start.22) | collective-permute-done | bytes 2080 | tf_op jit(solution)/shard_map/ppermute | solution.py:51
  (70 shorter events, 18.7 us)
Async XLA Ops:
  6.7 5.9 %collective-permute-start = (bf16[16,8192]{1,0:T(8,128)(2,1)S(1)}, bf16[16,8192]{1,0:T(8,128)(2,1)S(1)}, u32[]{:S(2)}, u32[]{:S(2)}) collective-permute-start(bf16[16,8192]{1,0:T(8,128)(2,1)S(1)} %get-tuple-element.59), channel_id=1, source_target_pairs={{0,1},{2,3},{4,5},{6,7},{8,9},{10,11},{12,13},{14,15},{16,17},{18,... | collective-permute-start | bytes 786440 | tf_op jit(solution)/shard_map/ppermute | solution.py:44
  12.8 9.3 %collective-permute-start.1 = (bf16[32,8192]{1,0:T(8,128)(2,1)S(1)}, bf16[32,8192]{1,0:T(8,128)(2,1)S(1)}, u32[]{:S(2)}, u32[]{:S(2)}) collective-permute-start(bf16[32,8192]{1,0:T(8,128)(2,1)S(1)} %constant_dynamic-update-slice_fusion), channel_id=1, source_target_pairs={{1,2},{3,4},{5,6},{9,10},{11,12},{13,14},{17,18},{19,20},{21,22},{... | collective-permute-start | bytes 1572872 | tf_op jit(solution)/shard_map/ppermute | solution.py:44
  13.6 17.2 %collective-permute-start.3 = (bf16[16,8192]{1,0:T(8,128)(2,1)S(1)}, bf16[16,8192]{1,0:T(8,128)(2,1)S(1)}, u32[]{:S(2)}, u32[]{:S(2)}) collective-permute-start(bf16[16,8192]{1,0:T(8,128)(2,1)S(1)} %constant_dynamic-update-slice_fusion.2), channel_id=1, source_target_pairs={{0,8},{8,0},{16,24},{24,16},{1,9},{9,1},{17,25},{25,17},{2,10},{10... | collective-permute-start | bytes 786440 | tf_op jit(solution)/shard_map/ppermute | solution.py:35
  16.0 14.9 %collective-permute-start.4 = (bf16[16,8192]{1,0:T(8,128)(2,1)S(1)}, bf16[16,8192]{1,0:T(8,128)(2,1)S(1)}, u32[]{:S(2)}, u32[]{:S(2)}) collective-permute-start(bf16[16,8192]{1,0:T(8,128)(2,1)S(1)} %constant_dynamic-update-slice_fusion.2), channel_id=1, source_target_pairs={{0,16},{8,24},{16,0},{24,8},{1,17},{9,25},{17,1},{25,9},{2,18},{10... | collective-permute-start | bytes 786440 | tf_op jit(solution)/shard_map/ppermute | solution.py:35
  17.5 13.3 %collective-permute-start.5 = (bf16[16,8192]{1,0:T(8,128)(2,1)S(1)}, bf16[16,8192]{1,0:T(8,128)(2,1)S(1)}, u32[]{:S(2)}, u32[]{:S(2)}) collective-permute-start(bf16[16,8192]{1,0:T(8,128)(2,1)S(1)} %constant_dynamic-update-slice_fusion.2), channel_id=1, source_target_pairs={{0,24},{8,16},{16,8},{24,0},{1,25},{9,17},{17,9},{25,1},{2,26},{10... | collective-permute-start | bytes 786440 | tf_op jit(solution)/shard_map/ppermute | solution.py:35
  25.2 5.8 %collective-permute-start.2 = (bf16[32,8192]{1,0:T(8,128)(2,1)S(1)}, bf16[32,8192]{1,0:T(8,128)(2,1)S(1)}, u32[]{:S(2)}, u32[]{:S(2)}) collective-permute-start(bf16[32,8192]{1,0:T(8,128)(2,1)S(1)} %get-tuple-element.67), channel_id=1, source_target_pairs={{0,1},{2,3},{4,5},{6,7},{8,9},{10,11},{12,13},{14,15},{16,17},{18,... | collective-permute-start | bytes 1572872 | tf_op jit(solution)/shard_map/ppermute | solution.py:44
  31.2 17.7 %collective-permute-start.6 = (bf16[32,8192]{1,0:T(8,128)(2,1)S(1)}, bf16[32,8192]{1,0:T(8,128)(2,1)S(1)}, u32[]{:S(2)}, u32[]{:S(2)}) collective-permute-start(bf16[32,8192]{1,0:T(8,128)(2,1)S(1)} %get-tuple-element.77), channel_id=1, source_target_pairs={{1,2},{3,4},{5,6},{9,10},{11,12},{13,14},{17,18},{19,20},{21,22},{... | collective-permute-start | bytes 1572872 | tf_op jit(solution)/shard_map/ppermute | solution.py:44
  37.1 18.9 %collective-permute-start.10 = (bf16[64,512]{1,0:T(8,128)(2,1)S(1)}, bf16[64,512]{1,0:T(8,128)(2,1)S(1)}, u32[]{:S(2)}, u32[]{:S(2)}) collective-permute-start(bf16[64,512]{1,0:T(8,128)(2,1)S(1)} %get-tuple-element.99.refs_2_), channel_id=1, source_target_pairs={{0,6},{1,7},{8,14},{9,15},{16,22},{17,23},{24,30},{25,31}} | collective-permute-start | bytes 196616 | tf_op jit(solution)/shard_map/ppermute | solution.py:44
  44.8 11.2 %collective-permute-start.8 = (bf16[64,512]{1,0:T(8,128)(2,1)S(1)}, bf16[64,512]{1,0:T(8,128)(2,1)S(1)}, u32[]{:S(2)}, u32[]{:S(2)}) collective-permute-start(bf16[64,512]{1,0:T(8,128)(2,1)S(1)} %get-tuple-element.99.refs_2_), channel_id=1, source_target_pairs={{0,2},{1,3},{2,4},{3,5},{4,6},{5,7},{8,10},{9,11},{10,12},{11,13},... | collective-permute-start | bytes 196616 | tf_op jit(solution)/shard_map/ppermute | solution.py:44
  46.1 9.9 %collective-permute-start.9 = (bf16[64,512]{1,0:T(8,128)(2,1)S(1)}, bf16[64,512]{1,0:T(8,128)(2,1)S(1)}, u32[]{:S(2)}, u32[]{:S(2)}) collective-permute-start(bf16[64,512]{1,0:T(8,128)(2,1)S(1)} %get-tuple-element.99.refs_2_), channel_id=1, source_target_pairs={{0,4},{1,5},{2,6},{3,7},{8,12},{9,13},{10,14},{11,15},{16,20},{17,... | collective-permute-start | bytes 196616 | tf_op jit(solution)/shard_map/ppermute | solution.py:44
  52.0 4.0 %collective-permute-start.7 = (bf16[32,8192]{1,0:T(8,128)(2,1)S(1)}, bf16[32,8192]{1,0:T(8,128)(2,1)S(1)}, u32[]{:S(2)}, u32[]{:S(2)}) collective-permute-start(bf16[32,8192]{1,0:T(8,128)(2,1)S(1)} %get-tuple-element.83), channel_id=1, source_target_pairs={{0,1},{2,3},{4,5},{6,7},{8,9},{10,11},{12,13},{14,15},{16,17},{18,... | collective-permute-start | bytes 1572872 | tf_op jit(solution)/shard_map/ppermute | solution.py:44
  56.1 9.1 %collective-permute-start.11 = (bf16[32,8192]{1,0:T(8,128)(2,1)S(1)}, bf16[32,8192]{1,0:T(8,128)(2,1)S(1)}, u32[]{:S(2)}, u32[]{:S(2)}) collective-permute-start(bf16[32,8192]{1,0:T(8,128)(2,1)S(1)} %get-tuple-element.89), channel_id=1, source_target_pairs={{1,2},{3,4},{5,6},{9,10},{11,12},{13,14},{17,18},{19,20},{21,22},{... | collective-permute-start | bytes 1572872 | tf_op jit(solution)/shard_map/ppermute | solution.py:44
  56.8 4.5 %collective-permute-start.12 = (bf16[80,512]{1,0:T(8,128)(2,1)S(1)}, bf16[80,512]{1,0:T(8,128)(2,1)S(1)}, u32[]{:S(2)}, u32[]{:S(2)}) collective-permute-start(bf16[80,512]{1,0:T(8,128)(2,1)S(1)} %pad_maximum_fusion.2.refs_6_), channel_id=1, source_target_pairs={{0,8},{8,0},{16,24},{24,16},{1,9},{9,1},{17,25},{25,17},{2,10},{10... | collective-permute-start | bytes 245768 | tf_op jit(solution)/shard_map/ppermute | solution.py:35
  58.3 4.4 %collective-permute-start.13 = (bf16[80,512]{1,0:T(8,128)(2,1)S(1)}, bf16[80,512]{1,0:T(8,128)(2,1)S(1)}, u32[]{:S(2)}, u32[]{:S(2)}) collective-permute-start(bf16[80,512]{1,0:T(8,128)(2,1)S(1)} %pad_maximum_fusion.2.refs_6_), channel_id=1, source_target_pairs={{0,16},{8,24},{16,0},{24,8},{1,17},{9,25},{17,1},{25,9},{2,18},{10... | collective-permute-start | bytes 245768 | tf_op jit(solution)/shard_map/ppermute | solution.py:35
  59.9 5.3 %collective-permute-start.14 = (bf16[80,512]{1,0:T(8,128)(2,1)S(1)}, bf16[80,512]{1,0:T(8,128)(2,1)S(1)}, u32[]{:S(2)}, u32[]{:S(2)}) collective-permute-start(bf16[80,512]{1,0:T(8,128)(2,1)S(1)} %pad_maximum_fusion.2.refs_6_), channel_id=1, source_target_pairs={{0,24},{8,16},{16,8},{24,0},{1,25},{9,17},{17,9},{25,1},{2,26},{10... | collective-permute-start | bytes 245768 | tf_op jit(solution)/shard_map/ppermute | solution.py:35
  68.3 3.2 %collective-permute-start.15 = (bf16[32,8192]{1,0:T(8,128)(2,1)S(1)}, bf16[32,8192]{1,0:T(8,128)(2,1)S(1)}, u32[]{:S(2)}, u32[]{:S(2)}) collective-permute-start(bf16[32,8192]{1,0:T(8,128)(2,1)S(1)} %get-tuple-element.95), channel_id=1, source_target_pairs={{0,1},{2,3},{4,5},{6,7},{8,9},{10,11},{12,13},{14,15},{16,17},{18,... | collective-permute-start | bytes 1572872 | tf_op jit(solution)/shard_map/ppermute | solution.py:44
  69.9 1.6 %collective-permute-start.16 = (bf16[4,64,512]{2,1,0:T(8,128)(2,1)S(1)}, bf16[4,64,512]{2,1,0:T(8,128)(2,1)S(1)}, u32[]{:S(2)}, u32[]{:S(2)}) collective-permute-start(bf16[4,64,512]{2,1,0:T(8,128)(2,1)S(1)} %pad_maximum_fusion.1), channel_id=1, source_target_pairs={{0,1},{1,0},{2,3},{3,2},{4,5},{5,4},{6,7},{7,6},{8,9},{9,8},{10,11... | collective-permute-start | bytes 786440 | tf_op jit(solution)/shard_map/ppermute | solution.py:35
  71.5 4.7 %collective-permute-start.17 = (bf16[32,512]{1,0:T(8,128)(2,1)S(1)}, bf16[32,512]{1,0:T(8,128)(2,1)S(1)}, u32[]{:S(2)}, u32[]{:S(2)}) collective-permute-start(bf16[32,512]{1,0:T(8,128)(2,1)S(1)} %shard_map.111.refs_2_), channel_id=1, source_target_pairs={{0,8},{8,0},{16,24},{24,16},{1,9},{9,1},{17,25},{25,17},{2,10},{10... | collective-permute-start | bytes 98312 | tf_op jit(solution)/shard_map/ppermute | solution.py:35
  72.9 3.9 %collective-permute-start.18 = (bf16[32,512]{1,0:T(8,128)(2,1)S(1)}, bf16[32,512]{1,0:T(8,128)(2,1)S(1)}, u32[]{:S(2)}, u32[]{:S(2)}) collective-permute-start(bf16[32,512]{1,0:T(8,128)(2,1)S(1)} %shard_map.111.refs_2_), channel_id=1, source_target_pairs={{0,16},{8,24},{16,0},{24,8},{1,17},{9,25},{17,1},{25,9},{2,18},{10... | collective-permute-start | bytes 98312 | tf_op jit(solution)/shard_map/ppermute | solution.py:35
  73.5 4.8 %collective-permute-start.19 = (bf16[32,512]{1,0:T(8,128)(2,1)S(1)}, bf16[32,512]{1,0:T(8,128)(2,1)S(1)}, u32[]{:S(2)}, u32[]{:S(2)}) collective-permute-start(bf16[32,512]{1,0:T(8,128)(2,1)S(1)} %shard_map.111.refs_2_), channel_id=1, source_target_pairs={{0,24},{8,16},{16,8},{24,0},{1,25},{9,17},{17,9},{25,1},{2,26},{10... | collective-permute-start | bytes 98312 | tf_op jit(solution)/shard_map/ppermute | solution.py:35
  79.0 1.2 %collective-permute-start.20 = (f32[8,64]{1,0:T(8,128)S(1)}, f32[8,64]{1,0:T(8,128)S(1)}, u32[]{:S(2)}, u32[]{:S(2)}) collective-permute-start(f32[8,64]{1,0:T(8,128)S(1)} %shard_map.113), channel_id=1, source_target_pairs={{0,1},{1,0},{2,3},{3,2},{4,5},{5,4},{6,7},{7,6},{8,9},{9,8},{10,11... | collective-permute-start | bytes 6152 | tf_op jit(solution)/shard_map/ppermute | solution.py:35
  80.1 6.2 %collective-permute-start.21 = (f32[8,64]{1,0:T(8,128)S(1)}, f32[8,64]{1,0:T(8,128)S(1)}, u32[]{:S(2)}, u32[]{:S(2)}) collective-permute-start(f32[8,64]{1,0:T(8,128)S(1)} %add.3.refs_0_), channel_id=1, source_target_pairs={{0,2},{1,3},{2,4},{3,5},{4,6},{5,7},{6,0},{7,1},{8,10},{9,11},{10,... | collective-permute-start | bytes 6152 | tf_op jit(solution)/shard_map/ppermute | solution.py:51
  83.9 4.5 %collective-permute-start.22 = (f32[8,64]{1,0:T(8,128)S(1)}, f32[8,64]{1,0:T(8,128)S(1)}, u32[]{:S(2)}, u32[]{:S(2)}) collective-permute-start(f32[8,64]{1,0:T(8,128)S(1)} %add.3.refs_0_), channel_id=1, source_target_pairs={{0,4},{1,5},{2,6},{3,7},{4,0},{5,1},{6,2},{7,3},{8,12},{9,13},{10,... | collective-permute-start | bytes 6152 | tf_op jit(solution)/shard_map/ppermute | solution.py:51
  83.9 4.5 %collective-permute-start.23 = (f32[8,64]{1,0:T(8,128)S(1)}, f32[8,64]{1,0:T(8,128)S(1)}, u32[]{:S(2)}, u32[]{:S(2)}) collective-permute-start(f32[8,64]{1,0:T(8,128)S(1)} %add.3.refs_0_), channel_id=1, source_target_pairs={{0,6},{1,7},{2,0},{3,1},{4,2},{5,3},{6,4},{7,5},{8,14},{9,15},{10,... | collective-permute-start | bytes 6152 | tf_op jit(solution)/shard_map/ppermute | solution.py:51
  (8 other events, 66.0 us)

commit v9 on v8

--- a/solution.py
+++ b/solution.py
@@ -103,19 +103,13 @@
 
 
 def prime_kernel(
-    cols_hbm, values_hbm, expand, down, kept, kept_down, raised, own, cols, values, few, sems
+    cols_hbm, values_hbm, expand, kept, raised, own, cols, values, few, sems
 ):
     step = expand.shape[1] // PARTS
-    deep = down.shape[0] // PARTS
     small = fetch([(cols_hbm, cols), (values_hbm, values)], few)
     begin(small)
-    wide = [pl.ds(part * step, step) for part in range(PARTS)]
-    tall = [pl.ds(part * deep, deep) for part in range(PARTS)]
-    copies = fetch(
-        [(expand.at[:, span], kept.at[:, span]) for span in wide]
-        + [(down.at[span], kept_down.at[span]) for span in tall],
-        sems,
-    )
+    spans = [pl.ds(part * step, step) for part in range(PARTS)]
+    copies = fetch([(expand.at[:, span], kept.at[:, span]) for span in spans], sems)
     begin(copies)
     rows = own.shape[0]
     q_dev = rows // 2
@@ -130,8 +124,12 @@
         raised[:, span] = found.astype(bf16)
         above = jnp.concatenate([values[:, span].astype(f32), found[q_dev:rows]])
         own[:, span] = above.astype(bf16)
-    for part in range(PARTS, 2 * PARTS):
-        arrive(copies, part)
+
+
+def keep_kernel(down, kept, sem):
+    copy = pltpu.make_async_copy(down, kept, sem)
+    copy.start()
+    copy.wait()
 
 
 def hidden_kernel(q_dev, cols_hbm, down, raised, cols, few):
@@ -308,38 +306,32 @@
             moved=weight_bytes,
         )
 
-    expand, down, raised, own = call(
+    expand, raised, own = call(
         prime_kernel,
-        (inner_cols[0], value_rows[0], adapter_expand[0], adapter_down[0]),
-        "hhhh",
-        [
-            ((rank, width), bf16),
-            ((width, rank), bf16),
-            ((count, width), bf16),
-            ((rows, width), bf16),
-        ],
+        (inner_cols[0], value_rows[0], adapter_expand[0]),
+        "hhh",
+        [((rank, width), bf16), ((count, width), bf16), ((rows, width), bf16)],
         [
             VMEM(inner_cols.shape[1:], bf16),
             VMEM((q_dev, width), bf16),
             pltpu.SemaphoreType.DMA((2,)),
-            pltpu.SemaphoreType.DMA((2 * PARTS,)),
+            pltpu.SemaphoreType.DMA((PARTS,)),
         ],
         flops=pass_flops,
         moved=2 * weight_bytes,
     )
 
     arrived = upward(own, 0, 1, 2)
-    (hid,) = tie([hidden_cols[0]], own)
-    (hidden,) = call(
-        functools.partial(hidden_kernel, q_dev),
-        (hid, down),
-        "hv",
-        [((count, width), bf16)],
-        [VMEM(hidden_cols.shape[1:], bf16), pltpu.SemaphoreType.DMA((1,))],
-        flops=2 * count * width * rank,
-        moved=weight_bytes,
-    )
-    arrived, hidden = lax.optimization_barrier((arrived, hidden))
+    (source,) = tie([adapter_down[0]], own)
+    (down,) = call(
+        keep_kernel,
+        (source,),
+        "h",
+        [((width, rank), bf16)],
+        [pltpu.SemaphoreType.DMA],
+        moved=2 * weight_bytes,
+    )
+    arrived, down = lax.optimization_barrier((arrived, down))
     lower_ranks, leaving = through(1, arrived, jnp.zeros((rows, rank), bf16))
     moving = jnp.concatenate([leaving, own])
 
@@ -373,8 +365,17 @@
         found, leaving = through(0, arrived, empty)
         arrived = upward(leaving, 0, 1, 2)
         if slot == 1:
-            lifted.append(lift(cut, tok_dev, leaving))
-            wide = jnp.concatenate(tie(wide, lifted[1]))
+            (hid,) = tie([hidden_cols[0]], leaving)
+            (hidden,) = call(
+                functools.partial(hidden_kernel, q_dev),
+                (hid, down),
+                "hv",
+                [((count, width), bf16)],
+                [VMEM(hidden_cols.shape[1:], bf16), pltpu.SemaphoreType.DMA((1,))],
+                flops=2 * count * width * rank,
+                moved=weight_bytes,
+            )
+            wide = jnp.concatenate(tie(wide, hidden))
             arrived, wide = lax.optimization_barrier((arrived, wide))
         if slot == 2:
             (cot,) = tie([cotangent], leaving)
@@ -403,7 +404,8 @@
         if slot == top - 1:
             (early,) = tie([jnp.concatenate([lower_ranks] + slots)], leaving)
             early = spread(early, "dp")
-            arrived, *early = lax.optimization_barrier((arrived, *early))
+            lifted.append(lift(cut, tok_dev, leaving))
+            arrived, lifted[1], *early = lax.optimization_barrier((arrived, lifted[1], *early))
 
     (late,) = call(
         last_kernel,

time: 89.5 us -> 86.7 us (0.969)
  waiting for transfers between devices: 11.7 us -> 8.27 us
  Pallas kernels: 31.1 us -> 32.2 us
    ppermute x11, waiting for transfers between devices: 9.51 us -> 6.11 us  [swap(): lax.ppermute(value, axis, [(source, source ^ distance) for source in rang...]
    pallas_call x15 -> x16, Pallas kernels: 31.1 us -> 32.2 us  [call(): pl.pallas_call(kernel, in_specs=[pl.BlockSpec(memory_space=space[place])...]
  transfers between devices with their start and end apart: 24 -> 24, of which waited for: 8 -> 6; matrix products, arithmetic and copies ran while one was open for 6% -> 6% of each run, Pallas kernels for 22% -> 27%
where the time goes in v9:
time: 86.7 us; the launch traced here: 86.3 us
  starting transfers between devices  37.5 us (43%)
  Pallas kernels  32.2 us (37%)
  waiting for transfers between devices  8.27 us (10%)
  matrix products  5.32 us (6%)
  local copies, waits for them, and re-layouts  2.3 us (3%)
    pallas_call x16, Pallas kernels, call(): pl.pallas_call(kernel, in_specs=[pl.BlockSpec(memory_space=space[place])...  32.2 us
    ppermute x10, starting transfers between devices, upward(): lax.ppermute(value, 'pipe', [(source, source + hop) for source in range(f...  20.7 us
    ppermute x11, starting transfers between devices, swap(): lax.ppermute(value, axis, [(source, source ^ distance) for source in rang...  11.3 us
    ppermute x11, waiting for transfers between devices, swap(): lax.ppermute(value, axis, [(source, source ^ distance) for source in rang...  6.11 us
    ppermute x3, starting transfers between devices, around(): lax.ppermute(value, 'pipe', [(source, (source + 2 * hop) % count) for sou...  5.53 us
    dot_general x2, matrix products, dot_nt(): lax.dot_general(a, b, (((1,), (1,)), ((), ())), preferred_element_type=f3...  5.32 us
    unnamed x18, local copies, waits for them, and re-layouts  2.26 us
    ppermute x3, waiting for transfers between devices, around(): lax.ppermute(value, 'pipe', [(source, (source + 2 * hop) % count) for sou...  2.14 us
  transfers between devices with their start and end apart: 24, of which 6 were waited for; matrix products, arithmetic and copies ran while one was open for 6% of the time, Pallas kernels for 27%

profile of v9, /device:TPU:0, one launch (start us, length us, event | category | flops | bytes accessed | tf_op | source)
XLA Modules:
  0.0 86.3 jit_solution(6614916599151124663)
XLA Ops:
  0.0 4.6 %shard_map.100 = (bf16[512,8192]{1,0:T(8,128)(2,1)S(1)}, bf16[64,8192]{1,0:T(8,128)(2,1)S(1)}, bf16[16,8192]{1,0:T(8,128)(2,1)S(1)}) custom-call(bf16[32,512]{1,0:T(8,128)(2,1)} %bitcast.37, bf16[8,8192]{1,0:T(8,128)(2,1)} %bitcast.34, bf16[512,8192]{1,0:T(8,128)(2,1)} %bitcast.30), custom_call_target="tpu_custom_call" | custom-call | flops 134217728 | bytes 16777216 | tf_op jit(solution)/shard_map/pallas_call | solution.py:67
  4.6 2.4 %collective-permute-start = (bf16[16,8192]{1,0:T(8,128)(2,1)S(1)}, bf16[16,8192]{1,0:T(8,128)(2,1)S(1)}, u32[]{:S(2)}, u32[]{:S(2)}) collective-permute-start(bf16[16,8192]{1,0:T(8,128)(2,1)S(1)} %get-tuple-element.60), channel_id=1, source_target_pairs={{0,1},{2,3},{4,5},{6,7},{8,9},{10,11},{12,13},{14,15},{16,17},{18,... | collective-permute-start | bytes 786440 | tf_op jit(solution)/shard_map/ppermute | solution.py:44
  7.0 3.4 %shard_map.101.down = bf16[8192,512]{1,0:T(8,128)(2,1)S(1)} custom-call(bf16[8192,512]{1,0:T(8,128)(2,1)} %bitcast.31), custom_call_target="tpu_custom_call" | custom-call | bytes 16777216 | tf_op jit(solution)/shard_map/pallas_call | solution.py:67
  11.5 2.4 %collective-permute-start.3 = (bf16[16,8192]{1,0:T(8,128)(2,1)S(1)}, bf16[16,8192]{1,0:T(8,128)(2,1)S(1)}, u32[]{:S(2)}, u32[]{:S(2)}) collective-permute-start(bf16[16,8192]{1,0:T(8,128)(2,1)S(1)} %constant_dynamic-update-slice_fusion.2), channel_id=1, source_target_pairs={{0,8},{8,0},{16,24},{24,16},{1,9},{9,1},{17,25},{25,17},{2,10},{10... | collective-permute-start | bytes 786440 | tf_op jit(solution)/shard_map/ppermute | solution.py:35
  13.9 1.5 %collective-permute-start.4 = (bf16[16,8192]{1,0:T(8,128)(2,1)S(1)}, bf16[16,8192]{1,0:T(8,128)(2,1)S(1)}, u32[]{:S(2)}, u32[]{:S(2)}) collective-permute-start(bf16[16,8192]{1,0:T(8,128)(2,1)S(1)} %constant_dynamic-update-slice_fusion.2), channel_id=1, source_target_pairs={{0,16},{8,24},{16,0},{24,8},{1,17},{9,25},{17,1},{25,9},{2,18},{10... | collective-permute-start | bytes 786440 | tf_op jit(solution)/shard_map/ppermute | solution.py:35
  15.4 4.5 %shard_map.103.refs_0_ = bf16[320,512]{1,0:T(8,128)(2,1)S(1)} custom-call(bf16[512,8192]{1,0:T(8,128)(2,1)} %cotangent.1, bf16[512,8192]{1,0:T(8,128)(2,1)S(1)} %get-tuple-element.64.expand), custom_call_target="tpu_custom_call" | custom-call | flops 2684354560 | bytes 8388608 | tf_op jit(solution)/shard_map/pallas_call | solution.py:67
  20.0 3.1 %shard_map.104 = (bf16[32,512]{1,0:T(8,128)(2,1)S(1)}, bf16[32,8192]{1,0:T(8,128)(2,1)S(1)}) custom-call(bf16[32,8192]{1,0:T(8,128)(2,1)S(1)} %collective-permute-done.1.arrived, bf16[32,512]{1,0:T(8,128)(2,1)S(1)} %broadcast_in_dim.12.before, bf16[8192,512]{1,0:T(8,128)(2,1)S(1)} %shard_map.101.down, bf16[512,8192]{1,0:T(8,128)(2,1)S(1)} %get-tuple-element.64.expand), custom_call_target="tpu_custom_call" | custom-call | flops 268435456 | bytes 8388608 | tf_op jit(solution)/shard_map/pallas_call | solution.py:67
  23.1 1.4 %collective-permute-start.2 = (bf16[32,8192]{1,0:T(8,128)(2,1)S(1)}, bf16[32,8192]{1,0:T(8,128)(2,1)S(1)}, u32[]{:S(2)}, u32[]{:S(2)}) collective-permute-start(bf16[32,8192]{1,0:T(8,128)(2,1)S(1)} %get-tuple-element.68), channel_id=1, source_target_pairs={{0,1},{2,3},{4,5},{6,7},{8,9},{10,11},{12,13},{14,15},{16,17},{18,... | collective-permute-start | bytes 1572872 | tf_op jit(solution)/shard_map/ppermute | solution.py:44
  24.5 3.5 %shard_map.105.hidden = bf16[64,8192]{1,0:T(8,128)(2,1)S(1)} custom-call(bf16[32,512]{1,0:T(8,128)(2,1)} %bitcast.38, bf16[8192,512]{1,0:T(8,128)(2,1)S(1)} %shard_map.101.down), custom_call_target="tpu_custom_call" | custom-call | flops 536870912 | bytes 8388608 | tf_op jit(solution)/shard_map/pallas_call | solution.py:67
  31.5 2.7 %fusion.5 = (bf16[64,512]{1,0:T(8,128)(2,1)S(1)}, f32[64,512]{1,0:T(8,128)S(1)}) fusion(f32[512]{0:T(512)S(1)} %convert_bitcast_fusion, bf16[64,8192]{1,0:T(8,128)(2,1)S(1)} %get-tuple-element.81, bf16[1,512,8192]{2,1,0:T(8,128)(2,1)S(1)} %bitcast.33), kind=kOutput, calls=%fused_computation.12 | convolution fusion | flops 536936448 | bytes 9635840 | tf_op jit(solution)/shard_map/dot_general | solution.py:28
  34.2 7.7 %collective-permute-start.10 = (bf16[64,512]{1,0:T(8,128)(2,1)S(1)}, bf16[64,512]{1,0:T(8,128)(2,1)S(1)}, u32[]{:S(2)}, u32[]{:S(2)}) collective-permute-start(bf16[64,512]{1,0:T(8,128)(2,1)S(1)} %get-tuple-element.100.refs_2_), channel_id=1, source_target_pairs={{0,6},{1,7},{8,14},{9,15},{16,22},{17,23},{24,30},{25,31}} | collective-permute-start | bytes 196616 | tf_op jit(solution)/shard_map/ppermute | solution.py:44
  43.2 2.7 %collective-permute-start.9 = (bf16[64,512]{1,0:T(8,128)(2,1)S(1)}, bf16[64,512]{1,0:T(8,128)(2,1)S(1)}, u32[]{:S(2)}, u32[]{:S(2)}) collective-permute-start(bf16[64,512]{1,0:T(8,128)(2,1)S(1)} %get-tuple-element.100.refs_2_), channel_id=1, source_target_pairs={{0,4},{1,5},{2,6},{3,7},{8,12},{9,13},{10,14},{11,15},{16,20},{17,... | collective-permute-start | bytes 196616 | tf_op jit(solution)/shard_map/ppermute | solution.py:44
  46.0 3.1 %shard_map.108 = (bf16[32,512]{1,0:T(8,128)(2,1)S(1)}, bf16[32,8192]{1,0:T(8,128)(2,1)S(1)}) custom-call(bf16[32,8192]{1,0:T(8,128)(2,1)S(1)} %collective-permute-done.6.arrived, bf16[32,512]{1,0:T(8,128)(2,1)S(1)} %broadcast_in_dim.12.before, bf16[8192,512]{1,0:T(8,128)(2,1)S(1)} %shard_map.101.down, bf16[512,8192]{1,0:T(8,128)(2,1)S(1)} %get-tuple-element.64.expand), custom_call_target="tpu_custom_call" | custom-call | flops 268435456 | bytes 8388608 | tf_op jit(solution)/shard_map/pallas_call | solution.py:67
  50.4 2.7 %fusion.6.right = f32[64,512]{1,0:T(8,128)S(1)} fusion(bf16[64,8192]{1,0:T(8,128)(2,1)S(1)} %get-tuple-element.84, bf16[512,8192]{1,0:T(8,128)(2,1)S(1)} %bitcast.29), kind=kOutput, calls=%fused_computation.13 | convolution fusion | flops 536870912 | bytes 9568256 | tf_op jit(solution)/shard_map/dot_general | solution.py:28
  53.9 1.6 %collective-permute-start.12 = (bf16[80,512]{1,0:T(8,128)(2,1)S(1)}, bf16[80,512]{1,0:T(8,128)(2,1)S(1)}, u32[]{:S(2)}, u32[]{:S(2)}) collective-permute-start(bf16[80,512]{1,0:T(8,128)(2,1)S(1)} %pad_maximum_fusion.2.refs_6_), channel_id=1, source_target_pairs={{0,8},{8,0},{16,24},{24,16},{1,9},{9,1},{17,25},{25,17},{2,10},{10... | collective-permute-start | bytes 245768 | tf_op jit(solution)/shard_map/ppermute | solution.py:35
  55.4 1.5 %collective-permute-start.13 = (bf16[80,512]{1,0:T(8,128)(2,1)S(1)}, bf16[80,512]{1,0:T(8,128)(2,1)S(1)}, u32[]{:S(2)}, u32[]{:S(2)}) collective-permute-start(bf16[80,512]{1,0:T(8,128)(2,1)S(1)} %pad_maximum_fusion.2.refs_6_), channel_id=1, source_target_pairs={{0,16},{8,24},{16,0},{24,8},{1,17},{9,25},{17,1},{25,9},{2,18},{10... | collective-permute-start | bytes 245768 | tf_op jit(solution)/shard_map/ppermute | solution.py:35
  57.4 4.2 %shard_map.110.refs_1_ = bf16[192,512]{1,0:T(8,128)(2,1)S(1)} custom-call(bf16[512,8192]{1,0:T(8,128)(2,1)} %cotangent.1, bf16[512,8192]{1,0:T(8,128)(2,1)S(1)} %get-tuple-element.64.expand), custom_call_target="tpu_custom_call" | custom-call | flops 1610612736 | bytes 8388608 | tf_op jit(solution)/shard_map/pallas_call | solution.py:67
  62.3 3.1 %shard_map.111 = (bf16[32,512]{1,0:T(8,128)(2,1)S(1)}, bf16[32,8192]{1,0:T(8,128)(2,1)S(1)}) custom-call(bf16[32,8192]{1,0:T(8,128)(2,1)S(1)} %collective-permute-done.11.arrived, bf16[32,512]{1,0:T(8,128)(2,1)S(1)} %broadcast_in_dim.12.before, bf16[8192,512]{1,0:T(8,128)(2,1)S(1)} %shard_map.101.down, bf16[512,8192]{1,0:T(8,128)(2,1)S(1)} %get-tuple-element.64.expand), custom_call_target="tpu_custom_call" | custom-call | flops 268435456 | bytes 8388608 | tf_op jit(solution)/shard_map/pallas_call | solution.py:67
  66.8 1.7 %collective-permute-done.16.others = bf16[4,64,512]{2,1,0:T(8,128)(2,1)S(1)} collective-permute-done((bf16[4,64,512]{2,1,0:T(8,128)(2,1)S(1)}, bf16[4,64,512]{2,1,0:T(8,128)(2,1)S(1)}, u32[]{:S(2)}, u32[]{:S(2)}) %collective-permute-start.16) | collective-permute-done | bytes 262176 | tf_op jit(solution)/shard_map/ppermute | solution.py:35
  68.6 1.4 %collective-permute-start.17 = (bf16[32,512]{1,0:T(8,128)(2,1)S(1)}, bf16[32,512]{1,0:T(8,128)(2,1)S(1)}, u32[]{:S(2)}, u32[]{:S(2)}) collective-permute-start(bf16[32,512]{1,0:T(8,128)(2,1)S(1)} %shard_map.112.refs_2_), channel_id=1, source_target_pairs={{0,8},{8,0},{16,24},{24,16},{1,9},{9,1},{17,25},{25,17},{2,10},{10... | collective-permute-start | bytes 98312 | tf_op jit(solution)/shard_map/ppermute | solution.py:35
  73.9 2.1 %collective-permute-done.19.refs_5_ = bf16[32,512]{1,0:T(8,128)(2,1)S(1)} collective-permute-done((bf16[32,512]{1,0:T(8,128)(2,1)S(1)}, bf16[32,512]{1,0:T(8,128)(2,1)S(1)}, u32[]{:S(2)}, u32[]{:S(2)}) %collective-permute-start.19) | collective-permute-done | bytes 32800 | tf_op jit(solution)/shard_map/ppermute | solution.py:35
  77.9 3.2 %collective-permute-start.21 = (f32[8,64]{1,0:T(8,128)S(1)}, f32[8,64]{1,0:T(8,128)S(1)}, u32[]{:S(2)}, u32[]{:S(2)}) collective-permute-start(f32[8,64]{1,0:T(8,128)S(1)} %add.3.refs_0_), channel_id=1, source_target_pairs={{0,2},{1,3},{2,4},{3,5},{4,6},{5,7},{6,0},{7,1},{8,10},{9,11},{10,... | collective-permute-start | bytes 6152 | tf_op jit(solution)/shard_map/ppermute | solution.py:51
  81.0 2.4 %collective-permute-start.23 = (f32[8,64]{1,0:T(8,128)S(1)}, f32[8,64]{1,0:T(8,128)S(1)}, u32[]{:S(2)}, u32[]{:S(2)}) collective-permute-start(f32[8,64]{1,0:T(8,128)S(1)} %add.3.refs_0_), channel_id=1, source_target_pairs={{0,6},{1,7},{2,0},{3,1},{4,2},{5,3},{6,4},{7,5},{8,14},{9,15},{10,... | collective-permute-start | bytes 6152 | tf_op jit(solution)/shard_map/ppermute | solution.py:51
  83.4 2.1 %collective-permute-done.22.refs_2_ = f32[8,64]{1,0:T(8,128)S(1)} collective-permute-done((f32[8,64]{1,0:T(8,128)S(1)}, f32[8,64]{1,0:T(8,128)S(1)}, u32[]{:S(2)}, u32[]{:S(2)}) %collective-permute-start.22) | collective-permute-done | bytes 2080 | tf_op jit(solution)/shard_map/ppermute | solution.py:51
  (71 shorter events, 16.9 us)
Async XLA Ops:
  4.6 5.9 %collective-permute-start = (bf16[16,8192]{1,0:T(8,128)(2,1)S(1)}, bf16[16,8192]{1,0:T(8,128)(2,1)S(1)}, u32[]{:S(2)}, u32[]{:S(2)}) collective-permute-start(bf16[16,8192]{1,0:T(8,128)(2,1)S(1)} %get-tuple-element.60), channel_id=1, source_target_pairs={{0,1},{2,3},{4,5},{6,7},{8,9},{10,11},{12,13},{14,15},{16,17},{18,... | collective-permute-start | bytes 786440 | tf_op jit(solution)/shard_map/ppermute | solution.py:44
  10.6 9.3 %collective-permute-start.1 = (bf16[32,8192]{1,0:T(8,128)(2,1)S(1)}, bf16[32,8192]{1,0:T(8,128)(2,1)S(1)}, u32[]{:S(2)}, u32[]{:S(2)}) collective-permute-start(bf16[32,8192]{1,0:T(8,128)(2,1)S(1)} %constant_dynamic-update-slice_fusion), channel_id=1, source_target_pairs={{1,2},{3,4},{5,6},{9,10},{11,12},{13,14},{17,18},{19,20},{21,22},{... | collective-permute-start | bytes 1572872 | tf_op jit(solution)/shard_map/ppermute | solution.py:44
  11.5 16.5 %collective-permute-start.3 = (bf16[16,8192]{1,0:T(8,128)(2,1)S(1)}, bf16[16,8192]{1,0:T(8,128)(2,1)S(1)}, u32[]{:S(2)}, u32[]{:S(2)}) collective-permute-start(bf16[16,8192]{1,0:T(8,128)(2,1)S(1)} %constant_dynamic-update-slice_fusion.2), channel_id=1, source_target_pairs={{0,8},{8,0},{16,24},{24,16},{1,9},{9,1},{17,25},{25,17},{2,10},{10... | collective-permute-start | bytes 786440 | tf_op jit(solution)/shard_map/ppermute | solution.py:35
  13.9 14.1 %collective-permute-start.4 = (bf16[16,8192]{1,0:T(8,128)(2,1)S(1)}, bf16[16,8192]{1,0:T(8,128)(2,1)S(1)}, u32[]{:S(2)}, u32[]{:S(2)}) collective-permute-start(bf16[16,8192]{1,0:T(8,128)(2,1)S(1)} %constant_dynamic-update-slice_fusion.2), channel_id=1, source_target_pairs={{0,16},{8,24},{16,0},{24,8},{1,17},{9,25},{17,1},{25,9},{2,18},{10... | collective-permute-start | bytes 786440 | tf_op jit(solution)/shard_map/ppermute | solution.py:35
  15.4 12.6 %collective-permute-start.5 = (bf16[16,8192]{1,0:T(8,128)(2,1)S(1)}, bf16[16,8192]{1,0:T(8,128)(2,1)S(1)}, u32[]{:S(2)}, u32[]{:S(2)}) collective-permute-start(bf16[16,8192]{1,0:T(8,128)(2,1)S(1)} %constant_dynamic-update-slice_fusion.2), channel_id=1, source_target_pairs={{0,24},{8,16},{16,8},{24,0},{1,25},{9,17},{17,9},{25,1},{2,26},{10... | collective-permute-start | bytes 786440 | tf_op jit(solution)/shard_map/ppermute | solution.py:35
  23.1 5.0 %collective-permute-start.2 = (bf16[32,8192]{1,0:T(8,128)(2,1)S(1)}, bf16[32,8192]{1,0:T(8,128)(2,1)S(1)}, u32[]{:S(2)}, u32[]{:S(2)}) collective-permute-start(bf16[32,8192]{1,0:T(8,128)(2,1)S(1)} %get-tuple-element.68), channel_id=1, source_target_pairs={{0,1},{2,3},{4,5},{6,7},{8,9},{10,11},{12,13},{14,15},{16,17},{18,... | collective-permute-start | bytes 1572872 | tf_op jit(solution)/shard_map/ppermute | solution.py:44
  28.1 17.8 %collective-permute-start.6 = (bf16[32,8192]{1,0:T(8,128)(2,1)S(1)}, bf16[32,8192]{1,0:T(8,128)(2,1)S(1)}, u32[]{:S(2)}, u32[]{:S(2)}) collective-permute-start(bf16[32,8192]{1,0:T(8,128)(2,1)S(1)} %get-tuple-element.78), channel_id=1, source_target_pairs={{1,2},{3,4},{5,6},{9,10},{11,12},{13,14},{17,18},{19,20},{21,22},{... | collective-permute-start | bytes 1572872 | tf_op jit(solution)/shard_map/ppermute | solution.py:44
  34.2 18.9 %collective-permute-start.10 = (bf16[64,512]{1,0:T(8,128)(2,1)S(1)}, bf16[64,512]{1,0:T(8,128)(2,1)S(1)}, u32[]{:S(2)}, u32[]{:S(2)}) collective-permute-start(bf16[64,512]{1,0:T(8,128)(2,1)S(1)} %get-tuple-element.100.refs_2_), channel_id=1, source_target_pairs={{0,6},{1,7},{8,14},{9,15},{16,22},{17,23},{24,30},{25,31}} | collective-permute-start | bytes 196616 | tf_op jit(solution)/shard_map/ppermute | solution.py:44
  41.9 11.2 %collective-permute-start.8 = (bf16[64,512]{1,0:T(8,128)(2,1)S(1)}, bf16[64,512]{1,0:T(8,128)(2,1)S(1)}, u32[]{:S(2)}, u32[]{:S(2)}) collective-permute-start(bf16[64,512]{1,0:T(8,128)(2,1)S(1)} %get-tuple-element.100.refs_2_), channel_id=1, source_target_pairs={{0,2},{1,3},{2,4},{3,5},{4,6},{5,7},{8,10},{9,11},{10,12},{11,13},... | collective-permute-start | bytes 196616 | tf_op jit(solution)/shard_map/ppermute | solution.py:44
  43.2 9.9 %collective-permute-start.9 = (bf16[64,512]{1,0:T(8,128)(2,1)S(1)}, bf16[64,512]{1,0:T(8,128)(2,1)S(1)}, u32[]{:S(2)}, u32[]{:S(2)}) collective-permute-start(bf16[64,512]{1,0:T(8,128)(2,1)S(1)} %get-tuple-element.100.refs_2_), channel_id=1, source_target_pairs={{0,4},{1,5},{2,6},{3,7},{8,12},{9,13},{10,14},{11,15},{16,20},{17,... | collective-permute-start | bytes 196616 | tf_op jit(solution)/shard_map/ppermute | solution.py:44
  49.1 4.0 %collective-permute-start.7 = (bf16[32,8192]{1,0:T(8,128)(2,1)S(1)}, bf16[32,8192]{1,0:T(8,128)(2,1)S(1)}, u32[]{:S(2)}, u32[]{:S(2)}) collective-permute-start(bf16[32,8192]{1,0:T(8,128)(2,1)S(1)} %get-tuple-element.83), channel_id=1, source_target_pairs={{0,1},{2,3},{4,5},{6,7},{8,9},{10,11},{12,13},{14,15},{16,17},{18,... | collective-permute-start | bytes 1572872 | tf_op jit(solution)/shard_map/ppermute | solution.py:44
  53.2 9.1 %collective-permute-start.11 = (bf16[32,8192]{1,0:T(8,128)(2,1)S(1)}, bf16[32,8192]{1,0:T(8,128)(2,1)S(1)}, u32[]{:S(2)}, u32[]{:S(2)}) collective-permute-start(bf16[32,8192]{1,0:T(8,128)(2,1)S(1)} %get-tuple-element.89), channel_id=1, source_target_pairs={{1,2},{3,4},{5,6},{9,10},{11,12},{13,14},{17,18},{19,20},{21,22},{... | collective-permute-start | bytes 1572872 | tf_op jit(solution)/shard_map/ppermute | solution.py:44
  53.9 7.8 %collective-permute-start.12 = (bf16[80,512]{1,0:T(8,128)(2,1)S(1)}, bf16[80,512]{1,0:T(8,128)(2,1)S(1)}, u32[]{:S(2)}, u32[]{:S(2)}) collective-permute-start(bf16[80,512]{1,0:T(8,128)(2,1)S(1)} %pad_maximum_fusion.2.refs_6_), channel_id=1, source_target_pairs={{0,8},{8,0},{16,24},{24,16},{1,9},{9,1},{17,25},{25,17},{2,10},{10... | collective-permute-start | bytes 245768 | tf_op jit(solution)/shard_map/ppermute | solution.py:35
  55.4 6.2 %collective-permute-start.13 = (bf16[80,512]{1,0:T(8,128)(2,1)S(1)}, bf16[80,512]{1,0:T(8,128)(2,1)S(1)}, u32[]{:S(2)}, u32[]{:S(2)}) collective-permute-start(bf16[80,512]{1,0:T(8,128)(2,1)S(1)} %pad_maximum_fusion.2.refs_6_), channel_id=1, source_target_pairs={{0,16},{8,24},{16,0},{24,8},{1,17},{9,25},{17,1},{25,9},{2,18},{10... | collective-permute-start | bytes 245768 | tf_op jit(solution)/shard_map/ppermute | solution.py:35
  57.0 5.4 %collective-permute-start.14 = (bf16[80,512]{1,0:T(8,128)(2,1)S(1)}, bf16[80,512]{1,0:T(8,128)(2,1)S(1)}, u32[]{:S(2)}, u32[]{:S(2)}) collective-permute-start(bf16[80,512]{1,0:T(8,128)(2,1)S(1)} %pad_maximum_fusion.2.refs_6_), channel_id=1, source_target_pairs={{0,24},{8,16},{16,8},{24,0},{1,25},{9,17},{17,9},{25,1},{2,26},{10... | collective-permute-start | bytes 245768 | tf_op jit(solution)/shard_map/ppermute | solution.py:35
  65.4 3.2 %collective-permute-start.15 = (bf16[32,8192]{1,0:T(8,128)(2,1)S(1)}, bf16[32,8192]{1,0:T(8,128)(2,1)S(1)}, u32[]{:S(2)}, u32[]{:S(2)}) collective-permute-start(bf16[32,8192]{1,0:T(8,128)(2,1)S(1)} %get-tuple-element.96), channel_id=1, source_target_pairs={{0,1},{2,3},{4,5},{6,7},{8,9},{10,11},{12,13},{14,15},{16,17},{18,... | collective-permute-start | bytes 1572872 | tf_op jit(solution)/shard_map/ppermute | solution.py:44
  66.8 1.8 %collective-permute-start.16 = (bf16[4,64,512]{2,1,0:T(8,128)(2,1)S(1)}, bf16[4,64,512]{2,1,0:T(8,128)(2,1)S(1)}, u32[]{:S(2)}, u32[]{:S(2)}) collective-permute-start(bf16[4,64,512]{2,1,0:T(8,128)(2,1)S(1)} %pad_maximum_fusion.1), channel_id=1, source_target_pairs={{0,1},{1,0},{2,3},{3,2},{4,5},{5,4},{6,7},{7,6},{8,9},{9,8},{10,11... | collective-permute-start | bytes 786440 | tf_op jit(solution)/shard_map/ppermute | solution.py:35
  68.6 4.7 %collective-permute-start.17 = (bf16[32,512]{1,0:T(8,128)(2,1)S(1)}, bf16[32,512]{1,0:T(8,128)(2,1)S(1)}, u32[]{:S(2)}, u32[]{:S(2)}) collective-permute-start(bf16[32,512]{1,0:T(8,128)(2,1)S(1)} %shard_map.112.refs_2_), channel_id=1, source_target_pairs={{0,8},{8,0},{16,24},{24,16},{1,9},{9,1},{17,25},{25,17},{2,10},{10... | collective-permute-start | bytes 98312 | tf_op jit(solution)/shard_map/ppermute | solution.py:35
  70.0 3.9 %collective-permute-start.18 = (bf16[32,512]{1,0:T(8,128)(2,1)S(1)}, bf16[32,512]{1,0:T(8,128)(2,1)S(1)}, u32[]{:S(2)}, u32[]{:S(2)}) collective-permute-start(bf16[32,512]{1,0:T(8,128)(2,1)S(1)} %shard_map.112.refs_2_), channel_id=1, source_target_pairs={{0,16},{8,24},{16,0},{24,8},{1,17},{9,25},{17,1},{25,9},{2,18},{10... | collective-permute-start | bytes 98312 | tf_op jit(solution)/shard_map/ppermute | solution.py:35
  71.2 4.8 %collective-permute-start.19 = (bf16[32,512]{1,0:T(8,128)(2,1)S(1)}, bf16[32,512]{1,0:T(8,128)(2,1)S(1)}, u32[]{:S(2)}, u32[]{:S(2)}) collective-permute-start(bf16[32,512]{1,0:T(8,128)(2,1)S(1)} %shard_map.112.refs_2_), channel_id=1, source_target_pairs={{0,24},{8,16},{16,8},{24,0},{1,25},{9,17},{17,9},{25,1},{2,26},{10... | collective-permute-start | bytes 98312 | tf_op jit(solution)/shard_map/ppermute | solution.py:35
  76.7 1.2 %collective-permute-start.20 = (f32[8,64]{1,0:T(8,128)S(1)}, f32[8,64]{1,0:T(8,128)S(1)}, u32[]{:S(2)}, u32[]{:S(2)}) collective-permute-start(f32[8,64]{1,0:T(8,128)S(1)} %shard_map.114), channel_id=1, source_target_pairs={{0,1},{1,0},{2,3},{3,2},{4,5},{5,4},{6,7},{7,6},{8,9},{9,8},{10,11... | collective-permute-start | bytes 6152 | tf_op jit(solution)/shard_map/ppermute | solution.py:35
  77.9 5.5 %collective-permute-start.21 = (f32[8,64]{1,0:T(8,128)S(1)}, f32[8,64]{1,0:T(8,128)S(1)}, u32[]{:S(2)}, u32[]{:S(2)}) collective-permute-start(f32[8,64]{1,0:T(8,128)S(1)} %add.3.refs_0_), channel_id=1, source_target_pairs={{0,2},{1,3},{2,4},{3,5},{4,6},{5,7},{6,0},{7,1},{8,10},{9,11},{10,... | collective-permute-start | bytes 6152 | tf_op jit(solution)/shard_map/ppermute | solution.py:51
  81.0 4.5 %collective-permute-start.22 = (f32[8,64]{1,0:T(8,128)S(1)}, f32[8,64]{1,0:T(8,128)S(1)}, u32[]{:S(2)}, u32[]{:S(2)}) collective-permute-start(f32[8,64]{1,0:T(8,128)S(1)} %add.3.refs_0_), channel_id=1, source_target_pairs={{0,4},{1,5},{2,6},{3,7},{4,0},{5,1},{6,2},{7,3},{8,12},{9,13},{10,... | collective-permute-start | bytes 6152 | tf_op jit(solution)/shard_map/ppermute | solution.py:51
  81.0 4.5 %collective-permute-start.23 = (f32[8,64]{1,0:T(8,128)S(1)}, f32[8,64]{1,0:T(8,128)S(1)}, u32[]{:S(2)}, u32[]{:S(2)}) collective-permute-start(f32[8,64]{1,0:T(8,128)S(1)} %add.3.refs_0_), channel_id=1, source_target_pairs={{0,6},{1,7},{2,0},{3,1},{4,2},{5,3},{6,4},{7,5},{8,14},{9,15},{10,... | collective-permute-start | bytes 6152 | tf_op jit(solution)/shard_map/ppermute | solution.py:51
  (8 other events, 63.6 us)

commit v10 on v9

--- a/solution.py
+++ b/solution.py
@@ -36,7 +36,8 @@
 
 
 def spread(value, axis):
-    return [value] + [swap(value, axis, d) for d in range(1, lax.axis_size(axis))]
+    far = [swap(value, axis, d) for d in reversed(range(1, lax.axis_size(axis)))]
+    return [value] + far[::-1]
 
 
 def upward(value, first, hop, stride):
@@ -103,13 +104,14 @@
 
 
 def prime_kernel(
-    cols_hbm, values_hbm, expand, kept, raised, own, cols, values, few, sems
+    cols_hbm, values_hbm, expand, down, kept, head, raised, own, cols, values, few, sems
 ):
     step = expand.shape[1] // PARTS
     small = fetch([(cols_hbm, cols), (values_hbm, values)], few)
     begin(small)
     spans = [pl.ds(part * step, step) for part in range(PARTS)]
-    copies = fetch([(expand.at[:, span], kept.at[:, span]) for span in spans], sems)
+    pairs = [(expand.at[:, span], kept.at[:, span]) for span in spans]
+    copies = fetch(pairs + [(down.at[pl.ds(0, head.shape[0])], head)], sems)
     begin(copies)
     rows = own.shape[0]
     q_dev = rows // 2
@@ -124,16 +126,24 @@
         raised[:, span] = found.astype(bf16)
         above = jnp.concatenate([values[:, span].astype(f32), found[q_dev:rows]])
         own[:, span] = above.astype(bf16)
-
-
-def keep_kernel(down, kept, sem):
-    copy = pltpu.make_async_copy(down, kept, sem)
+    arrive(copies, PARTS)
+
+
+def keep_kernel(down, rest, sem):
+    count = rest.shape[0]
+    copy = pltpu.make_async_copy(down.at[pl.ds(down.shape[0] - count, count)], rest, sem)
     copy.start()
     copy.wait()
 
 
-def hidden_kernel(q_dev, cols_hbm, down, raised, cols, few):
-    step = down.shape[0] // PARTS
+def down_rows(head, rest, at, count):
+    if at < head.shape[0]:
+        return head[at : at + count, :]
+    return rest[at - head.shape[0] : at - head.shape[0] + count, :]
+
+
+def hidden_kernel(q_dev, cols_hbm, head, rest, raised, cols, few):
+    step = raised.shape[1] // PARTS
     small = fetch([(cols_hbm, cols)], few)
     begin(small)
     laid = picks((raised.shape[0], cols.shape[0]), q_dev, 0).astype(bf16)
@@ -141,12 +151,12 @@
     laid = dot_nn(laid, cols[...]).astype(bf16)
     for part in range(PARTS):
         span = slice(part * step, (part + 1) * step)
-        raised[:, span] = (adapter_scale * dot_nt(laid, down[span, :])).astype(bf16)
-
-
-def through_kernel(turn, arrived, before, down, expand, ranks, leaving):
-    depth, width = down.shape
-    step = 2 * width
+        raised[:, span] = (adapter_scale * dot_nt(laid, down_rows(head, rest, part * step, step))).astype(bf16)
+
+
+def through_kernel(turn, arrived, before, head, rest, expand, ranks, leaving):
+    depth = arrived.shape[1]
+    step = 2 * ranks.shape[1]
     mine = lax.axis_index("pipe") % 2 == turn
 
     @pl.when(jnp.logical_not(mine))
@@ -157,7 +167,7 @@
     def _():
         total = jnp.zeros(ranks.shape, f32)
         for at in range(0, depth, step):
-            total += dot_nn(arrived[:, at : at + step], down[at : at + step, :])
+            total += dot_nn(arrived[:, at : at + step], down_rows(head, rest, at, step))
         found = total.astype(bf16)
         ranks[...] = found
         for at in range(0, depth, step):
@@ -165,9 +175,9 @@
             leaving[:, at : at + step] = (arrived[:, at : at + step].astype(f32) + more).astype(bf16)
 
 
-def last_kernel(arrived, before, down, ranks):
-    depth, width = down.shape
-    step = 2 * width
+def last_kernel(arrived, before, head, rest, ranks):
+    depth = arrived.shape[1]
+    step = 2 * ranks.shape[1]
     mine = lax.axis_index("pipe") % 2 == 1
 
     @pl.when(jnp.logical_not(mine))
@@ -178,7 +188,7 @@
     def _():
         total = jnp.zeros(ranks.shape, f32)
         for at in range(0, depth, step):
-            total += dot_nn(arrived[:, at : at + step], down[at : at + step, :])
+            total += dot_nn(arrived[:, at : at + step], down_rows(head, rest, at, step))
         ranks[...] = total.astype(bf16)
 
 
@@ -299,23 +309,29 @@
     def through(turn, arrived, before):
         return call(
             functools.partial(through_kernel, turn),
-            (arrived, before, down, expand),
-            "vvvv",
+            (arrived, before, *down, expand),
+            "vvvvv",
             [(before.shape, bf16), (arrived.shape, bf16)],
             flops=2 * pass_flops,
             moved=weight_bytes,
         )
 
-    expand, raised, own = call(
+    head = width // PARTS
+    expand, first, raised, own = call(
         prime_kernel,
-        (inner_cols[0], value_rows[0], adapter_expand[0]),
-        "hhh",
-        [((rank, width), bf16), ((count, width), bf16), ((rows, width), bf16)],
+        (inner_cols[0], value_rows[0], adapter_expand[0], adapter_down[0]),
+        "hhhh",
+        [
+            ((rank, width), bf16),
+            ((head, rank), bf16),
+            ((count, width), bf16),
+            ((rows, width), bf16),
+        ],
         [
             VMEM(inner_cols.shape[1:], bf16),
             VMEM((q_dev, width), bf16),
             pltpu.SemaphoreType.DMA((2,)),
-            pltpu.SemaphoreType.DMA((PARTS,)),
+            pltpu.SemaphoreType.DMA((PARTS + 1,)),
         ],
         flops=pass_flops,
         moved=2 * weight_bytes,
@@ -323,15 +339,16 @@
 
     arrived = upward(own, 0, 1, 2)
     (source,) = tie([adapter_down[0]], own)
-    (down,) = call(
+    (rest,) = call(
         keep_kernel,
         (source,),
         "h",
-        [((width, rank), bf16)],
+        [((width - head, rank), bf16)],
         [pltpu.SemaphoreType.DMA],
         moved=2 * weight_bytes,
     )
-    arrived, down = lax.optimization_barrier((arrived, down))
+    arrived, rest = lax.optimization_barrier((arrived, rest))
+    down = (first, rest)
     lower_ranks, leaving = through(1, arrived, jnp.zeros((rows, rank), bf16))
     moving = jnp.concatenate([leaving, own])
 
@@ -368,8 +385,8 @@
             (hid,) = tie([hidden_cols[0]], leaving)
             (hidden,) = call(
                 functools.partial(hidden_kernel, q_dev),
-                (hid, down),
-                "hv",
+                (hid, *down),
+                "hvv",
                 [((count, width), bf16)],
                 [VMEM(hidden_cols.shape[1:], bf16), pltpu.SemaphoreType.DMA((1,))],
                 flops=2 * count * width * rank,
@@ -409,8 +426,8 @@
 
     (late,) = call(
         last_kernel,
-        (arrived, found, down),
-        "vvv",
+        (arrived, found, *down),
+        "vvvv",
         [((2 * rows, rank), bf16)],
         flops=pass_flops,
         moved=weight_bytes,

time: 86.7 us -> 86.2 us (level)
  transfers between devices with their start and end apart: 24 -> 24, of which waited for: 6 -> 6; matrix products, arithmetic and copies ran while one was open for 6% -> 6% of each run, Pallas kernels for 27% -> 26%
where the time goes in v10:
time: 86.2 us; the launch traced here: 85.8 us
  starting transfers between devices  37.5 us (44%)
  Pallas kernels  31.7 us (37%)
  waiting for transfers between devices  8.27 us (10%)
  matrix products  5.32 us (6%)
  local copies, waits for them, and re-layouts  2.3 us (3%)
    pallas_call x16, Pallas kernels, call(): pl.pallas_call(kernel, in_specs=[pl.BlockSpec(memory_space=space[place])...  31.7 us
    ppermute x10, starting transfers between devices, upward(): lax.ppermute(value, 'pipe', [(source, source + hop) for source in range(f...  20.7 us
    ppermute x11, starting transfers between devices, swap(): lax.ppermute(value, axis, [(source, source ^ distance) for source in rang...  11.3 us
    ppermute x11, waiting for transfers between devices, swap(): lax.ppermute(value, axis, [(source, source ^ distance) for source in rang...  6.1 us
    ppermute x3, starting transfers between devices, around(): lax.ppermute(value, 'pipe', [(source, (source + 2 * hop) % count) for sou...  5.53 us
    dot_general x2, matrix products, dot_nt(): lax.dot_general(a, b, (((1,), (1,)), ((), ())), preferred_element_type=f3...  5.32 us
    unnamed x18, local copies, waits for them, and re-layouts  2.26 us
    ppermute x3, waiting for transfers between devices, around(): lax.ppermute(value, 'pipe', [(source, (source + 2 * hop) % count) for sou...  2.14 us
  transfers between devices with their start and end apart: 24, of which 6 were waited for; matrix products, arithmetic and copies ran while one was open for 6% of the time, Pallas kernels for 26%

profile of v10, /device:TPU:0, one launch (start us, length us, event | category | flops | bytes accessed | tf_op | source)
XLA Modules:
  0.0 85.8 jit_solution(17073720397301390197)
XLA Ops:
  0.0 4.7 %shard_map.100 = (bf16[512,8192]{1,0:T(8,128)(2,1)S(1)}, bf16[2048,512]{1,0:T(8,128)(2,1)S(1)}, bf16[64,8192]{1,0:T(8,128)(2,1)S(1)}, bf16[16,8192]{1,0:T(8,128)(2,1)S(1)}) custom-call(bf16[32,512]{1,0:T(8,128)(2,1)} %bitcast.38, bf16[8,8192]{1,0:T(8,128)(2,1)} %bitcast.35, bf16[512,8192]{1,0:T(8,128)(2,1)} %bitcast.32, bf16[8192,512]{1,0:T(8,128)(2,1)} %bitcast.30), custom_call_target="tpu_custom_call" | custom-call | flops 134217728 | bytes 16777216 | tf_op jit(solution)/shard_map/pallas_call | solution.py:68
  4.8 2.4 %collective-permute-start = (bf16[16,8192]{1,0:T(8,128)(2,1)S(1)}, bf16[16,8192]{1,0:T(8,128)(2,1)S(1)}, u32[]{:S(2)}, u32[]{:S(2)}) collective-permute-start(bf16[16,8192]{1,0:T(8,128)(2,1)S(1)} %get-tuple-element.61), channel_id=1, source_target_pairs={{0,1},{2,3},{4,5},{6,7},{8,9},{10,11},{12,13},{14,15},{16,17},{18,... | collective-permute-start | bytes 786440 | tf_op jit(solution)/shard_map/ppermute | solution.py:45
  7.1 2.8 %shard_map.101.rest = bf16[6144,512]{1,0:T(8,128)(2,1)S(1)} custom-call(bf16[8192,512]{1,0:T(8,128)(2,1)} %bitcast.31), custom_call_target="tpu_custom_call" | custom-call | bytes 16777216 | tf_op jit(solution)/shard_map/pallas_call | solution.py:68
  11.0 2.4 %collective-permute-start.3 = (bf16[16,8192]{1,0:T(8,128)(2,1)S(1)}, bf16[16,8192]{1,0:T(8,128)(2,1)S(1)}, u32[]{:S(2)}, u32[]{:S(2)}) collective-permute-start(bf16[16,8192]{1,0:T(8,128)(2,1)S(1)} %constant_dynamic-update-slice_fusion.2), channel_id=1, source_target_pairs={{0,8},{8,0},{16,24},{24,16},{1,9},{9,1},{17,25},{25,17},{2,10},{10... | collective-permute-start | bytes 786440 | tf_op jit(solution)/shard_map/ppermute | solution.py:35
  13.4 1.5 %collective-permute-start.4 = (bf16[16,8192]{1,0:T(8,128)(2,1)S(1)}, bf16[16,8192]{1,0:T(8,128)(2,1)S(1)}, u32[]{:S(2)}, u32[]{:S(2)}) collective-permute-start(bf16[16,8192]{1,0:T(8,128)(2,1)S(1)} %constant_dynamic-update-slice_fusion.2), channel_id=1, source_target_pairs={{0,16},{8,24},{16,0},{24,8},{1,17},{9,25},{17,1},{25,9},{2,18},{10... | collective-permute-start | bytes 786440 | tf_op jit(solution)/shard_map/ppermute | solution.py:35
  15.0 4.5 %shard_map.103.refs_0_ = bf16[320,512]{1,0:T(8,128)(2,1)S(1)} custom-call(bf16[512,8192]{1,0:T(8,128)(2,1)} %cotangent.1, bf16[512,8192]{1,0:T(8,128)(2,1)S(1)} %get-tuple-element.66.expand), custom_call_target="tpu_custom_call" | custom-call | flops 2684354560 | bytes 8388608 | tf_op jit(solution)/shard_map/pallas_call | solution.py:68
  19.5 3.1 %shard_map.104 = (bf16[32,512]{1,0:T(8,128)(2,1)S(1)}, bf16[32,8192]{1,0:T(8,128)(2,1)S(1)}) custom-call(bf16[32,8192]{1,0:T(8,128)(2,1)S(1)} %collective-permute-done.1.arrived, bf16[32,512]{1,0:T(8,128)(2,1)S(1)} %broadcast_in_dim.12.before, bf16[2048,512]{1,0:T(8,128)(2,1)S(1)} %get-tuple-element.64.head, bf16[6144,512]{1,0:T(8,128)(2,1)S(1)} %shard_map.101.rest, ...), custom_call_target="tpu_custom_call" | custom-call | flops 268435456 | bytes 8388608 | tf_op jit(solution)/shard_map/pallas_call | solution.py:68
  22.6 1.4 %collective-permute-start.2 = (bf16[32,8192]{1,0:T(8,128)(2,1)S(1)}, bf16[32,8192]{1,0:T(8,128)(2,1)S(1)}, u32[]{:S(2)}, u32[]{:S(2)}) collective-permute-start(bf16[32,8192]{1,0:T(8,128)(2,1)S(1)} %get-tuple-element.70), channel_id=1, source_target_pairs={{0,1},{2,3},{4,5},{6,7},{8,9},{10,11},{12,13},{14,15},{16,17},{18,... | collective-permute-start | bytes 1572872 | tf_op jit(solution)/shard_map/ppermute | solution.py:45
  24.0 3.5 %shard_map.105.hidden = bf16[64,8192]{1,0:T(8,128)(2,1)S(1)} custom-call(bf16[32,512]{1,0:T(8,128)(2,1)} %bitcast.39, bf16[2048,512]{1,0:T(8,128)(2,1)S(1)} %get-tuple-element.64.head, bf16[6144,512]{1,0:T(8,128)(2,1)S(1)} %shard_map.101.rest), custom_call_target="tpu_custom_call" | custom-call | flops 536870912 | bytes 8388608 | tf_op jit(solution)/shard_map/pallas_call | solution.py:68
  31.0 2.7 %fusion.5 = (bf16[64,512]{1,0:T(8,128)(2,1)S(1)}, f32[64,512]{1,0:T(8,128)S(1)}) fusion(f32[512]{0:T(512)S(1)} %convert_bitcast_fusion, bf16[64,8192]{1,0:T(8,128)(2,1)S(1)} %get-tuple-element.83, bf16[1,512,8192]{2,1,0:T(8,128)(2,1)S(1)} %bitcast.34), kind=kOutput, calls=%fused_computation.12 | convolution fusion | flops 536936448 | bytes 9635840 | tf_op jit(solution)/shard_map/dot_general | solution.py:28
  33.7 7.7 %collective-permute-start.10 = (bf16[64,512]{1,0:T(8,128)(2,1)S(1)}, bf16[64,512]{1,0:T(8,128)(2,1)S(1)}, u32[]{:S(2)}, u32[]{:S(2)}) collective-permute-start(bf16[64,512]{1,0:T(8,128)(2,1)S(1)} %get-tuple-element.102.refs_2_), channel_id=1, source_target_pairs={{0,6},{1,7},{8,14},{9,15},{16,22},{17,23},{24,30},{25,31}} | collective-permute-start | bytes 196616 | tf_op jit(solution)/shard_map/ppermute | solution.py:45
  42.8 2.7 %collective-permute-start.9 = (bf16[64,512]{1,0:T(8,128)(2,1)S(1)}, bf16[64,512]{1,0:T(8,128)(2,1)S(1)}, u32[]{:S(2)}, u32[]{:S(2)}) collective-permute-start(bf16[64,512]{1,0:T(8,128)(2,1)S(1)} %get-tuple-element.102.refs_2_), channel_id=1, source_target_pairs={{0,4},{1,5},{2,6},{3,7},{8,12},{9,13},{10,14},{11,15},{16,20},{17,... | collective-permute-start | bytes 196616 | tf_op jit(solution)/shard_map/ppermute | solution.py:45
  45.5 3.1 %shard_map.108 = (bf16[32,512]{1,0:T(8,128)(2,1)S(1)}, bf16[32,8192]{1,0:T(8,128)(2,1)S(1)}) custom-call(bf16[32,8192]{1,0:T(8,128)(2,1)S(1)} %collective-permute-done.6.arrived, bf16[32,512]{1,0:T(8,128)(2,1)S(1)} %broadcast_in_dim.12.before, bf16[2048,512]{1,0:T(8,128)(2,1)S(1)} %get-tuple-element.64.head, bf16[6144,512]{1,0:T(8,128)(2,1)S(1)} %shard_map.101.rest, ...), custom_call_target="tpu_custom_call" | custom-call | flops 268435456 | bytes 8388608 | tf_op jit(solution)/shard_map/pallas_call | solution.py:68
  50.0 2.7 %fusion.6.right = f32[64,512]{1,0:T(8,128)S(1)} fusion(bf16[64,8192]{1,0:T(8,128)(2,1)S(1)} %get-tuple-element.86, bf16[512,8192]{1,0:T(8,128)(2,1)S(1)} %bitcast.29), kind=kOutput, calls=%fused_computation.13 | convolution fusion | flops 536870912 | bytes 9568256 | tf_op jit(solution)/shard_map/dot_general | solution.py:28
  53.4 1.6 %collective-permute-start.12 = (bf16[80,512]{1,0:T(8,128)(2,1)S(1)}, bf16[80,512]{1,0:T(8,128)(2,1)S(1)}, u32[]{:S(2)}, u32[]{:S(2)}) collective-permute-start(bf16[80,512]{1,0:T(8,128)(2,1)S(1)} %pad_maximum_fusion.2.refs_6_), channel_id=1, source_target_pairs={{0,8},{8,0},{16,24},{24,16},{1,9},{9,1},{17,25},{25,17},{2,10},{10... | collective-permute-start | bytes 245768 | tf_op jit(solution)/shard_map/ppermute | solution.py:35
  55.0 1.5 %collective-permute-start.13 = (bf16[80,512]{1,0:T(8,128)(2,1)S(1)}, bf16[80,512]{1,0:T(8,128)(2,1)S(1)}, u32[]{:S(2)}, u32[]{:S(2)}) collective-permute-start(bf16[80,512]{1,0:T(8,128)(2,1)S(1)} %pad_maximum_fusion.2.refs_6_), channel_id=1, source_target_pairs={{0,16},{8,24},{16,0},{24,8},{1,17},{9,25},{17,1},{25,9},{2,18},{10... | collective-permute-start | bytes 245768 | tf_op jit(solution)/shard_map/ppermute | solution.py:35
  57.0 4.2 %shard_map.110.refs_1_ = bf16[192,512]{1,0:T(8,128)(2,1)S(1)} custom-call(bf16[512,8192]{1,0:T(8,128)(2,1)} %cotangent.1, bf16[512,8192]{1,0:T(8,128)(2,1)S(1)} %get-tuple-element.66.expand), custom_call_target="tpu_custom_call" | custom-call | flops 1610612736 | bytes 8388608 | tf_op jit(solution)/shard_map/pallas_call | solution.py:68
  61.8 3.1 %shard_map.111 = (bf16[32,512]{1,0:T(8,128)(2,1)S(1)}, bf16[32,8192]{1,0:T(8,128)(2,1)S(1)}) custom-call(bf16[32,8192]{1,0:T(8,128)(2,1)S(1)} %collective-permute-done.11.arrived, bf16[32,512]{1,0:T(8,128)(2,1)S(1)} %broadcast_in_dim.12.before, bf16[2048,512]{1,0:T(8,128)(2,1)S(1)} %get-tuple-element.64.head, bf16[6144,512]{1,0:T(8,128)(2,1)S(1)} %shard_map.101.rest, ...), custom_call_target="tpu_custom_call" | custom-call | flops 268435456 | bytes 8388608 | tf_op jit(solution)/shard_map/pallas_call | solution.py:68
  66.4 1.7 %collective-permute-done.16.others = bf16[4,64,512]{2,1,0:T(8,128)(2,1)S(1)} collective-permute-done((bf16[4,64,512]{2,1,0:T(8,128)(2,1)S(1)}, bf16[4,64,512]{2,1,0:T(8,128)(2,1)S(1)}, u32[]{:S(2)}, u32[]{:S(2)}) %collective-permute-start.16) | collective-permute-done | bytes 262176 | tf_op jit(solution)/shard_map/ppermute | solution.py:35
  68.1 1.4 %collective-permute-start.17 = (bf16[32,512]{1,0:T(8,128)(2,1)S(1)}, bf16[32,512]{1,0:T(8,128)(2,1)S(1)}, u32[]{:S(2)}, u32[]{:S(2)}) collective-permute-start(bf16[32,512]{1,0:T(8,128)(2,1)S(1)} %shard_map.112.refs_2_), channel_id=1, source_target_pairs={{0,8},{8,0},{16,24},{24,16},{1,9},{9,1},{17,25},{25,17},{2,10},{10... | collective-permute-start | bytes 98312 | tf_op jit(solution)/shard_map/ppermute | solution.py:35
  73.4 2.1 %collective-permute-done.19.refs_5_ = bf16[32,512]{1,0:T(8,128)(2,1)S(1)} collective-permute-done((bf16[32,512]{1,0:T(8,128)(2,1)S(1)}, bf16[32,512]{1,0:T(8,128)(2,1)S(1)}, u32[]{:S(2)}, u32[]{:S(2)}) %collective-permute-start.19) | collective-permute-done | bytes 32800 | tf_op jit(solution)/shard_map/ppermute | solution.py:35
  77.4 3.2 %collective-permute-start.21 = (f32[8,64]{1,0:T(8,128)S(1)}, f32[8,64]{1,0:T(8,128)S(1)}, u32[]{:S(2)}, u32[]{:S(2)}) collective-permute-start(f32[8,64]{1,0:T(8,128)S(1)} %add.3.refs_0_), channel_id=1, source_target_pairs={{0,2},{1,3},{2,4},{3,5},{4,6},{5,7},{6,0},{7,1},{8,10},{9,11},{10,... | collective-permute-start | bytes 6152 | tf_op jit(solution)/shard_map/ppermute | solution.py:52
  80.6 2.4 %collective-permute-start.23 = (f32[8,64]{1,0:T(8,128)S(1)}, f32[8,64]{1,0:T(8,128)S(1)}, u32[]{:S(2)}, u32[]{:S(2)}) collective-permute-start(f32[8,64]{1,0:T(8,128)S(1)} %add.3.refs_0_), channel_id=1, source_target_pairs={{0,6},{1,7},{2,0},{3,1},{4,2},{5,3},{6,4},{7,5},{8,14},{9,15},{10,... | collective-permute-start | bytes 6152 | tf_op jit(solution)/shard_map/ppermute | solution.py:52
  82.9 2.1 %collective-permute-done.22.refs_2_ = f32[8,64]{1,0:T(8,128)S(1)} collective-permute-done((f32[8,64]{1,0:T(8,128)S(1)}, f32[8,64]{1,0:T(8,128)S(1)}, u32[]{:S(2)}, u32[]{:S(2)}) %collective-permute-start.22) | collective-permute-done | bytes 2080 | tf_op jit(solution)/shard_map/ppermute | solution.py:52
  (71 shorter events, 16.9 us)
Async XLA Ops:
  4.8 5.3 %collective-permute-start = (bf16[16,8192]{1,0:T(8,128)(2,1)S(1)}, bf16[16,8192]{1,0:T(8,128)(2,1)S(1)}, u32[]{:S(2)}, u32[]{:S(2)}) collective-permute-start(bf16[16,8192]{1,0:T(8,128)(2,1)S(1)} %get-tuple-element.61), channel_id=1, source_target_pairs={{0,1},{2,3},{4,5},{6,7},{8,9},{10,11},{12,13},{14,15},{16,17},{18,... | collective-permute-start | bytes 786440 | tf_op jit(solution)/shard_map/ppermute | solution.py:45
  10.1 9.3 %collective-permute-start.1 = (bf16[32,8192]{1,0:T(8,128)(2,1)S(1)}, bf16[32,8192]{1,0:T(8,128)(2,1)S(1)}, u32[]{:S(2)}, u32[]{:S(2)}) collective-permute-start(bf16[32,8192]{1,0:T(8,128)(2,1)S(1)} %constant_dynamic-update-slice_fusion), channel_id=1, source_target_pairs={{1,2},{3,4},{5,6},{9,10},{11,12},{13,14},{17,18},{19,20},{21,22},{... | collective-permute-start | bytes 1572872 | tf_op jit(solution)/shard_map/ppermute | solution.py:45
  11.0 16.5 %collective-permute-start.3 = (bf16[16,8192]{1,0:T(8,128)(2,1)S(1)}, bf16[16,8192]{1,0:T(8,128)(2,1)S(1)}, u32[]{:S(2)}, u32[]{:S(2)}) collective-permute-start(bf16[16,8192]{1,0:T(8,128)(2,1)S(1)} %constant_dynamic-update-slice_fusion.2), channel_id=1, source_target_pairs={{0,8},{8,0},{16,24},{24,16},{1,9},{9,1},{17,25},{25,17},{2,10},{10... | collective-permute-start | bytes 786440 | tf_op jit(solution)/shard_map/ppermute | solution.py:35
  13.4 14.1 %collective-permute-start.4 = (bf16[16,8192]{1,0:T(8,128)(2,1)S(1)}, bf16[16,8192]{1,0:T(8,128)(2,1)S(1)}, u32[]{:S(2)}, u32[]{:S(2)}) collective-permute-start(bf16[16,8192]{1,0:T(8,128)(2,1)S(1)} %constant_dynamic-update-slice_fusion.2), channel_id=1, source_target_pairs={{0,16},{8,24},{16,0},{24,8},{1,17},{9,25},{17,1},{25,9},{2,18},{10... | collective-permute-start | bytes 786440 | tf_op jit(solution)/shard_map/ppermute | solution.py:35
  14.9 12.6 %collective-permute-start.5 = (bf16[16,8192]{1,0:T(8,128)(2,1)S(1)}, bf16[16,8192]{1,0:T(8,128)(2,1)S(1)}, u32[]{:S(2)}, u32[]{:S(2)}) collective-permute-start(bf16[16,8192]{1,0:T(8,128)(2,1)S(1)} %constant_dynamic-update-slice_fusion.2), channel_id=1, source_target_pairs={{0,24},{8,16},{16,8},{24,0},{1,25},{9,17},{17,9},{25,1},{2,26},{10... | collective-permute-start | bytes 786440 | tf_op jit(solution)/shard_map/ppermute | solution.py:35
  22.6 5.0 %collective-permute-start.2 = (bf16[32,8192]{1,0:T(8,128)(2,1)S(1)}, bf16[32,8192]{1,0:T(8,128)(2,1)S(1)}, u32[]{:S(2)}, u32[]{:S(2)}) collective-permute-start(bf16[32,8192]{1,0:T(8,128)(2,1)S(1)} %get-tuple-element.70), channel_id=1, source_target_pairs={{0,1},{2,3},{4,5},{6,7},{8,9},{10,11},{12,13},{14,15},{16,17},{18,... | collective-permute-start | bytes 1572872 | tf_op jit(solution)/shard_map/ppermute | solution.py:45
  27.7 17.8 %collective-permute-start.6 = (bf16[32,8192]{1,0:T(8,128)(2,1)S(1)}, bf16[32,8192]{1,0:T(8,128)(2,1)S(1)}, u32[]{:S(2)}, u32[]{:S(2)}) collective-permute-start(bf16[32,8192]{1,0:T(8,128)(2,1)S(1)} %get-tuple-element.80), channel_id=1, source_target_pairs={{1,2},{3,4},{5,6},{9,10},{11,12},{13,14},{17,18},{19,20},{21,22},{... | collective-permute-start | bytes 1572872 | tf_op jit(solution)/shard_map/ppermute | solution.py:45
  33.7 18.9 %collective-permute-start.10 = (bf16[64,512]{1,0:T(8,128)(2,1)S(1)}, bf16[64,512]{1,0:T(8,128)(2,1)S(1)}, u32[]{:S(2)}, u32[]{:S(2)}) collective-permute-start(bf16[64,512]{1,0:T(8,128)(2,1)S(1)} %get-tuple-element.102.refs_2_), channel_id=1, source_target_pairs={{0,6},{1,7},{8,14},{9,15},{16,22},{17,23},{24,30},{25,31}} | collective-permute-start | bytes 196616 | tf_op jit(solution)/shard_map/ppermute | solution.py:45
  41.5 11.2 %collective-permute-start.8 = (bf16[64,512]{1,0:T(8,128)(2,1)S(1)}, bf16[64,512]{1,0:T(8,128)(2,1)S(1)}, u32[]{:S(2)}, u32[]{:S(2)}) collective-permute-start(bf16[64,512]{1,0:T(8,128)(2,1)S(1)} %get-tuple-element.102.refs_2_), channel_id=1, source_target_pairs={{0,2},{1,3},{2,4},{3,5},{4,6},{5,7},{8,10},{9,11},{10,12},{11,13},... | collective-permute-start | bytes 196616 | tf_op jit(solution)/shard_map/ppermute | solution.py:45
  42.8 9.9 %collective-permute-start.9 = (bf16[64,512]{1,0:T(8,128)(2,1)S(1)}, bf16[64,512]{1,0:T(8,128)(2,1)S(1)}, u32[]{:S(2)}, u32[]{:S(2)}) collective-permute-start(bf16[64,512]{1,0:T(8,128)(2,1)S(1)} %get-tuple-element.102.refs_2_), channel_id=1, source_target_pairs={{0,4},{1,5},{2,6},{3,7},{8,12},{9,13},{10,14},{11,15},{16,20},{17,... | collective-permute-start | bytes 196616 | tf_op jit(solution)/shard_map/ppermute | solution.py:45
  48.6 4.0 %collective-permute-start.7 = (bf16[32,8192]{1,0:T(8,128)(2,1)S(1)}, bf16[32,8192]{1,0:T(8,128)(2,1)S(1)}, u32[]{:S(2)}, u32[]{:S(2)}) collective-permute-start(bf16[32,8192]{1,0:T(8,128)(2,1)S(1)} %get-tuple-element.85), channel_id=1, source_target_pairs={{0,1},{2,3},{4,5},{6,7},{8,9},{10,11},{12,13},{14,15},{16,17},{18,... | collective-permute-start | bytes 1572872 | tf_op jit(solution)/shard_map/ppermute | solution.py:45
  52.7 9.1 %collective-permute-start.11 = (bf16[32,8192]{1,0:T(8,128)(2,1)S(1)}, bf16[32,8192]{1,0:T(8,128)(2,1)S(1)}, u32[]{:S(2)}, u32[]{:S(2)}) collective-permute-start(bf16[32,8192]{1,0:T(8,128)(2,1)S(1)} %get-tuple-element.91), channel_id=1, source_target_pairs={{1,2},{3,4},{5,6},{9,10},{11,12},{13,14},{17,18},{19,20},{21,22},{... | collective-permute-start | bytes 1572872 | tf_op jit(solution)/shard_map/ppermute | solution.py:45
  53.4 7.8 %collective-permute-start.12 = (bf16[80,512]{1,0:T(8,128)(2,1)S(1)}, bf16[80,512]{1,0:T(8,128)(2,1)S(1)}, u32[]{:S(2)}, u32[]{:S(2)}) collective-permute-start(bf16[80,512]{1,0:T(8,128)(2,1)S(1)} %pad_maximum_fusion.2.refs_6_), channel_id=1, source_target_pairs={{0,8},{8,0},{16,24},{24,16},{1,9},{9,1},{17,25},{25,17},{2,10},{10... | collective-permute-start | bytes 245768 | tf_op jit(solution)/shard_map/ppermute | solution.py:35
  55.0 6.2 %collective-permute-start.13 = (bf16[80,512]{1,0:T(8,128)(2,1)S(1)}, bf16[80,512]{1,0:T(8,128)(2,1)S(1)}, u32[]{:S(2)}, u32[]{:S(2)}) collective-permute-start(bf16[80,512]{1,0:T(8,128)(2,1)S(1)} %pad_maximum_fusion.2.refs_6_), channel_id=1, source_target_pairs={{0,16},{8,24},{16,0},{24,8},{1,17},{9,25},{17,1},{25,9},{2,18},{10... | collective-permute-start | bytes 245768 | tf_op jit(solution)/shard_map/ppermute | solution.py:35
  56.5 5.3 %collective-permute-start.14 = (bf16[80,512]{1,0:T(8,128)(2,1)S(1)}, bf16[80,512]{1,0:T(8,128)(2,1)S(1)}, u32[]{:S(2)}, u32[]{:S(2)}) collective-permute-start(bf16[80,512]{1,0:T(8,128)(2,1)S(1)} %pad_maximum_fusion.2.refs_6_), channel_id=1, source_target_pairs={{0,24},{8,16},{16,8},{24,0},{1,25},{9,17},{17,9},{25,1},{2,26},{10... | collective-permute-start | bytes 245768 | tf_op jit(solution)/shard_map/ppermute | solution.py:35
  64.9 3.2 %collective-permute-start.15 = (bf16[32,8192]{1,0:T(8,128)(2,1)S(1)}, bf16[32,8192]{1,0:T(8,128)(2,1)S(1)}, u32[]{:S(2)}, u32[]{:S(2)}) collective-permute-start(bf16[32,8192]{1,0:T(8,128)(2,1)S(1)} %get-tuple-element.98), channel_id=1, source_target_pairs={{0,1},{2,3},{4,5},{6,7},{8,9},{10,11},{12,13},{14,15},{16,17},{18,... | collective-permute-start | bytes 1572872 | tf_op jit(solution)/shard_map/ppermute | solution.py:45
  66.3 1.8 %collective-permute-start.16 = (bf16[4,64,512]{2,1,0:T(8,128)(2,1)S(1)}, bf16[4,64,512]{2,1,0:T(8,128)(2,1)S(1)}, u32[]{:S(2)}, u32[]{:S(2)}) collective-permute-start(bf16[4,64,512]{2,1,0:T(8,128)(2,1)S(1)} %pad_maximum_fusion.1), channel_id=1, source_target_pairs={{0,1},{1,0},{2,3},{3,2},{4,5},{5,4},{6,7},{7,6},{8,9},{9,8},{10,11... | collective-permute-start | bytes 786440 | tf_op jit(solution)/shard_map/ppermute | solution.py:35
  68.1 4.7 %collective-permute-start.17 = (bf16[32,512]{1,0:T(8,128)(2,1)S(1)}, bf16[32,512]{1,0:T(8,128)(2,1)S(1)}, u32[]{:S(2)}, u32[]{:S(2)}) collective-permute-start(bf16[32,512]{1,0:T(8,128)(2,1)S(1)} %shard_map.112.refs_2_), channel_id=1, source_target_pairs={{0,8},{8,0},{16,24},{24,16},{1,9},{9,1},{17,25},{25,17},{2,10},{10... | collective-permute-start | bytes 98312 | tf_op jit(solution)/shard_map/ppermute | solution.py:35
  69.5 3.9 %collective-permute-start.18 = (bf16[32,512]{1,0:T(8,128)(2,1)S(1)}, bf16[32,512]{1,0:T(8,128)(2,1)S(1)}, u32[]{:S(2)}, u32[]{:S(2)}) collective-permute-start(bf16[32,512]{1,0:T(8,128)(2,1)S(1)} %shard_map.112.refs_2_), channel_id=1, source_target_pairs={{0,16},{8,24},{16,0},{24,8},{1,17},{9,25},{17,1},{25,9},{2,18},{10... | collective-permute-start | bytes 98312 | tf_op jit(solution)/shard_map/ppermute | solution.py:35
  70.8 4.8 %collective-permute-start.19 = (bf16[32,512]{1,0:T(8,128)(2,1)S(1)}, bf16[32,512]{1,0:T(8,128)(2,1)S(1)}, u32[]{:S(2)}, u32[]{:S(2)}) collective-permute-start(bf16[32,512]{1,0:T(8,128)(2,1)S(1)} %shard_map.112.refs_2_), channel_id=1, source_target_pairs={{0,24},{8,16},{16,8},{24,0},{1,25},{9,17},{17,9},{25,1},{2,26},{10... | collective-permute-start | bytes 98312 | tf_op jit(solution)/shard_map/ppermute | solution.py:35
  76.2 1.2 %collective-permute-start.20 = (f32[8,64]{1,0:T(8,128)S(1)}, f32[8,64]{1,0:T(8,128)S(1)}, u32[]{:S(2)}, u32[]{:S(2)}) collective-permute-start(f32[8,64]{1,0:T(8,128)S(1)} %shard_map.114), channel_id=1, source_target_pairs={{0,1},{1,0},{2,3},{3,2},{4,5},{5,4},{6,7},{7,6},{8,9},{9,8},{10,11... | collective-permute-start | bytes 6152 | tf_op jit(solution)/shard_map/ppermute | solution.py:35
  77.4 5.5 %collective-permute-start.21 = (f32[8,64]{1,0:T(8,128)S(1)}, f32[8,64]{1,0:T(8,128)S(1)}, u32[]{:S(2)}, u32[]{:S(2)}) collective-permute-start(f32[8,64]{1,0:T(8,128)S(1)} %add.3.refs_0_), channel_id=1, source_target_pairs={{0,2},{1,3},{2,4},{3,5},{4,6},{5,7},{6,0},{7,1},{8,10},{9,11},{10,... | collective-permute-start | bytes 6152 | tf_op jit(solution)/shard_map/ppermute | solution.py:52
  80.6 4.5 %collective-permute-start.22 = (f32[8,64]{1,0:T(8,128)S(1)}, f32[8,64]{1,0:T(8,128)S(1)}, u32[]{:S(2)}, u32[]{:S(2)}) collective-permute-start(f32[8,64]{1,0:T(8,128)S(1)} %add.3.refs_0_), channel_id=1, source_target_pairs={{0,4},{1,5},{2,6},{3,7},{4,0},{5,1},{6,2},{7,3},{8,12},{9,13},{10,... | collective-permute-start | bytes 6152 | tf_op jit(solution)/shard_map/ppermute | solution.py:52
  80.6 4.5 %collective-permute-start.23 = (f32[8,64]{1,0:T(8,128)S(1)}, f32[8,64]{1,0:T(8,128)S(1)}, u32[]{:S(2)}, u32[]{:S(2)}) collective-permute-start(f32[8,64]{1,0:T(8,128)S(1)} %add.3.refs_0_), channel_id=1, source_target_pairs={{0,6},{1,7},{2,0},{3,1},{4,2},{5,3},{6,4},{7,5},{8,14},{9,15},{10,... | collective-permute-start | bytes 6152 | tf_op jit(solution)/shard_map/ppermute | solution.py:52
  (8 other events, 65.4 us)

commit v11 on v10

--- a/solution.py
+++ b/solution.py
@@ -380,7 +380,7 @@
     empty = jnp.zeros((2 * rows, rank), bf16)
     for slot in range(1, chips):
         found, leaving = through(0, arrived, empty)
-        arrived = upward(leaving, 0, 1, 2)
+        arrived = upward(leaving, 2 * slot, 1, 2)
         if slot == 1:
             (hid,) = tie([hidden_cols[0]], leaving)
             (hidden,) = call(
@@ -404,7 +404,7 @@
             break
         found, leaving = through(1, arrived, found)
         slots.append(found)
-        arrived = upward(leaving, 1, 1, 2)
+        arrived = upward(leaving, 2 * slot + 1, 1, 2)
         if slot == 1:
             left_rows, right_rows = call(
                 functools.partial(weave_kernel, q_dev),

time: 86.2 us -> 84.7 us (0.983)
  starting transfers between devices: 37.5 us -> 34.5 us
  waiting for transfers between devices: 8.27 us -> 9.79 us
    ppermute x3, starting transfers between devices: 5.53 us -> 3.83 us  [around(): lax.ppermute(value, 'pipe', [(source, (source + 2 * hop) % count) for sou...]
    ppermute x3, waiting for transfers between devices: 2.14 us -> 3.59 us  [around(): lax.ppermute(value, 'pipe', [(source, (source + 2 * hop) % count) for sou...]
    ppermute x10, starting transfers between devices: 20.7 us -> 19.5 us  [upward(): lax.ppermute(value, 'pipe', [(source, source + hop) for source in range(f...]
  transfers between devices with their start and end apart: 24 -> 24, of which waited for: 6 -> 7; matrix products, arithmetic and copies ran while one was open for 6% -> 7% of each run, Pallas kernels for 26% -> 27%
where the time goes in v11:
time: 84.7 us; the launch traced here: 84.3 us
  starting transfers between devices  34.5 us (41%)
  Pallas kernels  31.7 us (37%)
  waiting for transfers between devices  9.79 us (12%)
  matrix products  5.32 us (6%)
  local copies, waits for them, and re-layouts  2.3 us (3%)
    pallas_call x16, Pallas kernels, call(): pl.pallas_call(kernel, in_specs=[pl.BlockSpec(memory_space=space[place])...  31.7 us
    ppermute x10, starting transfers between devices, upward(): lax.ppermute(value, 'pipe', [(source, source + hop) for source in range(f...  19.5 us
    ppermute x11, starting transfers between devices, swap(): lax.ppermute(value, axis, [(source, source ^ distance) for source in rang...  11.2 us
    ppermute x11, waiting for transfers between devices, swap(): lax.ppermute(value, axis, [(source, source ^ distance) for source in rang...  6.18 us
    dot_general x2, matrix products, dot_nt(): lax.dot_general(a, b, (((1,), (1,)), ((), ())), preferred_element_type=f3...  5.32 us
    ppermute x3, starting transfers between devices, around(): lax.ppermute(value, 'pipe', [(source, (source + 2 * hop) % count) for sou...  3.83 us
    ppermute x3, waiting for transfers between devices, around(): lax.ppermute(value, 'pipe', [(source, (source + 2 * hop) % count) for sou...  3.59 us
    unnamed x18, local copies, waits for them, and re-layouts  2.26 us
  transfers between devices with their start and end apart: 24, of which 7 were waited for; matrix products, arithmetic and copies ran while one was open for 7% of the time, Pallas kernels for 27%

profile of v11, /device:TPU:0, one launch (start us, length us, event | category | flops | bytes accessed | tf_op | source)
XLA Modules:
  0.0 84.3 jit_solution(5233331578578641269)
XLA Ops:
  0.0 4.7 %shard_map.100 = (bf16[512,8192]{1,0:T(8,128)(2,1)S(1)}, bf16[2048,512]{1,0:T(8,128)(2,1)S(1)}, bf16[64,8192]{1,0:T(8,128)(2,1)S(1)}, bf16[16,8192]{1,0:T(8,128)(2,1)S(1)}) custom-call(bf16[32,512]{1,0:T(8,128)(2,1)} %bitcast.38, bf16[8,8192]{1,0:T(8,128)(2,1)} %bitcast.35, bf16[512,8192]{1,0:T(8,128)(2,1)} %bitcast.32, bf16[8192,512]{1,0:T(8,128)(2,1)} %bitcast.30), custom_call_target="tpu_custom_call" | custom-call | flops 134217728 | bytes 16777216 | tf_op jit(solution)/shard_map/pallas_call | solution.py:68
  4.8 2.4 %collective-permute-start = (bf16[16,8192]{1,0:T(8,128)(2,1)S(1)}, bf16[16,8192]{1,0:T(8,128)(2,1)S(1)}, u32[]{:S(2)}, u32[]{:S(2)}) collective-permute-start(bf16[16,8192]{1,0:T(8,128)(2,1)S(1)} %get-tuple-element.61), channel_id=1, source_target_pairs={{0,1},{2,3},{4,5},{6,7},{8,9},{10,11},{12,13},{14,15},{16,17},{18,... | collective-permute-start | bytes 786440 | tf_op jit(solution)/shard_map/ppermute | solution.py:45
  7.1 2.8 %shard_map.101.rest = bf16[6144,512]{1,0:T(8,128)(2,1)S(1)} custom-call(bf16[8192,512]{1,0:T(8,128)(2,1)} %bitcast.31), custom_call_target="tpu_custom_call" | custom-call | bytes 16777216 | tf_op jit(solution)/shard_map/pallas_call | solution.py:68
  11.0 2.4 %collective-permute-start.3 = (bf16[16,8192]{1,0:T(8,128)(2,1)S(1)}, bf16[16,8192]{1,0:T(8,128)(2,1)S(1)}, u32[]{:S(2)}, u32[]{:S(2)}) collective-permute-start(bf16[16,8192]{1,0:T(8,128)(2,1)S(1)} %constant_dynamic-update-slice_fusion.2), channel_id=1, source_target_pairs={{0,8},{8,0},{16,24},{24,16},{1,9},{9,1},{17,25},{25,17},{2,10},{10... | collective-permute-start | bytes 786440 | tf_op jit(solution)/shard_map/ppermute | solution.py:35
  13.4 1.5 %collective-permute-start.4 = (bf16[16,8192]{1,0:T(8,128)(2,1)S(1)}, bf16[16,8192]{1,0:T(8,128)(2,1)S(1)}, u32[]{:S(2)}, u32[]{:S(2)}) collective-permute-start(bf16[16,8192]{1,0:T(8,128)(2,1)S(1)} %constant_dynamic-update-slice_fusion.2), channel_id=1, source_target_pairs={{0,16},{8,24},{16,0},{24,8},{1,17},{9,25},{17,1},{25,9},{2,18},{10... | collective-permute-start | bytes 786440 | tf_op jit(solution)/shard_map/ppermute | solution.py:35
  15.0 4.5 %shard_map.103.refs_0_ = bf16[320,512]{1,0:T(8,128)(2,1)S(1)} custom-call(bf16[512,8192]{1,0:T(8,128)(2,1)} %cotangent.1, bf16[512,8192]{1,0:T(8,128)(2,1)S(1)} %get-tuple-element.66.expand), custom_call_target="tpu_custom_call" | custom-call | flops 2684354560 | bytes 8388608 | tf_op jit(solution)/shard_map/pallas_call | solution.py:68
  19.5 3.1 %shard_map.104 = (bf16[32,512]{1,0:T(8,128)(2,1)S(1)}, bf16[32,8192]{1,0:T(8,128)(2,1)S(1)}) custom-call(bf16[32,8192]{1,0:T(8,128)(2,1)S(1)} %collective-permute-done.1.arrived, bf16[32,512]{1,0:T(8,128)(2,1)S(1)} %broadcast_in_dim.12.before, bf16[2048,512]{1,0:T(8,128)(2,1)S(1)} %get-tuple-element.64.head, bf16[6144,512]{1,0:T(8,128)(2,1)S(1)} %shard_map.101.rest, ...), custom_call_target="tpu_custom_call" | custom-call | flops 268435456 | bytes 8388608 | tf_op jit(solution)/shard_map/pallas_call | solution.py:68
  23.3 3.5 %shard_map.105.hidden = bf16[64,8192]{1,0:T(8,128)(2,1)S(1)} custom-call(bf16[32,512]{1,0:T(8,128)(2,1)} %bitcast.39, bf16[2048,512]{1,0:T(8,128)(2,1)S(1)} %get-tuple-element.64.head, bf16[6144,512]{1,0:T(8,128)(2,1)S(1)} %shard_map.101.rest), custom_call_target="tpu_custom_call" | custom-call | flops 536870912 | bytes 8388608 | tf_op jit(solution)/shard_map/pallas_call | solution.py:68
  29.0 1.3 %slice-done.3 = s8[4194304]{0:T(1024)(128)(4,1)S(1)} async-done(((s8[8388608]{0:T(1024)(128)(4,1)}), s8[4194304]{0:T(1024)(128)(4,1)S(1)}, s32[]{:S(2)}) %slice-start.3) | async-done | bytes 4194328
  30.3 2.7 %fusion.5 = (bf16[64,512]{1,0:T(8,128)(2,1)S(1)}, f32[64,512]{1,0:T(8,128)S(1)}) fusion(f32[512]{0:T(512)S(1)} %convert_bitcast_fusion, bf16[64,8192]{1,0:T(8,128)(2,1)S(1)} %get-tuple-element.83, bf16[1,512,8192]{2,1,0:T(8,128)(2,1)S(1)} %bitcast.34), kind=kOutput, calls=%fused_computation.12 | convolution fusion | flops 536936448 | bytes 9635840 | tf_op jit(solution)/shard_map/dot_general | solution.py:28
  33.0 8.5 %collective-permute-start.10 = (bf16[64,512]{1,0:T(8,128)(2,1)S(1)}, bf16[64,512]{1,0:T(8,128)(2,1)S(1)}, u32[]{:S(2)}, u32[]{:S(2)}) collective-permute-start(bf16[64,512]{1,0:T(8,128)(2,1)S(1)} %get-tuple-element.102.refs_2_), channel_id=1, source_target_pairs={{0,6},{1,7},{8,14},{9,15},{16,22},{17,23},{24,30},{25,31}} | collective-permute-start | bytes 196616 | tf_op jit(solution)/shard_map/ppermute | solution.py:45
  42.8 2.7 %collective-permute-start.9 = (bf16[64,512]{1,0:T(8,128)(2,1)S(1)}, bf16[64,512]{1,0:T(8,128)(2,1)S(1)}, u32[]{:S(2)}, u32[]{:S(2)}) collective-permute-start(bf16[64,512]{1,0:T(8,128)(2,1)S(1)} %get-tuple-element.102.refs_2_), channel_id=1, source_target_pairs={{0,4},{1,5},{2,6},{3,7},{8,12},{9,13},{10,14},{11,15},{16,20},{17,... | collective-permute-start | bytes 196616 | tf_op jit(solution)/shard_map/ppermute | solution.py:45
  45.5 3.1 %shard_map.108 = (bf16[32,512]{1,0:T(8,128)(2,1)S(1)}, bf16[32,8192]{1,0:T(8,128)(2,1)S(1)}) custom-call(bf16[32,8192]{1,0:T(8,128)(2,1)S(1)} %collective-permute-done.6.arrived, bf16[32,512]{1,0:T(8,128)(2,1)S(1)} %broadcast_in_dim.12.before, bf16[2048,512]{1,0:T(8,128)(2,1)S(1)} %get-tuple-element.64.head, bf16[6144,512]{1,0:T(8,128)(2,1)S(1)} %shard_map.101.rest, ...), custom_call_target="tpu_custom_call" | custom-call | flops 268435456 | bytes 8388608 | tf_op jit(solution)/shard_map/pallas_call | solution.py:68
  49.3 2.7 %fusion.6.right = f32[64,512]{1,0:T(8,128)S(1)} fusion(bf16[64,8192]{1,0:T(8,128)(2,1)S(1)} %get-tuple-element.86, bf16[512,8192]{1,0:T(8,128)(2,1)S(1)} %bitcast.29), kind=kOutput, calls=%fused_computation.13 | convolution fusion | flops 536870912 | bytes 9568256 | tf_op jit(solution)/shard_map/dot_general | solution.py:28
  52.8 1.6 %collective-permute-start.12 = (bf16[80,512]{1,0:T(8,128)(2,1)S(1)}, bf16[80,512]{1,0:T(8,128)(2,1)S(1)}, u32[]{:S(2)}, u32[]{:S(2)}) collective-permute-start(bf16[80,512]{1,0:T(8,128)(2,1)S(1)} %pad_maximum_fusion.2.refs_6_), channel_id=1, source_target_pairs={{0,8},{8,0},{16,24},{24,16},{1,9},{9,1},{17,25},{25,17},{2,10},{10... | collective-permute-start | bytes 245768 | tf_op jit(solution)/shard_map/ppermute | solution.py:35
  54.3 1.5 %collective-permute-start.13 = (bf16[80,512]{1,0:T(8,128)(2,1)S(1)}, bf16[80,512]{1,0:T(8,128)(2,1)S(1)}, u32[]{:S(2)}, u32[]{:S(2)}) collective-permute-start(bf16[80,512]{1,0:T(8,128)(2,1)S(1)} %pad_maximum_fusion.2.refs_6_), channel_id=1, source_target_pairs={{0,16},{8,24},{16,0},{24,8},{1,17},{9,25},{17,1},{25,9},{2,18},{10... | collective-permute-start | bytes 245768 | tf_op jit(solution)/shard_map/ppermute | solution.py:35
  56.3 4.2 %shard_map.110.refs_1_ = bf16[192,512]{1,0:T(8,128)(2,1)S(1)} custom-call(bf16[512,8192]{1,0:T(8,128)(2,1)} %cotangent.1, bf16[512,8192]{1,0:T(8,128)(2,1)S(1)} %get-tuple-element.66.expand), custom_call_target="tpu_custom_call" | custom-call | flops 1610612736 | bytes 8388608 | tf_op jit(solution)/shard_map/pallas_call | solution.py:68
  61.2 3.1 %shard_map.111 = (bf16[32,512]{1,0:T(8,128)(2,1)S(1)}, bf16[32,8192]{1,0:T(8,128)(2,1)S(1)}) custom-call(bf16[32,8192]{1,0:T(8,128)(2,1)S(1)} %collective-permute-done.11.arrived, bf16[32,512]{1,0:T(8,128)(2,1)S(1)} %broadcast_in_dim.12.before, bf16[2048,512]{1,0:T(8,128)(2,1)S(1)} %get-tuple-element.64.head, bf16[6144,512]{1,0:T(8,128)(2,1)S(1)} %shard_map.101.rest, ...), custom_call_target="tpu_custom_call" | custom-call | flops 268435456 | bytes 8388608 | tf_op jit(solution)/shard_map/pallas_call | solution.py:68
  65.1 1.5 %collective-permute-done.16.others = bf16[4,64,512]{2,1,0:T(8,128)(2,1)S(1)} collective-permute-done((bf16[4,64,512]{2,1,0:T(8,128)(2,1)S(1)}, bf16[4,64,512]{2,1,0:T(8,128)(2,1)S(1)}, u32[]{:S(2)}, u32[]{:S(2)}) %collective-permute-start.16) | collective-permute-done | bytes 262176 | tf_op jit(solution)/shard_map/ppermute | solution.py:35
  67.8 1.5 %collective-permute-start.18 = (bf16[32,512]{1,0:T(8,128)(2,1)S(1)}, bf16[32,512]{1,0:T(8,128)(2,1)S(1)}, u32[]{:S(2)}, u32[]{:S(2)}) collective-permute-start(bf16[32,512]{1,0:T(8,128)(2,1)S(1)} %shard_map.112.refs_2_), channel_id=1, source_target_pairs={{0,16},{8,24},{16,0},{24,8},{1,17},{9,25},{17,1},{25,9},{2,18},{10... | collective-permute-start | bytes 98312 | tf_op jit(solution)/shard_map/ppermute | solution.py:35
  71.7 2.6 %collective-permute-done.19.refs_5_ = bf16[32,512]{1,0:T(8,128)(2,1)S(1)} collective-permute-done((bf16[32,512]{1,0:T(8,128)(2,1)S(1)}, bf16[32,512]{1,0:T(8,128)(2,1)S(1)}, u32[]{:S(2)}, u32[]{:S(2)}) %collective-permute-start.19) | collective-permute-done | bytes 32800 | tf_op jit(solution)/shard_map/ppermute | solution.py:35
  76.1 3.8 %collective-permute-start.22 = (f32[8,64]{1,0:T(8,128)S(1)}, f32[8,64]{1,0:T(8,128)S(1)}, u32[]{:S(2)}, u32[]{:S(2)}) collective-permute-start(f32[8,64]{1,0:T(8,128)S(1)} %add.3.refs_0_), channel_id=1, source_target_pairs={{0,4},{1,5},{2,6},{3,7},{4,0},{5,1},{6,2},{7,3},{8,12},{9,13},{10,... | collective-permute-start | bytes 6152 | tf_op jit(solution)/shard_map/ppermute | solution.py:52
  80.0 1.6 %collective-permute-done.21.refs_1_ = f32[8,64]{1,0:T(8,128)S(1)} collective-permute-done((f32[8,64]{1,0:T(8,128)S(1)}, f32[8,64]{1,0:T(8,128)S(1)}, u32[]{:S(2)}, u32[]{:S(2)}) %collective-permute-start.21) | collective-permute-done | bytes 2080 | tf_op jit(solution)/shard_map/ppermute | solution.py:52
  81.6 2.0 %collective-permute-done.23.refs_3_ = f32[8,64]{1,0:T(8,128)S(1)} collective-permute-done((f32[8,64]{1,0:T(8,128)S(1)}, f32[8,64]{1,0:T(8,128)S(1)}, u32[]{:S(2)}, u32[]{:S(2)}) %collective-permute-start.23) | collective-permute-done | bytes 2080 | tf_op jit(solution)/shard_map/ppermute | solution.py:52
  (71 shorter events, 14.6 us)
Async XLA Ops:
  4.8 5.3 %collective-permute-start = (bf16[16,8192]{1,0:T(8,128)(2,1)S(1)}, bf16[16,8192]{1,0:T(8,128)(2,1)S(1)}, u32[]{:S(2)}, u32[]{:S(2)}) collective-permute-start(bf16[16,8192]{1,0:T(8,128)(2,1)S(1)} %get-tuple-element.61), channel_id=1, source_target_pairs={{0,1},{2,3},{4,5},{6,7},{8,9},{10,11},{12,13},{14,15},{16,17},{18,... | collective-permute-start | bytes 786440 | tf_op jit(solution)/shard_map/ppermute | solution.py:45
  10.1 9.3 %collective-permute-start.1 = (bf16[32,8192]{1,0:T(8,128)(2,1)S(1)}, bf16[32,8192]{1,0:T(8,128)(2,1)S(1)}, u32[]{:S(2)}, u32[]{:S(2)}) collective-permute-start(bf16[32,8192]{1,0:T(8,128)(2,1)S(1)} %constant_dynamic-update-slice_fusion), channel_id=1, source_target_pairs={{1,2},{3,4},{5,6},{9,10},{11,12},{13,14},{17,18},{19,20},{21,22},{... | collective-permute-start | bytes 1572872 | tf_op jit(solution)/shard_map/ppermute | solution.py:45
  11.0 15.7 %collective-permute-start.3 = (bf16[16,8192]{1,0:T(8,128)(2,1)S(1)}, bf16[16,8192]{1,0:T(8,128)(2,1)S(1)}, u32[]{:S(2)}, u32[]{:S(2)}) collective-permute-start(bf16[16,8192]{1,0:T(8,128)(2,1)S(1)} %constant_dynamic-update-slice_fusion.2), channel_id=1, source_target_pairs={{0,8},{8,0},{16,24},{24,16},{1,9},{9,1},{17,25},{25,17},{2,10},{10... | collective-permute-start | bytes 786440 | tf_op jit(solution)/shard_map/ppermute | solution.py:35
  13.4 13.4 %collective-permute-start.4 = (bf16[16,8192]{1,0:T(8,128)(2,1)S(1)}, bf16[16,8192]{1,0:T(8,128)(2,1)S(1)}, u32[]{:S(2)}, u32[]{:S(2)}) collective-permute-start(bf16[16,8192]{1,0:T(8,128)(2,1)S(1)} %constant_dynamic-update-slice_fusion.2), channel_id=1, source_target_pairs={{0,16},{8,24},{16,0},{24,8},{1,17},{9,25},{17,1},{25,9},{2,18},{10... | collective-permute-start | bytes 786440 | tf_op jit(solution)/shard_map/ppermute | solution.py:35
  14.9 11.9 %collective-permute-start.5 = (bf16[16,8192]{1,0:T(8,128)(2,1)S(1)}, bf16[16,8192]{1,0:T(8,128)(2,1)S(1)}, u32[]{:S(2)}, u32[]{:S(2)}) collective-permute-start(bf16[16,8192]{1,0:T(8,128)(2,1)S(1)} %constant_dynamic-update-slice_fusion.2), channel_id=1, source_target_pairs={{0,24},{8,16},{16,8},{24,0},{1,25},{9,17},{17,9},{25,1},{2,26},{10... | collective-permute-start | bytes 786440 | tf_op jit(solution)/shard_map/ppermute | solution.py:35
  22.6 4.3 %collective-permute-start.2 = (bf16[32,8192]{1,0:T(8,128)(2,1)S(1)}, bf16[32,8192]{1,0:T(8,128)(2,1)S(1)}, u32[]{:S(2)}, u32[]{:S(2)}) collective-permute-start(bf16[32,8192]{1,0:T(8,128)(2,1)S(1)} %get-tuple-element.70), channel_id=1, source_target_pairs={{2,3},{4,5},{6,7},{10,11},{12,13},{14,15},{18,19},{20,21},{22,23},... | collective-permute-start | bytes 1572872 | tf_op jit(solution)/shard_map/ppermute | solution.py:45
  26.9 18.6 %collective-permute-start.6 = (bf16[32,8192]{1,0:T(8,128)(2,1)S(1)}, bf16[32,8192]{1,0:T(8,128)(2,1)S(1)}, u32[]{:S(2)}, u32[]{:S(2)}) collective-permute-start(bf16[32,8192]{1,0:T(8,128)(2,1)S(1)} %get-tuple-element.80), channel_id=1, source_target_pairs={{3,4},{5,6},{11,12},{13,14},{19,20},{21,22},{27,28},{29,30}} | collective-permute-start | bytes 1572872 | tf_op jit(solution)/shard_map/ppermute | solution.py:45
  33.0 19.0 %collective-permute-start.10 = (bf16[64,512]{1,0:T(8,128)(2,1)S(1)}, bf16[64,512]{1,0:T(8,128)(2,1)S(1)}, u32[]{:S(2)}, u32[]{:S(2)}) collective-permute-start(bf16[64,512]{1,0:T(8,128)(2,1)S(1)} %get-tuple-element.102.refs_2_), channel_id=1, source_target_pairs={{0,6},{1,7},{8,14},{9,15},{16,22},{17,23},{24,30},{25,31}} | collective-permute-start | bytes 196616 | tf_op jit(solution)/shard_map/ppermute | solution.py:45
  41.5 10.5 %collective-permute-start.8 = (bf16[64,512]{1,0:T(8,128)(2,1)S(1)}, bf16[64,512]{1,0:T(8,128)(2,1)S(1)}, u32[]{:S(2)}, u32[]{:S(2)}) collective-permute-start(bf16[64,512]{1,0:T(8,128)(2,1)S(1)} %get-tuple-element.102.refs_2_), channel_id=1, source_target_pairs={{0,2},{1,3},{2,4},{3,5},{4,6},{5,7},{8,10},{9,11},{10,12},{11,13},... | collective-permute-start | bytes 196616 | tf_op jit(solution)/shard_map/ppermute | solution.py:45
  42.8 9.2 %collective-permute-start.9 = (bf16[64,512]{1,0:T(8,128)(2,1)S(1)}, bf16[64,512]{1,0:T(8,128)(2,1)S(1)}, u32[]{:S(2)}, u32[]{:S(2)}) collective-permute-start(bf16[64,512]{1,0:T(8,128)(2,1)S(1)} %get-tuple-element.102.refs_2_), channel_id=1, source_target_pairs={{0,4},{1,5},{2,6},{3,7},{8,12},{9,13},{10,14},{11,15},{16,20},{17,... | collective-permute-start | bytes 196616 | tf_op jit(solution)/shard_map/ppermute | solution.py:45
  48.6 3.4 %collective-permute-start.7 = (bf16[32,8192]{1,0:T(8,128)(2,1)S(1)}, bf16[32,8192]{1,0:T(8,128)(2,1)S(1)}, u32[]{:S(2)}, u32[]{:S(2)}) collective-permute-start(bf16[32,8192]{1,0:T(8,128)(2,1)S(1)} %get-tuple-element.85), channel_id=1, source_target_pairs={{4,5},{6,7},{12,13},{14,15},{20,21},{22,23},{28,29},{30,31}} | collective-permute-start | bytes 1572872 | tf_op jit(solution)/shard_map/ppermute | solution.py:45
  52.1 9.1 %collective-permute-start.11 = (bf16[32,8192]{1,0:T(8,128)(2,1)S(1)}, bf16[32,8192]{1,0:T(8,128)(2,1)S(1)}, u32[]{:S(2)}, u32[]{:S(2)}) collective-permute-start(bf16[32,8192]{1,0:T(8,128)(2,1)S(1)} %get-tuple-element.91), channel_id=1, source_target_pairs={{5,6},{13,14},{21,22},{29,30}} | collective-permute-start | bytes 1572872 | tf_op jit(solution)/shard_map/ppermute | solution.py:45
  52.8 7.8 %collective-permute-start.12 = (bf16[80,512]{1,0:T(8,128)(2,1)S(1)}, bf16[80,512]{1,0:T(8,128)(2,1)S(1)}, u32[]{:S(2)}, u32[]{:S(2)}) collective-permute-start(bf16[80,512]{1,0:T(8,128)(2,1)S(1)} %pad_maximum_fusion.2.refs_6_), channel_id=1, source_target_pairs={{0,8},{8,0},{16,24},{24,16},{1,9},{9,1},{17,25},{25,17},{2,10},{10... | collective-permute-start | bytes 245768 | tf_op jit(solution)/shard_map/ppermute | solution.py:35
  54.3 6.2 %collective-permute-start.13 = (bf16[80,512]{1,0:T(8,128)(2,1)S(1)}, bf16[80,512]{1,0:T(8,128)(2,1)S(1)}, u32[]{:S(2)}, u32[]{:S(2)}) collective-permute-start(bf16[80,512]{1,0:T(8,128)(2,1)S(1)} %pad_maximum_fusion.2.refs_6_), channel_id=1, source_target_pairs={{0,16},{8,24},{16,0},{24,8},{1,17},{9,25},{17,1},{25,9},{2,18},{10... | collective-permute-start | bytes 245768 | tf_op jit(solution)/shard_map/ppermute | solution.py:35
  55.9 5.3 %collective-permute-start.14 = (bf16[80,512]{1,0:T(8,128)(2,1)S(1)}, bf16[80,512]{1,0:T(8,128)(2,1)S(1)}, u32[]{:S(2)}, u32[]{:S(2)}) collective-permute-start(bf16[80,512]{1,0:T(8,128)(2,1)S(1)} %pad_maximum_fusion.2.refs_6_), channel_id=1, source_target_pairs={{0,24},{8,16},{16,8},{24,0},{1,25},{9,17},{17,9},{25,1},{2,26},{10... | collective-permute-start | bytes 245768 | tf_op jit(solution)/shard_map/ppermute | solution.py:35
  64.3 2.4 %collective-permute-start.15 = (bf16[32,8192]{1,0:T(8,128)(2,1)S(1)}, bf16[32,8192]{1,0:T(8,128)(2,1)S(1)}, u32[]{:S(2)}, u32[]{:S(2)}) collective-permute-start(bf16[32,8192]{1,0:T(8,128)(2,1)S(1)} %get-tuple-element.98), channel_id=1, source_target_pairs={{6,7},{14,15},{22,23},{30,31}} | collective-permute-start | bytes 1572872 | tf_op jit(solution)/shard_map/ppermute | solution.py:45
  65.0 1.6 %collective-permute-start.16 = (bf16[4,64,512]{2,1,0:T(8,128)(2,1)S(1)}, bf16[4,64,512]{2,1,0:T(8,128)(2,1)S(1)}, u32[]{:S(2)}, u32[]{:S(2)}) collective-permute-start(bf16[4,64,512]{2,1,0:T(8,128)(2,1)S(1)} %pad_maximum_fusion.1), channel_id=1, source_target_pairs={{0,1},{1,0},{2,3},{3,2},{4,5},{5,4},{6,7},{7,6},{8,9},{9,8},{10,11... | collective-permute-start | bytes 786440 | tf_op jit(solution)/shard_map/ppermute | solution.py:35
  66.6 4.7 %collective-permute-start.17 = (bf16[32,512]{1,0:T(8,128)(2,1)S(1)}, bf16[32,512]{1,0:T(8,128)(2,1)S(1)}, u32[]{:S(2)}, u32[]{:S(2)}) collective-permute-start(bf16[32,512]{1,0:T(8,128)(2,1)S(1)} %shard_map.112.refs_2_), channel_id=1, source_target_pairs={{0,8},{8,0},{16,24},{24,16},{1,9},{9,1},{17,25},{25,17},{2,10},{10... | collective-permute-start | bytes 98312 | tf_op jit(solution)/shard_map/ppermute | solution.py:35
  67.8 3.9 %collective-permute-start.18 = (bf16[32,512]{1,0:T(8,128)(2,1)S(1)}, bf16[32,512]{1,0:T(8,128)(2,1)S(1)}, u32[]{:S(2)}, u32[]{:S(2)}) collective-permute-start(bf16[32,512]{1,0:T(8,128)(2,1)S(1)} %shard_map.112.refs_2_), channel_id=1, source_target_pairs={{0,16},{8,24},{16,0},{24,8},{1,17},{9,25},{17,1},{25,9},{2,18},{10... | collective-permute-start | bytes 98312 | tf_op jit(solution)/shard_map/ppermute | solution.py:35
  69.3 5.0 %collective-permute-start.19 = (bf16[32,512]{1,0:T(8,128)(2,1)S(1)}, bf16[32,512]{1,0:T(8,128)(2,1)S(1)}, u32[]{:S(2)}, u32[]{:S(2)}) collective-permute-start(bf16[32,512]{1,0:T(8,128)(2,1)S(1)} %shard_map.112.refs_2_), channel_id=1, source_target_pairs={{0,24},{8,16},{16,8},{24,0},{1,25},{9,17},{17,9},{25,1},{2,26},{10... | collective-permute-start | bytes 98312 | tf_op jit(solution)/shard_map/ppermute | solution.py:35
  75.0 1.2 %collective-permute-start.20 = (f32[8,64]{1,0:T(8,128)S(1)}, f32[8,64]{1,0:T(8,128)S(1)}, u32[]{:S(2)}, u32[]{:S(2)}) collective-permute-start(f32[8,64]{1,0:T(8,128)S(1)} %shard_map.114), channel_id=1, source_target_pairs={{0,1},{1,0},{2,3},{3,2},{4,5},{5,4},{6,7},{7,6},{8,9},{9,8},{10,11... | collective-permute-start | bytes 6152 | tf_op jit(solution)/shard_map/ppermute | solution.py:35
  76.1 5.4 %collective-permute-start.21 = (f32[8,64]{1,0:T(8,128)S(1)}, f32[8,64]{1,0:T(8,128)S(1)}, u32[]{:S(2)}, u32[]{:S(2)}) collective-permute-start(f32[8,64]{1,0:T(8,128)S(1)} %add.3.refs_0_), channel_id=1, source_target_pairs={{0,2},{1,3},{2,4},{3,5},{4,6},{5,7},{6,0},{7,1},{8,10},{9,11},{10,... | collective-permute-start | bytes 6152 | tf_op jit(solution)/shard_map/ppermute | solution.py:52
  76.1 5.4 %collective-permute-start.22 = (f32[8,64]{1,0:T(8,128)S(1)}, f32[8,64]{1,0:T(8,128)S(1)}, u32[]{:S(2)}, u32[]{:S(2)}) collective-permute-start(f32[8,64]{1,0:T(8,128)S(1)} %add.3.refs_0_), channel_id=1, source_target_pairs={{0,4},{1,5},{2,6},{3,7},{4,0},{5,1},{6,2},{7,3},{8,12},{9,13},{10,... | collective-permute-start | bytes 6152 | tf_op jit(solution)/shard_map/ppermute | solution.py:52
  80.0 3.6 %collective-permute-start.23 = (f32[8,64]{1,0:T(8,128)S(1)}, f32[8,64]{1,0:T(8,128)S(1)}, u32[]{:S(2)}, u32[]{:S(2)}) collective-permute-start(f32[8,64]{1,0:T(8,128)S(1)} %add.3.refs_0_), channel_id=1, source_target_pairs={{0,6},{1,7},{2,0},{3,1},{4,2},{5,3},{6,4},{7,5},{8,14},{9,15},{10,... | collective-permute-start | bytes 6152 | tf_op jit(solution)/shard_map/ppermute | solution.py:52
  (8 other events, 64.7 us)

commit v12 on v11

--- a/solution.py
+++ b/solution.py
@@ -154,10 +154,15 @@
         raised[:, span] = (adapter_scale * dot_nt(laid, down_rows(head, rest, part * step, step))).astype(bf16)
 
 
-def through_kernel(turn, arrived, before, head, rest, expand, ranks, leaving):
+def on_turn(core, slot):
+    layer = lax.axis_index("pipe")
+    return jnp.logical_and(layer % 2 == core, layer // 2 >= slot)
+
+
+def through_kernel(core, slot, arrived, before, head, rest, expand, ranks, leaving):
     depth = arrived.shape[1]
     step = 2 * ranks.shape[1]
-    mine = lax.axis_index("pipe") % 2 == turn
+    mine = on_turn(core, slot)
 
     @pl.when(jnp.logical_not(mine))
     def _():
@@ -175,10 +180,10 @@
             leaving[:, at : at + step] = (arrived[:, at : at + step].astype(f32) + more).astype(bf16)
 
 
-def last_kernel(arrived, before, head, rest, ranks):
+def last_kernel(slot, arrived, before, head, rest, ranks):
     depth = arrived.shape[1]
     step = 2 * ranks.shape[1]
-    mine = lax.axis_index("pipe") % 2 == 1
+    mine = on_turn(1, slot)
 
     @pl.when(jnp.logical_not(mine))
     def _():
@@ -306,9 +311,9 @@
     offsets = lax.broadcasted_iota(jnp.int32, (ex_dev, SLOT), 1)
     live = (offsets < lengths[:, None]).astype(f32).reshape(1, tok_dev)
 
-    def through(turn, arrived, before):
+    def through(core, slot, arrived, before):
         return call(
-            functools.partial(through_kernel, turn),
+            functools.partial(through_kernel, core, slot),
             (arrived, before, *down, expand),
             "vvvvv",
             [(before.shape, bf16), (arrived.shape, bf16)],
@@ -349,7 +354,7 @@
     )
     arrived, rest = lax.optimization_barrier((arrived, rest))
     down = (first, rest)
-    lower_ranks, leaving = through(1, arrived, jnp.zeros((rows, rank), bf16))
+    lower_ranks, leaving = through(1, 0, arrived, jnp.zeros((rows, rank), bf16))
     moving = jnp.concatenate([leaving, own])
 
     cut = tok_dev * 5 // 8
@@ -379,7 +384,7 @@
     slots = []
     empty = jnp.zeros((2 * rows, rank), bf16)
     for slot in range(1, chips):
-        found, leaving = through(0, arrived, empty)
+        found, leaving = through(0, slot, arrived, empty)
         arrived = upward(leaving, 2 * slot, 1, 2)
         if slot == 1:
             (hid,) = tie([hidden_cols[0]], leaving)
@@ -402,7 +407,7 @@
             others = swap(jnp.stack(tie(left_up, leaving)), "pipe", 1)
             arrived, others = lax.optimization_barrier((arrived, others))
             break
-        found, leaving = through(1, arrived, found)
+        found, leaving = through(1, slot, arrived, found)
         slots.append(found)
         arrived = upward(leaving, 2 * slot + 1, 1, 2)
         if slot == 1:
@@ -425,7 +430,7 @@
             arrived, lifted[1], *early = lax.optimization_barrier((arrived, lifted[1], *early))
 
     (late,) = call(
-        last_kernel,
+        functools.partial(last_kernel, top),
         (arrived, found, *down),
         "vvvv",
         [((2 * rows, rank), bf16)],

time: 84.7 us -> 84.7 us (level)
  Pallas kernels: 31.7 us -> 22.6 us
  starting transfers between devices: 34.5 us -> 41.8 us
  waiting for transfers between devices: 9.79 us -> 11.7 us
    pallas_call x16, Pallas kernels: 31.7 us -> 22.6 us  [call(): pl.pallas_call(kernel, in_specs=[pl.BlockSpec(memory_space=space[place])...]
    ppermute x3, starting transfers between devices: 3.83 us -> 10.1 us  [around(): lax.ppermute(value, 'pipe', [(source, (source + 2 * hop) % count) for sou...]
    ppermute x11, waiting for transfers between devices: 6.18 us -> 8.11 us  [swap(): lax.ppermute(value, axis, [(source, source ^ distance) for source in rang...]
    ppermute x10, starting transfers between devices: 19.5 us -> 20.6 us  [upward(): lax.ppermute(value, 'pipe', [(source, source + hop) for source in range(f...]
  transfers between devices with their start and end apart: 24 -> 24, of which waited for: 7 -> 10; matrix products, arithmetic and copies ran while one was open for 7% -> 7% of each run, Pallas kernels for 27% -> 19%
where the time goes in v12:
time: 84.7 us; the launch traced here: 84.3 us
  starting transfers between devices  41.8 us (49%)
  Pallas kernels  22.6 us (27%)
  waiting for transfers between devices  11.7 us (14%)
  matrix products  5.32 us (6%)
  local copies, waits for them, and re-layouts  2.3 us (3%)
    pallas_call x16, Pallas kernels, call(): pl.pallas_call(kernel, in_specs=[pl.BlockSpec(memory_space=space[place])...  22.6 us
    ppermute x10, starting transfers between devices, upward(): lax.ppermute(value, 'pipe', [(source, source + hop) for source in range(f...  20.6 us
    ppermute x11, starting transfers between devices, swap(): lax.ppermute(value, axis, [(source, source ^ distance) for source in rang...  11.1 us
    ppermute x3, starting transfers between devices, around(): lax.ppermute(value, 'pipe', [(source, (source + 2 * hop) % count) for sou...  10.1 us
    ppermute x11, waiting for transfers between devices, swap(): lax.ppermute(value, axis, [(source, source ^ distance) for source in rang...  8.11 us
    dot_general x2, matrix products, dot_nt(): lax.dot_general(a, b, (((1,), (1,)), ((), ())), preferred_element_type=f3...  5.32 us
    ppermute x3, waiting for transfers between devices, around(): lax.ppermute(value, 'pipe', [(source, (source + 2 * hop) % count) for sou...  3.6 us
    unnamed x18, local copies, waits for them, and re-layouts  2.26 us
  transfers between devices with their start and end apart: 24, of which 10 were waited for; matrix products, arithmetic and copies ran while one was open for 7% of the time, Pallas kernels for 19%

profile of v12, /device:TPU:0, one launch (start us, length us, event | category | flops | bytes accessed | tf_op | source)
XLA Modules:
  0.0 84.3 jit_solution(5178839390964494096)
XLA Ops:
  0.0 4.7 %shard_map.100 = (bf16[512,8192]{1,0:T(8,128)(2,1)S(1)}, bf16[2048,512]{1,0:T(8,128)(2,1)S(1)}, bf16[64,8192]{1,0:T(8,128)(2,1)S(1)}, bf16[16,8192]{1,0:T(8,128)(2,1)S(1)}) custom-call(bf16[32,512]{1,0:T(8,128)(2,1)} %bitcast.38, bf16[8,8192]{1,0:T(8,128)(2,1)} %bitcast.35, bf16[512,8192]{1,0:T(8,128)(2,1)} %bitcast.32, bf16[8192,512]{1,0:T(8,128)(2,1)} %bitcast.30), custom_call_target="tpu_custom_call" | custom-call | flops 134217728 | bytes 16777216 | tf_op jit(solution)/shard_map/pallas_call | solution.py:68
  4.8 2.4 %collective-permute-start = (bf16[16,8192]{1,0:T(8,128)(2,1)S(1)}, bf16[16,8192]{1,0:T(8,128)(2,1)S(1)}, u32[]{:S(2)}, u32[]{:S(2)}) collective-permute-start(bf16[16,8192]{1,0:T(8,128)(2,1)S(1)} %get-tuple-element.61), channel_id=1, source_target_pairs={{0,1},{2,3},{4,5},{6,7},{8,9},{10,11},{12,13},{14,15},{16,17},{18,... | collective-permute-start | bytes 786440 | tf_op jit(solution)/shard_map/ppermute | solution.py:45
  7.1 2.8 %shard_map.101.rest = bf16[6144,512]{1,0:T(8,128)(2,1)S(1)} custom-call(bf16[8192,512]{1,0:T(8,128)(2,1)} %bitcast.31), custom_call_target="tpu_custom_call" | custom-call | bytes 16777216 | tf_op jit(solution)/shard_map/pallas_call | solution.py:68
  11.0 2.4 %collective-permute-start.3 = (bf16[16,8192]{1,0:T(8,128)(2,1)S(1)}, bf16[16,8192]{1,0:T(8,128)(2,1)S(1)}, u32[]{:S(2)}, u32[]{:S(2)}) collective-permute-start(bf16[16,8192]{1,0:T(8,128)(2,1)S(1)} %constant_dynamic-update-slice_fusion.2), channel_id=1, source_target_pairs={{0,8},{8,0},{16,24},{24,16},{1,9},{9,1},{17,25},{25,17},{2,10},{10... | collective-permute-start | bytes 786440 | tf_op jit(solution)/shard_map/ppermute | solution.py:35
  13.4 1.5 %collective-permute-start.4 = (bf16[16,8192]{1,0:T(8,128)(2,1)S(1)}, bf16[16,8192]{1,0:T(8,128)(2,1)S(1)}, u32[]{:S(2)}, u32[]{:S(2)}) collective-permute-start(bf16[16,8192]{1,0:T(8,128)(2,1)S(1)} %constant_dynamic-update-slice_fusion.2), channel_id=1, source_target_pairs={{0,16},{8,24},{16,0},{24,8},{1,17},{9,25},{17,1},{25,9},{2,18},{10... | collective-permute-start | bytes 786440 | tf_op jit(solution)/shard_map/ppermute | solution.py:35
  15.0 4.5 %shard_map.103.refs_0_ = bf16[320,512]{1,0:T(8,128)(2,1)S(1)} custom-call(bf16[512,8192]{1,0:T(8,128)(2,1)} %cotangent.1, bf16[512,8192]{1,0:T(8,128)(2,1)S(1)} %get-tuple-element.66.expand), custom_call_target="tpu_custom_call" | custom-call | flops 2684354560 | bytes 8388608 | tf_op jit(solution)/shard_map/pallas_call | solution.py:68
  20.2 3.5 %shard_map.105.hidden = bf16[64,8192]{1,0:T(8,128)(2,1)S(1)} custom-call(bf16[32,512]{1,0:T(8,128)(2,1)} %bitcast.39, bf16[2048,512]{1,0:T(8,128)(2,1)S(1)} %get-tuple-element.64.head, bf16[6144,512]{1,0:T(8,128)(2,1)S(1)} %shard_map.101.rest), custom_call_target="tpu_custom_call" | custom-call | flops 536870912 | bytes 8388608 | tf_op jit(solution)/shard_map/pallas_call | solution.py:68
  23.7 1.8 %collective-permute-done.4 = bf16[16,8192]{1,0:T(8,128)(2,1)S(1)} collective-permute-done((bf16[16,8192]{1,0:T(8,128)(2,1)S(1)}, bf16[16,8192]{1,0:T(8,128)(2,1)S(1)}, u32[]{:S(2)}, u32[]{:S(2)}) %collective-permute-start.4) | collective-permute-done | bytes 262176 | tf_op jit(solution)/shard_map/ppermute | solution.py:35
  27.9 1.3 %slice-done.3 = s8[4194304]{0:T(1024)(128)(4,1)S(1)} async-done(((s8[8388608]{0:T(1024)(128)(4,1)}), s8[4194304]{0:T(1024)(128)(4,1)S(1)}, s32[]{:S(2)}) %slice-start.3) | async-done | bytes 4194328
  29.2 2.7 %fusion.5 = (bf16[64,512]{1,0:T(8,128)(2,1)S(1)}, f32[64,512]{1,0:T(8,128)S(1)}) fusion(f32[512]{0:T(512)S(1)} %convert_bitcast_fusion, bf16[64,8192]{1,0:T(8,128)(2,1)S(1)} %get-tuple-element.83, bf16[1,512,8192]{2,1,0:T(8,128)(2,1)S(1)} %bitcast.34), kind=kOutput, calls=%fused_computation.12 | convolution fusion | flops 536936448 | bytes 9635840 | tf_op jit(solution)/shard_map/dot_general | solution.py:28
  31.9 9.6 %collective-permute-start.10 = (bf16[64,512]{1,0:T(8,128)(2,1)S(1)}, bf16[64,512]{1,0:T(8,128)(2,1)S(1)}, u32[]{:S(2)}, u32[]{:S(2)}) collective-permute-start(bf16[64,512]{1,0:T(8,128)(2,1)S(1)} %get-tuple-element.102.refs_2_), channel_id=1, source_target_pairs={{0,6},{1,7},{8,14},{9,15},{16,22},{17,23},{24,30},{25,31}} | collective-permute-start | bytes 196616 | tf_op jit(solution)/shard_map/ppermute | solution.py:45
  41.5 1.3 %collective-permute-start.8 = (bf16[64,512]{1,0:T(8,128)(2,1)S(1)}, bf16[64,512]{1,0:T(8,128)(2,1)S(1)}, u32[]{:S(2)}, u32[]{:S(2)}) collective-permute-start(bf16[64,512]{1,0:T(8,128)(2,1)S(1)} %get-tuple-element.102.refs_2_), channel_id=1, source_target_pairs={{0,2},{1,3},{2,4},{3,5},{4,6},{5,7},{8,10},{9,11},{10,12},{11,13},... | collective-permute-start | bytes 196616 | tf_op jit(solution)/shard_map/ppermute | solution.py:45
  42.8 2.7 %collective-permute-start.9 = (bf16[64,512]{1,0:T(8,128)(2,1)S(1)}, bf16[64,512]{1,0:T(8,128)(2,1)S(1)}, u32[]{:S(2)}, u32[]{:S(2)}) collective-permute-start(bf16[64,512]{1,0:T(8,128)(2,1)S(1)} %get-tuple-element.102.refs_2_), channel_id=1, source_target_pairs={{0,4},{1,5},{2,6},{3,7},{8,12},{9,13},{10,14},{11,15},{16,20},{17,... | collective-permute-start | bytes 196616 | tf_op jit(solution)/shard_map/ppermute | solution.py:45
  46.3 2.7 %fusion.6.right = f32[64,512]{1,0:T(8,128)S(1)} fusion(bf16[64,8192]{1,0:T(8,128)(2,1)S(1)} %get-tuple-element.86, bf16[512,8192]{1,0:T(8,128)(2,1)S(1)} %bitcast.29), kind=kOutput, calls=%fused_computation.13 | convolution fusion | flops 536870912 | bytes 9568256 | tf_op jit(solution)/shard_map/dot_general | solution.py:28
  49.8 1.6 %collective-permute-start.12 = (bf16[80,512]{1,0:T(8,128)(2,1)S(1)}, bf16[80,512]{1,0:T(8,128)(2,1)S(1)}, u32[]{:S(2)}, u32[]{:S(2)}) collective-permute-start(bf16[80,512]{1,0:T(8,128)(2,1)S(1)} %pad_maximum_fusion.2.refs_6_), channel_id=1, source_target_pairs={{0,8},{8,0},{16,24},{24,16},{1,9},{9,1},{17,25},{25,17},{2,10},{10... | collective-permute-start | bytes 245768 | tf_op jit(solution)/shard_map/ppermute | solution.py:35
  51.3 1.5 %collective-permute-start.13 = (bf16[80,512]{1,0:T(8,128)(2,1)S(1)}, bf16[80,512]{1,0:T(8,128)(2,1)S(1)}, u32[]{:S(2)}, u32[]{:S(2)}) collective-permute-start(bf16[80,512]{1,0:T(8,128)(2,1)S(1)} %pad_maximum_fusion.2.refs_6_), channel_id=1, source_target_pairs={{0,16},{8,24},{16,0},{24,8},{1,17},{9,25},{17,1},{25,9},{2,18},{10... | collective-permute-start | bytes 245768 | tf_op jit(solution)/shard_map/ppermute | solution.py:35
  53.3 4.2 %shard_map.110.refs_1_ = bf16[192,512]{1,0:T(8,128)(2,1)S(1)} custom-call(bf16[512,8192]{1,0:T(8,128)(2,1)} %cotangent.1, bf16[512,8192]{1,0:T(8,128)(2,1)S(1)} %get-tuple-element.66.expand), custom_call_target="tpu_custom_call" | custom-call | flops 1610612736 | bytes 8388608 | tf_op jit(solution)/shard_map/pallas_call | solution.py:68
  59.0 1.5 %collective-permute-done.16.others = bf16[4,64,512]{2,1,0:T(8,128)(2,1)S(1)} collective-permute-done((bf16[4,64,512]{2,1,0:T(8,128)(2,1)S(1)}, bf16[4,64,512]{2,1,0:T(8,128)(2,1)S(1)}, u32[]{:S(2)}, u32[]{:S(2)}) %collective-permute-start.16) | collective-permute-done | bytes 262176 | tf_op jit(solution)/shard_map/ppermute | solution.py:35
  61.7 1.5 %collective-permute-start.18 = (bf16[32,512]{1,0:T(8,128)(2,1)S(1)}, bf16[32,512]{1,0:T(8,128)(2,1)S(1)}, u32[]{:S(2)}, u32[]{:S(2)}) collective-permute-start(bf16[32,512]{1,0:T(8,128)(2,1)S(1)} %shard_map.112.refs_2_), channel_id=1, source_target_pairs={{0,16},{8,24},{16,0},{24,8},{1,17},{9,25},{17,1},{25,9},{2,18},{10... | collective-permute-start | bytes 98312 | tf_op jit(solution)/shard_map/ppermute | solution.py:35
  64.0 1.2 %shard_map.113.early = f32[8,64]{1,0:T(8,128)S(1)} custom-call(f32[64,512]{1,0:T(8,128)S(1)} %get-tuple-element.118.left, f32[64,512]{1,0:T(8,128)S(1)} %fusion.6.right, bf16[4,64,512]{2,1,0:T(8,128)(2,1)S(1)} %collective-permute-done.16.others, bf16[320,512]{1,0:T(8,128)(2,1)S(1)} %shard_map.103.refs_0_, bf16[192,512]{1,0:T(8,128)(2,1)S(1)} %shard_map.110.refs_1_, ...), custom_call_target="tpu_custom_call" | custom-call | flops 268435456 | bytes 8388608 | tf_op jit(solution)/shard_map/pallas_call | solution.py:68
  65.6 2.4 %collective-permute-done.19.refs_5_ = bf16[32,512]{1,0:T(8,128)(2,1)S(1)} collective-permute-done((bf16[32,512]{1,0:T(8,128)(2,1)S(1)}, bf16[32,512]{1,0:T(8,128)(2,1)S(1)}, u32[]{:S(2)}, u32[]{:S(2)}) %collective-permute-start.19) | collective-permute-done | bytes 32800 | tf_op jit(solution)/shard_map/ppermute | solution.py:35
  68.7 1.2 %collective-permute-done.20 = f32[8,64]{1,0:T(8,128)S(1)} collective-permute-done((f32[8,64]{1,0:T(8,128)S(1)}, f32[8,64]{1,0:T(8,128)S(1)}, u32[]{:S(2)}, u32[]{:S(2)}) %collective-permute-start.20) | collective-permute-done | bytes 2080 | tf_op jit(solution)/shard_map/ppermute | solution.py:35
  69.9 10.1 %collective-permute-start.22 = (f32[8,64]{1,0:T(8,128)S(1)}, f32[8,64]{1,0:T(8,128)S(1)}, u32[]{:S(2)}, u32[]{:S(2)}) collective-permute-start(f32[8,64]{1,0:T(8,128)S(1)} %add.3.refs_0_), channel_id=1, source_target_pairs={{0,4},{1,5},{2,6},{3,7},{4,0},{5,1},{6,2},{7,3},{8,12},{9,13},{10,... | collective-permute-start | bytes 6152 | tf_op jit(solution)/shard_map/ppermute | solution.py:52
  81.6 2.0 %collective-permute-done.23.refs_3_ = f32[8,64]{1,0:T(8,128)S(1)} collective-permute-done((f32[8,64]{1,0:T(8,128)S(1)}, f32[8,64]{1,0:T(8,128)S(1)}, u32[]{:S(2)}, u32[]{:S(2)}) %collective-permute-start.23) | collective-permute-done | bytes 2080 | tf_op jit(solution)/shard_map/ppermute | solution.py:52
  (71 shorter events, 12.9 us)
Async XLA Ops:
  4.8 5.3 %collective-permute-start = (bf16[16,8192]{1,0:T(8,128)(2,1)S(1)}, bf16[16,8192]{1,0:T(8,128)(2,1)S(1)}, u32[]{:S(2)}, u32[]{:S(2)}) collective-permute-start(bf16[16,8192]{1,0:T(8,128)(2,1)S(1)} %get-tuple-element.61), channel_id=1, source_target_pairs={{0,1},{2,3},{4,5},{6,7},{8,9},{10,11},{12,13},{14,15},{16,17},{18,... | collective-permute-start | bytes 786440 | tf_op jit(solution)/shard_map/ppermute | solution.py:45
  10.1 9.3 %collective-permute-start.1 = (bf16[32,8192]{1,0:T(8,128)(2,1)S(1)}, bf16[32,8192]{1,0:T(8,128)(2,1)S(1)}, u32[]{:S(2)}, u32[]{:S(2)}) collective-permute-start(bf16[32,8192]{1,0:T(8,128)(2,1)S(1)} %constant_dynamic-update-slice_fusion), channel_id=1, source_target_pairs={{1,2},{3,4},{5,6},{9,10},{11,12},{13,14},{17,18},{19,20},{21,22},{... | collective-permute-start | bytes 1572872 | tf_op jit(solution)/shard_map/ppermute | solution.py:45
  11.0 12.7 %collective-permute-start.3 = (bf16[16,8192]{1,0:T(8,128)(2,1)S(1)}, bf16[16,8192]{1,0:T(8,128)(2,1)S(1)}, u32[]{:S(2)}, u32[]{:S(2)}) collective-permute-start(bf16[16,8192]{1,0:T(8,128)(2,1)S(1)} %constant_dynamic-update-slice_fusion.2), channel_id=1, source_target_pairs={{0,8},{8,0},{16,24},{24,16},{1,9},{9,1},{17,25},{25,17},{2,10},{10... | collective-permute-start | bytes 786440 | tf_op jit(solution)/shard_map/ppermute | solution.py:35
  13.4 12.1 %collective-permute-start.4 = (bf16[16,8192]{1,0:T(8,128)(2,1)S(1)}, bf16[16,8192]{1,0:T(8,128)(2,1)S(1)}, u32[]{:S(2)}, u32[]{:S(2)}) collective-permute-start(bf16[16,8192]{1,0:T(8,128)(2,1)S(1)} %constant_dynamic-update-slice_fusion.2), channel_id=1, source_target_pairs={{0,16},{8,24},{16,0},{24,8},{1,17},{9,25},{17,1},{25,9},{2,18},{10... | collective-permute-start | bytes 786440 | tf_op jit(solution)/shard_map/ppermute | solution.py:35
  14.9 10.8 %collective-permute-start.5 = (bf16[16,8192]{1,0:T(8,128)(2,1)S(1)}, bf16[16,8192]{1,0:T(8,128)(2,1)S(1)}, u32[]{:S(2)}, u32[]{:S(2)}) collective-permute-start(bf16[16,8192]{1,0:T(8,128)(2,1)S(1)} %constant_dynamic-update-slice_fusion.2), channel_id=1, source_target_pairs={{0,24},{8,16},{16,8},{24,0},{1,25},{9,17},{17,9},{25,1},{2,26},{10... | collective-permute-start | bytes 786440 | tf_op jit(solution)/shard_map/ppermute | solution.py:35
  19.5 6.3 %collective-permute-start.2 = (bf16[32,8192]{1,0:T(8,128)(2,1)S(1)}, bf16[32,8192]{1,0:T(8,128)(2,1)S(1)}, u32[]{:S(2)}, u32[]{:S(2)}) collective-permute-start(bf16[32,8192]{1,0:T(8,128)(2,1)S(1)} %get-tuple-element.70), channel_id=1, source_target_pairs={{2,3},{4,5},{6,7},{10,11},{12,13},{14,15},{18,19},{20,21},{22,23},... | collective-permute-start | bytes 1572872 | tf_op jit(solution)/shard_map/ppermute | solution.py:45
  25.9 19.7 %collective-permute-start.6 = (bf16[32,8192]{1,0:T(8,128)(2,1)S(1)}, bf16[32,8192]{1,0:T(8,128)(2,1)S(1)}, u32[]{:S(2)}, u32[]{:S(2)}) collective-permute-start(bf16[32,8192]{1,0:T(8,128)(2,1)S(1)} %get-tuple-element.80), channel_id=1, source_target_pairs={{3,4},{5,6},{11,12},{13,14},{19,20},{21,22},{27,28},{29,30}} | collective-permute-start | bytes 1572872 | tf_op jit(solution)/shard_map/ppermute | solution.py:45
  31.9 17.1 %collective-permute-start.10 = (bf16[64,512]{1,0:T(8,128)(2,1)S(1)}, bf16[64,512]{1,0:T(8,128)(2,1)S(1)}, u32[]{:S(2)}, u32[]{:S(2)}) collective-permute-start(bf16[64,512]{1,0:T(8,128)(2,1)S(1)} %get-tuple-element.102.refs_2_), channel_id=1, source_target_pairs={{0,6},{1,7},{8,14},{9,15},{16,22},{17,23},{24,30},{25,31}} | collective-permute-start | bytes 196616 | tf_op jit(solution)/shard_map/ppermute | solution.py:45
  41.5 7.5 %collective-permute-start.8 = (bf16[64,512]{1,0:T(8,128)(2,1)S(1)}, bf16[64,512]{1,0:T(8,128)(2,1)S(1)}, u32[]{:S(2)}, u32[]{:S(2)}) collective-permute-start(bf16[64,512]{1,0:T(8,128)(2,1)S(1)} %get-tuple-element.102.refs_2_), channel_id=1, source_target_pairs={{0,2},{1,3},{2,4},{3,5},{4,6},{5,7},{8,10},{9,11},{10,12},{11,13},... | collective-permute-start | bytes 196616 | tf_op jit(solution)/shard_map/ppermute | solution.py:45
  42.8 6.2 %collective-permute-start.9 = (bf16[64,512]{1,0:T(8,128)(2,1)S(1)}, bf16[64,512]{1,0:T(8,128)(2,1)S(1)}, u32[]{:S(2)}, u32[]{:S(2)}) collective-permute-start(bf16[64,512]{1,0:T(8,128)(2,1)S(1)} %get-tuple-element.102.refs_2_), channel_id=1, source_target_pairs={{0,4},{1,5},{2,6},{3,7},{8,12},{9,13},{10,14},{11,15},{16,20},{17,... | collective-permute-start | bytes 196616 | tf_op jit(solution)/shard_map/ppermute | solution.py:45
  45.6 3.4 %collective-permute-start.7 = (bf16[32,8192]{1,0:T(8,128)(2,1)S(1)}, bf16[32,8192]{1,0:T(8,128)(2,1)S(1)}, u32[]{:S(2)}, u32[]{:S(2)}) collective-permute-start(bf16[32,8192]{1,0:T(8,128)(2,1)S(1)} %get-tuple-element.85), channel_id=1, source_target_pairs={{4,5},{6,7},{12,13},{14,15},{20,21},{22,23},{28,29},{30,31}} | collective-permute-start | bytes 1572872 | tf_op jit(solution)/shard_map/ppermute | solution.py:45
  49.0 9.1 %collective-permute-start.11 = (bf16[32,8192]{1,0:T(8,128)(2,1)S(1)}, bf16[32,8192]{1,0:T(8,128)(2,1)S(1)}, u32[]{:S(2)}, u32[]{:S(2)}) collective-permute-start(bf16[32,8192]{1,0:T(8,128)(2,1)S(1)} %get-tuple-element.91), channel_id=1, source_target_pairs={{5,6},{13,14},{21,22},{29,30}} | collective-permute-start | bytes 1572872 | tf_op jit(solution)/shard_map/ppermute | solution.py:45
  49.8 7.8 %collective-permute-start.12 = (bf16[80,512]{1,0:T(8,128)(2,1)S(1)}, bf16[80,512]{1,0:T(8,128)(2,1)S(1)}, u32[]{:S(2)}, u32[]{:S(2)}) collective-permute-start(bf16[80,512]{1,0:T(8,128)(2,1)S(1)} %pad_maximum_fusion.2.refs_6_), channel_id=1, source_target_pairs={{0,8},{8,0},{16,24},{24,16},{1,9},{9,1},{17,25},{25,17},{2,10},{10... | collective-permute-start | bytes 245768 | tf_op jit(solution)/shard_map/ppermute | solution.py:35
  51.3 6.2 %collective-permute-start.13 = (bf16[80,512]{1,0:T(8,128)(2,1)S(1)}, bf16[80,512]{1,0:T(8,128)(2,1)S(1)}, u32[]{:S(2)}, u32[]{:S(2)}) collective-permute-start(bf16[80,512]{1,0:T(8,128)(2,1)S(1)} %pad_maximum_fusion.2.refs_6_), channel_id=1, source_target_pairs={{0,16},{8,24},{16,0},{24,8},{1,17},{9,25},{17,1},{25,9},{2,18},{10... | collective-permute-start | bytes 245768 | tf_op jit(solution)/shard_map/ppermute | solution.py:35
  52.8 5.3 %collective-permute-start.14 = (bf16[80,512]{1,0:T(8,128)(2,1)S(1)}, bf16[80,512]{1,0:T(8,128)(2,1)S(1)}, u32[]{:S(2)}, u32[]{:S(2)}) collective-permute-start(bf16[80,512]{1,0:T(8,128)(2,1)S(1)} %pad_maximum_fusion.2.refs_6_), channel_id=1, source_target_pairs={{0,24},{8,16},{16,8},{24,0},{1,25},{9,17},{17,9},{25,1},{2,26},{10... | collective-permute-start | bytes 245768 | tf_op jit(solution)/shard_map/ppermute | solution.py:35
  58.2 2.4 %collective-permute-start.15 = (bf16[32,8192]{1,0:T(8,128)(2,1)S(1)}, bf16[32,8192]{1,0:T(8,128)(2,1)S(1)}, u32[]{:S(2)}, u32[]{:S(2)}) collective-permute-start(bf16[32,8192]{1,0:T(8,128)(2,1)S(1)} %get-tuple-element.98), channel_id=1, source_target_pairs={{6,7},{14,15},{22,23},{30,31}} | collective-permute-start | bytes 1572872 | tf_op jit(solution)/shard_map/ppermute | solution.py:45
  58.9 1.6 %collective-permute-start.16 = (bf16[4,64,512]{2,1,0:T(8,128)(2,1)S(1)}, bf16[4,64,512]{2,1,0:T(8,128)(2,1)S(1)}, u32[]{:S(2)}, u32[]{:S(2)}) collective-permute-start(bf16[4,64,512]{2,1,0:T(8,128)(2,1)S(1)} %pad_maximum_fusion.1), channel_id=1, source_target_pairs={{0,1},{1,0},{2,3},{3,2},{4,5},{5,4},{6,7},{7,6},{8,9},{9,8},{10,11... | collective-permute-start | bytes 786440 | tf_op jit(solution)/shard_map/ppermute | solution.py:35
  60.5 4.7 %collective-permute-start.17 = (bf16[32,512]{1,0:T(8,128)(2,1)S(1)}, bf16[32,512]{1,0:T(8,128)(2,1)S(1)}, u32[]{:S(2)}, u32[]{:S(2)}) collective-permute-start(bf16[32,512]{1,0:T(8,128)(2,1)S(1)} %shard_map.112.refs_2_), channel_id=1, source_target_pairs={{0,8},{8,0},{16,24},{24,16},{1,9},{9,1},{17,25},{25,17},{2,10},{10... | collective-permute-start | bytes 98312 | tf_op jit(solution)/shard_map/ppermute | solution.py:35
  61.7 3.9 %collective-permute-start.18 = (bf16[32,512]{1,0:T(8,128)(2,1)S(1)}, bf16[32,512]{1,0:T(8,128)(2,1)S(1)}, u32[]{:S(2)}, u32[]{:S(2)}) collective-permute-start(bf16[32,512]{1,0:T(8,128)(2,1)S(1)} %shard_map.112.refs_2_), channel_id=1, source_target_pairs={{0,16},{8,24},{16,0},{24,8},{1,17},{9,25},{17,1},{25,9},{2,18},{10... | collective-permute-start | bytes 98312 | tf_op jit(solution)/shard_map/ppermute | solution.py:35
  63.2 4.8 %collective-permute-start.19 = (bf16[32,512]{1,0:T(8,128)(2,1)S(1)}, bf16[32,512]{1,0:T(8,128)(2,1)S(1)}, u32[]{:S(2)}, u32[]{:S(2)}) collective-permute-start(bf16[32,512]{1,0:T(8,128)(2,1)S(1)} %shard_map.112.refs_2_), channel_id=1, source_target_pairs={{0,24},{8,16},{16,8},{24,0},{1,25},{9,17},{17,9},{25,1},{2,26},{10... | collective-permute-start | bytes 98312 | tf_op jit(solution)/shard_map/ppermute | solution.py:35
  68.7 1.2 %collective-permute-start.20 = (f32[8,64]{1,0:T(8,128)S(1)}, f32[8,64]{1,0:T(8,128)S(1)}, u32[]{:S(2)}, u32[]{:S(2)}) collective-permute-start(f32[8,64]{1,0:T(8,128)S(1)} %shard_map.114), channel_id=1, source_target_pairs={{0,1},{1,0},{2,3},{3,2},{4,5},{5,4},{6,7},{7,6},{8,9},{9,8},{10,11... | collective-permute-start | bytes 6152 | tf_op jit(solution)/shard_map/ppermute | solution.py:35
  69.9 11.1 %collective-permute-start.21 = (f32[8,64]{1,0:T(8,128)S(1)}, f32[8,64]{1,0:T(8,128)S(1)}, u32[]{:S(2)}, u32[]{:S(2)}) collective-permute-start(f32[8,64]{1,0:T(8,128)S(1)} %add.3.refs_0_), channel_id=1, source_target_pairs={{0,2},{1,3},{2,4},{3,5},{4,6},{5,7},{6,0},{7,1},{8,10},{9,11},{10,... | collective-permute-start | bytes 6152 | tf_op jit(solution)/shard_map/ppermute | solution.py:52
  69.9 11.7 %collective-permute-start.22 = (f32[8,64]{1,0:T(8,128)S(1)}, f32[8,64]{1,0:T(8,128)S(1)}, u32[]{:S(2)}, u32[]{:S(2)}) collective-permute-start(f32[8,64]{1,0:T(8,128)S(1)} %add.3.refs_0_), channel_id=1, source_target_pairs={{0,4},{1,5},{2,6},{3,7},{4,0},{5,1},{6,2},{7,3},{8,12},{9,13},{10,... | collective-permute-start | bytes 6152 | tf_op jit(solution)/shard_map/ppermute | solution.py:52
  80.0 3.6 %collective-permute-start.23 = (f32[8,64]{1,0:T(8,128)S(1)}, f32[8,64]{1,0:T(8,128)S(1)}, u32[]{:S(2)}, u32[]{:S(2)}) collective-permute-start(f32[8,64]{1,0:T(8,128)S(1)} %add.3.refs_0_), channel_id=1, source_target_pairs={{0,6},{1,7},{2,0},{3,1},{4,2},{5,3},{6,4},{7,5},{8,14},{9,15},{10,... | collective-permute-start | bytes 6152 | tf_op jit(solution)/shard_map/ppermute | solution.py:52
  (8 other events, 66.9 us)

commit v13 on v12

--- a/solution.py
+++ b/solution.py
@@ -47,11 +47,9 @@
     )
 
 
-def around(value, hop):
-    count = lax.axis_size("pipe")
-    return lax.ppermute(
-        value, "pipe", [(source, (source + 2 * hop) % count) for source in range(count)]
-    )
+def between(value, chips):
+    pairs = [(2 * source + core, 2 * target + core) for source, target in chips for core in (0, 1)]
+    return lax.ppermute(value, "pipe", pairs)
 
 
 def tie(values, token):
@@ -456,11 +454,16 @@
         moved=weight_bytes // 8,
     )
     sums = sums + swap(sums, "pipe", 1)
-    parts = [sums] + [around(sums, hop) for hop in range(1, chips)]
+    below = [between(sums, [(z, (z + hop) % top) for z in range(top)]) for hop in range(1, top)]
+    for part in below:
+        sums = sums + part
+    crossing = [[(top, z)] for z in range(top)]
+    crossing[-1].append((top - 1, top))
+    parts = [sums] + [between(sums, chosen) for chosen in crossing]
     (scores,) = call(
         functools.partial(final_kernel, q_dev),
         (query_example[None], *parts),
-        "v" * (1 + chips),
+        "v" * (1 + len(parts)),
         [((ex_dev, columns * q_dev), f32)],
         kept=jax.ShapeDtypeStruct,
     )

time: 84.7 us -> 89.1 us (1.052)
  waiting for transfers between devices: 11.7 us -> 14.9 us
  starting transfers between devices: 41.8 us -> 42.7 us
    ppermute x3 -> x5, waiting for transfers between devices: 3.6 us -> 6.78 us  [between(): return lax.ppermute(value, 'pipe', pairs)]
    ppermute x3 -> x5, starting transfers between devices: 10.1 us -> 11.1 us  [between(): return lax.ppermute(value, 'pipe', pairs)]
  transfers between devices with their start and end apart: 24 -> 26, of which waited for: 10 -> 9; matrix products, arithmetic and copies ran while one was open for 7% -> 6% of each run, Pallas kernels for 19% -> 19%
where the time goes in v13:
time: 89.1 us; the launch traced here: 88.5 us
  starting transfers between devices  42.7 us (48%)
  Pallas kernels  22.6 us (25%)
  waiting for transfers between devices  14.9 us (17%)
  matrix products  5.32 us (6%)
  local copies, waits for them, and re-layouts  2.3 us (3%)
    pallas_call x16, Pallas kernels, call(): pl.pallas_call(kernel, in_specs=[pl.BlockSpec(memory_space=space[place])...  22.6 us
    ppermute x10, starting transfers between devices, upward(): lax.ppermute(value, 'pipe', [(source, source + hop) for source in range(f...  20.6 us
    ppermute x5, starting transfers between devices, between(): return lax.ppermute(value, 'pipe', pairs)  11.1 us
    ppermute x11, starting transfers between devices, swap(): lax.ppermute(value, axis, [(source, source ^ distance) for source in rang...  11.1 us
    ppermute x11, waiting for transfers between devices, swap(): lax.ppermute(value, axis, [(source, source ^ distance) for source in rang...  8.11 us
    ppermute x5, waiting for transfers between devices, between(): return lax.ppermute(value, 'pipe', pairs)  6.78 us
    dot_general x2, matrix products, dot_nt(): lax.dot_general(a, b, (((1,), (1,)), ((), ())), preferred_element_type=f3...  5.32 us
    unnamed x18, local copies, waits for them, and re-layouts  2.26 us
  transfers between devices with their start and end apart: 26, of which 9 were waited for; matrix products, arithmetic and copies ran while one was open for 6% of the time, Pallas kernels for 19%

profile of v13, /device:TPU:0, one launch (start us, length us, event | category | flops | bytes accessed | tf_op | source)
XLA Modules:
  0.0 88.5 jit_solution(16357132207744673933)
XLA Ops:
  0.0 4.7 %shard_map.100 = (bf16[512,8192]{1,0:T(8,128)(2,1)S(1)}, bf16[2048,512]{1,0:T(8,128)(2,1)S(1)}, bf16[64,8192]{1,0:T(8,128)(2,1)S(1)}, bf16[16,8192]{1,0:T(8,128)(2,1)S(1)}) custom-call(bf16[32,512]{1,0:T(8,128)(2,1)} %bitcast.38, bf16[8,8192]{1,0:T(8,128)(2,1)} %bitcast.35, bf16[512,8192]{1,0:T(8,128)(2,1)} %bitcast.32, bf16[8192,512]{1,0:T(8,128)(2,1)} %bitcast.30), custom_call_target="tpu_custom_call" | custom-call | flops 134217728 | bytes 16777216 | tf_op jit(solution)/shard_map/pallas_call | solution.py:66
  4.8 2.4 %collective-permute-start = (bf16[16,8192]{1,0:T(8,128)(2,1)S(1)}, bf16[16,8192]{1,0:T(8,128)(2,1)S(1)}, u32[]{:S(2)}, u32[]{:S(2)}) collective-permute-start(bf16[16,8192]{1,0:T(8,128)(2,1)S(1)} %get-tuple-element.61), channel_id=1, source_target_pairs={{0,1},{2,3},{4,5},{6,7},{8,9},{10,11},{12,13},{14,15},{16,17},{18,... | collective-permute-start | bytes 786440 | tf_op jit(solution)/shard_map/ppermute | solution.py:45
  7.1 2.8 %shard_map.101.rest = bf16[6144,512]{1,0:T(8,128)(2,1)S(1)} custom-call(bf16[8192,512]{1,0:T(8,128)(2,1)} %bitcast.31), custom_call_target="tpu_custom_call" | custom-call | bytes 16777216 | tf_op jit(solution)/shard_map/pallas_call | solution.py:66
  11.0 2.4 %collective-permute-start.3 = (bf16[16,8192]{1,0:T(8,128)(2,1)S(1)}, bf16[16,8192]{1,0:T(8,128)(2,1)S(1)}, u32[]{:S(2)}, u32[]{:S(2)}) collective-permute-start(bf16[16,8192]{1,0:T(8,128)(2,1)S(1)} %constant_dynamic-update-slice_fusion.2), channel_id=1, source_target_pairs={{0,8},{8,0},{16,24},{24,16},{1,9},{9,1},{17,25},{25,17},{2,10},{10... | collective-permute-start | bytes 786440 | tf_op jit(solution)/shard_map/ppermute | solution.py:35
  13.4 1.5 %collective-permute-start.4 = (bf16[16,8192]{1,0:T(8,128)(2,1)S(1)}, bf16[16,8192]{1,0:T(8,128)(2,1)S(1)}, u32[]{:S(2)}, u32[]{:S(2)}) collective-permute-start(bf16[16,8192]{1,0:T(8,128)(2,1)S(1)} %constant_dynamic-update-slice_fusion.2), channel_id=1, source_target_pairs={{0,16},{8,24},{16,0},{24,8},{1,17},{9,25},{17,1},{25,9},{2,18},{10... | collective-permute-start | bytes 786440 | tf_op jit(solution)/shard_map/ppermute | solution.py:35
  15.0 4.5 %shard_map.103.refs_0_ = bf16[320,512]{1,0:T(8,128)(2,1)S(1)} custom-call(bf16[512,8192]{1,0:T(8,128)(2,1)} %cotangent.1, bf16[512,8192]{1,0:T(8,128)(2,1)S(1)} %get-tuple-element.66.expand), custom_call_target="tpu_custom_call" | custom-call | flops 2684354560 | bytes 8388608 | tf_op jit(solution)/shard_map/pallas_call | solution.py:66
  20.2 3.5 %shard_map.105.hidden = bf16[64,8192]{1,0:T(8,128)(2,1)S(1)} custom-call(bf16[32,512]{1,0:T(8,128)(2,1)} %bitcast.39, bf16[2048,512]{1,0:T(8,128)(2,1)S(1)} %get-tuple-element.64.head, bf16[6144,512]{1,0:T(8,128)(2,1)S(1)} %shard_map.101.rest), custom_call_target="tpu_custom_call" | custom-call | flops 536870912 | bytes 8388608 | tf_op jit(solution)/shard_map/pallas_call | solution.py:66
  23.7 1.8 %collective-permute-done.4 = bf16[16,8192]{1,0:T(8,128)(2,1)S(1)} collective-permute-done((bf16[16,8192]{1,0:T(8,128)(2,1)S(1)}, bf16[16,8192]{1,0:T(8,128)(2,1)S(1)}, u32[]{:S(2)}, u32[]{:S(2)}) %collective-permute-start.4) | collective-permute-done | bytes 262176 | tf_op jit(solution)/shard_map/ppermute | solution.py:35
  27.9 1.3 %slice-done.3 = s8[4194304]{0:T(1024)(128)(4,1)S(1)} async-done(((s8[8388608]{0:T(1024)(128)(4,1)}), s8[4194304]{0:T(1024)(128)(4,1)S(1)}, s32[]{:S(2)}) %slice-start.3) | async-done | bytes 4194328
  29.2 2.7 %fusion.5 = (bf16[64,512]{1,0:T(8,128)(2,1)S(1)}, f32[64,512]{1,0:T(8,128)S(1)}) fusion(f32[512]{0:T(512)S(1)} %convert_bitcast_fusion, bf16[64,8192]{1,0:T(8,128)(2,1)S(1)} %get-tuple-element.83, bf16[1,512,8192]{2,1,0:T(8,128)(2,1)S(1)} %bitcast.34), kind=kOutput, calls=%fused_computation.13 | convolution fusion | flops 536936448 | bytes 9635840 | tf_op jit(solution)/shard_map/dot_general | solution.py:28
  31.9 9.6 %collective-permute-start.10 = (bf16[64,512]{1,0:T(8,128)(2,1)S(1)}, bf16[64,512]{1,0:T(8,128)(2,1)S(1)}, u32[]{:S(2)}, u32[]{:S(2)}) collective-permute-start(bf16[64,512]{1,0:T(8,128)(2,1)S(1)} %get-tuple-element.102.refs_2_), channel_id=1, source_target_pairs={{0,6},{1,7},{8,14},{9,15},{16,22},{17,23},{24,30},{25,31}} | collective-permute-start | bytes 196616 | tf_op jit(solution)/shard_map/ppermute | solution.py:45
  41.5 1.3 %collective-permute-start.8 = (bf16[64,512]{1,0:T(8,128)(2,1)S(1)}, bf16[64,512]{1,0:T(8,128)(2,1)S(1)}, u32[]{:S(2)}, u32[]{:S(2)}) collective-permute-start(bf16[64,512]{1,0:T(8,128)(2,1)S(1)} %get-tuple-element.102.refs_2_), channel_id=1, source_target_pairs={{0,2},{1,3},{2,4},{3,5},{4,6},{5,7},{8,10},{9,11},{10,12},{11,13},... | collective-permute-start | bytes 196616 | tf_op jit(solution)/shard_map/ppermute | solution.py:45
  42.8 2.7 %collective-permute-start.9 = (bf16[64,512]{1,0:T(8,128)(2,1)S(1)}, bf16[64,512]{1,0:T(8,128)(2,1)S(1)}, u32[]{:S(2)}, u32[]{:S(2)}) collective-permute-start(bf16[64,512]{1,0:T(8,128)(2,1)S(1)} %get-tuple-element.102.refs_2_), channel_id=1, source_target_pairs={{0,4},{1,5},{2,6},{3,7},{8,12},{9,13},{10,14},{11,15},{16,20},{17,... | collective-permute-start | bytes 196616 | tf_op jit(solution)/shard_map/ppermute | solution.py:45
  46.3 2.7 %fusion.6.right = f32[64,512]{1,0:T(8,128)S(1)} fusion(bf16[64,8192]{1,0:T(8,128)(2,1)S(1)} %get-tuple-element.86, bf16[512,8192]{1,0:T(8,128)(2,1)S(1)} %bitcast.29), kind=kOutput, calls=%fused_computation.14 | convolution fusion | flops 536870912 | bytes 9568256 | tf_op jit(solution)/shard_map/dot_general | solution.py:28
  49.8 1.6 %collective-permute-start.12 = (bf16[80,512]{1,0:T(8,128)(2,1)S(1)}, bf16[80,512]{1,0:T(8,128)(2,1)S(1)}, u32[]{:S(2)}, u32[]{:S(2)}) collective-permute-start(bf16[80,512]{1,0:T(8,128)(2,1)S(1)} %pad_maximum_fusion.2.refs_6_), channel_id=1, source_target_pairs={{0,8},{8,0},{16,24},{24,16},{1,9},{9,1},{17,25},{25,17},{2,10},{10... | collective-permute-start | bytes 245768 | tf_op jit(solution)/shard_map/ppermute | solution.py:35
  51.3 1.5 %collective-permute-start.13 = (bf16[80,512]{1,0:T(8,128)(2,1)S(1)}, bf16[80,512]{1,0:T(8,128)(2,1)S(1)}, u32[]{:S(2)}, u32[]{:S(2)}) collective-permute-start(bf16[80,512]{1,0:T(8,128)(2,1)S(1)} %pad_maximum_fusion.2.refs_6_), channel_id=1, source_target_pairs={{0,16},{8,24},{16,0},{24,8},{1,17},{9,25},{17,1},{25,9},{2,18},{10... | collective-permute-start | bytes 245768 | tf_op jit(solution)/shard_map/ppermute | solution.py:35
  53.3 4.2 %shard_map.110.refs_1_ = bf16[192,512]{1,0:T(8,128)(2,1)S(1)} custom-call(bf16[512,8192]{1,0:T(8,128)(2,1)} %cotangent.1, bf16[512,8192]{1,0:T(8,128)(2,1)S(1)} %get-tuple-element.66.expand), custom_call_target="tpu_custom_call" | custom-call | flops 1610612736 | bytes 8388608 | tf_op jit(solution)/shard_map/pallas_call | solution.py:66
  59.0 1.5 %collective-permute-done.16.others = bf16[4,64,512]{2,1,0:T(8,128)(2,1)S(1)} collective-permute-done((bf16[4,64,512]{2,1,0:T(8,128)(2,1)S(1)}, bf16[4,64,512]{2,1,0:T(8,128)(2,1)S(1)}, u32[]{:S(2)}, u32[]{:S(2)}) %collective-permute-start.16) | collective-permute-done | bytes 262176 | tf_op jit(solution)/shard_map/ppermute | solution.py:35
  61.7 1.5 %collective-permute-start.18 = (bf16[32,512]{1,0:T(8,128)(2,1)S(1)}, bf16[32,512]{1,0:T(8,128)(2,1)S(1)}, u32[]{:S(2)}, u32[]{:S(2)}) collective-permute-start(bf16[32,512]{1,0:T(8,128)(2,1)S(1)} %shard_map.112.refs_2_), channel_id=1, source_target_pairs={{0,16},{8,24},{16,0},{24,8},{1,17},{9,25},{17,1},{25,9},{2,18},{10... | collective-permute-start | bytes 98312 | tf_op jit(solution)/shard_map/ppermute | solution.py:35
  65.6 2.4 %collective-permute-done.19.refs_5_ = bf16[32,512]{1,0:T(8,128)(2,1)S(1)} collective-permute-done((bf16[32,512]{1,0:T(8,128)(2,1)S(1)}, bf16[32,512]{1,0:T(8,128)(2,1)S(1)}, u32[]{:S(2)}, u32[]{:S(2)}) %collective-permute-start.19) | collective-permute-done | bytes 32800 | tf_op jit(solution)/shard_map/ppermute | solution.py:35
  69.9 1.9 %collective-permute-start.21 = (f32[8,64]{1,0:T(8,128)S(1)}, f32[8,64]{1,0:T(8,128)S(1)}, u32[]{:S(2)}, u32[]{:S(2)}) collective-permute-start(f32[8,64]{1,0:T(8,128)S(1)} %add.9), channel_id=1, source_target_pairs={{0,2},{1,3},{2,4},{3,5},{4,0},{5,1},{8,10},{9,11},{10,12},{11,13},... | collective-permute-start | bytes 6152 | tf_op jit(solution)/shard_map/ppermute | solution.py:52
  71.8 6.6 %collective-permute-start.22 = (f32[8,64]{1,0:T(8,128)S(1)}, f32[8,64]{1,0:T(8,128)S(1)}, u32[]{:S(2)}, u32[]{:S(2)}) collective-permute-start(f32[8,64]{1,0:T(8,128)S(1)} %add.9), channel_id=1, source_target_pairs={{0,4},{1,5},{2,0},{3,1},{4,2},{5,3},{8,12},{9,13},{10,8},{11,9},{1... | collective-permute-start | bytes 6152 | tf_op jit(solution)/shard_map/ppermute | solution.py:52
  78.4 2.1 %collective-permute-done.22 = f32[8,64]{1,0:T(8,128)S(1)} collective-permute-done((f32[8,64]{1,0:T(8,128)S(1)}, f32[8,64]{1,0:T(8,128)S(1)}, u32[]{:S(2)}, u32[]{:S(2)}) %collective-permute-start.22) | collective-permute-done | bytes 2080 | tf_op jit(solution)/shard_map/ppermute | solution.py:52
  83.1 4.7 %collective-permute-done.23.refs_1_ = f32[8,64]{1,0:T(8,128)S(1)} collective-permute-done((f32[8,64]{1,0:T(8,128)S(1)}, f32[8,64]{1,0:T(8,128)S(1)}, u32[]{:S(2)}, u32[]{:S(2)}) %collective-permute-start.23) | collective-permute-done | bytes 2080 | tf_op jit(solution)/shard_map/ppermute | solution.py:52
  (76 shorter events, 16.3 us)
Async XLA Ops:
  4.8 5.3 %collective-permute-start = (bf16[16,8192]{1,0:T(8,128)(2,1)S(1)}, bf16[16,8192]{1,0:T(8,128)(2,1)S(1)}, u32[]{:S(2)}, u32[]{:S(2)}) collective-permute-start(bf16[16,8192]{1,0:T(8,128)(2,1)S(1)} %get-tuple-element.61), channel_id=1, source_target_pairs={{0,1},{2,3},{4,5},{6,7},{8,9},{10,11},{12,13},{14,15},{16,17},{18,... | collective-permute-start | bytes 786440 | tf_op jit(solution)/shard_map/ppermute | solution.py:45
  10.1 9.3 %collective-permute-start.1 = (bf16[32,8192]{1,0:T(8,128)(2,1)S(1)}, bf16[32,8192]{1,0:T(8,128)(2,1)S(1)}, u32[]{:S(2)}, u32[]{:S(2)}) collective-permute-start(bf16[32,8192]{1,0:T(8,128)(2,1)S(1)} %constant_dynamic-update-slice_fusion), channel_id=1, source_target_pairs={{1,2},{3,4},{5,6},{9,10},{11,12},{13,14},{17,18},{19,20},{21,22},{... | collective-permute-start | bytes 1572872 | tf_op jit(solution)/shard_map/ppermute | solution.py:45
  11.0 12.7 %collective-permute-start.3 = (bf16[16,8192]{1,0:T(8,128)(2,1)S(1)}, bf16[16,8192]{1,0:T(8,128)(2,1)S(1)}, u32[]{:S(2)}, u32[]{:S(2)}) collective-permute-start(bf16[16,8192]{1,0:T(8,128)(2,1)S(1)} %constant_dynamic-update-slice_fusion.2), channel_id=1, source_target_pairs={{0,8},{8,0},{16,24},{24,16},{1,9},{9,1},{17,25},{25,17},{2,10},{10... | collective-permute-start | bytes 786440 | tf_op jit(solution)/shard_map/ppermute | solution.py:35
  13.4 12.1 %collective-permute-start.4 = (bf16[16,8192]{1,0:T(8,128)(2,1)S(1)}, bf16[16,8192]{1,0:T(8,128)(2,1)S(1)}, u32[]{:S(2)}, u32[]{:S(2)}) collective-permute-start(bf16[16,8192]{1,0:T(8,128)(2,1)S(1)} %constant_dynamic-update-slice_fusion.2), channel_id=1, source_target_pairs={{0,16},{8,24},{16,0},{24,8},{1,17},{9,25},{17,1},{25,9},{2,18},{10... | collective-permute-start | bytes 786440 | tf_op jit(solution)/shard_map/ppermute | solution.py:35
  14.9 10.8 %collective-permute-start.5 = (bf16[16,8192]{1,0:T(8,128)(2,1)S(1)}, bf16[16,8192]{1,0:T(8,128)(2,1)S(1)}, u32[]{:S(2)}, u32[]{:S(2)}) collective-permute-start(bf16[16,8192]{1,0:T(8,128)(2,1)S(1)} %constant_dynamic-update-slice_fusion.2), channel_id=1, source_target_pairs={{0,24},{8,16},{16,8},{24,0},{1,25},{9,17},{17,9},{25,1},{2,26},{10... | collective-permute-start | bytes 786440 | tf_op jit(solution)/shard_map/ppermute | solution.py:35
  19.5 6.3 %collective-permute-start.2 = (bf16[32,8192]{1,0:T(8,128)(2,1)S(1)}, bf16[32,8192]{1,0:T(8,128)(2,1)S(1)}, u32[]{:S(2)}, u32[]{:S(2)}) collective-permute-start(bf16[32,8192]{1,0:T(8,128)(2,1)S(1)} %get-tuple-element.70), channel_id=1, source_target_pairs={{2,3},{4,5},{6,7},{10,11},{12,13},{14,15},{18,19},{20,21},{22,23},... | collective-permute-start | bytes 1572872 | tf_op jit(solution)/shard_map/ppermute | solution.py:45
  25.9 19.7 %collective-permute-start.6 = (bf16[32,8192]{1,0:T(8,128)(2,1)S(1)}, bf16[32,8192]{1,0:T(8,128)(2,1)S(1)}, u32[]{:S(2)}, u32[]{:S(2)}) collective-permute-start(bf16[32,8192]{1,0:T(8,128)(2,1)S(1)} %get-tuple-element.80), channel_id=1, source_target_pairs={{3,4},{5,6},{11,12},{13,14},{19,20},{21,22},{27,28},{29,30}} | collective-permute-start | bytes 1572872 | tf_op jit(solution)/shard_map/ppermute | solution.py:45
  31.9 17.1 %collective-permute-start.10 = (bf16[64,512]{1,0:T(8,128)(2,1)S(1)}, bf16[64,512]{1,0:T(8,128)(2,1)S(1)}, u32[]{:S(2)}, u32[]{:S(2)}) collective-permute-start(bf16[64,512]{1,0:T(8,128)(2,1)S(1)} %get-tuple-element.102.refs_2_), channel_id=1, source_target_pairs={{0,6},{1,7},{8,14},{9,15},{16,22},{17,23},{24,30},{25,31}} | collective-permute-start | bytes 196616 | tf_op jit(solution)/shard_map/ppermute | solution.py:45
  41.5 7.5 %collective-permute-start.8 = (bf16[64,512]{1,0:T(8,128)(2,1)S(1)}, bf16[64,512]{1,0:T(8,128)(2,1)S(1)}, u32[]{:S(2)}, u32[]{:S(2)}) collective-permute-start(bf16[64,512]{1,0:T(8,128)(2,1)S(1)} %get-tuple-element.102.refs_2_), channel_id=1, source_target_pairs={{0,2},{1,3},{2,4},{3,5},{4,6},{5,7},{8,10},{9,11},{10,12},{11,13},... | collective-permute-start | bytes 196616 | tf_op jit(solution)/shard_map/ppermute | solution.py:45
  42.8 6.2 %collective-permute-start.9 = (bf16[64,512]{1,0:T(8,128)(2,1)S(1)}, bf16[64,512]{1,0:T(8,128)(2,1)S(1)}, u32[]{:S(2)}, u32[]{:S(2)}) collective-permute-start(bf16[64,512]{1,0:T(8,128)(2,1)S(1)} %get-tuple-element.102.refs_2_), channel_id=1, source_target_pairs={{0,4},{1,5},{2,6},{3,7},{8,12},{9,13},{10,14},{11,15},{16,20},{17,... | collective-permute-start | bytes 196616 | tf_op jit(solution)/shard_map/ppermute | solution.py:45
  45.6 3.4 %collective-permute-start.7 = (bf16[32,8192]{1,0:T(8,128)(2,1)S(1)}, bf16[32,8192]{1,0:T(8,128)(2,1)S(1)}, u32[]{:S(2)}, u32[]{:S(2)}) collective-permute-start(bf16[32,8192]{1,0:T(8,128)(2,1)S(1)} %get-tuple-element.85), channel_id=1, source_target_pairs={{4,5},{6,7},{12,13},{14,15},{20,21},{22,23},{28,29},{30,31}} | collective-permute-start | bytes 1572872 | tf_op jit(solution)/shard_map/ppermute | solution.py:45
  49.0 9.1 %collective-permute-start.11 = (bf16[32,8192]{1,0:T(8,128)(2,1)S(1)}, bf16[32,8192]{1,0:T(8,128)(2,1)S(1)}, u32[]{:S(2)}, u32[]{:S(2)}) collective-permute-start(bf16[32,8192]{1,0:T(8,128)(2,1)S(1)} %get-tuple-element.91), channel_id=1, source_target_pairs={{5,6},{13,14},{21,22},{29,30}} | collective-permute-start | bytes 1572872 | tf_op jit(solution)/shard_map/ppermute | solution.py:45
  49.8 7.8 %collective-permute-start.12 = (bf16[80,512]{1,0:T(8,128)(2,1)S(1)}, bf16[80,512]{1,0:T(8,128)(2,1)S(1)}, u32[]{:S(2)}, u32[]{:S(2)}) collective-permute-start(bf16[80,512]{1,0:T(8,128)(2,1)S(1)} %pad_maximum_fusion.2.refs_6_), channel_id=1, source_target_pairs={{0,8},{8,0},{16,24},{24,16},{1,9},{9,1},{17,25},{25,17},{2,10},{10... | collective-permute-start | bytes 245768 | tf_op jit(solution)/shard_map/ppermute | solution.py:35
  51.3 6.2 %collective-permute-start.13 = (bf16[80,512]{1,0:T(8,128)(2,1)S(1)}, bf16[80,512]{1,0:T(8,128)(2,1)S(1)}, u32[]{:S(2)}, u32[]{:S(2)}) collective-permute-start(bf16[80,512]{1,0:T(8,128)(2,1)S(1)} %pad_maximum_fusion.2.refs_6_), channel_id=1, source_target_pairs={{0,16},{8,24},{16,0},{24,8},{1,17},{9,25},{17,1},{25,9},{2,18},{10... | collective-permute-start | bytes 245768 | tf_op jit(solution)/shard_map/ppermute | solution.py:35
  52.8 5.3 %collective-permute-start.14 = (bf16[80,512]{1,0:T(8,128)(2,1)S(1)}, bf16[80,512]{1,0:T(8,128)(2,1)S(1)}, u32[]{:S(2)}, u32[]{:S(2)}) collective-permute-start(bf16[80,512]{1,0:T(8,128)(2,1)S(1)} %pad_maximum_fusion.2.refs_6_), channel_id=1, source_target_pairs={{0,24},{8,16},{16,8},{24,0},{1,25},{9,17},{17,9},{25,1},{2,26},{10... | collective-permute-start | bytes 245768 | tf_op jit(solution)/shard_map/ppermute | solution.py:35
  58.2 2.4 %collective-permute-start.15 = (bf16[32,8192]{1,0:T(8,128)(2,1)S(1)}, bf16[32,8192]{1,0:T(8,128)(2,1)S(1)}, u32[]{:S(2)}, u32[]{:S(2)}) collective-permute-start(bf16[32,8192]{1,0:T(8,128)(2,1)S(1)} %get-tuple-element.98), channel_id=1, source_target_pairs={{6,7},{14,15},{22,23},{30,31}} | collective-permute-start | bytes 1572872 | tf_op jit(solution)/shard_map/ppermute | solution.py:45
  60.5 4.7 %collective-permute-start.17 = (bf16[32,512]{1,0:T(8,128)(2,1)S(1)}, bf16[32,512]{1,0:T(8,128)(2,1)S(1)}, u32[]{:S(2)}, u32[]{:S(2)}) collective-permute-start(bf16[32,512]{1,0:T(8,128)(2,1)S(1)} %shard_map.112.refs_2_), channel_id=1, source_target_pairs={{0,8},{8,0},{16,24},{24,16},{1,9},{9,1},{17,25},{25,17},{2,10},{10... | collective-permute-start | bytes 98312 | tf_op jit(solution)/shard_map/ppermute | solution.py:35
  61.7 3.9 %collective-permute-start.18 = (bf16[32,512]{1,0:T(8,128)(2,1)S(1)}, bf16[32,512]{1,0:T(8,128)(2,1)S(1)}, u32[]{:S(2)}, u32[]{:S(2)}) collective-permute-start(bf16[32,512]{1,0:T(8,128)(2,1)S(1)} %shard_map.112.refs_2_), channel_id=1, source_target_pairs={{0,16},{8,24},{16,0},{24,8},{1,17},{9,25},{17,1},{25,9},{2,18},{10... | collective-permute-start | bytes 98312 | tf_op jit(solution)/shard_map/ppermute | solution.py:35
  63.2 4.8 %collective-permute-start.19 = (bf16[32,512]{1,0:T(8,128)(2,1)S(1)}, bf16[32,512]{1,0:T(8,128)(2,1)S(1)}, u32[]{:S(2)}, u32[]{:S(2)}) collective-permute-start(bf16[32,512]{1,0:T(8,128)(2,1)S(1)} %shard_map.112.refs_2_), channel_id=1, source_target_pairs={{0,24},{8,16},{16,8},{24,0},{1,25},{9,17},{17,9},{25,1},{2,26},{10... | collective-permute-start | bytes 98312 | tf_op jit(solution)/shard_map/ppermute | solution.py:35
  69.9 8.5 %collective-permute-start.21 = (f32[8,64]{1,0:T(8,128)S(1)}, f32[8,64]{1,0:T(8,128)S(1)}, u32[]{:S(2)}, u32[]{:S(2)}) collective-permute-start(f32[8,64]{1,0:T(8,128)S(1)} %add.9), channel_id=1, source_target_pairs={{0,2},{1,3},{2,4},{3,5},{4,0},{5,1},{8,10},{9,11},{10,12},{11,13},... | collective-permute-start | bytes 6152 | tf_op jit(solution)/shard_map/ppermute | solution.py:52
  71.8 8.7 %collective-permute-start.22 = (f32[8,64]{1,0:T(8,128)S(1)}, f32[8,64]{1,0:T(8,128)S(1)}, u32[]{:S(2)}, u32[]{:S(2)}) collective-permute-start(f32[8,64]{1,0:T(8,128)S(1)} %add.9), channel_id=1, source_target_pairs={{0,4},{1,5},{2,0},{3,1},{4,2},{5,3},{8,12},{9,13},{10,8},{11,9},{1... | collective-permute-start | bytes 6152 | tf_op jit(solution)/shard_map/ppermute | solution.py:52
  80.5 7.3 %collective-permute-start.23 = (f32[8,64]{1,0:T(8,128)S(1)}, f32[8,64]{1,0:T(8,128)S(1)}, u32[]{:S(2)}, u32[]{:S(2)}) collective-permute-start(f32[8,64]{1,0:T(8,128)S(1)} %add_add_fusion.refs_0_), channel_id=1, source_target_pairs={{6,0},{7,1},{14,8},{15,9},{22,16},{23,17},{30,24},{31,25}} | collective-permute-start | bytes 6152 | tf_op jit(solution)/shard_map/ppermute | solution.py:52
  81.8 6.0 %collective-permute-start.24 = (f32[8,64]{1,0:T(8,128)S(1)}, f32[8,64]{1,0:T(8,128)S(1)}, u32[]{:S(2)}, u32[]{:S(2)}) collective-permute-start(f32[8,64]{1,0:T(8,128)S(1)} %add_add_fusion.refs_0_), channel_id=1, source_target_pairs={{6,2},{7,3},{14,10},{15,11},{22,18},{23,19},{30,26},{31,27}} | collective-permute-start | bytes 6152 | tf_op jit(solution)/shard_map/ppermute | solution.py:52
  82.4 5.3 %collective-permute-start.25 = (f32[8,64]{1,0:T(8,128)S(1)}, f32[8,64]{1,0:T(8,128)S(1)}, u32[]{:S(2)}, u32[]{:S(2)}) collective-permute-start(f32[8,64]{1,0:T(8,128)S(1)} %add_add_fusion.refs_0_), channel_id=1, source_target_pairs={{6,4},{7,5},{4,6},{5,7},{14,12},{15,13},{12,14},{13,15},{22,20},{2... | collective-permute-start | bytes 6152 | tf_op jit(solution)/shard_map/ppermute | solution.py:52
  (10 other events, 73.9 us)

commit v14 on v13

--- a/solution.py
+++ b/solution.py
@@ -319,7 +319,7 @@
             moved=weight_bytes,
         )
 
-    head = width // PARTS
+    head = width // 2
     expand, first, raised, own = call(
         prime_kernel,
         (inner_cols[0], value_rows[0], adapter_expand[0], adapter_down[0]),
@@ -454,12 +454,9 @@
         moved=weight_bytes // 8,
     )
     sums = sums + swap(sums, "pipe", 1)
-    below = [between(sums, [(z, (z + hop) % top) for z in range(top)]) for hop in range(1, top)]
-    for part in below:
-        sums = sums + part
-    crossing = [[(top, z)] for z in range(top)]
-    crossing[-1].append((top - 1, top))
-    parts = [sums] + [between(sums, chosen) for chosen in crossing]
+    below = [[(z, (z + hop) % top) for z in range(top)] for hop in range(1, top)]
+    crossing = [[(top, z), (z, top)] for z in range(top)]
+    parts = [sums] + [between(sums, chosen) for chosen in below + crossing]
     (scores,) = call(
         functools.partial(final_kernel, q_dev),
         (query_example[None], *parts),

time: 89.1 us -> 87.7 us (0.984)
  waiting for transfers between devices: 14.9 us -> 9.78 us
  starting transfers between devices: 42.7 us -> 45.7 us
    ppermute x5, waiting for transfers between devices: 6.78 us -> 1.65 us  [between(): return lax.ppermute(value, 'pipe', pairs)]
    ppermute x5, starting transfers between devices: 11.1 us -> 14.1 us  [between(): return lax.ppermute(value, 'pipe', pairs)]
  transfers between devices with their start and end apart: 26 -> 26, of which waited for: 9 -> 8; matrix products, arithmetic and copies ran while one was open for 6% -> 6% of each run, Pallas kernels for 19% -> 18%
where the time goes in v14:
time: 87.7 us; the launch traced here: 86.4 us
  starting transfers between devices  45.7 us (52%)
  Pallas kernels  22.6 us (26%)
  waiting for transfers between devices  9.78 us (11%)
  matrix products  5.32 us (6%)
  local copies, waits for them, and re-layouts  2.3 us (3%)
    pallas_call x16, Pallas kernels, call(): pl.pallas_call(kernel, in_specs=[pl.BlockSpec(memory_space=space[place])...  22.6 us
    ppermute x10, starting transfers between devices, upward(): lax.ppermute(value, 'pipe', [(source, source + hop) for source in range(f...  20.6 us
    ppermute x5, starting transfers between devices, between(): return lax.ppermute(value, 'pipe', pairs)  14.1 us
    ppermute x11, starting transfers between devices, swap(): lax.ppermute(value, axis, [(source, source ^ distance) for source in rang...  11.1 us
    ppermute x11, waiting for transfers between devices, swap(): lax.ppermute(value, axis, [(source, source ^ distance) for source in rang...  8.11 us
    dot_general x2, matrix products, dot_nt(): lax.dot_general(a, b, (((1,), (1,)), ((), ())), preferred_element_type=f3...  5.32 us
    unnamed x18, local copies, waits for them, and re-layouts  2.26 us
  transfers between devices with their start and end apart: 26, of which 8 were waited for; matrix products, arithmetic and copies ran while one was open for 6% of the time, Pallas kernels for 18%

profile of v14, /device:TPU:0, one launch (start us, length us, event | category | flops | bytes accessed | tf_op | source)
XLA Modules:
  0.0 86.4 jit_solution(11793437595036888356)
XLA Ops:
  0.0 5.3 %shard_map.100 = (bf16[512,8192]{1,0:T(8,128)(2,1)S(1)}, bf16[4096,512]{1,0:T(8,128)(2,1)S(1)}, bf16[64,8192]{1,0:T(8,128)(2,1)S(1)}, bf16[16,8192]{1,0:T(8,128)(2,1)S(1)}) custom-call(bf16[32,512]{1,0:T(8,128)(2,1)} %bitcast.38, bf16[8,8192]{1,0:T(8,128)(2,1)} %bitcast.35, bf16[512,8192]{1,0:T(8,128)(2,1)} %bitcast.32, bf16[8192,512]{1,0:T(8,128)(2,1)} %bitcast.30), custom_call_target="tpu_custom_call" | custom-call | flops 134217728 | bytes 16777216 | tf_op jit(solution)/shard_map/pallas_call | solution.py:66
  5.4 2.4 %collective-permute-start = (bf16[16,8192]{1,0:T(8,128)(2,1)S(1)}, bf16[16,8192]{1,0:T(8,128)(2,1)S(1)}, u32[]{:S(2)}, u32[]{:S(2)}) collective-permute-start(bf16[16,8192]{1,0:T(8,128)(2,1)S(1)} %get-tuple-element.61), channel_id=1, source_target_pairs={{0,1},{2,3},{4,5},{6,7},{8,9},{10,11},{12,13},{14,15},{16,17},{18,... | collective-permute-start | bytes 786440 | tf_op jit(solution)/shard_map/ppermute | solution.py:45
  7.7 2.2 %shard_map.101.rest = bf16[4096,512]{1,0:T(8,128)(2,1)S(1)} custom-call(bf16[8192,512]{1,0:T(8,128)(2,1)} %bitcast.31), custom_call_target="tpu_custom_call" | custom-call | bytes 16777216 | tf_op jit(solution)/shard_map/pallas_call | solution.py:66
  11.0 2.4 %collective-permute-start.3 = (bf16[16,8192]{1,0:T(8,128)(2,1)S(1)}, bf16[16,8192]{1,0:T(8,128)(2,1)S(1)}, u32[]{:S(2)}, u32[]{:S(2)}) collective-permute-start(bf16[16,8192]{1,0:T(8,128)(2,1)S(1)} %constant_dynamic-update-slice_fusion.2), channel_id=1, source_target_pairs={{0,8},{8,0},{16,24},{24,16},{1,9},{9,1},{17,25},{25,17},{2,10},{10... | collective-permute-start | bytes 786440 | tf_op jit(solution)/shard_map/ppermute | solution.py:35
  13.4 1.5 %collective-permute-start.4 = (bf16[16,8192]{1,0:T(8,128)(2,1)S(1)}, bf16[16,8192]{1,0:T(8,128)(2,1)S(1)}, u32[]{:S(2)}, u32[]{:S(2)}) collective-permute-start(bf16[16,8192]{1,0:T(8,128)(2,1)S(1)} %constant_dynamic-update-slice_fusion.2), channel_id=1, source_target_pairs={{0,16},{8,24},{16,0},{24,8},{1,17},{9,25},{17,1},{25,9},{2,18},{10... | collective-permute-start | bytes 786440 | tf_op jit(solution)/shard_map/ppermute | solution.py:35
  15.0 4.5 %shard_map.103.refs_0_ = bf16[320,512]{1,0:T(8,128)(2,1)S(1)} custom-call(bf16[512,8192]{1,0:T(8,128)(2,1)} %cotangent.1, bf16[512,8192]{1,0:T(8,128)(2,1)S(1)} %get-tuple-element.66.expand), custom_call_target="tpu_custom_call" | custom-call | flops 2684354560 | bytes 8388608 | tf_op jit(solution)/shard_map/pallas_call | solution.py:66
  20.2 3.5 %shard_map.105.hidden = bf16[64,8192]{1,0:T(8,128)(2,1)S(1)} custom-call(bf16[32,512]{1,0:T(8,128)(2,1)} %bitcast.39, bf16[4096,512]{1,0:T(8,128)(2,1)S(1)} %get-tuple-element.64.head, bf16[4096,512]{1,0:T(8,128)(2,1)S(1)} %shard_map.101.rest), custom_call_target="tpu_custom_call" | custom-call | flops 536870912 | bytes 8388608 | tf_op jit(solution)/shard_map/pallas_call | solution.py:66
  23.7 1.8 %collective-permute-done.4 = bf16[16,8192]{1,0:T(8,128)(2,1)S(1)} collective-permute-done((bf16[16,8192]{1,0:T(8,128)(2,1)S(1)}, bf16[16,8192]{1,0:T(8,128)(2,1)S(1)}, u32[]{:S(2)}, u32[]{:S(2)}) %collective-permute-start.4) | collective-permute-done | bytes 262176 | tf_op jit(solution)/shard_map/ppermute | solution.py:35
  27.9 1.3 %slice-done.3 = s8[4194304]{0:T(1024)(128)(4,1)S(1)} async-done(((s8[8388608]{0:T(1024)(128)(4,1)}), s8[4194304]{0:T(1024)(128)(4,1)S(1)}, s32[]{:S(2)}) %slice-start.3) | async-done | bytes 4194328
  29.2 2.7 %fusion.5 = (bf16[64,512]{1,0:T(8,128)(2,1)S(1)}, f32[64,512]{1,0:T(8,128)S(1)}) fusion(f32[512]{0:T(512)S(1)} %convert_bitcast_fusion, bf16[64,8192]{1,0:T(8,128)(2,1)S(1)} %get-tuple-element.83, bf16[1,512,8192]{2,1,0:T(8,128)(2,1)S(1)} %bitcast.34), kind=kOutput, calls=%fused_computation.12 | convolution fusion | flops 536936448 | bytes 9635840 | tf_op jit(solution)/shard_map/dot_general | solution.py:28
  31.9 9.6 %collective-permute-start.10 = (bf16[64,512]{1,0:T(8,128)(2,1)S(1)}, bf16[64,512]{1,0:T(8,128)(2,1)S(1)}, u32[]{:S(2)}, u32[]{:S(2)}) collective-permute-start(bf16[64,512]{1,0:T(8,128)(2,1)S(1)} %get-tuple-element.102.refs_2_), channel_id=1, source_target_pairs={{0,6},{1,7},{8,14},{9,15},{16,22},{17,23},{24,30},{25,31}} | collective-permute-start | bytes 196616 | tf_op jit(solution)/shard_map/ppermute | solution.py:45
  41.5 1.3 %collective-permute-start.8 = (bf16[64,512]{1,0:T(8,128)(2,1)S(1)}, bf16[64,512]{1,0:T(8,128)(2,1)S(1)}, u32[]{:S(2)}, u32[]{:S(2)}) collective-permute-start(bf16[64,512]{1,0:T(8,128)(2,1)S(1)} %get-tuple-element.102.refs_2_), channel_id=1, source_target_pairs={{0,2},{1,3},{2,4},{3,5},{4,6},{5,7},{8,10},{9,11},{10,12},{11,13},... | collective-permute-start | bytes 196616 | tf_op jit(solution)/shard_map/ppermute | solution.py:45
  42.8 2.7 %collective-permute-start.9 = (bf16[64,512]{1,0:T(8,128)(2,1)S(1)}, bf16[64,512]{1,0:T(8,128)(2,1)S(1)}, u32[]{:S(2)}, u32[]{:S(2)}) collective-permute-start(bf16[64,512]{1,0:T(8,128)(2,1)S(1)} %get-tuple-element.102.refs_2_), channel_id=1, source_target_pairs={{0,4},{1,5},{2,6},{3,7},{8,12},{9,13},{10,14},{11,15},{16,20},{17,... | collective-permute-start | bytes 196616 | tf_op jit(solution)/shard_map/ppermute | solution.py:45
  46.3 2.7 %fusion.6.right = f32[64,512]{1,0:T(8,128)S(1)} fusion(bf16[64,8192]{1,0:T(8,128)(2,1)S(1)} %get-tuple-element.86, bf16[512,8192]{1,0:T(8,128)(2,1)S(1)} %bitcast.29), kind=kOutput, calls=%fused_computation.13 | convolution fusion | flops 536870912 | bytes 9568256 | tf_op jit(solution)/shard_map/dot_general | solution.py:28
  49.7 1.6 %collective-permute-start.12 = (bf16[80,512]{1,0:T(8,128)(2,1)S(1)}, bf16[80,512]{1,0:T(8,128)(2,1)S(1)}, u32[]{:S(2)}, u32[]{:S(2)}) collective-permute-start(bf16[80,512]{1,0:T(8,128)(2,1)S(1)} %pad_maximum_fusion.2.refs_6_), channel_id=1, source_target_pairs={{0,8},{8,0},{16,24},{24,16},{1,9},{9,1},{17,25},{25,17},{2,10},{10... | collective-permute-start | bytes 245768 | tf_op jit(solution)/shard_map/ppermute | solution.py:35
  51.3 1.5 %collective-permute-start.13 = (bf16[80,512]{1,0:T(8,128)(2,1)S(1)}, bf16[80,512]{1,0:T(8,128)(2,1)S(1)}, u32[]{:S(2)}, u32[]{:S(2)}) collective-permute-start(bf16[80,512]{1,0:T(8,128)(2,1)S(1)} %pad_maximum_fusion.2.refs_6_), channel_id=1, source_target_pairs={{0,16},{8,24},{16,0},{24,8},{1,17},{9,25},{17,1},{25,9},{2,18},{10... | collective-permute-start | bytes 245768 | tf_op jit(solution)/shard_map/ppermute | solution.py:35
  53.3 4.2 %shard_map.110.refs_1_ = bf16[192,512]{1,0:T(8,128)(2,1)S(1)} custom-call(bf16[512,8192]{1,0:T(8,128)(2,1)} %cotangent.1, bf16[512,8192]{1,0:T(8,128)(2,1)S(1)} %get-tuple-element.66.expand), custom_call_target="tpu_custom_call" | custom-call | flops 1610612736 | bytes 8388608 | tf_op jit(solution)/shard_map/pallas_call | solution.py:66
  59.0 1.5 %collective-permute-done.16.others = bf16[4,64,512]{2,1,0:T(8,128)(2,1)S(1)} collective-permute-done((bf16[4,64,512]{2,1,0:T(8,128)(2,1)S(1)}, bf16[4,64,512]{2,1,0:T(8,128)(2,1)S(1)}, u32[]{:S(2)}, u32[]{:S(2)}) %collective-permute-start.16) | collective-permute-done | bytes 262176 | tf_op jit(solution)/shard_map/ppermute | solution.py:35
  61.7 1.5 %collective-permute-start.18 = (bf16[32,512]{1,0:T(8,128)(2,1)S(1)}, bf16[32,512]{1,0:T(8,128)(2,1)S(1)}, u32[]{:S(2)}, u32[]{:S(2)}) collective-permute-start(bf16[32,512]{1,0:T(8,128)(2,1)S(1)} %shard_map.112.refs_2_), channel_id=1, source_target_pairs={{0,16},{8,24},{16,0},{24,8},{1,17},{9,25},{17,1},{25,9},{2,18},{10... | collective-permute-start | bytes 98312 | tf_op jit(solution)/shard_map/ppermute | solution.py:35
  65.6 2.4 %collective-permute-done.19.refs_5_ = bf16[32,512]{1,0:T(8,128)(2,1)S(1)} collective-permute-done((bf16[32,512]{1,0:T(8,128)(2,1)S(1)}, bf16[32,512]{1,0:T(8,128)(2,1)S(1)}, u32[]{:S(2)}, u32[]{:S(2)}) %collective-permute-start.19) | collective-permute-done | bytes 32800 | tf_op jit(solution)/shard_map/ppermute | solution.py:35
  69.8 1.9 %collective-permute-start.21 = (f32[8,64]{1,0:T(8,128)S(1)}, f32[8,64]{1,0:T(8,128)S(1)}, u32[]{:S(2)}, u32[]{:S(2)}) collective-permute-start(f32[8,64]{1,0:T(8,128)S(1)} %add.3.refs_0_), channel_id=1, source_target_pairs={{0,2},{1,3},{2,4},{3,5},{4,0},{5,1},{8,10},{9,11},{10,12},{11,13},... | collective-permute-start | bytes 6152 | tf_op jit(solution)/shard_map/ppermute | solution.py:52
  71.8 6.6 %collective-permute-start.22 = (f32[8,64]{1,0:T(8,128)S(1)}, f32[8,64]{1,0:T(8,128)S(1)}, u32[]{:S(2)}, u32[]{:S(2)}) collective-permute-start(f32[8,64]{1,0:T(8,128)S(1)} %add.3.refs_0_), channel_id=1, source_target_pairs={{0,4},{1,5},{2,0},{3,1},{4,2},{5,3},{8,12},{9,13},{10,8},{11,9},{1... | collective-permute-start | bytes 6152 | tf_op jit(solution)/shard_map/ppermute | solution.py:52
  78.3 4.3 %collective-permute-start.23 = (f32[8,64]{1,0:T(8,128)S(1)}, f32[8,64]{1,0:T(8,128)S(1)}, u32[]{:S(2)}, u32[]{:S(2)}) collective-permute-start(f32[8,64]{1,0:T(8,128)S(1)} %add.3.refs_0_), channel_id=1, source_target_pairs={{6,0},{7,1},{0,6},{1,7},{14,8},{15,9},{8,14},{9,15},{22,16},{23,17... | collective-permute-start | bytes 6152 | tf_op jit(solution)/shard_map/ppermute | solution.py:52
  84.0 1.6 %collective-permute-done.23.refs_3_ = f32[8,64]{1,0:T(8,128)S(1)} collective-permute-done((f32[8,64]{1,0:T(8,128)S(1)}, f32[8,64]{1,0:T(8,128)S(1)}, u32[]{:S(2)}, u32[]{:S(2)}) %collective-permute-start.23) | collective-permute-done | bytes 2080 | tf_op jit(solution)/shard_map/ppermute | solution.py:52
  (75 shorter events, 15.0 us)
Async XLA Ops:
  5.4 4.7 %collective-permute-start = (bf16[16,8192]{1,0:T(8,128)(2,1)S(1)}, bf16[16,8192]{1,0:T(8,128)(2,1)S(1)}, u32[]{:S(2)}, u32[]{:S(2)}) collective-permute-start(bf16[16,8192]{1,0:T(8,128)(2,1)S(1)} %get-tuple-element.61), channel_id=1, source_target_pairs={{0,1},{2,3},{4,5},{6,7},{8,9},{10,11},{12,13},{14,15},{16,17},{18,... | collective-permute-start | bytes 786440 | tf_op jit(solution)/shard_map/ppermute | solution.py:45
  10.1 9.3 %collective-permute-start.1 = (bf16[32,8192]{1,0:T(8,128)(2,1)S(1)}, bf16[32,8192]{1,0:T(8,128)(2,1)S(1)}, u32[]{:S(2)}, u32[]{:S(2)}) collective-permute-start(bf16[32,8192]{1,0:T(8,128)(2,1)S(1)} %constant_dynamic-update-slice_fusion), channel_id=1, source_target_pairs={{1,2},{3,4},{5,6},{9,10},{11,12},{13,14},{17,18},{19,20},{21,22},{... | collective-permute-start | bytes 1572872 | tf_op jit(solution)/shard_map/ppermute | solution.py:45
  11.0 12.7 %collective-permute-start.3 = (bf16[16,8192]{1,0:T(8,128)(2,1)S(1)}, bf16[16,8192]{1,0:T(8,128)(2,1)S(1)}, u32[]{:S(2)}, u32[]{:S(2)}) collective-permute-start(bf16[16,8192]{1,0:T(8,128)(2,1)S(1)} %constant_dynamic-update-slice_fusion.2), channel_id=1, source_target_pairs={{0,8},{8,0},{16,24},{24,16},{1,9},{9,1},{17,25},{25,17},{2,10},{10... | collective-permute-start | bytes 786440 | tf_op jit(solution)/shard_map/ppermute | solution.py:35
  13.4 12.1 %collective-permute-start.4 = (bf16[16,8192]{1,0:T(8,128)(2,1)S(1)}, bf16[16,8192]{1,0:T(8,128)(2,1)S(1)}, u32[]{:S(2)}, u32[]{:S(2)}) collective-permute-start(bf16[16,8192]{1,0:T(8,128)(2,1)S(1)} %constant_dynamic-update-slice_fusion.2), channel_id=1, source_target_pairs={{0,16},{8,24},{16,0},{24,8},{1,17},{9,25},{17,1},{25,9},{2,18},{10... | collective-permute-start | bytes 786440 | tf_op jit(solution)/shard_map/ppermute | solution.py:35
  14.9 10.8 %collective-permute-start.5 = (bf16[16,8192]{1,0:T(8,128)(2,1)S(1)}, bf16[16,8192]{1,0:T(8,128)(2,1)S(1)}, u32[]{:S(2)}, u32[]{:S(2)}) collective-permute-start(bf16[16,8192]{1,0:T(8,128)(2,1)S(1)} %constant_dynamic-update-slice_fusion.2), channel_id=1, source_target_pairs={{0,24},{8,16},{16,8},{24,0},{1,25},{9,17},{17,9},{25,1},{2,26},{10... | collective-permute-start | bytes 786440 | tf_op jit(solution)/shard_map/ppermute | solution.py:35
  19.5 6.3 %collective-permute-start.2 = (bf16[32,8192]{1,0:T(8,128)(2,1)S(1)}, bf16[32,8192]{1,0:T(8,128)(2,1)S(1)}, u32[]{:S(2)}, u32[]{:S(2)}) collective-permute-start(bf16[32,8192]{1,0:T(8,128)(2,1)S(1)} %get-tuple-element.70), channel_id=1, source_target_pairs={{2,3},{4,5},{6,7},{10,11},{12,13},{14,15},{18,19},{20,21},{22,23},... | collective-permute-start | bytes 1572872 | tf_op jit(solution)/shard_map/ppermute | solution.py:45
  25.9 19.7 %collective-permute-start.6 = (bf16[32,8192]{1,0:T(8,128)(2,1)S(1)}, bf16[32,8192]{1,0:T(8,128)(2,1)S(1)}, u32[]{:S(2)}, u32[]{:S(2)}) collective-permute-start(bf16[32,8192]{1,0:T(8,128)(2,1)S(1)} %get-tuple-element.80), channel_id=1, source_target_pairs={{3,4},{5,6},{11,12},{13,14},{19,20},{21,22},{27,28},{29,30}} | collective-permute-start | bytes 1572872 | tf_op jit(solution)/shard_map/ppermute | solution.py:45
  31.9 17.0 %collective-permute-start.10 = (bf16[64,512]{1,0:T(8,128)(2,1)S(1)}, bf16[64,512]{1,0:T(8,128)(2,1)S(1)}, u32[]{:S(2)}, u32[]{:S(2)}) collective-permute-start(bf16[64,512]{1,0:T(8,128)(2,1)S(1)} %get-tuple-element.102.refs_2_), channel_id=1, source_target_pairs={{0,6},{1,7},{8,14},{9,15},{16,22},{17,23},{24,30},{25,31}} | collective-permute-start | bytes 196616 | tf_op jit(solution)/shard_map/ppermute | solution.py:45
  41.5 7.5 %collective-permute-start.8 = (bf16[64,512]{1,0:T(8,128)(2,1)S(1)}, bf16[64,512]{1,0:T(8,128)(2,1)S(1)}, u32[]{:S(2)}, u32[]{:S(2)}) collective-permute-start(bf16[64,512]{1,0:T(8,128)(2,1)S(1)} %get-tuple-element.102.refs_2_), channel_id=1, source_target_pairs={{0,2},{1,3},{2,4},{3,5},{4,6},{5,7},{8,10},{9,11},{10,12},{11,13},... | collective-permute-start | bytes 196616 | tf_op jit(solution)/shard_map/ppermute | solution.py:45
  42.8 6.2 %collective-permute-start.9 = (bf16[64,512]{1,0:T(8,128)(2,1)S(1)}, bf16[64,512]{1,0:T(8,128)(2,1)S(1)}, u32[]{:S(2)}, u32[]{:S(2)}) collective-permute-start(bf16[64,512]{1,0:T(8,128)(2,1)S(1)} %get-tuple-element.102.refs_2_), channel_id=1, source_target_pairs={{0,4},{1,5},{2,6},{3,7},{8,12},{9,13},{10,14},{11,15},{16,20},{17,... | collective-permute-start | bytes 196616 | tf_op jit(solution)/shard_map/ppermute | solution.py:45
  45.6 3.4 %collective-permute-start.7 = (bf16[32,8192]{1,0:T(8,128)(2,1)S(1)}, bf16[32,8192]{1,0:T(8,128)(2,1)S(1)}, u32[]{:S(2)}, u32[]{:S(2)}) collective-permute-start(bf16[32,8192]{1,0:T(8,128)(2,1)S(1)} %get-tuple-element.85), channel_id=1, source_target_pairs={{4,5},{6,7},{12,13},{14,15},{20,21},{22,23},{28,29},{30,31}} | collective-permute-start | bytes 1572872 | tf_op jit(solution)/shard_map/ppermute | solution.py:45
  49.0 9.1 %collective-permute-start.11 = (bf16[32,8192]{1,0:T(8,128)(2,1)S(1)}, bf16[32,8192]{1,0:T(8,128)(2,1)S(1)}, u32[]{:S(2)}, u32[]{:S(2)}) collective-permute-start(bf16[32,8192]{1,0:T(8,128)(2,1)S(1)} %get-tuple-element.91), channel_id=1, source_target_pairs={{5,6},{13,14},{21,22},{29,30}} | collective-permute-start | bytes 1572872 | tf_op jit(solution)/shard_map/ppermute | solution.py:45
  49.7 7.8 %collective-permute-start.12 = (bf16[80,512]{1,0:T(8,128)(2,1)S(1)}, bf16[80,512]{1,0:T(8,128)(2,1)S(1)}, u32[]{:S(2)}, u32[]{:S(2)}) collective-permute-start(bf16[80,512]{1,0:T(8,128)(2,1)S(1)} %pad_maximum_fusion.2.refs_6_), channel_id=1, source_target_pairs={{0,8},{8,0},{16,24},{24,16},{1,9},{9,1},{17,25},{25,17},{2,10},{10... | collective-permute-start | bytes 245768 | tf_op jit(solution)/shard_map/ppermute | solution.py:35
  51.3 6.2 %collective-permute-start.13 = (bf16[80,512]{1,0:T(8,128)(2,1)S(1)}, bf16[80,512]{1,0:T(8,128)(2,1)S(1)}, u32[]{:S(2)}, u32[]{:S(2)}) collective-permute-start(bf16[80,512]{1,0:T(8,128)(2,1)S(1)} %pad_maximum_fusion.2.refs_6_), channel_id=1, source_target_pairs={{0,16},{8,24},{16,0},{24,8},{1,17},{9,25},{17,1},{25,9},{2,18},{10... | collective-permute-start | bytes 245768 | tf_op jit(solution)/shard_map/ppermute | solution.py:35
  52.8 5.3 %collective-permute-start.14 = (bf16[80,512]{1,0:T(8,128)(2,1)S(1)}, bf16[80,512]{1,0:T(8,128)(2,1)S(1)}, u32[]{:S(2)}, u32[]{:S(2)}) collective-permute-start(bf16[80,512]{1,0:T(8,128)(2,1)S(1)} %pad_maximum_fusion.2.refs_6_), channel_id=1, source_target_pairs={{0,24},{8,16},{16,8},{24,0},{1,25},{9,17},{17,9},{25,1},{2,26},{10... | collective-permute-start | bytes 245768 | tf_op jit(solution)/shard_map/ppermute | solution.py:35
  58.2 2.4 %collective-permute-start.15 = (bf16[32,8192]{1,0:T(8,128)(2,1)S(1)}, bf16[32,8192]{1,0:T(8,128)(2,1)S(1)}, u32[]{:S(2)}, u32[]{:S(2)}) collective-permute-start(bf16[32,8192]{1,0:T(8,128)(2,1)S(1)} %get-tuple-element.98), channel_id=1, source_target_pairs={{6,7},{14,15},{22,23},{30,31}} | collective-permute-start | bytes 1572872 | tf_op jit(solution)/shard_map/ppermute | solution.py:45
  60.5 4.7 %collective-permute-start.17 = (bf16[32,512]{1,0:T(8,128)(2,1)S(1)}, bf16[32,512]{1,0:T(8,128)(2,1)S(1)}, u32[]{:S(2)}, u32[]{:S(2)}) collective-permute-start(bf16[32,512]{1,0:T(8,128)(2,1)S(1)} %shard_map.112.refs_2_), channel_id=1, source_target_pairs={{0,8},{8,0},{16,24},{24,16},{1,9},{9,1},{17,25},{25,17},{2,10},{10... | collective-permute-start | bytes 98312 | tf_op jit(solution)/shard_map/ppermute | solution.py:35
  61.7 3.9 %collective-permute-start.18 = (bf16[32,512]{1,0:T(8,128)(2,1)S(1)}, bf16[32,512]{1,0:T(8,128)(2,1)S(1)}, u32[]{:S(2)}, u32[]{:S(2)}) collective-permute-start(bf16[32,512]{1,0:T(8,128)(2,1)S(1)} %shard_map.112.refs_2_), channel_id=1, source_target_pairs={{0,16},{8,24},{16,0},{24,8},{1,17},{9,25},{17,1},{25,9},{2,18},{10... | collective-permute-start | bytes 98312 | tf_op jit(solution)/shard_map/ppermute | solution.py:35
  63.2 4.8 %collective-permute-start.19 = (bf16[32,512]{1,0:T(8,128)(2,1)S(1)}, bf16[32,512]{1,0:T(8,128)(2,1)S(1)}, u32[]{:S(2)}, u32[]{:S(2)}) collective-permute-start(bf16[32,512]{1,0:T(8,128)(2,1)S(1)} %shard_map.112.refs_2_), channel_id=1, source_target_pairs={{0,24},{8,16},{16,8},{24,0},{1,25},{9,17},{17,9},{25,1},{2,26},{10... | collective-permute-start | bytes 98312 | tf_op jit(solution)/shard_map/ppermute | solution.py:35
  69.8 14.1 %collective-permute-start.21 = (f32[8,64]{1,0:T(8,128)S(1)}, f32[8,64]{1,0:T(8,128)S(1)}, u32[]{:S(2)}, u32[]{:S(2)}) collective-permute-start(f32[8,64]{1,0:T(8,128)S(1)} %add.3.refs_0_), channel_id=1, source_target_pairs={{0,2},{1,3},{2,4},{3,5},{4,0},{5,1},{8,10},{9,11},{10,12},{11,13},... | collective-permute-start | bytes 6152 | tf_op jit(solution)/shard_map/ppermute | solution.py:52
  71.8 12.2 %collective-permute-start.22 = (f32[8,64]{1,0:T(8,128)S(1)}, f32[8,64]{1,0:T(8,128)S(1)}, u32[]{:S(2)}, u32[]{:S(2)}) collective-permute-start(f32[8,64]{1,0:T(8,128)S(1)} %add.3.refs_0_), channel_id=1, source_target_pairs={{0,4},{1,5},{2,0},{3,1},{4,2},{5,3},{8,12},{9,13},{10,8},{11,9},{1... | collective-permute-start | bytes 6152 | tf_op jit(solution)/shard_map/ppermute | solution.py:52
  78.3 7.3 %collective-permute-start.23 = (f32[8,64]{1,0:T(8,128)S(1)}, f32[8,64]{1,0:T(8,128)S(1)}, u32[]{:S(2)}, u32[]{:S(2)}) collective-permute-start(f32[8,64]{1,0:T(8,128)S(1)} %add.3.refs_0_), channel_id=1, source_target_pairs={{6,0},{7,1},{0,6},{1,7},{14,8},{15,9},{8,14},{9,15},{22,16},{23,17... | collective-permute-start | bytes 6152 | tf_op jit(solution)/shard_map/ppermute | solution.py:52
  82.7 3.0 %collective-permute-start.24 = (f32[8,64]{1,0:T(8,128)S(1)}, f32[8,64]{1,0:T(8,128)S(1)}, u32[]{:S(2)}, u32[]{:S(2)}) collective-permute-start(f32[8,64]{1,0:T(8,128)S(1)} %add.3.refs_0_), channel_id=1, source_target_pairs={{6,2},{7,3},{2,6},{3,7},{14,10},{15,11},{10,14},{11,15},{22,18},{2... | collective-permute-start | bytes 6152 | tf_op jit(solution)/shard_map/ppermute | solution.py:52
  83.3 2.3 %collective-permute-start.25 = (f32[8,64]{1,0:T(8,128)S(1)}, f32[8,64]{1,0:T(8,128)S(1)}, u32[]{:S(2)}, u32[]{:S(2)}) collective-permute-start(f32[8,64]{1,0:T(8,128)S(1)} %add.3.refs_0_), channel_id=1, source_target_pairs={{6,4},{7,5},{4,6},{5,7},{14,12},{15,13},{12,14},{13,15},{22,20},{2... | collective-permute-start | bytes 6152 | tf_op jit(solution)/shard_map/ppermute | solution.py:52
  (10 other events, 71.1 us)

commit v15 on v12

--- a/solution.py
+++ b/solution.py
@@ -321,7 +321,7 @@
             moved=weight_bytes,
         )
 
-    head = width // PARTS
+    head = width // 2
     expand, first, raised, own = call(
         prime_kernel,
         (inner_cols[0], value_rows[0], adapter_expand[0], adapter_down[0]),

time: 84.7 us -> 84.7 us (level)
  no operation moved by 1% of the time
where the time goes in v15:
time: 84.7 us; the launch traced here: 84.3 us
  starting transfers between devices  41.8 us (49%)
  Pallas kernels  22.6 us (27%)
  waiting for transfers between devices  11.7 us (14%)
  matrix products  5.32 us (6%)
  local copies, waits for them, and re-layouts  2.3 us (3%)
    pallas_call x16, Pallas kernels, call(): pl.pallas_call(kernel, in_specs=[pl.BlockSpec(memory_space=space[place])...  22.6 us
    ppermute x10, starting transfers between devices, upward(): lax.ppermute(value, 'pipe', [(source, source + hop) for source in range(f...  20.6 us
    ppermute x11, starting transfers between devices, swap(): lax.ppermute(value, axis, [(source, source ^ distance) for source in rang...  11.1 us
    ppermute x3, starting transfers between devices, around(): lax.ppermute(value, 'pipe', [(source, (source + 2 * hop) % count) for sou...  10.1 us
    ppermute x11, waiting for transfers between devices, swap(): lax.ppermute(value, axis, [(source, source ^ distance) for source in rang...  8.11 us
    dot_general x2, matrix products, dot_nt(): lax.dot_general(a, b, (((1,), (1,)), ((), ())), preferred_element_type=f3...  5.32 us
    ppermute x3, waiting for transfers between devices, around(): lax.ppermute(value, 'pipe', [(source, (source + 2 * hop) % count) for sou...  3.6 us
    unnamed x18, local copies, waits for them, and re-layouts  2.26 us
  transfers between devices with their start and end apart: 24, of which 10 were waited for; matrix products, arithmetic and copies ran while one was open for 7% of the time, Pallas kernels for 19%

profile of v15, /device:TPU:0, one launch (start us, length us, event | category | flops | bytes accessed | tf_op | source)
XLA Modules:
  0.0 84.3 jit_solution(246789309632436201)
XLA Ops:
  0.0 5.3 %shard_map.100 = (bf16[512,8192]{1,0:T(8,128)(2,1)S(1)}, bf16[4096,512]{1,0:T(8,128)(2,1)S(1)}, bf16[64,8192]{1,0:T(8,128)(2,1)S(1)}, bf16[16,8192]{1,0:T(8,128)(2,1)S(1)}) custom-call(bf16[32,512]{1,0:T(8,128)(2,1)} %bitcast.38, bf16[8,8192]{1,0:T(8,128)(2,1)} %bitcast.35, bf16[512,8192]{1,0:T(8,128)(2,1)} %bitcast.32, bf16[8192,512]{1,0:T(8,128)(2,1)} %bitcast.30), custom_call_target="tpu_custom_call" | custom-call | flops 134217728 | bytes 16777216 | tf_op jit(solution)/shard_map/pallas_call | solution.py:68
  5.4 2.4 %collective-permute-start = (bf16[16,8192]{1,0:T(8,128)(2,1)S(1)}, bf16[16,8192]{1,0:T(8,128)(2,1)S(1)}, u32[]{:S(2)}, u32[]{:S(2)}) collective-permute-start(bf16[16,8192]{1,0:T(8,128)(2,1)S(1)} %get-tuple-element.61), channel_id=1, source_target_pairs={{0,1},{2,3},{4,5},{6,7},{8,9},{10,11},{12,13},{14,15},{16,17},{18,... | collective-permute-start | bytes 786440 | tf_op jit(solution)/shard_map/ppermute | solution.py:45
  7.7 2.2 %shard_map.101.rest = bf16[4096,512]{1,0:T(8,128)(2,1)S(1)} custom-call(bf16[8192,512]{1,0:T(8,128)(2,1)} %bitcast.31), custom_call_target="tpu_custom_call" | custom-call | bytes 16777216 | tf_op jit(solution)/shard_map/pallas_call | solution.py:68
  11.0 2.4 %collective-permute-start.3 = (bf16[16,8192]{1,0:T(8,128)(2,1)S(1)}, bf16[16,8192]{1,0:T(8,128)(2,1)S(1)}, u32[]{:S(2)}, u32[]{:S(2)}) collective-permute-start(bf16[16,8192]{1,0:T(8,128)(2,1)S(1)} %constant_dynamic-update-slice_fusion.2), channel_id=1, source_target_pairs={{0,8},{8,0},{16,24},{24,16},{1,9},{9,1},{17,25},{25,17},{2,10},{10... | collective-permute-start | bytes 786440 | tf_op jit(solution)/shard_map/ppermute | solution.py:35
  13.4 1.5 %collective-permute-start.4 = (bf16[16,8192]{1,0:T(8,128)(2,1)S(1)}, bf16[16,8192]{1,0:T(8,128)(2,1)S(1)}, u32[]{:S(2)}, u32[]{:S(2)}) collective-permute-start(bf16[16,8192]{1,0:T(8,128)(2,1)S(1)} %constant_dynamic-update-slice_fusion.2), channel_id=1, source_target_pairs={{0,16},{8,24},{16,0},{24,8},{1,17},{9,25},{17,1},{25,9},{2,18},{10... | collective-permute-start | bytes 786440 | tf_op jit(solution)/shard_map/ppermute | solution.py:35
  15.0 4.5 %shard_map.103.refs_0_ = bf16[320,512]{1,0:T(8,128)(2,1)S(1)} custom-call(bf16[512,8192]{1,0:T(8,128)(2,1)} %cotangent.1, bf16[512,8192]{1,0:T(8,128)(2,1)S(1)} %get-tuple-element.66.expand), custom_call_target="tpu_custom_call" | custom-call | flops 2684354560 | bytes 8388608 | tf_op jit(solution)/shard_map/pallas_call | solution.py:68
  20.2 3.5 %shard_map.105.hidden = bf16[64,8192]{1,0:T(8,128)(2,1)S(1)} custom-call(bf16[32,512]{1,0:T(8,128)(2,1)} %bitcast.39, bf16[4096,512]{1,0:T(8,128)(2,1)S(1)} %get-tuple-element.64.head, bf16[4096,512]{1,0:T(8,128)(2,1)S(1)} %shard_map.101.rest), custom_call_target="tpu_custom_call" | custom-call | flops 536870912 | bytes 8388608 | tf_op jit(solution)/shard_map/pallas_call | solution.py:68
  23.7 1.8 %collective-permute-done.4 = bf16[16,8192]{1,0:T(8,128)(2,1)S(1)} collective-permute-done((bf16[16,8192]{1,0:T(8,128)(2,1)S(1)}, bf16[16,8192]{1,0:T(8,128)(2,1)S(1)}, u32[]{:S(2)}, u32[]{:S(2)}) %collective-permute-start.4) | collective-permute-done | bytes 262176 | tf_op jit(solution)/shard_map/ppermute | solution.py:35
  27.9 1.3 %slice-done.3 = s8[4194304]{0:T(1024)(128)(4,1)S(1)} async-done(((s8[8388608]{0:T(1024)(128)(4,1)}), s8[4194304]{0:T(1024)(128)(4,1)S(1)}, s32[]{:S(2)}) %slice-start.3) | async-done | bytes 4194328
  29.2 2.7 %fusion.5 = (bf16[64,512]{1,0:T(8,128)(2,1)S(1)}, f32[64,512]{1,0:T(8,128)S(1)}) fusion(f32[512]{0:T(512)S(1)} %convert_bitcast_fusion, bf16[64,8192]{1,0:T(8,128)(2,1)S(1)} %get-tuple-element.83, bf16[1,512,8192]{2,1,0:T(8,128)(2,1)S(1)} %bitcast.34), kind=kOutput, calls=%fused_computation.12 | convolution fusion | flops 536936448 | bytes 9635840 | tf_op jit(solution)/shard_map/dot_general | solution.py:28
  31.9 9.6 %collective-permute-start.10 = (bf16[64,512]{1,0:T(8,128)(2,1)S(1)}, bf16[64,512]{1,0:T(8,128)(2,1)S(1)}, u32[]{:S(2)}, u32[]{:S(2)}) collective-permute-start(bf16[64,512]{1,0:T(8,128)(2,1)S(1)} %get-tuple-element.102.refs_2_), channel_id=1, source_target_pairs={{0,6},{1,7},{8,14},{9,15},{16,22},{17,23},{24,30},{25,31}} | collective-permute-start | bytes 196616 | tf_op jit(solution)/shard_map/ppermute | solution.py:45
  41.5 1.3 %collective-permute-start.8 = (bf16[64,512]{1,0:T(8,128)(2,1)S(1)}, bf16[64,512]{1,0:T(8,128)(2,1)S(1)}, u32[]{:S(2)}, u32[]{:S(2)}) collective-permute-start(bf16[64,512]{1,0:T(8,128)(2,1)S(1)} %get-tuple-element.102.refs_2_), channel_id=1, source_target_pairs={{0,2},{1,3},{2,4},{3,5},{4,6},{5,7},{8,10},{9,11},{10,12},{11,13},... | collective-permute-start | bytes 196616 | tf_op jit(solution)/shard_map/ppermute | solution.py:45
  42.8 2.7 %collective-permute-start.9 = (bf16[64,512]{1,0:T(8,128)(2,1)S(1)}, bf16[64,512]{1,0:T(8,128)(2,1)S(1)}, u32[]{:S(2)}, u32[]{:S(2)}) collective-permute-start(bf16[64,512]{1,0:T(8,128)(2,1)S(1)} %get-tuple-element.102.refs_2_), channel_id=1, source_target_pairs={{0,4},{1,5},{2,6},{3,7},{8,12},{9,13},{10,14},{11,15},{16,20},{17,... | collective-permute-start | bytes 196616 | tf_op jit(solution)/shard_map/ppermute | solution.py:45
  46.3 2.7 %fusion.6.right = f32[64,512]{1,0:T(8,128)S(1)} fusion(bf16[64,8192]{1,0:T(8,128)(2,1)S(1)} %get-tuple-element.86, bf16[512,8192]{1,0:T(8,128)(2,1)S(1)} %bitcast.29), kind=kOutput, calls=%fused_computation.13 | convolution fusion | flops 536870912 | bytes 9568256 | tf_op jit(solution)/shard_map/dot_general | solution.py:28
  49.7 1.6 %collective-permute-start.12 = (bf16[80,512]{1,0:T(8,128)(2,1)S(1)}, bf16[80,512]{1,0:T(8,128)(2,1)S(1)}, u32[]{:S(2)}, u32[]{:S(2)}) collective-permute-start(bf16[80,512]{1,0:T(8,128)(2,1)S(1)} %pad_maximum_fusion.2.refs_6_), channel_id=1, source_target_pairs={{0,8},{8,0},{16,24},{24,16},{1,9},{9,1},{17,25},{25,17},{2,10},{10... | collective-permute-start | bytes 245768 | tf_op jit(solution)/shard_map/ppermute | solution.py:35
  51.3 1.5 %collective-permute-start.13 = (bf16[80,512]{1,0:T(8,128)(2,1)S(1)}, bf16[80,512]{1,0:T(8,128)(2,1)S(1)}, u32[]{:S(2)}, u32[]{:S(2)}) collective-permute-start(bf16[80,512]{1,0:T(8,128)(2,1)S(1)} %pad_maximum_fusion.2.refs_6_), channel_id=1, source_target_pairs={{0,16},{8,24},{16,0},{24,8},{1,17},{9,25},{17,1},{25,9},{2,18},{10... | collective-permute-start | bytes 245768 | tf_op jit(solution)/shard_map/ppermute | solution.py:35
  53.3 4.2 %shard_map.110.refs_1_ = bf16[192,512]{1,0:T(8,128)(2,1)S(1)} custom-call(bf16[512,8192]{1,0:T(8,128)(2,1)} %cotangent.1, bf16[512,8192]{1,0:T(8,128)(2,1)S(1)} %get-tuple-element.66.expand), custom_call_target="tpu_custom_call" | custom-call | flops 1610612736 | bytes 8388608 | tf_op jit(solution)/shard_map/pallas_call | solution.py:68
  59.0 1.5 %collective-permute-done.16.others = bf16[4,64,512]{2,1,0:T(8,128)(2,1)S(1)} collective-permute-done((bf16[4,64,512]{2,1,0:T(8,128)(2,1)S(1)}, bf16[4,64,512]{2,1,0:T(8,128)(2,1)S(1)}, u32[]{:S(2)}, u32[]{:S(2)}) %collective-permute-start.16) | collective-permute-done | bytes 262176 | tf_op jit(solution)/shard_map/ppermute | solution.py:35
  61.7 1.5 %collective-permute-start.18 = (bf16[32,512]{1,0:T(8,128)(2,1)S(1)}, bf16[32,512]{1,0:T(8,128)(2,1)S(1)}, u32[]{:S(2)}, u32[]{:S(2)}) collective-permute-start(bf16[32,512]{1,0:T(8,128)(2,1)S(1)} %shard_map.112.refs_2_), channel_id=1, source_target_pairs={{0,16},{8,24},{16,0},{24,8},{1,17},{9,25},{17,1},{25,9},{2,18},{10... | collective-permute-start | bytes 98312 | tf_op jit(solution)/shard_map/ppermute | solution.py:35
  64.0 1.2 %shard_map.113.early = f32[8,64]{1,0:T(8,128)S(1)} custom-call(f32[64,512]{1,0:T(8,128)S(1)} %get-tuple-element.118.left, f32[64,512]{1,0:T(8,128)S(1)} %fusion.6.right, bf16[4,64,512]{2,1,0:T(8,128)(2,1)S(1)} %collective-permute-done.16.others, bf16[320,512]{1,0:T(8,128)(2,1)S(1)} %shard_map.103.refs_0_, bf16[192,512]{1,0:T(8,128)(2,1)S(1)} %shard_map.110.refs_1_, ...), custom_call_target="tpu_custom_call" | custom-call | flops 268435456 | bytes 8388608 | tf_op jit(solution)/shard_map/pallas_call | solution.py:68
  65.6 2.4 %collective-permute-done.19.refs_5_ = bf16[32,512]{1,0:T(8,128)(2,1)S(1)} collective-permute-done((bf16[32,512]{1,0:T(8,128)(2,1)S(1)}, bf16[32,512]{1,0:T(8,128)(2,1)S(1)}, u32[]{:S(2)}, u32[]{:S(2)}) %collective-permute-start.19) | collective-permute-done | bytes 32800 | tf_op jit(solution)/shard_map/ppermute | solution.py:35
  68.7 1.2 %collective-permute-done.20 = f32[8,64]{1,0:T(8,128)S(1)} collective-permute-done((f32[8,64]{1,0:T(8,128)S(1)}, f32[8,64]{1,0:T(8,128)S(1)}, u32[]{:S(2)}, u32[]{:S(2)}) %collective-permute-start.20) | collective-permute-done | bytes 2080 | tf_op jit(solution)/shard_map/ppermute | solution.py:35
  69.8 10.1 %collective-permute-start.22 = (f32[8,64]{1,0:T(8,128)S(1)}, f32[8,64]{1,0:T(8,128)S(1)}, u32[]{:S(2)}, u32[]{:S(2)}) collective-permute-start(f32[8,64]{1,0:T(8,128)S(1)} %add.3.refs_0_), channel_id=1, source_target_pairs={{0,4},{1,5},{2,6},{3,7},{4,0},{5,1},{6,2},{7,3},{8,12},{9,13},{10,... | collective-permute-start | bytes 6152 | tf_op jit(solution)/shard_map/ppermute | solution.py:52
  81.6 2.0 %collective-permute-done.23.refs_3_ = f32[8,64]{1,0:T(8,128)S(1)} collective-permute-done((f32[8,64]{1,0:T(8,128)S(1)}, f32[8,64]{1,0:T(8,128)S(1)}, u32[]{:S(2)}, u32[]{:S(2)}) %collective-permute-start.23) | collective-permute-done | bytes 2080 | tf_op jit(solution)/shard_map/ppermute | solution.py:52
  (71 shorter events, 12.9 us)
Async XLA Ops:
  5.4 4.7 %collective-permute-start = (bf16[16,8192]{1,0:T(8,128)(2,1)S(1)}, bf16[16,8192]{1,0:T(8,128)(2,1)S(1)}, u32[]{:S(2)}, u32[]{:S(2)}) collective-permute-start(bf16[16,8192]{1,0:T(8,128)(2,1)S(1)} %get-tuple-element.61), channel_id=1, source_target_pairs={{0,1},{2,3},{4,5},{6,7},{8,9},{10,11},{12,13},{14,15},{16,17},{18,... | collective-permute-start | bytes 786440 | tf_op jit(solution)/shard_map/ppermute | solution.py:45
  10.1 9.3 %collective-permute-start.1 = (bf16[32,8192]{1,0:T(8,128)(2,1)S(1)}, bf16[32,8192]{1,0:T(8,128)(2,1)S(1)}, u32[]{:S(2)}, u32[]{:S(2)}) collective-permute-start(bf16[32,8192]{1,0:T(8,128)(2,1)S(1)} %constant_dynamic-update-slice_fusion), channel_id=1, source_target_pairs={{1,2},{3,4},{5,6},{9,10},{11,12},{13,14},{17,18},{19,20},{21,22},{... | collective-permute-start | bytes 1572872 | tf_op jit(solution)/shard_map/ppermute | solution.py:45
  11.0 12.7 %collective-permute-start.3 = (bf16[16,8192]{1,0:T(8,128)(2,1)S(1)}, bf16[16,8192]{1,0:T(8,128)(2,1)S(1)}, u32[]{:S(2)}, u32[]{:S(2)}) collective-permute-start(bf16[16,8192]{1,0:T(8,128)(2,1)S(1)} %constant_dynamic-update-slice_fusion.2), channel_id=1, source_target_pairs={{0,8},{8,0},{16,24},{24,16},{1,9},{9,1},{17,25},{25,17},{2,10},{10... | collective-permute-start | bytes 786440 | tf_op jit(solution)/shard_map/ppermute | solution.py:35
  13.4 12.1 %collective-permute-start.4 = (bf16[16,8192]{1,0:T(8,128)(2,1)S(1)}, bf16[16,8192]{1,0:T(8,128)(2,1)S(1)}, u32[]{:S(2)}, u32[]{:S(2)}) collective-permute-start(bf16[16,8192]{1,0:T(8,128)(2,1)S(1)} %constant_dynamic-update-slice_fusion.2), channel_id=1, source_target_pairs={{0,16},{8,24},{16,0},{24,8},{1,17},{9,25},{17,1},{25,9},{2,18},{10... | collective-permute-start | bytes 786440 | tf_op jit(solution)/shard_map/ppermute | solution.py:35
  14.9 10.8 %collective-permute-start.5 = (bf16[16,8192]{1,0:T(8,128)(2,1)S(1)}, bf16[16,8192]{1,0:T(8,128)(2,1)S(1)}, u32[]{:S(2)}, u32[]{:S(2)}) collective-permute-start(bf16[16,8192]{1,0:T(8,128)(2,1)S(1)} %constant_dynamic-update-slice_fusion.2), channel_id=1, source_target_pairs={{0,24},{8,16},{16,8},{24,0},{1,25},{9,17},{17,9},{25,1},{2,26},{10... | collective-permute-start | bytes 786440 | tf_op jit(solution)/shard_map/ppermute | solution.py:35
  19.5 6.3 %collective-permute-start.2 = (bf16[32,8192]{1,0:T(8,128)(2,1)S(1)}, bf16[32,8192]{1,0:T(8,128)(2,1)S(1)}, u32[]{:S(2)}, u32[]{:S(2)}) collective-permute-start(bf16[32,8192]{1,0:T(8,128)(2,1)S(1)} %get-tuple-element.70), channel_id=1, source_target_pairs={{2,3},{4,5},{6,7},{10,11},{12,13},{14,15},{18,19},{20,21},{22,23},... | collective-permute-start | bytes 1572872 | tf_op jit(solution)/shard_map/ppermute | solution.py:45
  25.9 19.7 %collective-permute-start.6 = (bf16[32,8192]{1,0:T(8,128)(2,1)S(1)}, bf16[32,8192]{1,0:T(8,128)(2,1)S(1)}, u32[]{:S(2)}, u32[]{:S(2)}) collective-permute-start(bf16[32,8192]{1,0:T(8,128)(2,1)S(1)} %get-tuple-element.80), channel_id=1, source_target_pairs={{3,4},{5,6},{11,12},{13,14},{19,20},{21,22},{27,28},{29,30}} | collective-permute-start | bytes 1572872 | tf_op jit(solution)/shard_map/ppermute | solution.py:45
  31.9 17.0 %collective-permute-start.10 = (bf16[64,512]{1,0:T(8,128)(2,1)S(1)}, bf16[64,512]{1,0:T(8,128)(2,1)S(1)}, u32[]{:S(2)}, u32[]{:S(2)}) collective-permute-start(bf16[64,512]{1,0:T(8,128)(2,1)S(1)} %get-tuple-element.102.refs_2_), channel_id=1, source_target_pairs={{0,6},{1,7},{8,14},{9,15},{16,22},{17,23},{24,30},{25,31}} | collective-permute-start | bytes 196616 | tf_op jit(solution)/shard_map/ppermute | solution.py:45
  41.5 7.5 %collective-permute-start.8 = (bf16[64,512]{1,0:T(8,128)(2,1)S(1)}, bf16[64,512]{1,0:T(8,128)(2,1)S(1)}, u32[]{:S(2)}, u32[]{:S(2)}) collective-permute-start(bf16[64,512]{1,0:T(8,128)(2,1)S(1)} %get-tuple-element.102.refs_2_), channel_id=1, source_target_pairs={{0,2},{1,3},{2,4},{3,5},{4,6},{5,7},{8,10},{9,11},{10,12},{11,13},... | collective-permute-start | bytes 196616 | tf_op jit(solution)/shard_map/ppermute | solution.py:45
  42.8 6.2 %collective-permute-start.9 = (bf16[64,512]{1,0:T(8,128)(2,1)S(1)}, bf16[64,512]{1,0:T(8,128)(2,1)S(1)}, u32[]{:S(2)}, u32[]{:S(2)}) collective-permute-start(bf16[64,512]{1,0:T(8,128)(2,1)S(1)} %get-tuple-element.102.refs_2_), channel_id=1, source_target_pairs={{0,4},{1,5},{2,6},{3,7},{8,12},{9,13},{10,14},{11,15},{16,20},{17,... | collective-permute-start | bytes 196616 | tf_op jit(solution)/shard_map/ppermute | solution.py:45
  45.6 3.4 %collective-permute-start.7 = (bf16[32,8192]{1,0:T(8,128)(2,1)S(1)}, bf16[32,8192]{1,0:T(8,128)(2,1)S(1)}, u32[]{:S(2)}, u32[]{:S(2)}) collective-permute-start(bf16[32,8192]{1,0:T(8,128)(2,1)S(1)} %get-tuple-element.85), channel_id=1, source_target_pairs={{4,5},{6,7},{12,13},{14,15},{20,21},{22,23},{28,29},{30,31}} | collective-permute-start | bytes 1572872 | tf_op jit(solution)/shard_map/ppermute | solution.py:45
  49.0 9.1 %collective-permute-start.11 = (bf16[32,8192]{1,0:T(8,128)(2,1)S(1)}, bf16[32,8192]{1,0:T(8,128)(2,1)S(1)}, u32[]{:S(2)}, u32[]{:S(2)}) collective-permute-start(bf16[32,8192]{1,0:T(8,128)(2,1)S(1)} %get-tuple-element.91), channel_id=1, source_target_pairs={{5,6},{13,14},{21,22},{29,30}} | collective-permute-start | bytes 1572872 | tf_op jit(solution)/shard_map/ppermute | solution.py:45
  49.7 7.8 %collective-permute-start.12 = (bf16[80,512]{1,0:T(8,128)(2,1)S(1)}, bf16[80,512]{1,0:T(8,128)(2,1)S(1)}, u32[]{:S(2)}, u32[]{:S(2)}) collective-permute-start(bf16[80,512]{1,0:T(8,128)(2,1)S(1)} %pad_maximum_fusion.2.refs_6_), channel_id=1, source_target_pairs={{0,8},{8,0},{16,24},{24,16},{1,9},{9,1},{17,25},{25,17},{2,10},{10... | collective-permute-start | bytes 245768 | tf_op jit(solution)/shard_map/ppermute | solution.py:35
  51.3 6.2 %collective-permute-start.13 = (bf16[80,512]{1,0:T(8,128)(2,1)S(1)}, bf16[80,512]{1,0:T(8,128)(2,1)S(1)}, u32[]{:S(2)}, u32[]{:S(2)}) collective-permute-start(bf16[80,512]{1,0:T(8,128)(2,1)S(1)} %pad_maximum_fusion.2.refs_6_), channel_id=1, source_target_pairs={{0,16},{8,24},{16,0},{24,8},{1,17},{9,25},{17,1},{25,9},{2,18},{10... | collective-permute-start | bytes 245768 | tf_op jit(solution)/shard_map/ppermute | solution.py:35
  52.8 5.3 %collective-permute-start.14 = (bf16[80,512]{1,0:T(8,128)(2,1)S(1)}, bf16[80,512]{1,0:T(8,128)(2,1)S(1)}, u32[]{:S(2)}, u32[]{:S(2)}) collective-permute-start(bf16[80,512]{1,0:T(8,128)(2,1)S(1)} %pad_maximum_fusion.2.refs_6_), channel_id=1, source_target_pairs={{0,24},{8,16},{16,8},{24,0},{1,25},{9,17},{17,9},{25,1},{2,26},{10... | collective-permute-start | bytes 245768 | tf_op jit(solution)/shard_map/ppermute | solution.py:35
  58.2 2.4 %collective-permute-start.15 = (bf16[32,8192]{1,0:T(8,128)(2,1)S(1)}, bf16[32,8192]{1,0:T(8,128)(2,1)S(1)}, u32[]{:S(2)}, u32[]{:S(2)}) collective-permute-start(bf16[32,8192]{1,0:T(8,128)(2,1)S(1)} %get-tuple-element.98), channel_id=1, source_target_pairs={{6,7},{14,15},{22,23},{30,31}} | collective-permute-start | bytes 1572872 | tf_op jit(solution)/shard_map/ppermute | solution.py:45
  58.9 1.6 %collective-permute-start.16 = (bf16[4,64,512]{2,1,0:T(8,128)(2,1)S(1)}, bf16[4,64,512]{2,1,0:T(8,128)(2,1)S(1)}, u32[]{:S(2)}, u32[]{:S(2)}) collective-permute-start(bf16[4,64,512]{2,1,0:T(8,128)(2,1)S(1)} %pad_maximum_fusion.1), channel_id=1, source_target_pairs={{0,1},{1,0},{2,3},{3,2},{4,5},{5,4},{6,7},{7,6},{8,9},{9,8},{10,11... | collective-permute-start | bytes 786440 | tf_op jit(solution)/shard_map/ppermute | solution.py:35
  60.5 4.7 %collective-permute-start.17 = (bf16[32,512]{1,0:T(8,128)(2,1)S(1)}, bf16[32,512]{1,0:T(8,128)(2,1)S(1)}, u32[]{:S(2)}, u32[]{:S(2)}) collective-permute-start(bf16[32,512]{1,0:T(8,128)(2,1)S(1)} %shard_map.112.refs_2_), channel_id=1, source_target_pairs={{0,8},{8,0},{16,24},{24,16},{1,9},{9,1},{17,25},{25,17},{2,10},{10... | collective-permute-start | bytes 98312 | tf_op jit(solution)/shard_map/ppermute | solution.py:35
  61.7 3.9 %collective-permute-start.18 = (bf16[32,512]{1,0:T(8,128)(2,1)S(1)}, bf16[32,512]{1,0:T(8,128)(2,1)S(1)}, u32[]{:S(2)}, u32[]{:S(2)}) collective-permute-start(bf16[32,512]{1,0:T(8,128)(2,1)S(1)} %shard_map.112.refs_2_), channel_id=1, source_target_pairs={{0,16},{8,24},{16,0},{24,8},{1,17},{9,25},{17,1},{25,9},{2,18},{10... | collective-permute-start | bytes 98312 | tf_op jit(solution)/shard_map/ppermute | solution.py:35
  63.2 4.8 %collective-permute-start.19 = (bf16[32,512]{1,0:T(8,128)(2,1)S(1)}, bf16[32,512]{1,0:T(8,128)(2,1)S(1)}, u32[]{:S(2)}, u32[]{:S(2)}) collective-permute-start(bf16[32,512]{1,0:T(8,128)(2,1)S(1)} %shard_map.112.refs_2_), channel_id=1, source_target_pairs={{0,24},{8,16},{16,8},{24,0},{1,25},{9,17},{17,9},{25,1},{2,26},{10... | collective-permute-start | bytes 98312 | tf_op jit(solution)/shard_map/ppermute | solution.py:35
  68.7 1.2 %collective-permute-start.20 = (f32[8,64]{1,0:T(8,128)S(1)}, f32[8,64]{1,0:T(8,128)S(1)}, u32[]{:S(2)}, u32[]{:S(2)}) collective-permute-start(f32[8,64]{1,0:T(8,128)S(1)} %shard_map.114), channel_id=1, source_target_pairs={{0,1},{1,0},{2,3},{3,2},{4,5},{5,4},{6,7},{7,6},{8,9},{9,8},{10,11... | collective-permute-start | bytes 6152 | tf_op jit(solution)/shard_map/ppermute | solution.py:35
  69.8 11.1 %collective-permute-start.21 = (f32[8,64]{1,0:T(8,128)S(1)}, f32[8,64]{1,0:T(8,128)S(1)}, u32[]{:S(2)}, u32[]{:S(2)}) collective-permute-start(f32[8,64]{1,0:T(8,128)S(1)} %add.3.refs_0_), channel_id=1, source_target_pairs={{0,2},{1,3},{2,4},{3,5},{4,6},{5,7},{6,0},{7,1},{8,10},{9,11},{10,... | collective-permute-start | bytes 6152 | tf_op jit(solution)/shard_map/ppermute | solution.py:52
  69.8 11.7 %collective-permute-start.22 = (f32[8,64]{1,0:T(8,128)S(1)}, f32[8,64]{1,0:T(8,128)S(1)}, u32[]{:S(2)}, u32[]{:S(2)}) collective-permute-start(f32[8,64]{1,0:T(8,128)S(1)} %add.3.refs_0_), channel_id=1, source_target_pairs={{0,4},{1,5},{2,6},{3,7},{4,0},{5,1},{6,2},{7,3},{8,12},{9,13},{10,... | collective-permute-start | bytes 6152 | tf_op jit(solution)/shard_map/ppermute | solution.py:52
  80.0 3.6 %collective-permute-start.23 = (f32[8,64]{1,0:T(8,128)S(1)}, f32[8,64]{1,0:T(8,128)S(1)}, u32[]{:S(2)}, u32[]{:S(2)}) collective-permute-start(f32[8,64]{1,0:T(8,128)S(1)} %add.3.refs_0_), channel_id=1, source_target_pairs={{0,6},{1,7},{2,0},{3,1},{4,2},{5,3},{6,4},{7,5},{8,14},{9,15},{10,... | collective-permute-start | bytes 6152 | tf_op jit(solution)/shard_map/ppermute | solution.py:52
  (8 other events, 66.3 us)
